TPU v7x, 32 devices: a whole 2x2x4 slice. The times are simulated.
32 devices in a mesh: row: 8 (over z, y), col: 4 (over x, core).
Axes of the slice: x: 2, y: 2, z: 4, core: 2. Of those that a mesh axis runs over, the one named last changes fastest.
Arguments:
- right_side: float32 [3, 8192, 512], P(None, 'row', 'col'), may hold values from -48 to 48
- onsite: float32 [8192], P('row'), may hold values from 8 to 16
- energies: float32 [512], P('col'), may hold values from -1 to -0.25
- ks_tiles: bfloat16 [64, 24, 128, 128], P('row'), may hold values from -1 to 1
- correlation_tiles: bfloat16 [64, 8, 128, 128], P('row'), may hold values from -0.1875 to 0.1875
- tile_slot: int32 [64, 24], P('row'), may hold values from 0 to 27, as said below
- readers: int32 [8, 7, 4], P('row'), may hold values from 0 to 7, as said below
Outputs:
- solution_field: float32 [3, 8192, 512], P(None, 'row', 'col')
- residual: float32 [3, 8192, 512], P(None, 'row', 'col')
Inputs may be any that keep to these rules, and one draw needn't show every extreme that they name: readers[p, o] holds 4 distinct local cluster numbers of row device p; they are read by the row device whose index is p - o + 3, cyclically. `tile_slot`: slots are distinct within one cluster row; on each row device every slot is named by some tile.
All inputs are finite; a program needn't handle non-finite values.
Results may differ from a plain program's by a relative error of at most 0.0023.
Values may be sent and summed in bfloat16 or wider, within the bound.
No kernel may reach another device: no remote copies, remote signals or barrier semaphores. Data moves between devices by JAX's collectives and lax.ppermute only.
A program may use at most 128 MiB of HBM per device.

v0:
```python
import jax
import jax.numpy as jnp
from jax import lax
from jax.sharding import PartitionSpec as P

ITERS = 2


def shifted(array, axis, by):
    count = lax.axis_size(axis)
    return lax.ppermute(array, axis, [(i, (i + by) % count) for i in range(count)])


def body(right_side, onsite, energies, ks_tiles, correlation_tiles, tile_slot, readers):
    fields, rows, orbitals = right_side.shape
    clusters, tiles_row, width, _ = ks_tiles.shape
    tiles_correlation = correlation_tiles.shape[1]
    span = readers.shape[1]
    served = readers.shape[2]
    middle = (span - 1) // 2
    slots = span * served
    onehot = (tile_slot[:, :, None] == jnp.arange(slots, dtype=jnp.int32)[None, None, :]).astype(
        jnp.bfloat16
    )
    dense_ks = jnp.einsum("cks,ckab->casb", onehot, ks_tiles, preferred_element_type=jnp.float32)
    dense_ks = dense_ks.astype(jnp.bfloat16).reshape(clusters * width, slots * width)
    correlation_slot = tile_slot[:, :tiles_correlation]

    def squares(vector):
        return lax.psum(jnp.sum(vector * vector, axis=(1, 2)), ("row", "col"))

    solution_field = jnp.zeros_like(right_side)
    residual = right_side
    direction = right_side
    norm_now = squares(residual)
    for step in range(ITERS):
        blocks = direction.astype(jnp.bfloat16).reshape(fields, clusters, width, orbitals)
        outgoing = blocks[:, readers[0]]
        pieces = []
        for offset in range(span):
            if offset == middle:
                pieces.append(outgoing[:, offset])
            else:
                pieces.append(shifted(outgoing[:, offset], "row", middle - offset))
        received = jnp.stack(pieces, 1)
        gathered = received.reshape(fields, slots * width, orbitals)
        ks_part = jnp.einsum("rk,fkj->frj", dense_ks, gathered, preferred_element_type=jnp.float32)
        picked = gathered.reshape(fields, slots, width, orbitals)[:, correlation_slot]
        ov_part = jnp.einsum(
            "ckab,fckbj->fcaj", correlation_tiles, picked, preferred_element_type=jnp.float32
        )
        ov_part = ov_part.reshape(fields, rows, orbitals)
        image = onsite[None, :, None] * direction + (ks_part - ov_part * energies[None, None, :])
        bend = lax.psum(jnp.sum(direction * image, axis=(1, 2)), ("row", "col"))
        alpha = (norm_now / bend)[:, None, None]
        solution_field = solution_field + alpha * direction
        residual = residual - alpha * image
        norm_next = squares(residual)
        direction = residual + (norm_next / norm_now)[:, None, None] * direction
        norm_now = norm_next
    return (solution_field, residual)


def solution(mesh):
    placed = (
        P(None, "row", "col"),
        P("row"),
        P("col"),
        P("row", None, None, None),
        P("row", None, None, None),
        P("row", None),
        P("row", None, None),
    )
    return jax.shard_map(
        body,
        mesh=mesh,
        in_specs=placed,
        out_specs=(P(None, "row", "col"), P(None, "row", "col")),
        check_vma=False,
    )
```

profile of v0, /device:TPU:0, one launch (start us, length us, event | category | flops | bytes accessed | tf_op | source)
XLA Modules:
  0.0 405.5 jit_solution(16017202387931553153)
XLA Ops:
  2.4 2.2 multiply_reduce_fusion.3
  4.7 2.5 gather_fusion
  7.2 1.5 slice_bitcast_fusion.9
  8.6 4.0 collective-permute-start
  12.7 1.6 collective-permute-start.1
  14.2 1.5 collective-permute-start.2
  15.8 32.3 %collective-permute-done = bf16[3,4,128,128]{3,2,0,1:T(8,128)(2,1)S(1)} collective-permute-done((bf16[3,4,128,128]{3,2,0,1:T(8,128)(2,1)S(1)}, bf16[3,4,128,128]{3,2,0,1:T(8,128)(2,1)S(1)}, u32[]{:S(2)}, u32[]{:S(2)}) %collective-permute-start) | collective-permute-done | bytes 393248 | tf_op jit(solution)/shard_map/ppermute | solution.py:11
  52.3 11.1 %convert_bitcast_fusion = bf16[8,128,28,128]{3,2,1,0:T(8,128)(2,1)} fusion(bf16[8,24,128,128]{3,2,1,0:T(8,128)(2,1)} %param.10, s32[8,24]{1,0:T(8,128)S(1)} %copy-done.4), kind=kOutput, calls=%fused_computation.4 | convolution fusion | flops 179836160 | bytes 13632256 | tf_op jit(solution)/shard_map/cks,ckab->casb/dot_general | solution.py:25
  63.5 3.0 copy.42
  66.5 12.8 %reshape.105 = bf16[1024,3584,1]{1,0,2:T(8,128)(2,1)} reshape(bf16[8,128,28,128]{3,2,1,0:T(8,128)(2,1)} %convert_bitcast_fusion) | data formatting | bytes 14680064 | tf_op jit(solution)/shard_map/reshape | solution.py:26
  79.3 10.0 %collective-permute-start.5 = (bf16[3,4,128,128]{3,2,0,1:T(8,128)(2,1)S(1)}, bf16[3,4,128,128]{3,2,0,1:T(8,128)(2,1)S(1)}, u32[]{:S(2)}, u32[]{:S(2)}) collective-permute-start(bf16[3,4,128,128]{3,2,0,1:T(8,128)(2,1)S(1)} %get-tuple-element.17), channel_id=1, source_target_pairs={{0,20},{4,24},{8,28},{12,0},{16,4},{20,8},{24,12},{28,16},{1,21},{... | collective-permute-start | bytes 1179656 | tf_op jit(solution)/shard_map/ppermute | solution.py:11
  89.3 1.8 bitcast_dynamic-update-slice_fusion.8
  91.1 1.8 bitcast_dynamic-update-slice_fusion.7
  92.9 4.7 %collective-permute-done.5 = bf16[3,4,128,128]{3,2,0,1:T(8,128)(2,1)S(1)} collective-permute-done((bf16[3,4,128,128]{3,2,0,1:T(8,128)(2,1)S(1)}, bf16[3,4,128,128]{3,2,0,1:T(8,128)(2,1)S(1)}, u32[]{:S(2)}, u32[]{:S(2)}) %collective-permute-start.5) | collective-permute-done | bytes 393248 | tf_op jit(solution)/shard_map/ppermute | solution.py:11
  98.4 3.7 copy.39
  102.1 6.1 %copy.35 = bf16[3,7,4,128,128]{3,2,1,4,0:T(4,128)(2,1)} copy(bf16[3,7,4,128,128]{4,3,0,2,1:T(8,128)(2,1)} %bitcast_dynamic-update-slice_fusion.6) | data formatting | bytes 5505024 | tf_op jit(solution)/shard_map/stack | solution.py:45
  108.2 5.6 %reshape.60 = bf16[3,3584,128]{1,2,0:T(8,128)(2,1)} reshape(bf16[3,7,4,128,128]{3,2,1,4,0:T(4,128)(2,1)} %copy.35) | data formatting | bytes 5505024 | tf_op jit(solution)/shard_map/reshape | solution.py:46
  113.8 5.7 %gather_fusion.1 = bf16[64,3,128,128]{3,2,1,0:T(8,128)(2,1)} fusion(bf16[3,28,128,128]{3,2,1,0:T(8,128)(2,1)} %bitcast.129, s32[1024]{0:T(1024)S(1)} %get-tuple-element.32), kind=kCustom, calls=%fused_computation.1 | custom fusion | bytes 12583168 | tf_op jit(solution)/shard_map/gather | solution.py:48
  119.5 5.2 %fusion.7 = f32[3,8,128,128]{3,2,0,1:T(8,128)} fusion(bf16[3,8,8,128,128]{4,3,0,2,1:T(8,128)(2,1)} %bitcast.132, bf16[8,8,128,128]{3,2,1,0:T(8,128)(2,1)S(1)} %copy-done), kind=kOutput, calls=%fused_computation.22 | convolution fusion | flops 805306368 | bytes 9961472 | tf_op jit(solution)/shard_map/ckab,fckbj->fcaj/dot_general | solution.py:49
  124.7 3.1 copy.41
  127.7 2.5 reshape.62
  130.3 9.0 %multiply_reduce_fusion.2 = (f32[3]{0:T(128)S(1)}, f32[3,1024,128]{1,2,0:T(8,128)}) fusion(f32[3,1024,128]{1,2,0:T(8,128)} %copy.42, f32[3,1024,128]{1,2,0:T(8,128)} %reshape.62, f32[128]{0:T(128)S(1)} %copy-done.6, bf16[3,3584,128]{1,2,0:T(8,128)(2,1)} %reshape.60, bf16[1024,3584,1]{1,0,2:T(8,128)(2,1)} %reshape.105, f32[1024]{0:T(1024)S(1)} %copy-done.5), kind=kOutput, calls=%fused_computation.20 | convolution fusion | flops 2820931584 | bytes 14815756 | tf_op jit(solution)/shard_map/rk,fkj->frj/dot_general | solution.py:47
  139.3 48.9 %all-reduce = (f32[3]{0:T(128)S(1)}, f32[3]{0:T(128)S(1)}) all-reduce(f32[3]{0:T(128)S(1)} %get-tuple-element.26, f32[3]{0:T(128)S(1)} %get-tuple-element.28), channel_id=1, replica_groups=mesh['row'=8,'col'=4] {'row','col'}, use_global_device_ids=true, to_apply=%region_1.0 | all-reduce | flops 6 | bytes 48 | tf_op jit(solution)/shard_map/psum | solution.py:30
  188.2 2.3 multiply_reduce_fusion.1
  190.5 40.6 %psum.30 = f32[3]{0:T(128)S(1)} all-reduce(f32[3]{0:T(128)S(1)} %multiply_reduce_fusion.1), channel_id=1, replica_groups=mesh['row'=8,'col'=4] {'row','col'}, use_global_device_ids=true, to_apply=%region_5.0 | all-reduce | flops 3 | bytes 24 | tf_op jit(solution)/shard_map/psum | solution.py:30
  231.1 4.0 fusion.16
  235.1 1.5 copy.61
  236.6 2.5 gather_fusion.2
  239.1 1.5 slice_bitcast_fusion.3
  240.6 1.7 collective-permute-start.6
  244.9 32.9 %collective-permute-done.6 = bf16[3,4,128,128]{3,2,0,1:T(8,128)(2,1)S(1)} collective-permute-done((bf16[3,4,128,128]{3,2,0,1:T(8,128)(2,1)S(1)}, bf16[3,4,128,128]{3,2,0,1:T(8,128)(2,1)S(1)}, u32[]{:S(2)}, u32[]{:S(2)}) %collective-permute-start.6) | collective-permute-done | bytes 393248 | tf_op jit(solution)/shard_map/ppermute | solution.py:11
  279.2 1.4 collective-permute-start.11
  280.7 8.7 %collective-permute-done.9 = bf16[3,4,128,128]{3,2,0,1:T(8,128)(2,1)S(1)} collective-permute-done((bf16[3,4,128,128]{3,2,0,1:T(8,128)(2,1)S(1)}, bf16[3,4,128,128]{3,2,0,1:T(8,128)(2,1)S(1)}, u32[]{:S(2)}, u32[]{:S(2)}) %collective-permute-start.9) | collective-permute-done | bytes 393248 | tf_op jit(solution)/shard_map/ppermute | solution.py:11
  289.4 6.8 %collective-permute-done.10 = bf16[3,4,128,128]{3,2,0,1:T(8,128)(2,1)S(1)} collective-permute-done((bf16[3,4,128,128]{3,2,0,1:T(8,128)(2,1)S(1)}, bf16[3,4,128,128]{3,2,0,1:T(8,128)(2,1)S(1)}, u32[]{:S(2)}, u32[]{:S(2)}) %collective-permute-start.10) | collective-permute-done | bytes 393248 | tf_op jit(solution)/shard_map/ppermute | solution.py:11
  296.3 7.2 %collective-permute-done.11 = bf16[3,4,128,128]{3,2,0,1:T(8,128)(2,1)S(1)} collective-permute-done((bf16[3,4,128,128]{3,2,0,1:T(8,128)(2,1)S(1)}, bf16[3,4,128,128]{3,2,0,1:T(8,128)(2,1)S(1)}, u32[]{:S(2)}, u32[]{:S(2)}) %collective-permute-start.11) | collective-permute-done | bytes 393248 | tf_op jit(solution)/shard_map/ppermute | solution.py:11
  303.6 1.5 copy-done.1
  305.1 1.8 copy.49
  306.9 6.1 %copy.47 = bf16[3,7,4,128,128]{3,2,1,4,0:T(4,128)(2,1)} copy(bf16[3,7,4,128,128]{4,3,0,2,1:T(8,128)(2,1)} %copy-done.1) | data formatting | bytes 5505024 | tf_op jit(solution)/shard_map/stack | solution.py:45
  313.0 5.6 %reshape.64 = bf16[3,3584,128]{1,2,0:T(8,128)(2,1)} reshape(bf16[3,7,4,128,128]{3,2,1,4,0:T(4,128)(2,1)} %copy.47) | data formatting | bytes 5505024 | tf_op jit(solution)/shard_map/reshape | solution.py:46
  318.6 5.7 %gather_fusion.3 = bf16[64,3,128,128]{3,2,1,0:T(8,128)(2,1)} fusion(bf16[3,28,128,128]{3,2,1,0:T(8,128)(2,1)} %bitcast.130, s32[1024]{0:T(1024)S(1)} %get-tuple-element.32), kind=kCustom, calls=%fused_computation.3 | custom fusion | bytes 12583168 | tf_op jit(solution)/shard_map/gather | solution.py:48
  324.3 5.3 %fusion.10 = f32[3,8,128,128]{3,2,0,1:T(8,128)} fusion(bf16[3,8,8,128,128]{4,3,0,2,1:T(8,128)(2,1)} %bitcast.131, bf16[8,8,128,128]{3,2,1,0:T(8,128)(2,1)S(1)} %copy-done), kind=kOutput, calls=%fused_computation.23 | convolution fusion | flops 805306368 | bytes 9961472 | tf_op jit(solution)/shard_map/ckab,fckbj->fcaj/dot_general | solution.py:49
  329.6 3.0 copy.51
  332.6 2.6 reshape.65
  335.2 9.1 %multiply_reduce_fusion = (f32[3]{0:T(128)S(1)}, f32[3,1024,128]{1,2,0:T(8,128)}) fusion(f32[3,1024,128]{1,2,0:T(8,128)} %get-tuple-element.9, f32[3,1024,128]{1,2,0:T(8,128)} %reshape.65, f32[128]{0:T(128)S(1)} %copy-done.6, bf16[3,3584,128]{1,2,0:T(8,128)(2,1)} %reshape.64, bf16[1024,3584,1]{1,0,2:T(8,128)(2,1)} %reshape.105, f32[1024]{0:T(1024)S(1)} %copy-done.5), kind=kOutput, calls=%fused_computation.16 | convolution fusion | flops 2820931584 | bytes 14815756 | tf_op jit(solution)/shard_map/rk,fkj->frj/dot_general | solution.py:47
  344.3 49.4 %psum.31 = f32[3]{0:T(128)S(1)} all-reduce(f32[3]{0:T(128)S(1)} %get-tuple-element.30), channel_id=1, replica_groups=mesh['row'=8,'col'=4] {'row','col'}, use_global_device_ids=true, to_apply=%region_7.0 | all-reduce | flops 3 | bytes 24 | tf_op jit(solution)/shard_map/psum | solution.py:54
  393.8 5.6 %multiply_subtract_fusion = (f32[3,1024,128]{1,2,0:T(8,128)}, f32[3,1024,128]{1,2,0:T(8,128)}) fusion(f32[3,1024,128]{1,2,0:T(8,128)} %get-tuple-element.31, f32[3]{0:T(128)S(1)} %div.11, f32[3,1024,128]{1,2,0:T(8,128)} %copy.42, f32[3,1024,128]{1,2,0:T(8,128)} %get-tuple-element.29, f32[3]{0:T(128)S(1)} %div.9, f32[3,1024,128]{1,2,0:T(8,128)} %get-tuple-element.9), kind=kLoop, calls=%fused_computation.14 | loop fusion | flops 2752512 | bytes 9437208 | tf_op jit(solution)/shard_map/sub | solution.py:57
  399.4 3.0 copy.53
  402.5 3.0 copy.52
  (46 shorter events, 11.1 us)
Async XLA Ops:
  0.6 118.8 %copy-start = (bf16[8,8,128,128]{3,2,1,0:T(8,128)(2,1)S(1)}, bf16[8,8,128,128]{3,2,1,0:T(8,128)(2,1)}, u32[]{:S(2)}) copy-start(bf16[8,8,128,128]{3,2,1,0:T(8,128)(2,1)} %param.11) | copy-start | bytes 6291460
  7.2 43.3 %copy-start.3 = (bf16[28,3,128,128]{3,2,1,0:T(8,128)(2,1)S(1)}, bf16[28,3,128,128]{3,2,1,0:T(8,128)(2,1)}, u32[]{:S(2)}) copy-start(bf16[28,3,128,128]{3,2,1,0:T(8,128)(2,1)} %gather_fusion) | copy-start | bytes 8257540
  8.6 39.4 %collective-permute-start = (bf16[3,4,128,128]{3,2,0,1:T(8,128)(2,1)S(1)}, bf16[3,4,128,128]{3,2,0,1:T(8,128)(2,1)S(1)}, u32[]{:S(2)}, u32[]{:S(2)}) collective-permute-start(bf16[3,4,128,128]{3,2,0,1:T(8,128)(2,1)S(1)} %get-tuple-element.23), channel_id=1, source_target_pairs={{0,12},{4,16},{8,20},{12,24},{16,28},{20,0},{24,4},{28,8},{1,13},{... | collective-permute-start | bytes 1179656 | tf_op jit(solution)/shard_map/ppermute | solution.py:11
  12.7 36.2 %collective-permute-start.1 = (bf16[3,4,128,128]{3,2,0,1:T(8,128)(2,1)S(1)}, bf16[3,4,128,128]{3,2,0,1:T(8,128)(2,1)S(1)}, u32[]{:S(2)}, u32[]{:S(2)}) collective-permute-start(bf16[3,4,128,128]{3,2,0,1:T(8,128)(2,1)S(1)} %get-tuple-element.22), channel_id=1, source_target_pairs={{0,8},{4,12},{8,16},{12,20},{16,24},{20,28},{24,0},{28,4},{1,9},{5... | collective-permute-start | bytes 1179656 | tf_op jit(solution)/shard_map/ppermute | solution.py:11
  14.2 38.1 %copy-start.4 = (s32[8,24]{1,0:T(8,128)S(1)}, s32[8,24]{1,0:T(8,128)}, u32[]{:S(2)}) copy-start(s32[8,24]{1,0:T(8,128)} %param.12) | copy-start | bytes 2308
  14.2 35.4 %collective-permute-start.2 = (bf16[3,4,128,128]{3,2,0,1:T(8,128)(2,1)S(1)}, bf16[3,4,128,128]{3,2,0,1:T(8,128)(2,1)S(1)}, u32[]{:S(2)}, u32[]{:S(2)}) collective-permute-start(bf16[3,4,128,128]{3,2,0,1:T(8,128)(2,1)S(1)} %get-tuple-element.21), channel_id=1, source_target_pairs={{0,4},{4,8},{8,12},{12,16},{16,20},{20,24},{24,28},{28,0},{1,5},{5... | collective-permute-start | bytes 1179656 | tf_op jit(solution)/shard_map/ppermute | solution.py:11
  51.3 39.7 %collective-permute-start.4 = (bf16[3,4,128,128]{3,2,0,1:T(8,128)(2,1)S(1)}, bf16[3,4,128,128]{3,2,0,1:T(8,128)(2,1)}, u32[]{:S(2)}, u32[]{:S(2)}) collective-permute-start(bf16[3,4,128,128]{3,2,0,1:T(8,128)(2,1)S(1)} %get-tuple-element.18), channel_id=1, source_target_pairs={{0,24},{4,28},{8,0},{12,4},{16,8},{20,12},{24,16},{28,20},{1,25},{... | collective-permute-start | bytes 1179656 | tf_op jit(solution)/shard_map/ppermute | solution.py:11
  51.3 37.9 %collective-permute-start.3 = (bf16[3,4,128,128]{3,2,0,1:T(8,128)(2,1)S(1)}, bf16[3,4,128,128]{3,2,0,1:T(8,128)(2,1)}, u32[]{:S(2)}, u32[]{:S(2)}) collective-permute-start(bf16[3,4,128,128]{3,2,0,1:T(8,128)(2,1)S(1)} %get-tuple-element.19), channel_id=1, source_target_pairs={{0,28},{4,0},{8,4},{12,8},{16,12},{20,16},{24,20},{28,24},{1,29},{... | collective-permute-start | bytes 1179656 | tf_op jit(solution)/shard_map/ppermute | solution.py:11
  79.3 18.3 %collective-permute-start.5 = (bf16[3,4,128,128]{3,2,0,1:T(8,128)(2,1)S(1)}, bf16[3,4,128,128]{3,2,0,1:T(8,128)(2,1)S(1)}, u32[]{:S(2)}, u32[]{:S(2)}) collective-permute-start(bf16[3,4,128,128]{3,2,0,1:T(8,128)(2,1)S(1)} %get-tuple-element.17), channel_id=1, source_target_pairs={{0,20},{4,24},{8,28},{12,0},{16,4},{20,8},{24,12},{28,16},{1,21},{... | collective-permute-start | bytes 1179656 | tf_op jit(solution)/shard_map/ppermute | solution.py:11
  124.7 5.6 %copy-start.5 = (f32[1024]{0:T(1024)S(1)}, f32[1024]{0:T(1024)}, u32[]{:S(2)}) copy-start(f32[1024]{0:T(1024)} %param.8) | copy-start | bytes 12292
  124.7 5.6 %copy-start.6 = (f32[128]{0:T(128)S(1)}, f32[128]{0:T(128)}, u32[]{:S(2)}) copy-start(f32[128]{0:T(128)} %param.9) | copy-start | bytes 1540
  239.1 38.8 %copy-start.2 = (bf16[28,3,128,128]{3,2,1,0:T(8,128)(2,1)S(1)}, bf16[28,3,128,128]{3,2,1,0:T(8,128)(2,1)}, u32[]{:S(2)}) copy-start(bf16[28,3,128,128]{3,2,1,0:T(8,128)(2,1)} %gather_fusion.2) | copy-start | bytes 8257540
  240.6 37.2 %collective-permute-start.6 = (bf16[3,4,128,128]{3,2,0,1:T(8,128)(2,1)S(1)}, bf16[3,4,128,128]{3,2,0,1:T(8,128)(2,1)S(1)}, u32[]{:S(2)}, u32[]{:S(2)}) collective-permute-start(bf16[3,4,128,128]{3,2,0,1:T(8,128)(2,1)S(1)} %get-tuple-element.16), channel_id=1, source_target_pairs={{0,12},{4,16},{8,20},{12,24},{16,28},{20,0},{24,4},{28,8},{1,13},{... | collective-permute-start | bytes 1179656 | tf_op jit(solution)/shard_map/ppermute | solution.py:11
  242.3 35.5 %collective-permute-start.7 = (bf16[3,4,128,128]{3,2,0,1:T(8,128)(2,1)S(1)}, bf16[3,4,128,128]{3,2,0,1:T(8,128)(2,1)S(1)}, u32[]{:S(2)}, u32[]{:S(2)}) collective-permute-start(bf16[3,4,128,128]{3,2,0,1:T(8,128)(2,1)S(1)} %get-tuple-element.15), channel_id=1, source_target_pairs={{0,8},{4,12},{8,16},{12,20},{16,24},{20,28},{24,0},{28,4},{1,9},{5... | collective-permute-start | bytes 1179656 | tf_op jit(solution)/shard_map/ppermute | solution.py:11
  243.6 34.3 %collective-permute-start.8 = (bf16[3,4,128,128]{3,2,0,1:T(8,128)(2,1)S(1)}, bf16[3,4,128,128]{3,2,0,1:T(8,128)(2,1)S(1)}, u32[]{:S(2)}, u32[]{:S(2)}) collective-permute-start(bf16[3,4,128,128]{3,2,0,1:T(8,128)(2,1)S(1)} %get-tuple-element.14), channel_id=1, source_target_pairs={{0,4},{4,8},{8,12},{12,16},{16,20},{20,24},{24,28},{28,0},{1,5},{5... | collective-permute-start | bytes 1179656 | tf_op jit(solution)/shard_map/ppermute | solution.py:11
  278.2 11.2 %collective-permute-start.9 = (bf16[3,4,128,128]{3,2,0,1:T(8,128)(2,1)S(1)}, bf16[3,4,128,128]{3,2,0,1:T(8,128)(2,1)S(1)}, u32[]{:S(2)}, u32[]{:S(2)}) collective-permute-start(bf16[3,4,128,128]{3,2,0,1:T(8,128)(2,1)S(1)} %get-tuple-element.12), channel_id=1, source_target_pairs={{0,28},{4,0},{8,4},{12,8},{16,12},{20,16},{24,20},{28,24},{1,29},{... | collective-permute-start | bytes 1179656 | tf_op jit(solution)/shard_map/ppermute | solution.py:11
  278.2 18.0 %collective-permute-start.10 = (bf16[3,4,128,128]{3,2,0,1:T(8,128)(2,1)S(1)}, bf16[3,4,128,128]{3,2,0,1:T(8,128)(2,1)S(1)}, u32[]{:S(2)}, u32[]{:S(2)}) collective-permute-start(bf16[3,4,128,128]{3,2,0,1:T(8,128)(2,1)S(1)} %get-tuple-element.11), channel_id=1, source_target_pairs={{0,24},{4,28},{8,0},{12,4},{16,8},{20,12},{24,16},{28,20},{1,25},{... | collective-permute-start | bytes 1179656 | tf_op jit(solution)/shard_map/ppermute | solution.py:11
  279.2 24.3 %collective-permute-start.11 = (bf16[3,4,128,128]{3,2,0,1:T(8,128)(2,1)S(1)}, bf16[3,4,128,128]{3,2,0,1:T(8,128)(2,1)S(1)}, u32[]{:S(2)}, u32[]{:S(2)}) collective-permute-start(bf16[3,4,128,128]{3,2,0,1:T(8,128)(2,1)S(1)} %get-tuple-element.10), channel_id=1, source_target_pairs={{0,20},{4,24},{8,28},{12,0},{16,4},{20,8},{24,12},{28,16},{1,21},{... | collective-permute-start | bytes 1179656 | tf_op jit(solution)/shard_map/ppermute | solution.py:11
  303.5 1.6 copy-start.1
where the time goes:
time: 407 us; the launch traced here: 405 us
  blocking collectives  139 us (34%)
  local copies, waits for them, and re-layouts  92.7 us (23%)
  waiting for transfers between devices  92.6 us (23%)
  matrix products  39.7 us (10%)
  starting transfers between devices  24.9 us (6%)
  other arithmetic  15.8 us (4%)
    ppermute x12, waiting for transfers between devices, shifted(): lax.ppermute(array, axis, [(i, (i + by) % count) for i in range(count)])  92.6 us
    psum x2, blocking collectives, squares(): return lax.psum(jnp.sum(vector * vector, axis=(1, 2)), ('row', 'col'))  89.5 us
    psum x1, blocking collectives, body(): bend = lax.psum(jnp.sum(direction * image, axis=(1, 2)), ('row', 'col'))  49.4 us
    ppermute x12, starting transfers between devices, shifted(): lax.ppermute(array, axis, [(i, (i + by) % count) for i in range(count)])  24.9 us
    another operation x6, local copies, waits for them, and re-layouts, body(): received = jnp.stack(pieces, 1)  18.6 us
    dot_general x2, matrix products, body(): jnp.einsum('rk,fkj->frj', dense_ks, gathered, preferred_element_type=jnp....  18.1 us
    unnamed x27, local copies, waits for them, and re-layouts  16.8 us
    reshape x1, local copies, waits for them, and re-layouts, body(): dense_ks.astype(jnp.bfloat16).reshape(clusters * width, slots * width)  12.8 us
  transfers between devices with their start and end apart: 12, of which 6 were waited for; matrix products, arithmetic and copies ran while one was open for 8% of the time, Pallas kernels for 0%

commit v1 on v0

v1 whole, which is shorter than its diff:
```python
import functools

import jax
import jax.numpy as jnp
from jax import lax
from jax.experimental import pallas as pl
from jax.experimental.pallas import tpu as pltpu
from jax.sharding import PartitionSpec as P

EXTRA = 16
STEP = 2
LIMIT = 48 * 1024 * 1024


def shifted(array, axis, by):
    count = lax.axis_size(axis)
    return lax.ppermute(array, axis, [(i, (i + by) % count) for i in range(count)])


def summed(array):
    for axis in ("col", "row"):
        count = lax.axis_size(axis)
        if count & (count - 1):
            array = lax.psum(array, axis)
            continue
        hop = 1
        while hop < count:
            array = array + lax.ppermute(array, axis, [(i, i ^ hop) for i in range(count)])
            hop *= 2
    return array


def vmem():
    return pl.BlockSpec(memory_space=pltpu.VMEM)


def smem():
    return pl.BlockSpec(memory_space=pltpu.SMEM)


def params():
    return pltpu.CompilerParams(vmem_limit_bytes=LIMIT)


def column(row, width):
    return jnp.transpose(jnp.broadcast_to(row, (width, width)))


def wide(parts):
    return jnp.concatenate(parts, axis=1)


def pack_kernel(fields, width, readers, right_side, onsite, *messages):
    served = readers.shape[2]
    for offset, message in enumerate(messages):
        base = served * width
        message[base : base + EXTRA, :] = jnp.zeros((EXTRA, message.shape[1]), message.dtype)
        pieces = []
        for slot in range(served):
            cluster = readers[0, offset, slot]
            rows = pl.ds(pl.multiple_of(cluster * width, width), width)
            for field in range(fields):
                message[slot * width : (slot + 1) * width, field * width : (field + 1) * width] = (
                    right_side[field, rows, :].astype(message.dtype)
                )
            value = onsite[pl.ds(cluster, 1), :]
            high = value.astype(jnp.bfloat16).astype(jnp.float32)
            middle = (value - high).astype(jnp.bfloat16).astype(jnp.float32)
            pieces.append(wide([high, middle, value - high - middle]))
        pieces.append(jnp.zeros((EXTRA - served, 3 * width), jnp.float32))
        message[base : base + EXTRA, 0 : 3 * width] = jnp.concatenate(pieces, axis=0).astype(
            message.dtype
        )


def pack(readers, right_side, onsite):
    fields, rows, orbitals = right_side.shape
    span, served = readers.shape[1:]
    width = onsite.shape[1]
    shape = jax.ShapeDtypeStruct((served * width + EXTRA, fields * orbitals), jnp.bfloat16)
    return pl.pallas_call(
        functools.partial(pack_kernel, fields, width),
        out_shape=[shape] * span,
        in_specs=[smem(), vmem(), vmem()],
        out_specs=[vmem()] * span,
        compiler_params=params(),
        name="pack",
    )(readers, right_side, onsite)


def spread_kernel(served, slots, ks, correlation, spread, where):
    cluster = pl.program_id(0)
    ks_ref, correlation_ref = ks, correlation
    tile_slot, out = spread
    for kind, ref in enumerate((ks_ref, correlation_ref)):
        count = ref.shape[1]

        @pl.loop(0, slots)
        def _(slot):
            where[slot] = count

        @pl.loop(0, count)
        def _(tile):
            where[tile_slot[cluster, tile]] = tile

        for slot in range(slots):
            tile = where[slot]
            block = ref[0, jnp.minimum(tile, count - 1)]
            block = jnp.where(tile < count, block, jnp.zeros_like(block))
            width = block.shape[1]
            lanes = slice((slot % served) * width, (slot % served + 1) * width)
            out[slot // served, 0, kind, :, lanes] = block


def spread(tile_slot, ks_tiles, correlation_tiles, span, served):
    clusters, tiles, width, _ = ks_tiles.shape
    few = correlation_tiles.shape[1]

    def kernel(slot_ref, ks_ref, correlation_ref, out_ref, where):
        spread_kernel(served, span * served, ks_ref, correlation_ref, (slot_ref, out_ref), where)

    return pl.pallas_call(
        kernel,
        grid=(clusters,),
        out_shape=jax.ShapeDtypeStruct((span, clusters, 2, width, served * width), jnp.bfloat16),
        in_specs=[
            smem(),
            pl.BlockSpec((1, tiles, width, width), lambda i: (i, 0, 0, 0)),
            pl.BlockSpec((1, few, width, width), lambda i: (i, 0, 0, 0)),
        ],
        out_specs=pl.BlockSpec((span, 1, 2, width, served * width), lambda i: (0, i, 0, 0, 0)),
        scratch_shapes=[pltpu.SMEM((span * served,), jnp.int32)],
        compiler_params=params(),
        cost_estimate=pl.CostEstimate(flops=0, bytes_accessed=24 * 2**20, transcendentals=0),
        name="spread",
    )(tile_slot, ks_tiles, correlation_tiles)


def step_sizes(sums, fields, width):
    totals = jnp.sum(sums[...], axis=1, keepdims=True)
    alphas, growths = [], []
    for field in range(fields):
        norm = totals[field : field + 1]
        alpha = norm / totals[fields + field : fields + field + 1]
        after = alpha * alpha * totals[2 * fields + field : 2 * fields + field + 1] - norm
        alphas.append(jnp.broadcast_to(alpha, (1, width)))
        growths.append(jnp.broadcast_to(1.0 + after / norm, (1, width)))
    return wide(alphas), wide(growths)


def rebuild(first, second, sums, out, fields, orbitals, width):
    alpha, growth = step_sizes(sums, fields, orbitals)
    base = second.shape[0]
    for slot in range(base // width):
        tail = first[base : base + EXTRA, 0 : 3 * width].astype(jnp.float32)[slot : slot + 1]
        level = (tail[:, 2 * width :] + tail[:, width : 2 * width]) + tail[:, :width]
        level = column(level, width)
        level = wide([level] * (alpha.shape[1] // width))
        rows = slice(slot * width, (slot + 1) * width)
        value = (growth - alpha * level) * first[rows, :].astype(jnp.float32)
        value = value - alpha * second[rows, :].astype(jnp.float32)
        out[rows, :] = value.astype(out.dtype)


def products(blocks, vectors, base):
    total = None
    for block, vector in zip(blocks, vectors):
        left = block[0].reshape(-1, block.shape[-1])
        part = jnp.dot(left, vector[0:base, :], preferred_element_type=jnp.float32)
        total = part if total is None else total + part
    return total


def couple(dense, offsets, firsts, seconds, sums, total, finish):
    span, clusters, kinds, width, depth = dense.shape
    lanes = firsts[0].shape[1]
    count = len(offsets)
    second = seconds is not None
    fields = finish["right_side"].shape[0]
    orbitals = lanes // fields
    last = finish.get("now")
    had = total is not None

    inputs, specs = [], []
    for offset in offsets:
        inputs.append(dense)
        specs.append(
            pl.BlockSpec(
                (1, STEP, kinds, width, depth), functools.partial(lambda o, i: (o, i, 0, 0, 0), offset)
            )
        )
    whole = lambda a: pl.BlockSpec(a.shape, lambda i: (0,) * a.ndim)
    for message in firsts:
        inputs.append(message)
        specs.append(whole(message))
    if second:
        for message in seconds:
            inputs.append(message)
            specs.append(whole(message))
        inputs.append(sums)
        specs.append(whole(sums))
    total_spec = pl.BlockSpec((STEP, kinds, width, lanes), lambda i: (i, 0, 0, 0))
    if had:
        inputs.append(total)
        specs.append(total_spec)
    image_spec = pl.BlockSpec((STEP, width, lanes), lambda i: (i, 0, 0))
    image_shape = jax.ShapeDtypeStruct((clusters, width, lanes), jnp.float32)
    sums_shape = jax.ShapeDtypeStruct((16, orbitals), jnp.float32)
    scratch = []
    if second:
        scratch += [pltpu.VMEM((depth, lanes), jnp.bfloat16)] * count
    if last:
        right_side, onsite, energies, readers = (
            finish[k] for k in ("right_side", "onsite", "energies", "readers")
        )
        inputs += [right_side, onsite, energies]
        specs += [
            pl.BlockSpec((fields, STEP * width, orbitals), lambda i: (0, i, 0)),
            whole(onsite),
            whole(energies),
        ]
        if second:
            inputs.append(finish["image"])
            specs.append(image_spec)
            out_shape = [image_shape, sums_shape]
            out_specs = [image_spec, whole(sums_shape)]
        else:
            inputs.append(readers)
            specs.append(smem())
            message_shape = jax.ShapeDtypeStruct((depth, lanes), jnp.bfloat16)
            out_shape = [image_shape, sums_shape] + [message_shape] * span
            out_specs = [image_spec, whole(sums_shape)] + [whole(message_shape)] * span
            scratch.append(pltpu.VMEM((clusters, width, lanes), jnp.bfloat16))
    else:
        out_shape = jax.ShapeDtypeStruct((clusters, kinds, width, lanes), jnp.float32)
        out_specs = total_spec

    def kernel(*refs):
        refs = list(refs)
        take = lambda n: [refs.pop(0) for _ in range(n)]
        blocks = take(count)
        first_refs = take(count)
        if second:
            second_refs = take(count)
            (sums_ref,) = take(1)
        if had:
            (total_ref,) = take(1)
        if last:
            right_ref, onsite_ref, energies_ref, extra_ref = take(4)
            image_ref, out_sums = take(2)
            messages = [] if second else take(span)
        else:
            (out_ref,) = take(1)
        step = pl.program_id(0)
        if second:
            vectors = take(count)

            @pl.when(step == 0)
            def _():
                for index in range(count):
                    rebuild(
                        first_refs[index], second_refs[index], sums_ref, vectors[index], fields, orbitals, width
                    )

        else:
            vectors = first_refs
        value = products(blocks, vectors, depth).reshape(STEP, kinds, width, lanes)
        if had:
            value = value + total_ref[...]
        if not last:
            out_ref[...] = value
            return
        energy = wide([energies_ref[...]] * fields)
        if second:
            alpha, growth = step_sizes(sums_ref, fields, orbitals)
        collected = [[] for _ in range(9)]
        for local in range(STEP):
            cluster = step * STEP + local
            coupled = value[local, 0] - energy * value[local, 1]
            level = column(onsite_ref[pl.ds(cluster, 1), :], width)
            level = wide([level] * (lanes // width))
            right = wide([right_ref[f, local * width : (local + 1) * width, :] for f in range(fields)])
            if second:
                before = extra_ref[local]
                residual = right - alpha * before
                direction = growth * right - alpha * before
                image = level * direction + coupled
                terms = (direction * image, residual * residual)
            else:
                image = level * right + coupled
                refs[-1][cluster] = coupled.astype(jnp.bfloat16)
                terms = (right * right, right * image, image * image)
            image_ref[local] = image
            for q, term in enumerate(terms):
                line = jnp.sum(term, axis=0, keepdims=True)
                for f in range(fields):
                    collected[q * fields + f].append(line[:, f * orbitals : (f + 1) * orbitals])
        lines = []
        for parts in collected:
            if parts:
                line = parts[0]
                for part in parts[1:]:
                    line = line + part
                lines.append(line)
        lines.append(jnp.zeros((16 - len(lines), orbitals), jnp.float32))
        block = jnp.concatenate(lines, axis=0)

        @pl.when(step == 0)
        def _():
            out_sums[...] = block

        @pl.when(step > 0)
        def _():
            out_sums[...] += block

        if not second:

            @pl.when(step == pl.num_programs(0) - 1)
            def _():
                for offset, message in enumerate(messages):
                    for slot in range(depth // width):
                        message[slot * width : (slot + 1) * width, :] = refs[-1][
                            extra_ref[0, offset, slot]
                        ]

    return pl.pallas_call(
        kernel,
        grid=(clusters // STEP,),
        out_shape=out_shape,
        in_specs=specs,
        out_specs=out_specs,
        scratch_shapes=scratch,
        compiler_params=params(),
        cost_estimate=pl.CostEstimate(
            flops=2 * count * clusters * kinds * width * depth * lanes,
            bytes_accessed=8 * 2**20,
            transcendentals=0,
        ),
        name="couple",
    )(*inputs)


def final_kernel(fields, right_side, image, later, sums, sums_later, solution_field, residual):
    orbitals = right_side.shape[2]
    alpha, growth = step_sizes(sums, fields, orbitals)
    totals = jnp.sum(sums_later[...], axis=1, keepdims=True)
    for field in range(fields):
        lanes = slice(field * orbitals, (field + 1) * orbitals)
        step = totals[fields + field : fields + field + 1] / totals[field : field + 1]
        rows = right_side.shape[1]
        right = right_side[field]
        before = alpha[:, lanes] * image[:, :, lanes].reshape(rows, orbitals)
        direction = growth[:, lanes] * right - before
        solution_field[field] = alpha[:, lanes] * right + step * direction
        residual[field] = (right - before) - step * later[:, :, lanes].reshape(rows, orbitals)


def final(right_side, image, later, sums, sums_later):
    fields, rows, orbitals = right_side.shape
    clusters, width, lanes = image.shape
    vector = pl.BlockSpec((fields, STEP * width, orbitals), lambda i: (0, i, 0))
    block = pl.BlockSpec((STEP, width, lanes), lambda i: (i, 0, 0))
    small = pl.BlockSpec(sums.shape, lambda i: (0, 0))
    shape = jax.ShapeDtypeStruct(right_side.shape, jnp.float32)
    return pl.pallas_call(
        functools.partial(final_kernel, fields),
        grid=(clusters // STEP,),
        out_shape=[shape, shape],
        in_specs=[vector, block, block, small, small],
        out_specs=[vector, vector],
        compiler_params=params(),
        name="final",
    )(right_side, image, later, sums, sums_later)


def body(right_side, onsite, energies, ks_tiles, correlation_tiles, tile_slot, readers):
    span, served = readers.shape[1:]
    width = ks_tiles.shape[2]
    middle = (span - 1) // 2
    onsite = onsite.reshape(-1, width)
    energies = energies.reshape(1, -1)
    finish = dict(right_side=right_side, onsite=onsite, energies=energies, readers=readers)

    order = []
    for far in range(middle, 0, -1):
        order += [middle - far, middle + far]

    def exchange(messages):
        return [
            shifted(m, "row", middle - o) if o != middle else m for o, m in enumerate(messages)
        ]

    firsts = exchange(pack(readers, right_side, onsite))
    dense = spread(tile_slot, ks_tiles, correlation_tiles, span, served)
    groups = [[middle]] + [[o] for o in order]

    def operate(seconds, sums, finish):
        total = None
        for group in groups:
            now = group is groups[-1]
            total = couple(
                dense,
                group,
                [firsts[o] for o in group],
                None if seconds is None else [seconds[o] for o in group],
                sums,
                total,
                dict(finish, now=now),
            )
        return total

    image, sums, *messages = operate(None, None, finish)
    seconds = exchange(messages)
    sums = summed(sums)
    later, sums_later = operate(seconds, sums, dict(finish, image=image))
    sums_later = summed(sums_later)
    return tuple(final(right_side, image, later, sums, sums_later))


def solution(mesh):
    placed = (
        P(None, "row", "col"),
        P("row"),
        P("col"),
        P("row", None, None, None),
        P("row", None, None, None),
        P("row", None),
        P("row", None, None),
    )
    return jax.shard_map(
        body,
        mesh=mesh,
        in_specs=placed,
        out_specs=(P(None, "row", "col"), P(None, "row", "col")),
        check_vma=False,
    )
```

time: 407 us -> 190 us (0.47)
  blocking collectives: 139 us -> 0 us
  Pallas kernels: 0 us -> 77.5 us
  local copies, waits for them, and re-layouts: 92.7 us -> 24.7 us
  waiting for transfers between devices: 92.6 us -> 29.8 us
  matrix products: 39.7 us -> 0 us
  starting transfers between devices: 24.9 us -> 55.6 us
  other arithmetic: 15.8 us -> 0.03 us
    psum x3 -> x0, blocking collectives: 139 us -> none  [the longest x2 89.5 us: squares(): return lax.psum(jnp.sum(vector * vector, axis=(1, 2)), ('row', 'col'))]
    ppermute x12, waiting for transfers between devices: 92.6 us -> 0.03 us  [shifted(): lax.ppermute(array, axis, [(i, (i + by) % count) for i in range(count)])]
    pallas_call x0 -> x17, Pallas kernels: none -> 77.5 us  [the longest x14 59.8 us: couple(): pl.pallas_call(kernel, grid=(clusters // STEP,), out_shape=out_shape, in_...]
    dot_general x5 -> x0, matrix products: 39.7 us -> none  [the longest x2 18.1 us: body(): jnp.einsum('rk,fkj->frj', dense_ks, gathered, preferred_element_type=jnp....]
    reshape x6 -> x0, local copies, waits for them, and re-layouts: 30.6 us -> none  [the longest x1 12.8 us: body(): dense_ks.astype(jnp.bfloat16).reshape(clusters * width, slots * width)]
    ppermute x0 -> x10, waiting for transfers between devices: none -> 29.7 us  [summed(): lax.ppermute(array, axis, [(i, i ^ hop) for i in range(count)])]
    ppermute x0 -> x10, starting transfers between devices: none -> 21.7 us  [summed(): lax.ppermute(array, axis, [(i, i ^ hop) for i in range(count)])]
    another operation x6 -> x0, local copies, waits for them, and re-layouts: 18.6 us -> none  [body(): received = jnp.stack(pieces, 1)]
  transfers between devices with their start and end apart: 12 -> 22, of which waited for: 6 -> 10; matrix products, arithmetic and copies ran while one was open for 8% -> 0% of each run, Pallas kernels for 0% -> 34%
where the time goes in v1:
time: 190 us; the launch traced here: 189 us
  Pallas kernels  77.5 us (41%)
  starting transfers between devices  55.6 us (29%)
  waiting for transfers between devices  29.8 us (16%)
  local copies, waits for them, and re-layouts  24.7 us (13%)
    pallas_call x14, Pallas kernels, couple(): pl.pallas_call(kernel, grid=(clusters // STEP,), out_shape=out_shape, in_...  59.8 us
    ppermute x12, starting transfers between devices, shifted(): lax.ppermute(array, axis, [(i, (i + by) % count) for i in range(count)])  33.9 us
    ppermute x10, waiting for transfers between devices, summed(): lax.ppermute(array, axis, [(i, i ^ hop) for i in range(count)])  29.7 us
    unnamed x39, local copies, waits for them, and re-layouts  24.7 us
    ppermute x10, starting transfers between devices, summed(): lax.ppermute(array, axis, [(i, i ^ hop) for i in range(count)])  21.7 us
    pallas_call x1, Pallas kernels, spread(): pl.pallas_call(kernel, grid=(clusters,), out_shape=jax.ShapeDtypeStruct((...  13.7 us
  transfers between devices with their start and end apart: 22, of which 10 were waited for; matrix products, arithmetic and copies ran while one was open for 0% of the time, Pallas kernels for 34%

profile of v1, /device:TPU:0, one launch (start us, length us, event | category | flops | bytes accessed | tf_op | source)
XLA Modules:
  0.0 188.5 jit_solution(5370117149854953461)
XLA Ops:
  4.5 4.0 %collective-permute-start.5 = (bf16[528,384]{1,0:T(8,128)(2,1)S(1)}, bf16[528,384]{1,0:T(8,128)(2,1)S(1)}, u32[]{:S(2)}, u32[]{:S(2)}) collective-permute-start(bf16[528,384]{1,0:T(8,128)(2,1)S(1)} %get-tuple-element.25), channel_id=1, source_target_pairs={{0,12},{4,16},{8,20},{12,24},{16,28},{20,0},{24,4},{28,8},{1,13},{... | collective-permute-start | bytes 1216520 | tf_op jit(solution)/shard_map/ppermute | solution.py:17
  9.6 1.8 collective-permute-start.3
  11.4 2.0 %collective-permute-start.2 = (bf16[528,384]{1,0:T(8,128)(2,1)S(1)}, bf16[528,384]{1,0:T(8,128)(2,1)S(1)}, u32[]{:S(2)}, u32[]{:S(2)}) collective-permute-start(bf16[528,384]{1,0:T(8,128)(2,1)S(1)} %get-tuple-element.22), channel_id=1, source_target_pairs={{0,24},{4,28},{8,0},{12,4},{16,8},{20,12},{24,16},{28,20},{1,25},{... | collective-permute-start | bytes 1216520 | tf_op jit(solution)/shard_map/ppermute | solution.py:17
  13.4 2.6 %collective-permute-start.1 = (bf16[528,384]{1,0:T(8,128)(2,1)S(1)}, bf16[528,384]{1,0:T(8,128)(2,1)S(1)}, u32[]{:S(2)}, u32[]{:S(2)}) collective-permute-start(bf16[528,384]{1,0:T(8,128)(2,1)S(1)} %get-tuple-element.21), channel_id=1, source_target_pairs={{0,4},{4,8},{8,12},{12,16},{16,20},{20,24},{24,28},{28,0},{1,5},{5... | collective-permute-start | bytes 1216520 | tf_op jit(solution)/shard_map/ppermute | solution.py:17
  18.3 13.7 %spread.1.refs_0_ = bf16[7,8,2,128,512]{4,3,2,1,0:T(8,128)(2,1)} custom-call(s32[8,24]{1,0:T(8,128)S(1)} %copy-done.17, bf16[8,24,128,128]{3,2,1,0:T(8,128)(2,1)} %ks_ref.1, bf16[8,8,128,128]{3,2,1,0:T(8,128)(2,1)S(1)} %copy-done.14), custom_call_target="tpu_custom_call" | custom-call | bytes 25165824 | tf_op jit(solution)/shard_map/spread/pallas_call | solution.py:122
  32.0 2.1 %collective-permute-start = (bf16[528,384]{1,0:T(8,128)(2,1)S(1)}, bf16[528,384]{1,0:T(8,128)(2,1)S(1)}, u32[]{:S(2)}, u32[]{:S(2)}) collective-permute-start(bf16[528,384]{1,0:T(8,128)(2,1)S(1)} %get-tuple-element.20), channel_id=1, source_target_pairs={{0,28},{4,0},{8,4},{12,8},{16,12},{20,16},{24,20},{28,24},{1,29},{... | collective-permute-start | bytes 1216520 | tf_op jit(solution)/shard_map/ppermute | solution.py:17
  34.1 3.5 %couple.14.refs_2_ = f32[8,2,128,384]{3,2,1,0:T(8,128)S(1)} custom-call(bf16[7,8,2,128,512]{4,3,2,1,0:T(8,128)(2,1)} %spread.1.refs_0_, bf16[528,384]{1,0:T(8,128)(2,1)S(1)} %get-tuple-element.26.refs_1_), custom_call_target="tpu_custom_call" | custom-call | flops 805306368 | bytes 8388608 | tf_op jit(solution)/shard_map/couple/pallas_call | solution.py:326
  37.6 1.6 copy-done.8
  39.2 4.0 %couple.15.refs_2_ = f32[8,2,128,384]{3,2,1,0:T(8,128)S(1)} custom-call(bf16[7,8,2,128,512]{4,3,2,1,0:T(8,128)(2,1)} %spread.1.refs_0_, bf16[528,384]{1,0:T(8,128)(2,1)S(1)} %collective-permute-done.5.refs_1_, f32[8,2,128,384]{3,2,1,0:T(8,128)} %copy-done.8), custom_call_target="tpu_custom_call" | custom-call | flops 805306368 | bytes 8388608 | tf_op jit(solution)/shard_map/couple/pallas_call | solution.py:326
  43.3 1.6 copy-done.10
  44.9 4.1 %couple.16.refs_2_ = f32[8,2,128,384]{3,2,1,0:T(8,128)S(1)} custom-call(bf16[7,8,2,128,512]{4,3,2,1,0:T(8,128)(2,1)} %spread.1.refs_0_, bf16[528,384]{1,0:T(8,128)(2,1)S(1)} %collective-permute-done.4.refs_1_, f32[8,2,128,384]{3,2,1,0:T(8,128)} %copy-done.10), custom_call_target="tpu_custom_call" | custom-call | flops 805306368 | bytes 8388608 | tf_op jit(solution)/shard_map/couple/pallas_call | solution.py:326
  49.0 1.6 copy-done.11
  50.6 4.0 %couple.17.refs_2_ = f32[8,2,128,384]{3,2,1,0:T(8,128)S(1)} custom-call(bf16[7,8,2,128,512]{4,3,2,1,0:T(8,128)(2,1)} %spread.1.refs_0_, bf16[528,384]{1,0:T(8,128)(2,1)S(1)} %collective-permute-done.3.refs_1_, f32[8,2,128,384]{3,2,1,0:T(8,128)} %copy-done.11), custom_call_target="tpu_custom_call" | custom-call | flops 805306368 | bytes 8388608 | tf_op jit(solution)/shard_map/couple/pallas_call | solution.py:326
  54.7 1.6 copy-done.12
  56.3 4.1 %couple.18.refs_2_ = f32[8,2,128,384]{3,2,1,0:T(8,128)S(1)} custom-call(bf16[7,8,2,128,512]{4,3,2,1,0:T(8,128)(2,1)} %spread.1.refs_0_, bf16[528,384]{1,0:T(8,128)(2,1)S(1)} %collective-permute-done.2.refs_1_, f32[8,2,128,384]{3,2,1,0:T(8,128)} %copy-done.12), custom_call_target="tpu_custom_call" | custom-call | flops 805306368 | bytes 8388608 | tf_op jit(solution)/shard_map/couple/pallas_call | solution.py:326
  60.4 1.6 copy-done.13
  62.0 4.1 %couple.19.refs_2_ = f32[8,2,128,384]{3,2,1,0:T(8,128)S(1)} custom-call(bf16[7,8,2,128,512]{4,3,2,1,0:T(8,128)(2,1)} %spread.1.refs_0_, bf16[528,384]{1,0:T(8,128)(2,1)S(1)} %collective-permute-done.1.refs_1_, f32[8,2,128,384]{3,2,1,0:T(8,128)} %copy-done.13), custom_call_target="tpu_custom_call" | custom-call | flops 805306368 | bytes 8388608 | tf_op jit(solution)/shard_map/couple/pallas_call | solution.py:326
  66.1 1.6 copy-done.9
  67.7 4.8 %couple.20 = (f32[8,128,384]{2,1,0:T(8,128)S(1)}, f32[16,128]{1,0:T(8,128)S(1)}, bf16[512,384]{1,0:T(8,128)(2,1)S(1)}, bf16[512,384]{1,0:T(8,128)(2,1)S(1)}, bf1...) custom-call(bf16[7,8,2,128,512]{4,3,2,1,0:T(8,128)(2,1)} %spread.1.r, ...), custom_call_target="tpu_custom_call" | custom-call | flops 805306368 | bytes 8388608 | tf_op jit(solution)/shard_map/couple/pallas_call | solution.py:326
  72.6 6.8 %collective-permute-start.16 = (bf16[512,384]{1,0:T(8,128)(2,1)S(1)}, bf16[512,384]{1,0:T(8,128)(2,1)S(1)}, u32[]{:S(2)}, u32[]{:S(2)}) collective-permute-start(bf16[512,384]{1,0:T(8,128)(2,1)S(1)} %get-tuple-element.34), channel_id=1, source_target_pairs={{0,12},{4,16},{8,20},{12,24},{16,28},{20,0},{24,4},{28,8},{1,13},{... | collective-permute-start | bytes 1179656 | tf_op jit(solution)/shard_map/ppermute | solution.py:17
  79.4 8.8 %collective-permute-start.14 = (bf16[512,384]{1,0:T(8,128)(2,1)S(1)}, bf16[512,384]{1,0:T(8,128)(2,1)S(1)}, u32[]{:S(2)}, u32[]{:S(2)}) collective-permute-start(bf16[512,384]{1,0:T(8,128)(2,1)S(1)} %get-tuple-element.32), channel_id=1, source_target_pairs={{0,8},{4,12},{8,16},{12,20},{16,24},{20,28},{24,0},{28,4},{1,9},{5... | collective-permute-start | bytes 1179656 | tf_op jit(solution)/shard_map/ppermute | solution.py:17
  90.8 2.2 %collective-permute-done.8 = f32[16,128]{1,0:T(8,128)S(1)} collective-permute-done((f32[16,128]{1,0:T(8,128)S(1)}, f32[16,128]{1,0:T(8,128)S(1)}, u32[]{:S(2)}, u32[]{:S(2)}) %collective-permute-start.8) | collective-permute-done | bytes 8224 | tf_op jit(solution)/shard_map/ppermute | solution.py:28
  93.0 3.4 %collective-permute-start.9 = (f32[16,128]{1,0:T(8,128)S(1)}, f32[16,128]{1,0:T(8,128)S(1)}, u32[]{:S(2)}, u32[]{:S(2)}) collective-permute-start(f32[16,128]{1,0:T(8,128)S(1)} %add.31), channel_id=1, source_target_pairs={{0,4},{4,0},{8,12},{12,8},{16,20},{20,16},{24,28},{28,24},{1,5},{5... | collective-permute-start | bytes 24584 | tf_op jit(solution)/shard_map/ppermute | solution.py:28
  98.0 6.6 %collective-permute-start.10 = (f32[16,128]{1,0:T(8,128)S(1)}, f32[16,128]{1,0:T(8,128)S(1)}, u32[]{:S(2)}, u32[]{:S(2)}) collective-permute-start(f32[16,128]{1,0:T(8,128)S(1)} %add.32), channel_id=1, source_target_pairs={{0,8},{4,12},{8,0},{12,4},{16,24},{20,28},{24,16},{28,20},{1,9},{5... | collective-permute-start | bytes 24584 | tf_op jit(solution)/shard_map/ppermute | solution.py:28
  104.6 10.4 %collective-permute-done.10 = f32[16,128]{1,0:T(8,128)S(1)} collective-permute-done((f32[16,128]{1,0:T(8,128)S(1)}, f32[16,128]{1,0:T(8,128)S(1)}, u32[]{:S(2)}, u32[]{:S(2)}) %collective-permute-start.10) | collective-permute-done | bytes 8224 | tf_op jit(solution)/shard_map/ppermute | solution.py:28
  115.0 3.5 %collective-permute-start.11 = (f32[16,128]{1,0:T(8,128)S(1)}, f32[16,128]{1,0:T(8,128)S(1)}, u32[]{:S(2)}, u32[]{:S(2)}) collective-permute-start(f32[16,128]{1,0:T(8,128)S(1)} %add.33), channel_id=1, source_target_pairs={{0,16},{4,20},{8,24},{12,28},{16,0},{20,4},{24,8},{28,12},{1,17},{... | collective-permute-start | bytes 24584 | tf_op jit(solution)/shard_map/ppermute | solution.py:28
  118.6 4.2 %collective-permute-done.11 = f32[16,128]{1,0:T(8,128)S(1)} collective-permute-done((f32[16,128]{1,0:T(8,128)S(1)}, f32[16,128]{1,0:T(8,128)S(1)}, u32[]{:S(2)}, u32[]{:S(2)}) %collective-permute-start.11) | collective-permute-done | bytes 8224 | tf_op jit(solution)/shard_map/ppermute | solution.py:28
  122.8 3.1 %collective-permute-start.12 = (bf16[512,384]{1,0:T(8,128)(2,1)S(1)}, bf16[512,384]{1,0:T(8,128)(2,1)S(1)}, u32[]{:S(2)}, u32[]{:S(2)}) collective-permute-start(bf16[512,384]{1,0:T(8,128)(2,1)S(1)} %get-tuple-element.30), channel_id=1, source_target_pairs={{0,4},{4,8},{8,12},{12,16},{16,20},{20,24},{24,28},{28,0},{1,5},{5... | collective-permute-start | bytes 1179656 | tf_op jit(solution)/shard_map/ppermute | solution.py:17
  125.9 1.6 collective-permute-start.6
  127.5 3.9 %couple.21.refs_4_ = f32[8,2,128,384]{3,2,1,0:T(8,128)S(1)} custom-call(bf16[7,8,2,128,512]{4,3,2,1,0:T(8,128)(2,1)} %spread.1.refs_0_, bf16[528,384]{1,0:T(8,128)(2,1)S(1)} %get-tuple-element.26.refs_1_, bf16[512,384]{1,0:T(8,128)(2,1)S(1)} %get-tuple-element.35.refs_2_, f32[16,128]{1,0:T(8,128)S(1)} %add.34.refs_3_.sums), custom_call_target="tpu_custom_call" | custom-call | flops 805306368 | bytes 8388608 | tf_op jit(solution)/shard_map/couple/pallas_call | solution.py:326
  131.4 1.6 copy-done.7
  133.0 4.5 %couple.22.refs_4_ = f32[8,2,128,384]{3,2,1,0:T(8,128)S(1)} custom-call(bf16[7,8,2,128,512]{4,3,2,1,0:T(8,128)(2,1)} %spread.1.refs_0_, bf16[528,384]{1,0:T(8,128)(2,1)S(1)} %collective-permute-done.5.refs_1_, bf16[512,384]{1,0:T(8,128)(2,1)S(1)} %collective-permute-done.16.refs_2_, f32[16,128]{1,0:T(8,128)S(1)} %add.34.refs_3_.sums, ...), custom_call_target="tpu_custom_call" | custom-call | flops 805306368 | bytes 8388608 | tf_op jit(solution)/shard_map/couple/pallas_call | solution.py:326
  137.6 1.6 copy-done.3
  139.2 4.5 %couple.23.refs_4_ = f32[8,2,128,384]{3,2,1,0:T(8,128)S(1)} custom-call(bf16[7,8,2,128,512]{4,3,2,1,0:T(8,128)(2,1)} %spread.1.refs_0_, bf16[528,384]{1,0:T(8,128)(2,1)S(1)} %collective-permute-done.4.refs_1_, bf16[512,384]{1,0:T(8,128)(2,1)S(1)} %collective-permute-done.15.refs_2_, f32[16,128]{1,0:T(8,128)S(1)} %add.34.refs_3_.sums, ...), custom_call_target="tpu_custom_call" | custom-call | flops 805306368 | bytes 8388608 | tf_op jit(solution)/shard_map/couple/pallas_call | solution.py:326
  143.7 1.6 copy-done.4
  145.3 4.5 %couple.24.refs_4_ = f32[8,2,128,384]{3,2,1,0:T(8,128)S(1)} custom-call(bf16[7,8,2,128,512]{4,3,2,1,0:T(8,128)(2,1)} %spread.1.refs_0_, bf16[528,384]{1,0:T(8,128)(2,1)S(1)} %collective-permute-done.3.refs_1_, bf16[512,384]{1,0:T(8,128)(2,1)S(1)} %collective-permute-done.14.refs_2_, f32[16,128]{1,0:T(8,128)S(1)} %add.34.refs_3_.sums, ...), custom_call_target="tpu_custom_call" | custom-call | flops 805306368 | bytes 8388608 | tf_op jit(solution)/shard_map/couple/pallas_call | solution.py:326
  149.8 1.6 copy-done.5
  151.5 4.5 %couple.25.refs_4_ = f32[8,2,128,384]{3,2,1,0:T(8,128)S(1)} custom-call(bf16[7,8,2,128,512]{4,3,2,1,0:T(8,128)(2,1)} %spread.1.refs_0_, bf16[528,384]{1,0:T(8,128)(2,1)S(1)} %collective-permute-done.2.refs_1_, bf16[512,384]{1,0:T(8,128)(2,1)S(1)} %collective-permute-done.13.refs_2_, f32[16,128]{1,0:T(8,128)S(1)} %add.34.refs_3_.sums, ...), custom_call_target="tpu_custom_call" | custom-call | flops 805306368 | bytes 8388608 | tf_op jit(solution)/shard_map/couple/pallas_call | solution.py:326
  156.0 1.6 copy-done.6
  157.6 4.6 %couple.26.refs_4_ = f32[8,2,128,384]{3,2,1,0:T(8,128)S(1)} custom-call(bf16[7,8,2,128,512]{4,3,2,1,0:T(8,128)(2,1)} %spread.1.refs_0_, bf16[528,384]{1,0:T(8,128)(2,1)S(1)} %collective-permute-done.1.refs_1_, bf16[512,384]{1,0:T(8,128)(2,1)S(1)} %collective-permute-done.12.refs_2_, f32[16,128]{1,0:T(8,128)S(1)} %add.34.refs_3_.sums, ...), custom_call_target="tpu_custom_call" | custom-call | flops 805306368 | bytes 8388608 | tf_op jit(solution)/shard_map/couple/pallas_call | solution.py:326
  162.2 1.6 copy-done.2
  163.9 4.8 %couple.27 = (f32[8,128,384]{2,1,0:T(8,128)S(1)}, f32[16,128]{1,0:T(8,128)S(1)}) custom-call(bf16[7,8,2,128,512]{4,3,2,1,0:T(8,128)(2,1)} %spread.1.refs_0_, bf16[528,384]{1,0:T(8,128)(2,1)S(1)} %collective-permute-done.refs_1_, bf16[512,384]{1,0:T(8,128)(2,1)S(1)} %collective-permute-done.6.refs_2_, f32[16,128]{1,0:T(8,128)S(1)} %add.34.refs_3_.sums, ...), custom_call_target="tpu_custom_call" | custom-call | flops 805306368 | bytes 8388608 | tf_op jit(solution)/shard_map/couple/pallas_call | solution.py:326
  171.4 2.2 %collective-permute-done.18 = f32[16,128]{1,0:T(8,128)S(1)} collective-permute-done((f32[16,128]{1,0:T(8,128)S(1)}, f32[16,128]{1,0:T(8,128)S(1)}, u32[]{:S(2)}, u32[]{:S(2)}) %collective-permute-start.18) | collective-permute-done | bytes 8224 | tf_op jit(solution)/shard_map/ppermute | solution.py:28
  173.9 3.3 %collective-permute-done.19 = f32[16,128]{1,0:T(8,128)S(1)} collective-permute-done((f32[16,128]{1,0:T(8,128)S(1)}, f32[16,128]{1,0:T(8,128)S(1)}, u32[]{:S(2)}, u32[]{:S(2)}) %collective-permute-start.19) | collective-permute-done | bytes 8224 | tf_op jit(solution)/shard_map/ppermute | solution.py:28
  177.2 1.7 collective-permute-start.20
  178.9 2.0 %collective-permute-done.20 = f32[16,128]{1,0:T(8,128)S(1)} collective-permute-done((f32[16,128]{1,0:T(8,128)S(1)}, f32[16,128]{1,0:T(8,128)S(1)}, u32[]{:S(2)}, u32[]{:S(2)}) %collective-permute-start.20) | collective-permute-done | bytes 8224 | tf_op jit(solution)/shard_map/ppermute | solution.py:28
  180.9 3.0 %collective-permute-start.21 = (f32[16,128]{1,0:T(8,128)S(1)}, f32[16,128]{1,0:T(8,128)S(1)}, u32[]{:S(2)}, u32[]{:S(2)}) collective-permute-start(f32[16,128]{1,0:T(8,128)S(1)} %add.38), channel_id=1, source_target_pairs={{0,16},{4,20},{8,24},{12,28},{16,0},{20,4},{24,8},{28,12},{1,17},{... | collective-permute-start | bytes 24584 | tf_op jit(solution)/shard_map/ppermute | solution.py:28
  185.5 3.0 %final.1 = (f32[3,1024,128]{2,1,0:T(8,128)}, f32[3,1024,128]{2,1,0:T(8,128)}) custom-call(f32[3,1024,128]{2,1,0:T(8,128)S(1)} %copy-done.1, f32[8,128,384]{2,1,0:T(8,128)S(1)} %get-tuple-element.27.refs_8_.image, f32[8,128,384]{2,1,0:T(8,128)S(1)} %get-tuple-element.36.later, f32[16,128]{1,0:T(8,128)S(1)} %add.34.refs_3_.sums, f32[16,128]{1,0:T(8,128)S(1)} %add.39.sums_later), custom_call_target="tpu_custom_call" | custom-call | tf_op jit(solution)/shard_map/final/pallas_call | solution.py:365
  (62 shorter events, 16.3 us)
Async XLA Ops:
  1.4 1.4 copy-start
  2.8 0.7 copy-start.15
  4.5 27.5 %collective-permute-start.5 = (bf16[528,384]{1,0:T(8,128)(2,1)S(1)}, bf16[528,384]{1,0:T(8,128)(2,1)S(1)}, u32[]{:S(2)}, u32[]{:S(2)}) collective-permute-start(bf16[528,384]{1,0:T(8,128)(2,1)S(1)} %get-tuple-element.25), channel_id=1, source_target_pairs={{0,12},{4,16},{8,20},{12,24},{16,28},{20,0},{24,4},{28,8},{1,13},{... | collective-permute-start | bytes 1216520 | tf_op jit(solution)/shard_map/ppermute | solution.py:17
  8.5 36.4 %collective-permute-start.4 = (bf16[528,384]{1,0:T(8,128)(2,1)S(1)}, bf16[528,384]{1,0:T(8,128)(2,1)S(1)}, u32[]{:S(2)}, u32[]{:S(2)}) collective-permute-start(bf16[528,384]{1,0:T(8,128)(2,1)S(1)} %get-tuple-element.24), channel_id=1, source_target_pairs={{0,20},{4,24},{8,28},{12,0},{16,4},{20,8},{24,12},{28,16},{1,21},{... | collective-permute-start | bytes 1216520 | tf_op jit(solution)/shard_map/ppermute | solution.py:17
  9.6 41.0 %collective-permute-start.3 = (bf16[528,384]{1,0:T(8,128)(2,1)S(1)}, bf16[528,384]{1,0:T(8,128)(2,1)S(1)}, u32[]{:S(2)}, u32[]{:S(2)}) collective-permute-start(bf16[528,384]{1,0:T(8,128)(2,1)S(1)} %get-tuple-element.23), channel_id=1, source_target_pairs={{0,8},{4,12},{8,16},{12,20},{16,24},{20,28},{24,0},{28,4},{1,9},{5... | collective-permute-start | bytes 1216520 | tf_op jit(solution)/shard_map/ppermute | solution.py:17
  11.4 44.9 %collective-permute-start.2 = (bf16[528,384]{1,0:T(8,128)(2,1)S(1)}, bf16[528,384]{1,0:T(8,128)(2,1)S(1)}, u32[]{:S(2)}, u32[]{:S(2)}) collective-permute-start(bf16[528,384]{1,0:T(8,128)(2,1)S(1)} %get-tuple-element.22), channel_id=1, source_target_pairs={{0,24},{4,28},{8,0},{12,4},{16,8},{20,12},{24,16},{28,20},{1,25},{... | collective-permute-start | bytes 1216520 | tf_op jit(solution)/shard_map/ppermute | solution.py:17
  13.4 48.6 %collective-permute-start.1 = (bf16[528,384]{1,0:T(8,128)(2,1)S(1)}, bf16[528,384]{1,0:T(8,128)(2,1)S(1)}, u32[]{:S(2)}, u32[]{:S(2)}) collective-permute-start(bf16[528,384]{1,0:T(8,128)(2,1)S(1)} %get-tuple-element.21), channel_id=1, source_target_pairs={{0,4},{4,8},{8,12},{12,16},{16,20},{20,24},{24,28},{28,0},{1,5},{5... | collective-permute-start | bytes 1216520 | tf_op jit(solution)/shard_map/ppermute | solution.py:17
  16.1 1.6 copy-start.14
  17.6 0.7 copy-start.17
  32.0 35.7 %collective-permute-start = (bf16[528,384]{1,0:T(8,128)(2,1)S(1)}, bf16[528,384]{1,0:T(8,128)(2,1)S(1)}, u32[]{:S(2)}, u32[]{:S(2)}) collective-permute-start(bf16[528,384]{1,0:T(8,128)(2,1)S(1)} %get-tuple-element.20), channel_id=1, source_target_pairs={{0,28},{4,0},{8,4},{12,8},{16,12},{20,16},{24,20},{28,24},{1,29},{... | collective-permute-start | bytes 1216520 | tf_op jit(solution)/shard_map/ppermute | solution.py:17
  37.6 1.6 copy-start.8
  43.3 1.6 copy-start.10
  49.0 1.6 copy-start.11
  54.7 1.6 copy-start.12
  60.4 1.6 copy-start.13
  62.0 5.7 %copy-start.16 = (f32[1024]{0:T(1024)S(1)}, f32[1024]{0:T(1024)}, u32[]{:S(2)}) copy-start(f32[1024]{0:T(1024)} %param.8) | copy-start | bytes 12292
  62.0 5.7 %copy-start.18 = (f32[128]{0:T(128)S(1)}, f32[128]{0:T(128)}, u32[]{:S(2)}) copy-start(f32[128]{0:T(128)} %param.9) | copy-start | bytes 1540
  66.1 1.6 copy-start.9
  72.6 53.3 %collective-permute-start.16 = (bf16[512,384]{1,0:T(8,128)(2,1)S(1)}, bf16[512,384]{1,0:T(8,128)(2,1)S(1)}, u32[]{:S(2)}, u32[]{:S(2)}) collective-permute-start(bf16[512,384]{1,0:T(8,128)(2,1)S(1)} %get-tuple-element.34), channel_id=1, source_target_pairs={{0,12},{4,16},{8,20},{12,24},{16,28},{20,0},{24,4},{28,8},{1,13},{... | collective-permute-start | bytes 1179656 | tf_op jit(solution)/shard_map/ppermute | solution.py:17
  79.3 59.8 %collective-permute-start.15 = (bf16[512,384]{1,0:T(8,128)(2,1)S(1)}, bf16[512,384]{1,0:T(8,128)(2,1)S(1)}, u32[]{:S(2)}, u32[]{:S(2)}) collective-permute-start(bf16[512,384]{1,0:T(8,128)(2,1)S(1)} %get-tuple-element.33), channel_id=1, source_target_pairs={{0,20},{4,24},{8,28},{12,0},{16,4},{20,8},{24,12},{28,16},{1,21},{... | collective-permute-start | bytes 1179656 | tf_op jit(solution)/shard_map/ppermute | solution.py:17
  79.4 66.0 %collective-permute-start.14 = (bf16[512,384]{1,0:T(8,128)(2,1)S(1)}, bf16[512,384]{1,0:T(8,128)(2,1)S(1)}, u32[]{:S(2)}, u32[]{:S(2)}) collective-permute-start(bf16[512,384]{1,0:T(8,128)(2,1)S(1)} %get-tuple-element.32), channel_id=1, source_target_pairs={{0,8},{4,12},{8,16},{12,20},{16,24},{20,28},{24,0},{28,4},{1,9},{5... | collective-permute-start | bytes 1179656 | tf_op jit(solution)/shard_map/ppermute | solution.py:17
  88.1 63.3 %collective-permute-start.13 = (bf16[512,384]{1,0:T(8,128)(2,1)S(1)}, bf16[512,384]{1,0:T(8,128)(2,1)S(1)}, u32[]{:S(2)}, u32[]{:S(2)}) collective-permute-start(bf16[512,384]{1,0:T(8,128)(2,1)S(1)} %get-tuple-element.31), channel_id=1, source_target_pairs={{0,24},{4,28},{8,0},{12,4},{16,8},{20,12},{24,16},{28,20},{1,25},{... | collective-permute-start | bytes 1179656 | tf_op jit(solution)/shard_map/ppermute | solution.py:17
  88.1 1.2 collective-permute-start.7
  89.3 3.7 %collective-permute-start.8 = (f32[16,128]{1,0:T(8,128)S(1)}, f32[16,128]{1,0:T(8,128)S(1)}, u32[]{:S(2)}, u32[]{:S(2)}) collective-permute-start(f32[16,128]{1,0:T(8,128)S(1)} %add.30), channel_id=1, source_target_pairs={{0,2},{1,3},{2,0},{3,1},{4,6},{5,7},{6,4},{7,5},{8,10},{9,11},{10,... | collective-permute-start | bytes 24584 | tf_op jit(solution)/shard_map/ppermute | solution.py:28
  93.0 5.0 %collective-permute-start.9 = (f32[16,128]{1,0:T(8,128)S(1)}, f32[16,128]{1,0:T(8,128)S(1)}, u32[]{:S(2)}, u32[]{:S(2)}) collective-permute-start(f32[16,128]{1,0:T(8,128)S(1)} %add.31), channel_id=1, source_target_pairs={{0,4},{4,0},{8,12},{12,8},{16,20},{20,16},{24,28},{28,24},{1,5},{5... | collective-permute-start | bytes 24584 | tf_op jit(solution)/shard_map/ppermute | solution.py:28
  98.0 17.0 %collective-permute-start.10 = (f32[16,128]{1,0:T(8,128)S(1)}, f32[16,128]{1,0:T(8,128)S(1)}, u32[]{:S(2)}, u32[]{:S(2)}) collective-permute-start(f32[16,128]{1,0:T(8,128)S(1)} %add.32), channel_id=1, source_target_pairs={{0,8},{4,12},{8,0},{12,4},{16,24},{20,28},{24,16},{28,20},{1,9},{5... | collective-permute-start | bytes 24584 | tf_op jit(solution)/shard_map/ppermute | solution.py:28
  115.0 7.7 %collective-permute-start.11 = (f32[16,128]{1,0:T(8,128)S(1)}, f32[16,128]{1,0:T(8,128)S(1)}, u32[]{:S(2)}, u32[]{:S(2)}) collective-permute-start(f32[16,128]{1,0:T(8,128)S(1)} %add.33), channel_id=1, source_target_pairs={{0,16},{4,20},{8,24},{12,28},{16,0},{20,4},{24,8},{28,12},{1,17},{... | collective-permute-start | bytes 24584 | tf_op jit(solution)/shard_map/ppermute | solution.py:28
  122.8 34.9 %collective-permute-start.12 = (bf16[512,384]{1,0:T(8,128)(2,1)S(1)}, bf16[512,384]{1,0:T(8,128)(2,1)S(1)}, u32[]{:S(2)}, u32[]{:S(2)}) collective-permute-start(bf16[512,384]{1,0:T(8,128)(2,1)S(1)} %get-tuple-element.30), channel_id=1, source_target_pairs={{0,4},{4,8},{8,12},{12,16},{16,20},{20,24},{24,28},{28,0},{1,5},{5... | collective-permute-start | bytes 1179656 | tf_op jit(solution)/shard_map/ppermute | solution.py:17
  125.9 38.0 %collective-permute-start.6 = (bf16[512,384]{1,0:T(8,128)(2,1)S(1)}, bf16[512,384]{1,0:T(8,128)(2,1)S(1)}, u32[]{:S(2)}, u32[]{:S(2)}) collective-permute-start(bf16[512,384]{1,0:T(8,128)(2,1)S(1)} %get-tuple-element.28), channel_id=1, source_target_pairs={{0,28},{4,0},{8,4},{12,8},{16,12},{20,16},{24,20},{28,24},{1,29},{... | collective-permute-start | bytes 1179656 | tf_op jit(solution)/shard_map/ppermute | solution.py:17
  131.4 1.6 copy-start.7
  137.5 1.6 copy-start.3
  143.7 1.6 copy-start.4
  149.8 1.6 copy-start.5
  156.0 1.6 copy-start.6
  157.6 6.3 %copy-start.1 = (f32[3,1024,128]{2,1,0:T(8,128)S(1)}, f32[3,1024,128]{2,1,0:T(8,128)}, u32[]{:S(2)}) copy-start(f32[3,1024,128]{2,1,0:T(8,128)} %right_side.3) | copy-start | bytes 4718596
  162.2 1.6 copy-start.2
  168.7 1.2 collective-permute-start.17
  169.9 3.7 %collective-permute-start.18 = (f32[16,128]{1,0:T(8,128)S(1)}, f32[16,128]{1,0:T(8,128)S(1)}, u32[]{:S(2)}, u32[]{:S(2)}) collective-permute-start(f32[16,128]{1,0:T(8,128)S(1)} %add.35), channel_id=1, source_target_pairs={{0,2},{1,3},{2,0},{3,1},{4,6},{5,7},{6,4},{7,5},{8,10},{9,11},{10,... | collective-permute-start | bytes 24584 | tf_op jit(solution)/shard_map/ppermute | solution.py:28
  173.6 3.7 %collective-permute-start.19 = (f32[16,128]{1,0:T(8,128)S(1)}, f32[16,128]{1,0:T(8,128)S(1)}, u32[]{:S(2)}, u32[]{:S(2)}) collective-permute-start(f32[16,128]{1,0:T(8,128)S(1)} %add.36), channel_id=1, source_target_pairs={{0,4},{4,0},{8,12},{12,8},{16,20},{20,16},{24,28},{28,24},{1,5},{5... | collective-permute-start | bytes 24584 | tf_op jit(solution)/shard_map/ppermute | solution.py:28
  177.2 3.7 %collective-permute-start.20 = (f32[16,128]{1,0:T(8,128)S(1)}, f32[16,128]{1,0:T(8,128)S(1)}, u32[]{:S(2)}, u32[]{:S(2)}) collective-permute-start(f32[16,128]{1,0:T(8,128)S(1)} %add.37), channel_id=1, source_target_pairs={{0,8},{4,12},{8,0},{12,4},{16,24},{20,28},{24,16},{28,20},{1,9},{5... | collective-permute-start | bytes 24584 | tf_op jit(solution)/shard_map/ppermute | solution.py:28
  180.9 4.7 %collective-permute-start.21 = (f32[16,128]{1,0:T(8,128)S(1)}, f32[16,128]{1,0:T(8,128)S(1)}, u32[]{:S(2)}, u32[]{:S(2)}) collective-permute-start(f32[16,128]{1,0:T(8,128)S(1)} %add.38), channel_id=1, source_target_pairs={{0,16},{4,20},{8,24},{12,28},{16,0},{20,4},{24,8},{28,12},{1,17},{... | collective-permute-start | bytes 24584 | tf_op jit(solution)/shard_map/ppermute | solution.py:28

commit v2 on v0

v2 whole, which is shorter than its diff:
```python
import functools

import jax
import jax.numpy as jnp
from jax import lax
from jax.experimental import pallas as pl
from jax.experimental.pallas import tpu as pltpu
from jax.sharding import PartitionSpec as P

MIB = 2**20
LINES = 8


def shifted(array, axis, by):
    count = lax.axis_size(axis)
    return lax.ppermute(array, axis, [(i, (i + by) % count) for i in range(count)])


def rounds(axis):
    left, radices = lax.axis_size(axis), []
    if left % 2 == 0 and left > 4:
        radices, left = [2], left // 2
    while left > 1:
        radix = 4 if left % 4 == 0 else 2
        radices, left = radices + [radix], left // radix
    return radices


def summed(array):
    for axis in ("col", "row"):
        count = lax.axis_size(axis)
        if count & (count - 1):
            array = lax.psum(array, axis)
            continue
        hop = 1
        for radix in rounds(axis):
            others = [
                lax.ppermute(array, axis, [(i, i ^ (hop * k)) for i in range(count)])
                for k in range(1, radix)
            ]
            array = array + others[0]
            if radix == 4:
                array = array + (others[1] + others[2])
            hop *= radix
    return array


def vmem():
    return pl.BlockSpec(memory_space=pltpu.VMEM)


def smem():
    return pl.BlockSpec(memory_space=pltpu.SMEM)


def call(kernel, name, out_shape, specs, scratch=(), flops=0, moved=MIB, limit=12):
    return pl.pallas_call(
        kernel,
        out_shape=out_shape,
        in_specs=specs,
        out_specs=jax.tree.map(lambda _: vmem(), out_shape),
        scratch_shapes=list(scratch),
        compiler_params=pltpu.CompilerParams(vmem_limit_bytes=limit * MIB),
        cost_estimate=pl.CostEstimate(flops=flops, bytes_accessed=moved, transcendentals=0),
        name=name,
    )


def wide(parts):
    return jnp.concatenate(parts, axis=1)


def folded(term):
    return jnp.sum(term.reshape(-1, 8, term.shape[-1]), axis=0)


def lined(parts):
    lines = [jnp.sum(p, axis=0, keepdims=True) for p in parts]
    lines.append(jnp.zeros((LINES - len(lines), parts[0].shape[1]), jnp.float32))
    return jnp.concatenate(lines, axis=0)


def pack(readers, right_side, width):
    fields, rows, orbitals = right_side.shape
    span, served = readers.shape[1:]

    def kernel(readers_ref, right_ref, *messages):
        for offset, message in enumerate(messages):
            for slot in range(served):
                start = pl.multiple_of(readers_ref[0, offset, slot] * width, width)
                for field in range(fields):
                    message[
                        slot * width : (slot + 1) * width, field * orbitals : (field + 1) * orbitals
                    ] = right_ref[field, pl.ds(start, width), :].astype(jnp.bfloat16)

    shape = jax.ShapeDtypeStruct((served * width, fields * orbitals), jnp.bfloat16)
    return call(kernel, "pack", [shape] * span, [smem(), vmem()])(readers, right_side)


def early(right_side, onsite):
    fields, rows, orbitals = right_side.shape
    clusters, width = onsite.shape
    lanes = fields * orbitals

    def kernel(right_ref, onsite_ref, sums_ref, level_ref):
        norm = [jnp.zeros((8, orbitals), jnp.float32) for _ in range(fields)]
        heavy = list(norm)
        for cluster in range(clusters):
            level = jnp.transpose(
                jnp.broadcast_to(onsite_ref[cluster : cluster + 1, :], (width, width))
            )
            level_ref[cluster] = level
            for field in range(fields):
                right = right_ref[field, cluster * width : (cluster + 1) * width, :]
                square = right * right
                norm[field] += folded(square)
                heavy[field] += folded(square * level)
        sums_ref[...] = lined([wide(norm), wide(heavy)])

    return call(
        kernel,
        "early",
        [
            jax.ShapeDtypeStruct((LINES, lanes), jnp.float32),
            jax.ShapeDtypeStruct((clusters, width, width), jnp.float32),
        ],
        [vmem(), vmem()],
        flops=4 * MIB,
        moved=4 * MIB,
    )(right_side, onsite)


def spread(tile_slot, ks_tiles, correlation_tiles, span, served):
    clusters, _, width, _ = ks_tiles.shape
    slots = span * served

    def kernel(slot_ref, ks_ref, correlation_ref, out_ref, where):
        @pl.loop(0, clusters)
        def _(cluster):
            for kind, ref in enumerate((ks_ref, correlation_ref)):
                count = ref.shape[1]
                for slot in range(slots):
                    where[slot] = count
                for tile in range(count):
                    where[slot_ref[cluster, tile]] = tile
                for slot in range(slots):
                    tile = where[slot]
                    block = ref[cluster, jnp.minimum(tile, count - 1)]
                    block = jnp.where(tile < count, block, jnp.zeros_like(block))
                    lane = slot % served * width
                    out_ref[
                        slot // served, cluster, kind * width : (kind + 1) * width, lane : lane + width
                    ] = block

    return call(
        kernel,
        "spread",
        jax.ShapeDtypeStruct((span, clusters, 2 * width, served * width), jnp.bfloat16),
        [smem(), vmem(), vmem()],
        [pltpu.SMEM((slots,), jnp.int32)],
        moved=16 * MIB,
    )(tile_slot, ks_tiles, correlation_tiles)


def product(dense_ref, offsets, vectors, cluster, energy):
    value = None
    for offset, vector in zip(offsets, vectors):
        part = jnp.dot(dense_ref[offset, cluster], vector[...], preferred_element_type=jnp.float32)
        value = part if value is None else value + part
    half = value.shape[0] // 2
    return value[:half] - energy * value[half:]


def work(dense, offsets, lanes):
    return 2 * len(offsets) * dense.shape[1] * dense.shape[2] * dense.shape[3] * lanes


def couple(dense, offsets, vectors, energies, total):
    _, clusters, height, _ = dense.shape
    lanes = vectors[0].shape[1]
    count = len(offsets)
    had = total is not None

    def kernel(*refs):
        dense_ref, energies_ref, out_ref = refs[0], refs[1], refs[-1]
        energy = energies_ref[...]

        @pl.loop(0, clusters)
        def _(cluster):
            value = product(dense_ref, offsets, refs[2 : 2 + count], cluster, energy)
            if had:
                value = value + refs[2 + count][cluster]
            out_ref[cluster] = value

    inputs = [dense, energies, *vectors] + ([total] if had else [])
    return call(
        kernel,
        "couple",
        jax.ShapeDtypeStruct((clusters, height // 2, lanes), jnp.float32),
        [vmem()] * len(inputs),
        flops=work(dense, offsets, lanes),
        moved=4 * MIB,
    )(*inputs)


def per_field(values, orbitals):
    return wide([jnp.broadcast_to(v, (1, orbitals)) for v in values])


def totals(sums, line, fields):
    orbitals = sums.shape[1] // fields
    return [
        jnp.sum(sums[line : line + 1, f * orbitals : (f + 1) * orbitals], axis=1, keepdims=True)
        for f in range(fields)
    ]


def center(first, fields):
    norm, heavy = totals(first, 0, fields), totals(first, 1, fields)
    return per_field([h / n for h, n in zip(heavy, norm)], first.shape[1] // fields)


def step_sizes(first, second, fields):
    orbitals = first.shape[1] // fields
    norm = totals(first, 0, fields)
    alpha = [n / b for n, b in zip(norm, totals(second, 0, fields))]
    growth = [a * a * s / n for a, s, n in zip(alpha, totals(second, 1, fields), norm)]
    return per_field(alpha, orbitals), per_field(growth, orbitals)


def finish_first(dense, offsets, vectors, energies, total, right_side, level, first, readers):
    _, clusters, height, depth = dense.shape
    lanes = vectors[0].shape[1]
    fields = right_side.shape[0]
    width = height // 2
    count = len(offsets)
    span, served = readers.shape[1:]

    def kernel(dense_ref, energies_ref, *refs):
        vector_refs, refs = refs[:count], refs[count:]
        total_ref, right_ref, level_ref, first_ref, readers_ref, image_ref, sums_ref = refs[:7]
        messages, (bend, square, outgoing) = refs[7 : 7 + span], refs[7 + span :]
        energy = energies_ref[...]
        middle = center(first_ref, fields)
        bend[...] = jnp.zeros_like(bend)
        square[...] = jnp.zeros_like(square)

        @pl.loop(0, clusters)
        def _(cluster):
            value = product(dense_ref, offsets, vector_refs, cluster, energy) + total_ref[cluster]
            rows = pl.ds(pl.multiple_of(cluster * width, width), width)
            right = wide([right_ref[f, rows, :] for f in range(fields)])
            image = wide([level_ref[cluster]] * fields) * right + value
            image_ref[cluster] = image
            outgoing[cluster] = (image - middle * right).astype(jnp.bfloat16)
            bend[...] += folded(right * image)
            square[...] += folded(image * image)

        for offset, message in enumerate(messages):
            for slot in range(served):
                message[slot * width : (slot + 1) * width, :] = outgoing[readers_ref[0, offset, slot]]
        sums_ref[...] = lined([bend[...], square[...]])

    message = jax.ShapeDtypeStruct((depth, lanes), jnp.bfloat16)
    return call(
        kernel,
        "finish_first",
        [
            jax.ShapeDtypeStruct((clusters, width, lanes), jnp.float32),
            jax.ShapeDtypeStruct((LINES, lanes), jnp.float32),
        ]
        + [message] * span,
        [vmem()] * (2 + count + 4) + [smem()],
        [pltpu.VMEM((8, lanes), jnp.float32)] * 2
        + [pltpu.VMEM((clusters, width, lanes), jnp.bfloat16)],
        flops=work(dense, offsets, lanes),
        moved=8 * MIB,
    )(dense, energies, *vectors, total, right_side, level, first, readers)


def finish_second(dense, offsets, vectors, energies, total, right_side, level, image, first, second):
    _, clusters, height, _ = dense.shape
    lanes = vectors[0].shape[1]
    fields = right_side.shape[0]
    width = height // 2
    count = len(offsets)

    def kernel(dense_ref, energies_ref, *refs):
        vector_refs, refs = refs[:count], refs[count:]
        total_ref, right_ref, level_ref, image_ref, first_ref, second_ref = refs[:6]
        later_ref, sums_ref, bend, square = refs[6:]
        energy = energies_ref[...]
        middle = center(first_ref, fields)
        alpha, growth = step_sizes(first_ref, second_ref, fields)
        bend[...] = jnp.zeros_like(bend)
        square[...] = jnp.zeros_like(square)

        @pl.loop(0, clusters)
        def _(cluster):
            value = product(dense_ref, offsets, vector_refs, cluster, energy) + total_ref[cluster]
            rows = pl.ds(pl.multiple_of(cluster * width, width), width)
            right = wide([right_ref[f, rows, :] for f in range(fields)])
            onsite = wide([level_ref[cluster]] * fields)
            before = image_ref[cluster]
            coupled = before - onsite * right
            residual = right - alpha * before
            direction = growth * right - alpha * before
            later = onsite * direction + (growth - alpha * middle) * coupled - alpha * value
            later_ref[cluster] = later
            square[...] += folded(residual * residual)
            bend[...] += folded(direction * later)

        sums_ref[...] = lined([square[...], bend[...]])

    return call(
        kernel,
        "finish_second",
        [
            jax.ShapeDtypeStruct((clusters, width, lanes), jnp.float32),
            jax.ShapeDtypeStruct((LINES, lanes), jnp.float32),
        ],
        [vmem()] * (2 + count + 6),
        [pltpu.VMEM((8, lanes), jnp.float32)] * 2,
        flops=work(dense, offsets, lanes),
        moved=8 * MIB,
    )(dense, energies, *vectors, total, right_side, level, image, first, second)


def final(right_side, image, later, first, second, third):
    fields, rows, orbitals = right_side.shape
    clusters, width, lanes = image.shape
    blocks = 4
    each = clusters // blocks

    def kernel(right_ref, image_ref, later_ref, first_ref, second_ref, third_ref, solution_ref, residual_ref):
        step = pl.program_id(0)
        alpha, growth = step_sizes(first_ref, second_ref, fields)
        norm, bend = totals(third_ref, 0, fields), totals(third_ref, 1, fields)
        gain = per_field([n / b for n, b in zip(norm, bend)], orbitals)
        for local in range(each):
            cluster = step * each + local
            rows = pl.ds(pl.multiple_of(cluster * width, width), width)
            for field in range(fields):
                part = slice(field * orbitals, (field + 1) * orbitals)
                right = right_ref[field, rows, :]
                before = alpha[:, part] * image_ref[cluster, :, part]
                direction = growth[:, part] * right - before
                here = slice(local * width, (local + 1) * width)
                solution_ref[field, here, :] = alpha[:, part] * right + gain[:, part] * direction
                residual_ref[field, here, :] = (right - before) - gain[:, part] * later_ref[
                    cluster, :, part
                ]

    vector = pl.BlockSpec((fields, each * width, orbitals), lambda i: (0, i, 0))
    shape = jax.ShapeDtypeStruct(right_side.shape, jnp.float32)
    return pl.pallas_call(
        kernel,
        grid=(blocks,),
        out_shape=[shape, shape],
        in_specs=[vmem()] * 6,
        out_specs=[vector, vector],
        compiler_params=pltpu.CompilerParams(vmem_limit_bytes=12 * MIB),
        name="final",
    )(right_side, image, later, first, second, third)


def body(right_side, onsite, energies, ks_tiles, correlation_tiles, tile_slot, readers):
    fields = right_side.shape[0]
    span, served = readers.shape[1:]
    width = ks_tiles.shape[2]
    middle = (span - 1) // 2
    onsite = onsite.reshape(-1, width)
    energies = jnp.tile(energies.reshape(1, -1), (1, fields))

    order = [middle]
    for far in range(middle, 0, -1):
        order += [middle - far, middle + far]
    groups = [order[:1], order[1:3], order[3:5], order[5:6], order[6:]]

    def exchange(messages):
        return [shifted(m, "row", middle - o) if o != middle else m for o, m in enumerate(messages)]

    def partial(vectors):
        total = None
        for group in groups[:-1]:
            total = couple(dense, group, [vectors[o] for o in group], energies, total)
        return dense, groups[-1], [vectors[o] for o in groups[-1]], energies, total

    vectors = exchange(pack(readers, right_side, width))
    first, level = early(right_side, onsite)
    first = summed(first)
    dense = spread(tile_slot, ks_tiles, correlation_tiles, span, served)
    image, second, *messages = finish_first(*partial(vectors), right_side, level, first, readers)
    vectors = exchange(messages)
    second = summed(second)
    later, third = finish_second(*partial(vectors), right_side, level, image, first, second)
    third = summed(third)
    return tuple(final(right_side, image, later, first, second, third))


def solution(mesh):
    placed = (
        P(None, "row", "col"),
        P("row"),
        P("col"),
        P("row", None, None, None),
        P("row", None, None, None),
        P("row", None),
        P("row", None, None),
    )
    return jax.shard_map(
        body,
        mesh=mesh,
        in_specs=placed,
        out_specs=(P(None, "row", "col"), P(None, "row", "col")),
        check_vma=False,
    )
```

time: 407 us -> 181 us (0.44)
  blocking collectives: 139 us -> 0 us
  local copies, waits for them, and re-layouts: 92.7 us -> 7.25 us
  matrix products: 39.7 us -> 0 us
  Pallas kernels: 0 us -> 38.9 us
  starting transfers between devices: 24.9 us -> 57.3 us
  waiting for transfers between devices: 92.6 us -> 76 us
  other arithmetic: 15.8 us -> 0.05 us
    psum x3 -> x0, blocking collectives: 139 us -> none  [the longest x2 89.5 us: squares(): return lax.psum(jnp.sum(vector * vector, axis=(1, 2)), ('row', 'col'))]
    ppermute x12, waiting for transfers between devices: 92.6 us -> 15.4 us  [shifted(): lax.ppermute(array, axis, [(i, (i + by) % count) for i in range(count)])]
    ppermute x0 -> x21, waiting for transfers between devices: none -> 60.6 us  [summed(): lax.ppermute(array, axis, [(i, i ^ hop * k) for i in range(count)])]
    dot_general x5 -> x0, matrix products: 39.7 us -> none  [the longest x2 18.1 us: body(): jnp.einsum('rk,fkj->frj', dense_ks, gathered, preferred_element_type=jnp....]
    pallas_call x0 -> x14, Pallas kernels: none -> 38.9 us  [the longest x8 23.7 us: couple(): call(kernel, 'couple', jax.ShapeDtypeStruct((clusters, height // 2, lanes...]
    ppermute x0 -> x21, starting transfers between devices: none -> 35.3 us  [summed(): lax.ppermute(array, axis, [(i, i ^ hop * k) for i in range(count)])]
    reshape x6 -> x0, local copies, waits for them, and re-layouts: 30.6 us -> none  [the longest x1 12.8 us: body(): dense_ks.astype(jnp.bfloat16).reshape(clusters * width, slots * width)]
    another operation x6 -> x0, local copies, waits for them, and re-layouts: 18.6 us -> none  [body(): received = jnp.stack(pieces, 1)]
  transfers between devices with their start and end apart: 12 -> 33, of which waited for: 6 -> 16; matrix products, arithmetic and copies ran while one was open for 8% -> 0% of each run, Pallas kernels for 0% -> 16%
where the time goes in v2:
time: 181 us; the launch traced here: 180 us
  waiting for transfers between devices  76 us (42%)
  starting transfers between devices  57.3 us (32%)
  Pallas kernels  38.9 us (21%)
  local copies, waits for them, and re-layouts  7.25 us (4%)
    ppermute x21, waiting for transfers between devices, summed(): lax.ppermute(array, axis, [(i, i ^ hop * k) for i in range(count)])  60.6 us
    ppermute x21, starting transfers between devices, summed(): lax.ppermute(array, axis, [(i, i ^ hop * k) for i in range(count)])  35.3 us
    pallas_call x8, Pallas kernels, couple(): call(kernel, 'couple', jax.ShapeDtypeStruct((clusters, height // 2, lanes...  23.7 us
    ppermute x12, starting transfers between devices, shifted(): lax.ppermute(array, axis, [(i, (i + by) % count) for i in range(count)])  22 us
    ppermute x12, waiting for transfers between devices, shifted(): lax.ppermute(array, axis, [(i, (i + by) % count) for i in range(count)])  15.4 us
    unnamed x17, local copies, waits for them, and re-layouts  7.25 us
    pallas_call x1, Pallas kernels, spread(): call(kernel, 'spread', jax.ShapeDtypeStruct((span, clusters, 2 * width, s...  4.86 us
    pallas_call x1, Pallas kernels, finish_first(): call(kernel, 'finish_first', [jax.ShapeDtypeStruct((clusters, width, lane...  3.75 us
  transfers between devices with their start and end apart: 33, of which 16 were waited for; matrix products, arithmetic and copies ran while one was open for 0% of the time, Pallas kernels for 16%

profile of v2, /device:TPU:0, one launch (start us, length us, event | category | flops | bytes accessed | tf_op | source)
XLA Modules:
  0.0 180.3 jit_solution(4143869303046191827)
XLA Ops:
  0.7 1.4 copy-done.1
  3.0 2.4 %collective-permute-start.8 = (f32[8,384]{1,0:T(8,128)S(1)}, f32[8,384]{1,0:T(8,128)S(1)}, u32[]{:S(2)}, u32[]{:S(2)}) collective-permute-start(f32[8,384]{1,0:T(8,128)S(1)} %get-tuple-element.30), channel_id=1, source_target_pairs={{0,3},{1,2},{2,1},{3,0},{4,7},{5,6},{6,5},{7,4},{8,11},{9,10},{10,... | collective-permute-start | bytes 36872 | tf_op jit(solution)/shard_map/ppermute | solution.py:38
  6.9 1.0 pack.1
  7.9 2.8 %collective-permute-start.4 = (bf16[512,384]{1,0:T(8,128)(2,1)S(1)}, bf16[512,384]{1,0:T(8,128)(2,1)S(1)}, u32[]{:S(2)}, u32[]{:S(2)}) collective-permute-start(bf16[512,384]{1,0:T(8,128)(2,1)S(1)} %get-tuple-element.26), channel_id=1, source_target_pairs={{0,12},{4,16},{8,20},{12,24},{16,28},{20,0},{24,4},{28,8},{1,13},{... | collective-permute-start | bytes 1179656 | tf_op jit(solution)/shard_map/ppermute | solution.py:16
  10.7 1.6 collective-permute-start.9
  12.3 1.6 collective-permute-start.2
  13.9 1.2 collective-permute-start.5
  15.1 2.7 %collective-permute-start.12 = (f32[8,384]{1,0:T(8,128)S(1)}, f32[8,384]{1,0:T(8,128)S(1)}, u32[]{:S(2)}, u32[]{:S(2)}) collective-permute-start(f32[8,384]{1,0:T(8,128)S(1)} %add.66), channel_id=1, source_target_pairs={{0,24},{4,28},{8,16},{12,20},{16,8},{20,12},{24,0},{28,4},{1,25},{... | collective-permute-start | bytes 36872 | tf_op jit(solution)/shard_map/ppermute | solution.py:38
  17.8 6.4 %collective-permute-start.11 = (f32[8,384]{1,0:T(8,128)S(1)}, f32[8,384]{1,0:T(8,128)S(1)}, u32[]{:S(2)}, u32[]{:S(2)}) collective-permute-start(f32[8,384]{1,0:T(8,128)S(1)} %add.66), channel_id=1, source_target_pairs={{0,16},{4,20},{8,24},{12,28},{16,0},{20,4},{24,8},{28,12},{1,17},{... | collective-permute-start | bytes 36872 | tf_op jit(solution)/shard_map/ppermute | solution.py:38
  24.2 2.8 %copy-done.3 = bf16[8,24,128,128]{3,2,1,0:T(8,128)(2,1)S(1)} copy-done((bf16[8,24,128,128]{3,2,1,0:T(8,128)(2,1)S(1)}, bf16[8,24,128,128]{3,2,1,0:T(8,128)(2,1)}, u32[]{:S(2)}) %copy-start.3) | copy-done | bytes 6291480
  26.9 1.6 copy-done.4
  28.5 4.9 %spread.1.refs_0_.dense_ref = bf16[7,8,256,512]{3,2,1,0:T(8,128)(2,1)S(1)} custom-call(s32[8,24]{1,0:T(8,128)S(1)} %copy-done.6, bf16[8,24,128,128]{3,2,1,0:T(8,128)(2,1)S(1)} %copy-done.3, bf16[8,8,128,128]{3,2,1,0:T(8,128)(2,1)S(1)} %copy-done.4), custom_call_target="tpu_custom_call" | custom-call | bytes 16777216 | tf_op jit(solution)/shard_map/spread/pallas_call | solution.py:155
  33.4 6.1 %collective-permute-done.12 = f32[8,384]{1,0:T(8,128)S(1)} collective-permute-done((f32[8,384]{1,0:T(8,128)S(1)}, f32[8,384]{1,0:T(8,128)S(1)}, u32[]{:S(2)}, u32[]{:S(2)}) %collective-permute-start.12) | collective-permute-done | bytes 12320 | tf_op jit(solution)/shard_map/ppermute | solution.py:38
  39.5 1.6 collective-permute-start.3
  41.1 7.4 %collective-permute-done.11 = f32[8,384]{1,0:T(8,128)S(1)} collective-permute-done((f32[8,384]{1,0:T(8,128)S(1)}, f32[8,384]{1,0:T(8,128)S(1)}, u32[]{:S(2)}, u32[]{:S(2)}) %collective-permute-start.11) | collective-permute-done | bytes 12320 | tf_op jit(solution)/shard_map/ppermute | solution.py:38
  48.5 7.3 %collective-permute-start.10 = (f32[8,384]{1,0:T(8,128)S(1)}, f32[8,384]{1,0:T(8,128)S(1)}, u32[]{:S(2)}, u32[]{:S(2)}) collective-permute-start(f32[8,384]{1,0:T(8,128)S(1)} %add.66), channel_id=1, source_target_pairs={{0,8},{4,12},{8,0},{12,4},{16,24},{20,28},{24,16},{28,20},{1,9},{5... | collective-permute-start | bytes 36872 | tf_op jit(solution)/shard_map/ppermute | solution.py:38
  55.8 2.4 %couple.8.refs_4_ = f32[8,128,384]{2,1,0:T(8,128)S(1)} custom-call(bf16[7,8,256,512]{3,2,1,0:T(8,128)(2,1)S(1)} %spread.1.refs_0_.dense_ref, f32[1,384]{1,0:T(1,128)S(1)} %bitcast.7, bf16[512,384]{1,0:T(8,128)(2,1)S(1)} %get-tuple-element.28.refs_2_), custom_call_target="tpu_custom_call" | custom-call | flops 805306368 | bytes 4194304 | tf_op jit(solution)/shard_map/couple/pallas_call | solution.py:196
  58.2 6.3 %collective-permute-done.10 = f32[8,384]{1,0:T(8,128)S(1)} collective-permute-done((f32[8,384]{1,0:T(8,128)S(1)}, f32[8,384]{1,0:T(8,128)S(1)}, u32[]{:S(2)}, u32[]{:S(2)}) %collective-permute-start.10) | collective-permute-done | bytes 12320 | tf_op jit(solution)/shard_map/ppermute | solution.py:38
  64.5 4.1 %collective-permute-start = (bf16[512,384]{1,0:T(8,128)(2,1)S(1)}, bf16[512,384]{1,0:T(8,128)(2,1)S(1)}, u32[]{:S(2)}, u32[]{:S(2)}) collective-permute-start(bf16[512,384]{1,0:T(8,128)(2,1)S(1)} %get-tuple-element.22), channel_id=1, source_target_pairs={{0,28},{4,0},{8,4},{12,8},{16,12},{20,16},{24,20},{28,24},{1,29},{... | collective-permute-start | bytes 1179656 | tf_op jit(solution)/shard_map/ppermute | solution.py:16
  68.7 3.5 %couple.9.refs_4_ = f32[8,128,384]{2,1,0:T(8,128)S(1)} custom-call(bf16[7,8,256,512]{3,2,1,0:T(8,128)(2,1)S(1)} %spread.1.refs_0_.dense_ref, f32[1,384]{1,0:T(1,128)S(1)} %bitcast.8, bf16[512,384]{1,0:T(8,128)(2,1)S(1)} %collective-permute-done.4.refs_2_, bf16[512,384]{1,0:T(8,128)(2,1)S(1)} %collective-permute-done.5.refs_3_, f32[8,128,384]{2,1,0:T(8,128)S(1)} %couple.8.refs_4_), custom_call_target="tpu_custom_call" | custom-call | flops 1610612736 | bytes 4194304 | tf_op jit(solution)/shard_map/couple/pallas_call | solution.py:196
  72.2 3.5 %couple.10.refs_3_ = f32[8,128,384]{2,1,0:T(8,128)S(1)} custom-call(bf16[7,8,256,512]{3,2,1,0:T(8,128)(2,1)S(1)} %spread.1.refs_0_.dense_ref, f32[1,384]{1,0:T(1,128)S(1)} %bitcast.9, bf16[512,384]{1,0:T(8,128)(2,1)S(1)} %collective-permute-done.2.refs_2_, bf16[512,384]{1,0:T(8,128)(2,1)S(1)} %collective-permute-done.3.refs_3_, f32[8,128,384]{2,1,0:T(8,128)S(1)} %couple.9.refs_4_), custom_call_target="tpu_custom_call" | custom-call | flops 1610612736 | bytes 4194304 | tf_op jit(solution)/shard_map/couple/pallas_call | solution.py:196
  75.7 8.1 %collective-permute-done.1.refs_2_ = bf16[512,384]{1,0:T(8,128)(2,1)S(1)} collective-permute-done((bf16[512,384]{1,0:T(8,128)(2,1)S(1)}, bf16[512,384]{1,0:T(8,128)(2,1)S(1)}, u32[]{:S(2)}, u32[]{:S(2)}) %collective-permute-start.1) | collective-permute-done | bytes 393248 | tf_op jit(solution)/shard_map/ppermute | solution.py:16
  83.9 2.4 %couple.11.refs_1_ = f32[8,128,384]{2,1,0:T(8,128)S(1)} custom-call(bf16[7,8,256,512]{3,2,1,0:T(8,128)(2,1)S(1)} %spread.1.refs_0_.dense_ref, f32[1,384]{1,0:T(1,128)S(1)} %bitcast.10, bf16[512,384]{1,0:T(8,128)(2,1)S(1)} %collective-permute-done.1.refs_2_, f32[8,128,384]{2,1,0:T(8,128)S(1)} %couple.10.refs_3_), custom_call_target="tpu_custom_call" | custom-call | flops 805306368 | bytes 4194304 | tf_op jit(solution)/shard_map/couple/pallas_call | solution.py:196
  86.3 3.8 %finish_first.1 = (f32[8,128,384]{2,1,0:T(8,128)S(1)}, f32[8,384]{1,0:T(8,128)S(1)}, bf16[512,384]{1,0:T(8,128)(2,1)S(1)}, bf16[512,384]{1,0:T(8,128)(2,1)S(1)},...) custom-call(bf16[7,8,256,512]{3,2,1,0:T(8,128)(2,1)S(1)} %spread.1.r, ...), custom_call_target="tpu_custom_call" | custom-call | flops 805306368 | bytes 8388608 | tf_op jit(solution)/shard_map/finish_first/pallas_call | solution.py:265
  90.1 1.5 collective-permute-start.17
  93.5 3.0 %collective-permute-start.18 = (bf16[512,384]{1,0:T(8,128)(2,1)S(1)}, bf16[512,384]{1,0:T(8,128)(2,1)S(1)}, u32[]{:S(2)}, u32[]{:S(2)}) collective-permute-start(bf16[512,384]{1,0:T(8,128)(2,1)S(1)} %get-tuple-element.37), channel_id=1, source_target_pairs={{0,20},{4,24},{8,28},{12,0},{16,4},{20,8},{24,12},{28,16},{1,21},{... | collective-permute-start | bytes 1179656 | tf_op jit(solution)/shard_map/ppermute | solution.py:16
  96.5 2.8 %collective-permute-start.22 = (f32[8,384]{1,0:T(8,128)S(1)}, f32[8,384]{1,0:T(8,128)S(1)}, u32[]{:S(2)}, u32[]{:S(2)}) collective-permute-start(f32[8,384]{1,0:T(8,128)S(1)} %add_add_fusion.3), channel_id=1, source_target_pairs={{0,4},{4,0},{8,12},{12,8},{16,20},{20,16},{24,28},{28,24},{1,5},{5... | collective-permute-start | bytes 36872 | tf_op jit(solution)/shard_map/ppermute | solution.py:38
  99.3 12.5 %collective-permute-done.22 = f32[8,384]{1,0:T(8,128)S(1)} collective-permute-done((f32[8,384]{1,0:T(8,128)S(1)}, f32[8,384]{1,0:T(8,128)S(1)}, u32[]{:S(2)}, u32[]{:S(2)}) %collective-permute-start.22) | collective-permute-done | bytes 12320 | tf_op jit(solution)/shard_map/ppermute | solution.py:38
  112.1 4.1 %collective-permute-start.15 = (bf16[512,384]{1,0:T(8,128)(2,1)S(1)}, bf16[512,384]{1,0:T(8,128)(2,1)S(1)}, u32[]{:S(2)}, u32[]{:S(2)}) collective-permute-start(bf16[512,384]{1,0:T(8,128)(2,1)S(1)} %get-tuple-element.34), channel_id=1, source_target_pairs={{0,8},{4,12},{8,16},{12,20},{16,24},{20,28},{24,0},{28,4},{1,9},{5... | collective-permute-start | bytes 1179656 | tf_op jit(solution)/shard_map/ppermute | solution.py:16
  116.2 1.2 collective-permute-done.25
  117.4 13.8 %collective-permute-done.24 = f32[8,384]{1,0:T(8,128)S(1)} collective-permute-done((f32[8,384]{1,0:T(8,128)S(1)}, f32[8,384]{1,0:T(8,128)S(1)}, u32[]{:S(2)}, u32[]{:S(2)}) %collective-permute-start.24) | collective-permute-done | bytes 12320 | tf_op jit(solution)/shard_map/ppermute | solution.py:38
  131.6 2.4 %couple.12.refs_4_ = f32[8,128,384]{2,1,0:T(8,128)S(1)} custom-call(bf16[7,8,256,512]{3,2,1,0:T(8,128)(2,1)S(1)} %spread.1.refs_0_.dense_ref, f32[1,384]{1,0:T(1,128)S(1)} %bitcast.12, bf16[512,384]{1,0:T(8,128)(2,1)S(1)} %get-tuple-element.38.refs_2_), custom_call_target="tpu_custom_call" | custom-call | flops 805306368 | bytes 4194304 | tf_op jit(solution)/shard_map/couple/pallas_call | solution.py:196
  134.0 7.2 %collective-permute-done.23 = f32[8,384]{1,0:T(8,128)S(1)} collective-permute-done((f32[8,384]{1,0:T(8,128)S(1)}, f32[8,384]{1,0:T(8,128)S(1)}, u32[]{:S(2)}, u32[]{:S(2)}) %collective-permute-start.23) | collective-permute-done | bytes 12320 | tf_op jit(solution)/shard_map/ppermute | solution.py:38
  141.2 2.0 %collective-permute-start.14 = (bf16[512,384]{1,0:T(8,128)(2,1)S(1)}, bf16[512,384]{1,0:T(8,128)(2,1)S(1)}, u32[]{:S(2)}, u32[]{:S(2)}) collective-permute-start(bf16[512,384]{1,0:T(8,128)(2,1)S(1)} %get-tuple-element.33), channel_id=1, source_target_pairs={{0,4},{4,8},{8,12},{12,16},{16,20},{20,24},{24,28},{28,0},{1,5},{5... | collective-permute-start | bytes 1179656 | tf_op jit(solution)/shard_map/ppermute | solution.py:16
  143.2 3.5 %couple.13.refs_4_ = f32[8,128,384]{2,1,0:T(8,128)S(1)} custom-call(bf16[7,8,256,512]{3,2,1,0:T(8,128)(2,1)S(1)} %spread.1.refs_0_.dense_ref, f32[1,384]{1,0:T(1,128)S(1)} %bitcast.13, bf16[512,384]{1,0:T(8,128)(2,1)S(1)} %collective-permute-done.17.refs_2_, bf16[512,384]{1,0:T(8,128)(2,1)S(1)} %collective-permute-done.18.refs_3_, ...), custom_call_target="tpu_custom_call" | custom-call | flops 1610612736 | bytes 4194304 | tf_op jit(solution)/shard_map/couple/pallas_call | solution.py:196
  146.8 3.5 %couple.14.refs_3_ = f32[8,128,384]{2,1,0:T(8,128)S(1)} custom-call(bf16[7,8,256,512]{3,2,1,0:T(8,128)(2,1)S(1)} %spread.1.refs_0_.dense_ref, f32[1,384]{1,0:T(1,128)S(1)} %bitcast.14, bf16[512,384]{1,0:T(8,128)(2,1)S(1)} %collective-permute-done.15.refs_2_, bf16[512,384]{1,0:T(8,128)(2,1)S(1)} %collective-permute-done.16.refs_3_, ...), custom_call_target="tpu_custom_call" | custom-call | flops 1610612736 | bytes 4194304 | tf_op jit(solution)/shard_map/couple/pallas_call | solution.py:196
  150.3 6.6 %collective-permute-done.14.refs_2_ = bf16[512,384]{1,0:T(8,128)(2,1)S(1)} collective-permute-done((bf16[512,384]{1,0:T(8,128)(2,1)S(1)}, bf16[512,384]{1,0:T(8,128)(2,1)S(1)}, u32[]{:S(2)}, u32[]{:S(2)}) %collective-permute-start.14) | collective-permute-done | bytes 393248 | tf_op jit(solution)/shard_map/ppermute | solution.py:16
  156.9 2.4 %couple.15.refs_1_ = f32[8,128,384]{2,1,0:T(8,128)S(1)} custom-call(bf16[7,8,256,512]{3,2,1,0:T(8,128)(2,1)S(1)} %spread.1.refs_0_.dense_ref, f32[1,384]{1,0:T(1,128)S(1)} %bitcast.15, bf16[512,384]{1,0:T(8,128)(2,1)S(1)} %collective-permute-done.14.refs_2_, f32[8,128,384]{2,1,0:T(8,128)S(1)} %couple.14.refs_3_), custom_call_target="tpu_custom_call" | custom-call | flops 805306368 | bytes 4194304 | tf_op jit(solution)/shard_map/couple/pallas_call | solution.py:196
  159.9 2.7 %finish_second.1 = (f32[8,128,384]{2,1,0:T(8,128)S(1)}, f32[8,384]{1,0:T(8,128)S(1)}) custom-call(bf16[7,8,256,512]{3,2,1,0:T(8,128)(2,1)S(1)} %spread.1.refs_0_.dense_ref, f32[1,384]{1,0:T(1,128)S(1)} %bitcast.16, bf16[512,384]{1,0:T(8,128)(2,1)S(1)} %collective-permute-done.13.refs_0_, f32[8,128,384]{2,1,0:T(8,128)S(1)} %couple.15.refs_1_, ...), custom_call_target="tpu_custom_call" | custom-call | flops 805306368 | bytes 8388608 | tf_op jit(solution)/shard_map/finish_second/pallas_call | solution.py:315
  163.1 1.1 collective-permute-start.27
  164.6 1.3 collective-permute-done.28
  166.8 2.5 %collective-permute-start.29 = (f32[8,384]{1,0:T(8,128)S(1)}, f32[8,384]{1,0:T(8,128)S(1)}, u32[]{:S(2)}, u32[]{:S(2)}) collective-permute-start(f32[8,384]{1,0:T(8,128)S(1)} %add_add_fusion.1), channel_id=1, source_target_pairs={{0,4},{4,0},{8,12},{12,8},{16,20},{20,16},{24,28},{28,24},{1,5},{5... | collective-permute-start | bytes 36872 | tf_op jit(solution)/shard_map/ppermute | solution.py:38
  169.4 1.7 collective-permute-done.29
  171.0 1.5 collective-permute-start.32
  172.5 1.4 collective-permute-start.31
  174.0 1.5 collective-permute-start.30
  175.4 1.1 collective-permute-done.32
  177.7 2.7 %final.1 = (f32[3,1024,128]{2,1,0:T(8,128)}, f32[3,1024,128]{2,1,0:T(8,128)}) custom-call(f32[3,1024,128]{2,1,0:T(8,128)S(1)} %copy-done.2, f32[8,128,384]{2,1,0:T(8,128)S(1)} %get-tuple-element.31.refs_4_.image_ref, f32[8,128,384]{2,1,0:T(8,128)S(1)} %get-tuple-element.40.later_ref, f32[8,384]{1,0:T(8,128)S(1)} %add_add_fusion.4.refs_4_.refs_5_.first_ref, ...), custom_call_target="tpu_custom_call" | custom-call | tf_op jit(solution)/shard_map/final/pallas_call | solution.py:356
  (58 shorter events, 8.6 us)
Async XLA Ops:
  0.6 23.5 %copy-start = (f32[128]{0:T(128)S(1)}, f32[128]{0:T(128)}, u32[]{:S(2)}) copy-start(f32[128]{0:T(128)} %param.9) | copy-start | bytes 1540
  0.6 1.4 copy-start.1
  2.1 0.7 copy-start.5
  2.7 4.1 %copy-start.2 = (f32[3,1024,128]{2,1,0:T(8,128)S(1)}, f32[3,1024,128]{2,1,0:T(8,128)}, u32[]{:S(2)}) copy-start(f32[3,1024,128]{2,1,0:T(8,128)} %right_ref.5) | copy-start | bytes 4718596
  2.8 21.4 %copy-start.6 = (s32[8,24]{1,0:T(8,128)S(1)}, s32[8,24]{1,0:T(8,128)}, u32[]{:S(2)}) copy-start(s32[8,24]{1,0:T(8,128)} %slot_ref.1) | copy-start | bytes 2308
  3.0 7.7 %collective-permute-start.8 = (f32[8,384]{1,0:T(8,128)S(1)}, f32[8,384]{1,0:T(8,128)S(1)}, u32[]{:S(2)}, u32[]{:S(2)}) collective-permute-start(f32[8,384]{1,0:T(8,128)S(1)} %get-tuple-element.30), channel_id=1, source_target_pairs={{0,3},{1,2},{2,1},{3,0},{4,7},{5,6},{6,5},{7,4},{8,11},{9,10},{10,... | collective-permute-start | bytes 36872 | tf_op jit(solution)/shard_map/ppermute | solution.py:38
  5.4 5.3 %collective-permute-start.7 = (f32[8,384]{1,0:T(8,128)S(1)}, f32[8,384]{1,0:T(8,128)S(1)}, u32[]{:S(2)}, u32[]{:S(2)}) collective-permute-start(f32[8,384]{1,0:T(8,128)S(1)} %get-tuple-element.30), channel_id=1, source_target_pairs={{0,2},{1,3},{2,0},{3,1},{4,6},{5,7},{6,4},{7,5},{8,10},{9,11},{10,... | collective-permute-start | bytes 36872 | tf_op jit(solution)/shard_map/ppermute | solution.py:38
  6.1 4.6 %collective-permute-start.6 = (f32[8,384]{1,0:T(8,128)S(1)}, f32[8,384]{1,0:T(8,128)S(1)}, u32[]{:S(2)}, u32[]{:S(2)}) collective-permute-start(f32[8,384]{1,0:T(8,128)S(1)} %get-tuple-element.30), channel_id=1, source_target_pairs={{0,1},{1,0},{2,3},{3,2},{4,5},{5,4},{6,7},{7,6},{8,9},{9,8},{10,11... | collective-permute-start | bytes 36872 | tf_op jit(solution)/shard_map/ppermute | solution.py:38
  7.9 60.8 %collective-permute-start.4 = (bf16[512,384]{1,0:T(8,128)(2,1)S(1)}, bf16[512,384]{1,0:T(8,128)(2,1)S(1)}, u32[]{:S(2)}, u32[]{:S(2)}) collective-permute-start(bf16[512,384]{1,0:T(8,128)(2,1)S(1)} %get-tuple-element.26), channel_id=1, source_target_pairs={{0,12},{4,16},{8,20},{12,24},{16,28},{20,0},{24,4},{28,8},{1,13},{... | collective-permute-start | bytes 1179656 | tf_op jit(solution)/shard_map/ppermute | solution.py:16
  10.7 4.3 %collective-permute-start.9 = (f32[8,384]{1,0:T(8,128)S(1)}, f32[8,384]{1,0:T(8,128)S(1)}, u32[]{:S(2)}, u32[]{:S(2)}) collective-permute-start(f32[8,384]{1,0:T(8,128)S(1)} %add_add_fusion.5), channel_id=1, source_target_pairs={{0,4},{4,0},{8,12},{12,8},{16,20},{20,16},{24,28},{28,24},{1,5},{5... | collective-permute-start | bytes 36872 | tf_op jit(solution)/shard_map/ppermute | solution.py:38
  12.3 59.9 %collective-permute-start.2 = (bf16[512,384]{1,0:T(8,128)(2,1)S(1)}, bf16[512,384]{1,0:T(8,128)(2,1)S(1)}, u32[]{:S(2)}, u32[]{:S(2)}) collective-permute-start(bf16[512,384]{1,0:T(8,128)(2,1)S(1)} %get-tuple-element.24), channel_id=1, source_target_pairs={{0,8},{4,12},{8,16},{12,20},{16,24},{20,28},{24,0},{28,4},{1,9},{5... | collective-permute-start | bytes 1179656 | tf_op jit(solution)/shard_map/ppermute | solution.py:16
  13.9 54.8 %collective-permute-start.5 = (bf16[512,384]{1,0:T(8,128)(2,1)S(1)}, bf16[512,384]{1,0:T(8,128)(2,1)S(1)}, u32[]{:S(2)}, u32[]{:S(2)}) collective-permute-start(bf16[512,384]{1,0:T(8,128)(2,1)S(1)} %get-tuple-element.27), channel_id=1, source_target_pairs={{0,20},{4,24},{8,28},{12,0},{16,4},{20,8},{24,12},{28,16},{1,21},{... | collective-permute-start | bytes 1179656 | tf_op jit(solution)/shard_map/ppermute | solution.py:16
  15.1 24.4 %collective-permute-start.12 = (f32[8,384]{1,0:T(8,128)S(1)}, f32[8,384]{1,0:T(8,128)S(1)}, u32[]{:S(2)}, u32[]{:S(2)}) collective-permute-start(f32[8,384]{1,0:T(8,128)S(1)} %add.66), channel_id=1, source_target_pairs={{0,24},{4,28},{8,16},{12,20},{16,8},{20,12},{24,0},{28,4},{1,25},{... | collective-permute-start | bytes 36872 | tf_op jit(solution)/shard_map/ppermute | solution.py:38
  17.8 30.7 %collective-permute-start.11 = (f32[8,384]{1,0:T(8,128)S(1)}, f32[8,384]{1,0:T(8,128)S(1)}, u32[]{:S(2)}, u32[]{:S(2)}) collective-permute-start(f32[8,384]{1,0:T(8,128)S(1)} %add.66), channel_id=1, source_target_pairs={{0,16},{4,20},{8,24},{12,28},{16,0},{20,4},{24,8},{28,12},{1,17},{... | collective-permute-start | bytes 36872 | tf_op jit(solution)/shard_map/ppermute | solution.py:38
  24.1 2.8 %copy-start.3 = (bf16[8,24,128,128]{3,2,1,0:T(8,128)(2,1)S(1)}, bf16[8,24,128,128]{3,2,1,0:T(8,128)(2,1)}, u32[]{:S(2)}) copy-start(bf16[8,24,128,128]{3,2,1,0:T(8,128)(2,1)} %ks_ref.1) | copy-start | bytes 18874372
  26.9 1.6 copy-start.4
  39.5 32.7 %collective-permute-start.3 = (bf16[512,384]{1,0:T(8,128)(2,1)S(1)}, bf16[512,384]{1,0:T(8,128)(2,1)S(1)}, u32[]{:S(2)}, u32[]{:S(2)}) collective-permute-start(bf16[512,384]{1,0:T(8,128)(2,1)S(1)} %get-tuple-element.25), channel_id=1, source_target_pairs={{0,24},{4,28},{8,0},{12,4},{16,8},{20,12},{24,16},{28,20},{1,25},{... | collective-permute-start | bytes 1179656 | tf_op jit(solution)/shard_map/ppermute | solution.py:16
  48.5 16.0 %collective-permute-start.10 = (f32[8,384]{1,0:T(8,128)S(1)}, f32[8,384]{1,0:T(8,128)S(1)}, u32[]{:S(2)}, u32[]{:S(2)}) collective-permute-start(f32[8,384]{1,0:T(8,128)S(1)} %add.66), channel_id=1, source_target_pairs={{0,8},{4,12},{8,0},{12,4},{16,24},{20,28},{24,16},{28,20},{1,9},{5... | collective-permute-start | bytes 36872 | tf_op jit(solution)/shard_map/ppermute | solution.py:38
  64.5 21.8 %collective-permute-start = (bf16[512,384]{1,0:T(8,128)(2,1)S(1)}, bf16[512,384]{1,0:T(8,128)(2,1)S(1)}, u32[]{:S(2)}, u32[]{:S(2)}) collective-permute-start(bf16[512,384]{1,0:T(8,128)(2,1)S(1)} %get-tuple-element.22), channel_id=1, source_target_pairs={{0,28},{4,0},{8,4},{12,8},{16,12},{20,16},{24,20},{28,24},{1,29},{... | collective-permute-start | bytes 1179656 | tf_op jit(solution)/shard_map/ppermute | solution.py:16
  68.6 15.2 %collective-permute-start.1 = (bf16[512,384]{1,0:T(8,128)(2,1)S(1)}, bf16[512,384]{1,0:T(8,128)(2,1)S(1)}, u32[]{:S(2)}, u32[]{:S(2)}) collective-permute-start(bf16[512,384]{1,0:T(8,128)(2,1)S(1)} %get-tuple-element.23), channel_id=1, source_target_pairs={{0,4},{4,8},{8,12},{12,16},{16,20},{20,24},{24,28},{28,0},{1,5},{5... | collective-permute-start | bytes 1179656 | tf_op jit(solution)/shard_map/ppermute | solution.py:16
  90.1 51.1 %collective-permute-start.17 = (bf16[512,384]{1,0:T(8,128)(2,1)S(1)}, bf16[512,384]{1,0:T(8,128)(2,1)S(1)}, u32[]{:S(2)}, u32[]{:S(2)}) collective-permute-start(bf16[512,384]{1,0:T(8,128)(2,1)S(1)} %get-tuple-element.36), channel_id=1, source_target_pairs={{0,12},{4,16},{8,20},{12,24},{16,28},{20,0},{24,4},{28,8},{1,13},{... | collective-permute-start | bytes 1179656 | tf_op jit(solution)/shard_map/ppermute | solution.py:16
  91.6 4.9 %collective-permute-start.21 = (f32[8,384]{1,0:T(8,128)S(1)}, f32[8,384]{1,0:T(8,128)S(1)}, u32[]{:S(2)}, u32[]{:S(2)}) collective-permute-start(f32[8,384]{1,0:T(8,128)S(1)} %get-tuple-element.39), channel_id=1, source_target_pairs={{0,3},{1,2},{2,1},{3,0},{4,7},{5,6},{6,5},{7,4},{8,11},{9,10},{10,... | collective-permute-start | bytes 36872 | tf_op jit(solution)/shard_map/ppermute | solution.py:38
  92.3 4.2 %collective-permute-start.20 = (f32[8,384]{1,0:T(8,128)S(1)}, f32[8,384]{1,0:T(8,128)S(1)}, u32[]{:S(2)}, u32[]{:S(2)}) collective-permute-start(f32[8,384]{1,0:T(8,128)S(1)} %get-tuple-element.39), channel_id=1, source_target_pairs={{0,2},{1,3},{2,0},{3,1},{4,6},{5,7},{6,4},{7,5},{8,10},{9,11},{10,... | collective-permute-start | bytes 36872 | tf_op jit(solution)/shard_map/ppermute | solution.py:38
  93.0 3.5 %collective-permute-start.19 = (f32[8,384]{1,0:T(8,128)S(1)}, f32[8,384]{1,0:T(8,128)S(1)}, u32[]{:S(2)}, u32[]{:S(2)}) collective-permute-start(f32[8,384]{1,0:T(8,128)S(1)} %get-tuple-element.39), channel_id=1, source_target_pairs={{0,1},{1,0},{2,3},{3,2},{4,5},{5,4},{6,7},{7,6},{8,9},{9,8},{10,11... | collective-permute-start | bytes 36872 | tf_op jit(solution)/shard_map/ppermute | solution.py:38
  93.5 49.8 %collective-permute-start.18 = (bf16[512,384]{1,0:T(8,128)(2,1)S(1)}, bf16[512,384]{1,0:T(8,128)(2,1)S(1)}, u32[]{:S(2)}, u32[]{:S(2)}) collective-permute-start(bf16[512,384]{1,0:T(8,128)(2,1)S(1)} %get-tuple-element.37), channel_id=1, source_target_pairs={{0,20},{4,24},{8,28},{12,0},{16,4},{20,8},{24,12},{28,16},{1,21},{... | collective-permute-start | bytes 1179656 | tf_op jit(solution)/shard_map/ppermute | solution.py:16
  96.5 15.3 %collective-permute-start.22 = (f32[8,384]{1,0:T(8,128)S(1)}, f32[8,384]{1,0:T(8,128)S(1)}, u32[]{:S(2)}, u32[]{:S(2)}) collective-permute-start(f32[8,384]{1,0:T(8,128)S(1)} %add_add_fusion.3), channel_id=1, source_target_pairs={{0,4},{4,0},{8,12},{12,8},{16,20},{20,16},{24,28},{28,24},{1,5},{5... | collective-permute-start | bytes 36872 | tf_op jit(solution)/shard_map/ppermute | solution.py:38
  111.8 5.6 %collective-permute-start.25 = (f32[8,384]{1,0:T(8,128)S(1)}, f32[8,384]{1,0:T(8,128)S(1)}, u32[]{:S(2)}, u32[]{:S(2)}) collective-permute-start(f32[8,384]{1,0:T(8,128)S(1)} %add.73), channel_id=1, source_target_pairs={{0,24},{4,28},{8,16},{12,20},{16,8},{20,12},{24,0},{28,4},{1,25},{... | collective-permute-start | bytes 36872 | tf_op jit(solution)/shard_map/ppermute | solution.py:38
  111.8 19.4 %collective-permute-start.24 = (f32[8,384]{1,0:T(8,128)S(1)}, f32[8,384]{1,0:T(8,128)S(1)}, u32[]{:S(2)}, u32[]{:S(2)}) collective-permute-start(f32[8,384]{1,0:T(8,128)S(1)} %add.73), channel_id=1, source_target_pairs={{0,16},{4,20},{8,24},{12,28},{16,0},{20,4},{24,8},{28,12},{1,17},{... | collective-permute-start | bytes 36872 | tf_op jit(solution)/shard_map/ppermute | solution.py:38
  112.1 34.7 %collective-permute-start.15 = (bf16[512,384]{1,0:T(8,128)(2,1)S(1)}, bf16[512,384]{1,0:T(8,128)(2,1)S(1)}, u32[]{:S(2)}, u32[]{:S(2)}) collective-permute-start(bf16[512,384]{1,0:T(8,128)(2,1)S(1)} %get-tuple-element.34), channel_id=1, source_target_pairs={{0,8},{4,12},{8,16},{12,20},{16,24},{20,28},{24,0},{28,4},{1,9},{5... | collective-permute-start | bytes 1179656 | tf_op jit(solution)/shard_map/ppermute | solution.py:16
  117.4 29.4 %collective-permute-start.16 = (bf16[512,384]{1,0:T(8,128)(2,1)S(1)}, bf16[512,384]{1,0:T(8,128)(2,1)S(1)}, u32[]{:S(2)}, u32[]{:S(2)}) collective-permute-start(bf16[512,384]{1,0:T(8,128)(2,1)S(1)} %get-tuple-element.35), channel_id=1, source_target_pairs={{0,24},{4,28},{8,0},{12,4},{16,8},{20,12},{24,16},{28,20},{1,25},{... | collective-permute-start | bytes 1179656 | tf_op jit(solution)/shard_map/ppermute | solution.py:16
  131.2 10.0 %collective-permute-start.23 = (f32[8,384]{1,0:T(8,128)S(1)}, f32[8,384]{1,0:T(8,128)S(1)}, u32[]{:S(2)}, u32[]{:S(2)}) collective-permute-start(f32[8,384]{1,0:T(8,128)S(1)} %add.73), channel_id=1, source_target_pairs={{0,8},{4,12},{8,0},{12,4},{16,24},{20,28},{24,16},{28,20},{1,9},{5... | collective-permute-start | bytes 36872 | tf_op jit(solution)/shard_map/ppermute | solution.py:38
  141.2 18.7 %collective-permute-start.13 = (bf16[512,384]{1,0:T(8,128)(2,1)S(1)}, bf16[512,384]{1,0:T(8,128)(2,1)S(1)}, u32[]{:S(2)}, u32[]{:S(2)}) collective-permute-start(bf16[512,384]{1,0:T(8,128)(2,1)S(1)} %get-tuple-element.32), channel_id=1, source_target_pairs={{0,28},{4,0},{8,4},{12,8},{16,12},{20,16},{24,20},{28,24},{1,29},{... | collective-permute-start | bytes 1179656 | tf_op jit(solution)/shard_map/ppermute | solution.py:16
  141.2 15.7 %collective-permute-start.14 = (bf16[512,384]{1,0:T(8,128)(2,1)S(1)}, bf16[512,384]{1,0:T(8,128)(2,1)S(1)}, u32[]{:S(2)}, u32[]{:S(2)}) collective-permute-start(bf16[512,384]{1,0:T(8,128)(2,1)S(1)} %get-tuple-element.33), channel_id=1, source_target_pairs={{0,4},{4,8},{8,12},{12,16},{16,20},{20,24},{24,28},{28,0},{1,5},{5... | collective-permute-start | bytes 1179656 | tf_op jit(solution)/shard_map/ppermute | solution.py:16
  162.7 3.2 %collective-permute-start.28 = (f32[8,384]{1,0:T(8,128)S(1)}, f32[8,384]{1,0:T(8,128)S(1)}, u32[]{:S(2)}, u32[]{:S(2)}) collective-permute-start(f32[8,384]{1,0:T(8,128)S(1)} %get-tuple-element.41), channel_id=1, source_target_pairs={{0,3},{1,2},{2,1},{3,0},{4,7},{5,6},{6,5},{7,4},{8,11},{9,10},{10,... | collective-permute-start | bytes 36872 | tf_op jit(solution)/shard_map/ppermute | solution.py:38
  163.1 3.7 %collective-permute-start.27 = (f32[8,384]{1,0:T(8,128)S(1)}, f32[8,384]{1,0:T(8,128)S(1)}, u32[]{:S(2)}, u32[]{:S(2)}) collective-permute-start(f32[8,384]{1,0:T(8,128)S(1)} %get-tuple-element.41), channel_id=1, source_target_pairs={{0,2},{1,3},{2,0},{3,1},{4,6},{5,7},{6,4},{7,5},{8,10},{9,11},{10,... | collective-permute-start | bytes 36872 | tf_op jit(solution)/shard_map/ppermute | solution.py:38
  164.1 2.7 %collective-permute-start.26 = (f32[8,384]{1,0:T(8,128)S(1)}, f32[8,384]{1,0:T(8,128)S(1)}, u32[]{:S(2)}, u32[]{:S(2)}) collective-permute-start(f32[8,384]{1,0:T(8,128)S(1)} %get-tuple-element.41), channel_id=1, source_target_pairs={{0,1},{1,0},{2,3},{3,2},{4,5},{5,4},{6,7},{7,6},{8,9},{9,8},{10,11... | collective-permute-start | bytes 36872 | tf_op jit(solution)/shard_map/ppermute | solution.py:38
  166.8 4.2 %collective-permute-start.29 = (f32[8,384]{1,0:T(8,128)S(1)}, f32[8,384]{1,0:T(8,128)S(1)}, u32[]{:S(2)}, u32[]{:S(2)}) collective-permute-start(f32[8,384]{1,0:T(8,128)S(1)} %add_add_fusion.1), channel_id=1, source_target_pairs={{0,4},{4,0},{8,12},{12,8},{16,20},{20,16},{24,28},{28,24},{1,5},{5... | collective-permute-start | bytes 36872 | tf_op jit(solution)/shard_map/ppermute | solution.py:38
  171.0 5.5 %collective-permute-start.32 = (f32[8,384]{1,0:T(8,128)S(1)}, f32[8,384]{1,0:T(8,128)S(1)}, u32[]{:S(2)}, u32[]{:S(2)}) collective-permute-start(f32[8,384]{1,0:T(8,128)S(1)} %add.80), channel_id=1, source_target_pairs={{0,24},{4,28},{8,16},{12,20},{16,8},{20,12},{24,0},{28,4},{1,25},{... | collective-permute-start | bytes 36872 | tf_op jit(solution)/shard_map/ppermute | solution.py:38
  172.5 4.6 %collective-permute-start.31 = (f32[8,384]{1,0:T(8,128)S(1)}, f32[8,384]{1,0:T(8,128)S(1)}, u32[]{:S(2)}, u32[]{:S(2)}) collective-permute-start(f32[8,384]{1,0:T(8,128)S(1)} %add.80), channel_id=1, source_target_pairs={{0,16},{4,20},{8,24},{12,28},{16,0},{20,4},{24,8},{28,12},{1,17},{... | collective-permute-start | bytes 36872 | tf_op jit(solution)/shard_map/ppermute | solution.py:38
  174.0 3.7 %collective-permute-start.30 = (f32[8,384]{1,0:T(8,128)S(1)}, f32[8,384]{1,0:T(8,128)S(1)}, u32[]{:S(2)}, u32[]{:S(2)}) collective-permute-start(f32[8,384]{1,0:T(8,128)S(1)} %add.80), channel_id=1, source_target_pairs={{0,8},{4,12},{8,0},{12,4},{16,24},{20,28},{24,16},{28,20},{1,9},{5... | collective-permute-start | bytes 36872 | tf_op jit(solution)/shard_map/ppermute | solution.py:38

commit v3 on v2

v3 whole, which is shorter than its diff:
```python
import functools

import jax
import jax.numpy as jnp
from jax import lax
from jax.experimental import pallas as pl
from jax.experimental.pallas import tpu as pltpu
from jax.sharding import PartitionSpec as P

MIB = 2**20
EXTRA = 16


def shifted(array, axis, by):
    count = lax.axis_size(axis)
    return lax.ppermute(array, axis, [(i, (i + by) % count) for i in range(count)])


def rounds(axis):
    left, radices = lax.axis_size(axis), []
    if left % 2 == 0 and left > 4:
        radices, left = [2], left // 2
    while left > 1:
        radix = 4 if left % 4 == 0 else 2
        radices, left = radices + [radix], left // radix
    return radices


def summed(array):
    for axis in ("col", "row"):
        count = lax.axis_size(axis)
        if count & (count - 1):
            array = lax.psum(array, axis)
            continue
        hop = 1
        for radix in rounds(axis):
            others = [
                lax.ppermute(array, axis, [(i, i ^ (hop * k)) for i in range(count)])
                for k in range(1, radix)
            ]
            array = array + others[0]
            if radix == 4:
                array = array + (others[1] + others[2])
            hop *= radix
    return array


def vmem():
    return pl.BlockSpec(memory_space=pltpu.VMEM)


def smem():
    return pl.BlockSpec(memory_space=pltpu.SMEM)


def call(kernel, name, out_shape, specs, scratch=(), flops=0, moved=MIB, limit=12):
    return pl.pallas_call(
        kernel,
        out_shape=out_shape,
        in_specs=specs,
        out_specs=jax.tree.map(lambda _: vmem(), out_shape),
        scratch_shapes=list(scratch),
        compiler_params=pltpu.CompilerParams(vmem_limit_bytes=limit * MIB),
        cost_estimate=pl.CostEstimate(flops=flops, bytes_accessed=moved, transcendentals=0),
        name=name,
    )


def wide(parts):
    return jnp.concatenate(parts, axis=1)


def folded(term):
    return jnp.sum(term.reshape(-1, 8, term.shape[-1]), axis=0)


def lined(parts, lines):
    parts = [jnp.sum(p, axis=0, keepdims=True) for p in parts]
    parts.append(jnp.zeros((lines - len(parts), parts[0].shape[1]), jnp.float32))
    return jnp.concatenate(parts, axis=0)


def per_field(values, orbitals):
    return wide([jnp.broadcast_to(v, (1, orbitals)) for v in values])


def field_sums(lines, fields):
    orbitals = lines.shape[1] // fields
    return [
        jnp.sum(lines[:, f * orbitals : (f + 1) * orbitals], axis=1, keepdims=True)
        for f in range(fields)
    ]


def pack(readers, right_side, onsite):
    fields, rows, orbitals = right_side.shape
    span, served = readers.shape[1:]
    clusters, width = onsite.shape
    base = served * width

    def kernel(readers_ref, right_ref, onsite_ref, *messages):
        norm = [jnp.zeros((8, orbitals), jnp.float32)] * fields
        heavy = [jnp.zeros((8, orbitals), jnp.float32)] * fields
        for cluster in range(clusters):
            weight = jnp.broadcast_to(onsite_ref[cluster : cluster + 1, :], (8, width))
            for field in range(fields):
                right = right_ref[field, cluster * width : (cluster + 1) * width, :]
                square = right * right
                norm[field] += folded(square)
                heavy[field] += jnp.dot(weight, square, preferred_element_type=jnp.float32)
        centers = [
            jnp.sum(h[:1], axis=1, keepdims=True)
            / jnp.maximum(jnp.sum(jnp.sum(n, axis=0, keepdims=True), axis=1, keepdims=True), 1e-30)
            for h, n in zip(heavy, norm)
        ]
        center = jnp.broadcast_to(per_field(centers, orbitals), (EXTRA, fields * orbitals))
        center = center.astype(jnp.bfloat16)
        for offset, message in enumerate(messages):
            message[base : base + EXTRA, :] = center
            for slot in range(served):
                start = pl.multiple_of(readers_ref[0, offset, slot] * width, width)
                for field in range(fields):
                    message[
                        slot * width : (slot + 1) * width, field * orbitals : (field + 1) * orbitals
                    ] = right_ref[field, pl.ds(start, width), :].astype(jnp.bfloat16)

    shape = jax.ShapeDtypeStruct((base + EXTRA, fields * orbitals), jnp.bfloat16)
    return call(kernel, "pack", [shape] * span, [smem(), vmem(), vmem()])(
        readers, right_side, onsite
    )


def levels(onsite):
    clusters, width = onsite.shape

    def kernel(onsite_ref, level_ref):
        for cluster in range(clusters):
            level_ref[cluster] = jnp.transpose(
                jnp.broadcast_to(onsite_ref[cluster : cluster + 1, :], (width, width))
            )

    shape = jax.ShapeDtypeStruct((clusters, width, width), jnp.float32)
    return call(kernel, "levels", shape, [vmem()])(onsite)


def spread(tile_slot, ks_tiles, correlation_tiles, span, served):
    clusters, _, width, _ = ks_tiles.shape
    slots = span * served

    def kernel(slot_ref, ks_ref, correlation_ref, out_ref, where):
        @pl.loop(0, clusters)
        def _(cluster):
            for kind, ref in enumerate((ks_ref, correlation_ref)):
                count = ref.shape[1]
                for slot in range(slots):
                    where[slot] = count
                for tile in range(count):
                    where[slot_ref[cluster, tile]] = tile
                for slot in range(slots):
                    tile = where[slot]
                    block = ref[cluster, jnp.minimum(tile, count - 1)]
                    block = jnp.where(tile < count, block, jnp.zeros_like(block))
                    lane = slot % served * width
                    out_ref[
                        slot // served, cluster, kind * width : (kind + 1) * width, lane : lane + width
                    ] = block

    return call(
        kernel,
        "spread",
        jax.ShapeDtypeStruct((span, clusters, 2 * width, served * width), jnp.bfloat16),
        [smem(), vmem(), vmem()],
        [pltpu.SMEM((slots,), jnp.int32)],
        moved=16 * MIB,
    )(tile_slot, ks_tiles, correlation_tiles)


def products(dense_ref, offsets, vectors, cluster, energy):
    depth = dense_ref.shape[-1]
    for offset, vector in zip(offsets, vectors):
        value = jnp.dot(
            dense_ref[offset, cluster], vector[0:depth, :], preferred_element_type=jnp.float32
        )
        half = value.shape[0] // 2
        yield value[:half] - energy * value[half:]


def centers(vectors, depth):
    return [vector[depth : depth + EXTRA, :].astype(jnp.float32)[:1] for vector in vectors]


def work(dense, offsets, lanes):
    return 2 * len(offsets) * dense.shape[1] * dense.shape[2] * dense.shape[3] * lanes


def couple(dense, offsets, vectors, energies, sums):
    _, clusters, height, depth = dense.shape
    lanes = vectors[0].shape[1]
    count = len(offsets)
    outs = 2 if vectors[0].shape[0] > depth else 1

    def kernel(dense_ref, energies_ref, *refs):
        vector_refs, sum_refs, out_refs = refs[:count], refs[count:-outs], refs[-outs:]
        energy = wide([energies_ref[...]] * (lanes // energies_ref.shape[1]))
        weights = centers(vector_refs, depth) if outs == 2 else [None] * count

        @pl.loop(0, clusters)
        def _(cluster):
            values = [ref[cluster] for ref in sum_refs]
            parts = products(dense_ref, offsets, vector_refs, cluster, energy)
            for weight, part in zip(weights, parts):
                terms = [part] if weight is None else [part, weight * part]
                values = [v + t for v, t in zip(values, terms)] if values else terms
            for ref, value in zip(out_refs, values):
                ref[cluster] = value

    inputs = [dense, energies, *vectors, *sums]
    shape = jax.ShapeDtypeStruct((clusters, height // 2, lanes), jnp.float32)
    return call(
        kernel,
        "couple",
        [shape] * outs,
        [vmem()] * len(inputs),
        flops=work(dense, offsets, lanes),
        moved=4 * MIB,
    )(*inputs)


def finish_first(dense, offsets, vectors, energies, sums, right_side, level, own, readers):
    _, clusters, height, depth = dense.shape
    lanes = vectors[0].shape[1]
    fields = right_side.shape[0]
    width = height // 2
    count = len(offsets)
    span, served = readers.shape[1:]

    def kernel(dense_ref, energies_ref, *refs):
        vector_refs, refs = refs[:count], refs[count:]
        sum_ref, weighted_ref, right_ref, level_ref, own_ref, readers_ref = refs[:6]
        image_ref, shifted_ref, lines_ref = refs[6:9]
        messages, (norm, bend, square, outgoing) = refs[9 : 9 + span], refs[9 + span :]
        energy = wide([energies_ref[...]] * fields)
        weights = centers(vector_refs, depth)
        (center,) = centers([own_ref], depth)
        for ref in (norm, bend, square):
            ref[...] = jnp.zeros_like(ref)

        @pl.loop(0, clusters)
        def _(cluster):
            value, weighted = sum_ref[cluster], weighted_ref[cluster]
            for weight, part in zip(weights, products(dense_ref, offsets, vector_refs, cluster, energy)):
                value, weighted = value + part, weighted + weight * part
            shifted_ref[cluster] = weighted
            rows = pl.ds(pl.multiple_of(cluster * width, width), width)
            right = wide([right_ref[f, rows, :] for f in range(fields)])
            image = wide([level_ref[cluster]] * fields) * right + value
            image_ref[cluster] = image
            outgoing[cluster] = (image - center * right).astype(jnp.bfloat16)
            norm[...] += folded(right * right)
            bend[...] += folded(right * image)
            square[...] += folded(image * image)

        for offset, message in enumerate(messages):
            for slot in range(served):
                message[slot * width : (slot + 1) * width, :] = outgoing[readers_ref[0, offset, slot]]
        lines_ref[...] = lined([norm[...], bend[...], square[...]], 8)

    message = jax.ShapeDtypeStruct((depth, lanes), jnp.bfloat16)
    vector = jax.ShapeDtypeStruct((clusters, width, lanes), jnp.float32)
    return call(
        kernel,
        "finish_first",
        [vector, vector, jax.ShapeDtypeStruct((8, lanes), jnp.float32)] + [message] * span,
        [vmem()] * (2 + count + 5) + [smem()],
        [pltpu.VMEM((8, lanes), jnp.float32)] * 3
        + [pltpu.VMEM((clusters, width, lanes), jnp.bfloat16)],
        flops=work(dense, offsets, lanes),
        moved=8 * MIB,
    )(dense, energies, *vectors, *sums, right_side, level, own, readers)


def guesses(lines, fields):
    orbitals = lines.shape[1] // fields
    alphas, growths = [], []
    for column in field_sums(lines, fields):
        norm, bend, square = column[0:1], column[1:2], column[2:3]
        norm = jnp.maximum(norm, 1e-30)
        alpha = norm / jnp.maximum(bend, 4.0 * norm)
        alphas.append(alpha)
        growths.append(jnp.clip(alpha * alpha * square / norm, 1.0, 2.0))
    return per_field(alphas, orbitals), per_field(growths, orbitals)


def finish_second(dense, offsets, vectors, energies, sums, right_side, level, image, weighted, lines, devices):
    _, clusters, height, _ = dense.shape
    lanes = vectors[0].shape[1]
    fields = right_side.shape[0]
    width = height // 2
    count = len(offsets)
    spots = -(-devices // 128) * 128

    def kernel(dense_ref, energies_ref, *refs):
        vector_refs, refs = refs[:count], refs[count:]
        sum_ref, right_ref, level_ref, image_ref, weighted_ref, lines_ref = refs[:6]
        later_ref, out_ref, kept = refs[6], refs[7], refs[8]
        energy = wide([energies_ref[...]] * fields)
        alpha, growth = guesses(lines_ref[...], fields)
        kept[...] = jnp.zeros_like(kept)

        @pl.loop(0, clusters)
        def _(cluster):
            value = sum_ref[cluster] + weighted_ref[cluster]
            for part in products(dense_ref, offsets, vector_refs, cluster, energy):
                value = value + part
            rows = pl.ds(pl.multiple_of(cluster * width, width), width)
            right = wide([right_ref[f, rows, :] for f in range(fields)])
            first = image_ref[cluster]
            later = wide([level_ref[cluster]] * fields) * first + value
            later_ref[cluster] = later
            step = alpha * first
            residual = right - step
            direction = growth * right - step
            bent = growth * first - alpha * later
            terms = (
                residual * residual,
                residual * first,
                direction * bent,
                direction * first + right * bent,
                direction * later + first * bent,
                right * later + first * first,
                first * later,
            )
            for index, term in enumerate(terms):
                kept[index] += folded(term)

        count_terms = kept.shape[0]
        block = jnp.concatenate(
            [
                lines_ref[0:3, :],
                lined([kept[i] for i in range(count_terms)], count_terms + 1)[:count_terms],
            ],
            axis=0,
        )
        block = jnp.concatenate([block, jnp.zeros((16 - 3 - count_terms, lanes), jnp.float32)], axis=0)
        orbitals = lanes // fields
        place = lax.axis_index("row") * lax.axis_size("col") + lax.axis_index("col")
        here = lax.broadcasted_iota(jnp.int32, (16, spots), 1) == place
        line = lax.broadcasted_iota(jnp.int32, (16, spots), 0)
        for f, column in enumerate(field_sums(block, fields)):
            spread_out = jnp.broadcast_to(column, (16, spots))
            first_lane = slice(f * orbitals, f * orbitals + 1)
            spread_out = jnp.where(line == 10, jnp.broadcast_to(alpha[:, first_lane], (16, spots)), spread_out)
            spread_out = jnp.where(line == 11, jnp.broadcast_to(growth[:, first_lane], (16, spots)), spread_out)
            out_ref[f * 16 : (f + 1) * 16, :] = jnp.where(here, spread_out, 0.0)

    return call(
        kernel,
        "finish_second",
        [
            jax.ShapeDtypeStruct((clusters, width, lanes), jnp.float32),
            jax.ShapeDtypeStruct((16 * fields, spots), jnp.float32),
        ],
        [vmem()] * (2 + count + 6),
        [pltpu.VMEM((7, 8, lanes), jnp.float32)],
        flops=work(dense, offsets, lanes),
        moved=8 * MIB,
    )(dense, energies, *vectors, *sums, right_side, level, image, weighted, lines)


def step_sizes(gathered, fields, orbitals):
    alphas, growths, gains = [], [], []
    whole = lambda v: jnp.sum(v, axis=1, keepdims=True)
    for f in range(fields):
        line = [gathered[f * 16 + i : f * 16 + i + 1, :] for i in range(12)]
        norm = whole(line[0])
        alpha = norm / whole(line[1])
        growth = alpha * alpha * whole(line[2]) / norm
        off, more = alpha - line[10], growth - line[11]
        after = whole(line[3] - 2.0 * off * line[4] + off * off * line[2])
        bend = whole(
            line[5]
            + more * line[6]
            - off * line[7]
            + more * more * line[1]
            - more * off * line[8]
            + off * off * line[9]
        )
        alphas.append(alpha)
        growths.append(growth)
        gains.append(after / bend)
    return [per_field(v, orbitals) for v in (alphas, growths, gains)]


def final(right_side, image, later, gathered):
    fields, rows, orbitals = right_side.shape
    clusters, width, lanes = image.shape
    blocks = 4
    each = clusters // blocks

    def kernel(right_ref, image_ref, later_ref, gathered_ref, solution_ref, residual_ref):
        step = pl.program_id(0)
        alpha, growth, gain = step_sizes(gathered_ref[...], fields, orbitals)
        for local in range(each):
            cluster = step * each + local
            rows = pl.ds(pl.multiple_of(cluster * width, width), width)
            here = slice(local * width, (local + 1) * width)
            for field in range(fields):
                part = slice(field * orbitals, (field + 1) * orbitals)
                right = right_ref[field, rows, :]
                first = image_ref[cluster, :, part]
                moved = alpha[:, part] * first
                direction = growth[:, part] * right - moved
                bent = growth[:, part] * first - alpha[:, part] * later_ref[cluster, :, part]
                solution_ref[field, here, :] = alpha[:, part] * right + gain[:, part] * direction
                residual_ref[field, here, :] = (right - moved) - gain[:, part] * bent

    vector = pl.BlockSpec((fields, each * width, orbitals), lambda i: (0, i, 0))
    shape = jax.ShapeDtypeStruct(right_side.shape, jnp.float32)
    return pl.pallas_call(
        kernel,
        grid=(blocks,),
        out_shape=[shape, shape],
        in_specs=[vmem()] * 4,
        out_specs=[vector, vector],
        compiler_params=pltpu.CompilerParams(vmem_limit_bytes=12 * MIB),
        name="final",
    )(right_side, image, later, gathered)


def body(right_side, onsite, energies, ks_tiles, correlation_tiles, tile_slot, readers):
    span, served = readers.shape[1:]
    width = ks_tiles.shape[2]
    middle = (span - 1) // 2
    devices = lax.axis_size("row") * lax.axis_size("col")
    onsite = onsite.reshape(-1, width)
    energies = energies.reshape(1, -1)

    order = [middle]
    for far in range(middle, 0, -1):
        order += [middle - far, middle + far]
    groups = [order[:1], order[1:3], order[3:5], order[5:6], order[6:]]

    def exchange(messages):
        return [shifted(m, "row", middle - o) if o != middle else m for o, m in enumerate(messages)]

    def partial(vectors):
        sums = []
        for group in groups[:-1]:
            sums = couple(dense, group, [vectors[o] for o in group], energies, sums)
        return dense, groups[-1], [vectors[o] for o in groups[-1]], energies, sums

    vectors = exchange(pack(readers, right_side, onsite))
    own = vectors[middle]
    level = levels(onsite)
    dense = spread(tile_slot, ks_tiles, correlation_tiles, span, served)
    image, weighted, lines, *messages = finish_first(*partial(vectors), right_side, level, own, readers)
    vectors = exchange(messages)
    later, gathered = finish_second(
        *partial(vectors), right_side, level, image, weighted, lines, devices
    )
    return tuple(final(right_side, image, later, summed(gathered)))


def solution(mesh):
    placed = (
        P(None, "row", "col"),
        P("row"),
        P("col"),
        P("row", None, None, None),
        P("row", None, None, None),
        P("row", None),
        P("row", None, None),
    )
    return jax.shard_map(
        body,
        mesh=mesh,
        in_specs=placed,
        out_specs=(P(None, "row", "col"), P(None, "row", "col")),
        check_vma=False,
    )
```

time: 181 us -> 150 us (0.83)
  waiting for transfers between devices: 76 us -> 57.3 us
  starting transfers between devices: 57.3 us -> 43.3 us
  Pallas kernels: 38.9 us -> 41 us
    ppermute x21 -> x7, waiting for transfers between devices: 60.6 us -> 9.19 us  [summed(): lax.ppermute(array, axis, [(i, i ^ hop * k) for i in range(count)])]
    ppermute x12, waiting for transfers between devices: 15.4 us -> 48.2 us  [shifted(): lax.ppermute(array, axis, [(i, (i + by) % count) for i in range(count)])]
    ppermute x21 -> x7, starting transfers between devices: 35.3 us -> 11.2 us  [summed(): lax.ppermute(array, axis, [(i, i ^ hop * k) for i in range(count)])]
    ppermute x12, starting transfers between devices: 22 us -> 32.1 us  [shifted(): lax.ppermute(array, axis, [(i, (i + by) % count) for i in range(count)])]
  transfers between devices with their start and end apart: 33 -> 19, of which waited for: 16 -> 14; matrix products, arithmetic and copies ran while one was open for 0% -> 0% of each run, Pallas kernels for 16% -> 19%
where the time goes in v3:
time: 150 us
  waiting for transfers between devices  57.3 us (38%)
  starting transfers between devices  43.3 us (29%)
  Pallas kernels  41 us (27%)
  local copies, waits for them, and re-layouts  7.26 us (5%)
    ppermute x12, waiting for transfers between devices, shifted(): lax.ppermute(array, axis, [(i, (i + by) % count) for i in range(count)])  48.2 us
    ppermute x12, starting transfers between devices, shifted(): lax.ppermute(array, axis, [(i, (i + by) % count) for i in range(count)])  32.1 us
    pallas_call x8, Pallas kernels, couple(): call(kernel, 'couple', [shape] * outs, [vmem()] * len(inputs), flops=work...  23.6 us
    ppermute x7, starting transfers between devices, summed(): lax.ppermute(array, axis, [(i, i ^ hop * k) for i in range(count)])  11.2 us
    ppermute x7, waiting for transfers between devices, summed(): lax.ppermute(array, axis, [(i, i ^ hop * k) for i in range(count)])  9.19 us
    unnamed x17, local copies, waits for them, and re-layouts  7.26 us
    pallas_call x1, Pallas kernels, spread(): call(kernel, 'spread', jax.ShapeDtypeStruct((span, clusters, 2 * width, s...  4.86 us
    pallas_call x1, Pallas kernels, finish_second(): call(kernel, 'finish_second', [jax.ShapeDtypeStruct((clusters, width, lan...  3.93 us
  transfers between devices with their start and end apart: 19, of which 14 were waited for; matrix products, arithmetic and copies ran while one was open for 0% of the time, Pallas kernels for 19%

profile of v3, /device:TPU:0, one launch (start us, length us, event | category | flops | bytes accessed | tf_op | source)
XLA Modules:
  0.0 149.7 jit_solution(9914749889008466649)
XLA Ops:
  0.6 0.8 copy.9.readers_ref.refs_6_
  1.4 1.4 copy-done
  2.8 0.7 copy-done.5
  3.5 1.3 pack.1
  4.8 4.0 %collective-permute-start.4 = (bf16[528,384]{1,0:T(8,128)(2,1)S(1)}, bf16[528,384]{1,0:T(8,128)(2,1)S(1)}, u32[]{:S(2)}, u32[]{:S(2)}) collective-permute-start(bf16[528,384]{1,0:T(8,128)(2,1)S(1)} %get-tuple-element.33), channel_id=1, source_target_pairs={{0,12},{4,16},{8,20},{12,24},{16,28},{20,0},{24,4},{28,8},{1,13},{... | collective-permute-start | bytes 1216520 | tf_op jit(solution)/shard_map/ppermute | solution.py:16
  8.8 1.1 collective-permute-start.5
  9.9 1.8 %collective-permute-start.2 = (bf16[528,384]{1,0:T(8,128)(2,1)S(1)}, bf16[528,384]{1,0:T(8,128)(2,1)S(1)}, u32[]{:S(2)}, u32[]{:S(2)}) collective-permute-start(bf16[528,384]{1,0:T(8,128)(2,1)S(1)} %get-tuple-element.31), channel_id=1, source_target_pairs={{0,8},{4,12},{8,16},{12,20},{16,24},{20,28},{24,0},{28,4},{1,9},{5... | collective-permute-start | bytes 1216520 | tf_op jit(solution)/shard_map/ppermute | solution.py:16
  11.7 2.0 %collective-permute-start.3 = (bf16[528,384]{1,0:T(8,128)(2,1)S(1)}, bf16[528,384]{1,0:T(8,128)(2,1)S(1)}, u32[]{:S(2)}, u32[]{:S(2)}) collective-permute-start(bf16[528,384]{1,0:T(8,128)(2,1)S(1)} %get-tuple-element.32), channel_id=1, source_target_pairs={{0,24},{4,28},{8,0},{12,4},{16,8},{20,12},{24,16},{28,20},{1,25},{... | collective-permute-start | bytes 1216520 | tf_op jit(solution)/shard_map/ppermute | solution.py:16
  13.7 2.6 %collective-permute-start.1 = (bf16[528,384]{1,0:T(8,128)(2,1)S(1)}, bf16[528,384]{1,0:T(8,128)(2,1)S(1)}, u32[]{:S(2)}, u32[]{:S(2)}) collective-permute-start(bf16[528,384]{1,0:T(8,128)(2,1)S(1)} %get-tuple-element.30), channel_id=1, source_target_pairs={{0,4},{4,8},{8,12},{12,16},{16,20},{20,24},{24,28},{28,0},{1,5},{5... | collective-permute-start | bytes 1216520 | tf_op jit(solution)/shard_map/ppermute | solution.py:16
  16.4 2.8 %copy-done.2 = bf16[8,24,128,128]{3,2,1,0:T(8,128)(2,1)S(1)} copy-done((bf16[8,24,128,128]{3,2,1,0:T(8,128)(2,1)S(1)}, bf16[8,24,128,128]{3,2,1,0:T(8,128)(2,1)}, u32[]{:S(2)}) %copy-start.2) | copy-done | bytes 6291480
  19.1 1.6 %copy-done.3 = bf16[8,8,128,128]{3,2,1,0:T(8,128)(2,1)S(1)} copy-done((bf16[8,8,128,128]{3,2,1,0:T(8,128)(2,1)S(1)}, bf16[8,8,128,128]{3,2,1,0:T(8,128)(2,1)}, u32[]{:S(2)}) %copy-start.3) | copy-done | bytes 2097176
  20.7 4.9 %spread.1.dense_ref = bf16[7,8,256,512]{3,2,1,0:T(8,128)(2,1)S(1)} custom-call(s32[8,24]{1,0:T(8,128)S(1)} %copy-done.7, bf16[8,24,128,128]{3,2,1,0:T(8,128)(2,1)S(1)} %copy-done.2, bf16[8,8,128,128]{3,2,1,0:T(8,128)(2,1)S(1)} %copy-done.3), custom_call_target="tpu_custom_call" | custom-call | bytes 16777216 | tf_op jit(solution)/shard_map/spread/pallas_call | solution.py:168
  25.6 3.2 %collective-permute-done.4.refs_0_ = bf16[528,384]{1,0:T(8,128)(2,1)S(1)} collective-permute-done((bf16[528,384]{1,0:T(8,128)(2,1)S(1)}, bf16[528,384]{1,0:T(8,128)(2,1)S(1)}, u32[]{:S(2)}, u32[]{:S(2)}) %collective-permute-start.4) | collective-permute-done | bytes 405536 | tf_op jit(solution)/shard_map/ppermute | solution.py:16
  28.8 2.4 %couple.8 = (f32[8,128,384]{2,1,0:T(8,128)S(1)}, f32[8,128,384]{2,1,0:T(8,128)S(1)}) custom-call(bf16[7,8,256,512]{3,2,1,0:T(8,128)(2,1)S(1)} %spread.1.dense_ref, f32[1,128]{1,0:T(1,128)S(1)} %bitcast.2, bf16[528,384]{1,0:T(8,128)(2,1)S(1)} %get-tuple-element.35.refs_0_.refs_5_), custom_call_target="tpu_custom_call" | custom-call | flops 805306368 | bytes 4194304 | tf_op jit(solution)/shard_map/couple/pallas_call | solution.py:219
  31.2 0.2 levels.1.refs_4_.refs_3_
  31.4 3.6 %couple.9 = (f32[8,128,384]{2,1,0:T(8,128)S(1)}, f32[8,128,384]{2,1,0:T(8,128)S(1)}) custom-call(bf16[7,8,256,512]{3,2,1,0:T(8,128)(2,1)S(1)} %spread.1.dense_ref, f32[1,128]{1,0:T(1,128)S(1)} %bitcast.3, bf16[528,384]{1,0:T(8,128)(2,1)S(1)} %collective-permute-done.4.refs_0_, bf16[528,384]{1,0:T(8,128)(2,1)S(1)} %collective-permute-done.5.refs_1_, ...), custom_call_target="tpu_custom_call" | custom-call | flops 1610612736 | bytes 4194304 | tf_op jit(solution)/shard_map/couple/pallas_call | solution.py:219
  35.0 3.9 %collective-permute-done.2.refs_0_ = bf16[528,384]{1,0:T(8,128)(2,1)S(1)} collective-permute-done((bf16[528,384]{1,0:T(8,128)(2,1)S(1)}, bf16[528,384]{1,0:T(8,128)(2,1)S(1)}, u32[]{:S(2)}, u32[]{:S(2)}) %collective-permute-start.2) | collective-permute-done | bytes 405536 | tf_op jit(solution)/shard_map/ppermute | solution.py:16
  38.9 5.9 %collective-permute-done.3.refs_1_ = bf16[528,384]{1,0:T(8,128)(2,1)S(1)} collective-permute-done((bf16[528,384]{1,0:T(8,128)(2,1)S(1)}, bf16[528,384]{1,0:T(8,128)(2,1)S(1)}, u32[]{:S(2)}, u32[]{:S(2)}) %collective-permute-start.3) | collective-permute-done | bytes 405536 | tf_op jit(solution)/shard_map/ppermute | solution.py:16
  44.8 3.5 %couple.10 = (f32[8,128,384]{2,1,0:T(8,128)S(1)}, f32[8,128,384]{2,1,0:T(8,128)S(1)}) custom-call(bf16[7,8,256,512]{3,2,1,0:T(8,128)(2,1)S(1)} %spread.1.dense_ref, f32[1,128]{1,0:T(1,128)S(1)} %bitcast.4, bf16[528,384]{1,0:T(8,128)(2,1)S(1)} %collective-permute-done.2.refs_0_, bf16[528,384]{1,0:T(8,128)(2,1)S(1)} %collective-permute-done.3.refs_1_, ...), custom_call_target="tpu_custom_call" | custom-call | flops 1610612736 | bytes 4194304 | tf_op jit(solution)/shard_map/couple/pallas_call | solution.py:219
  48.3 7.9 %collective-permute-done.1.refs_0_ = bf16[528,384]{1,0:T(8,128)(2,1)S(1)} collective-permute-done((bf16[528,384]{1,0:T(8,128)(2,1)S(1)}, bf16[528,384]{1,0:T(8,128)(2,1)S(1)}, u32[]{:S(2)}, u32[]{:S(2)}) %collective-permute-start.1) | collective-permute-done | bytes 405536 | tf_op jit(solution)/shard_map/ppermute | solution.py:16
  56.2 2.5 %couple.11 = (f32[8,128,384]{2,1,0:T(8,128)S(1)}, f32[8,128,384]{2,1,0:T(8,128)S(1)}) custom-call(bf16[7,8,256,512]{3,2,1,0:T(8,128)(2,1)S(1)} %spread.1.dense_ref, f32[1,128]{1,0:T(1,128)S(1)} %bitcast.5, bf16[528,384]{1,0:T(8,128)(2,1)S(1)} %collective-permute-done.1.refs_0_, f32[8,128,384]{2,1,0:T(8,128)S(1)} %get-tuple-element.40.refs_1_, ...), custom_call_target="tpu_custom_call" | custom-call | flops 805306368 | bytes 4194304 | tf_op jit(solution)/shard_map/couple/pallas_call | solution.py:219
  58.7 3.8 %finish_first.1 = (f32[8,128,384]{2,1,0:T(8,128)S(1)}, f32[8,128,384]{2,1,0:T(8,128)S(1)}, f32[8,384]{1,0:T(8,128)S(1)}, bf16[512,384]{1,0:T(8,128)(2,1)S(1)}, b...) custom-call(bf16[7,8,256,512]{3,2,1,0:T(8,128)(2,1)S(1)} %spread.1.d, ...), custom_call_target="tpu_custom_call" | custom-call | flops 805306368 | bytes 8388608 | tf_op jit(solution)/shard_map/finish_first/pallas_call | solution.py:270
  62.5 10.7 %collective-permute-start.10 = (bf16[512,384]{1,0:T(8,128)(2,1)S(1)}, bf16[512,384]{1,0:T(8,128)(2,1)S(1)}, u32[]{:S(2)}, u32[]{:S(2)}) collective-permute-start(bf16[512,384]{1,0:T(8,128)(2,1)S(1)} %get-tuple-element.49), channel_id=1, source_target_pairs={{0,12},{4,16},{8,20},{12,24},{16,28},{20,0},{24,4},{28,8},{1,13},{... | collective-permute-start | bytes 1179656 | tf_op jit(solution)/shard_map/ppermute | solution.py:16
  73.2 3.1 %collective-permute-start.8 = (bf16[512,384]{1,0:T(8,128)(2,1)S(1)}, bf16[512,384]{1,0:T(8,128)(2,1)S(1)}, u32[]{:S(2)}, u32[]{:S(2)}) collective-permute-start(bf16[512,384]{1,0:T(8,128)(2,1)S(1)} %get-tuple-element.47), channel_id=1, source_target_pairs={{0,8},{4,12},{8,16},{12,20},{16,24},{20,28},{24,0},{28,4},{1,9},{5... | collective-permute-start | bytes 1179656 | tf_op jit(solution)/shard_map/ppermute | solution.py:16
  76.3 0.7 collective-permute-start.9
  77.0 2.6 %collective-permute-start.7 = (bf16[512,384]{1,0:T(8,128)(2,1)S(1)}, bf16[512,384]{1,0:T(8,128)(2,1)S(1)}, u32[]{:S(2)}, u32[]{:S(2)}) collective-permute-start(bf16[512,384]{1,0:T(8,128)(2,1)S(1)} %get-tuple-element.46), channel_id=1, source_target_pairs={{0,4},{4,8},{8,12},{12,16},{16,20},{20,24},{24,28},{28,0},{1,5},{5... | collective-permute-start | bytes 1179656 | tf_op jit(solution)/shard_map/ppermute | solution.py:16
  79.6 11.1 %collective-permute-done.10.refs_0_ = bf16[512,384]{1,0:T(8,128)(2,1)S(1)} collective-permute-done((bf16[512,384]{1,0:T(8,128)(2,1)S(1)}, bf16[512,384]{1,0:T(8,128)(2,1)S(1)}, u32[]{:S(2)}, u32[]{:S(2)}) %collective-permute-start.10) | collective-permute-done | bytes 393248 | tf_op jit(solution)/shard_map/ppermute | solution.py:16
  90.7 3.3 %collective-permute-start.6 = (bf16[512,384]{1,0:T(8,128)(2,1)S(1)}, bf16[512,384]{1,0:T(8,128)(2,1)S(1)}, u32[]{:S(2)}, u32[]{:S(2)}) collective-permute-start(bf16[512,384]{1,0:T(8,128)(2,1)S(1)} %get-tuple-element.45), channel_id=1, source_target_pairs={{0,28},{4,0},{8,4},{12,8},{16,12},{20,16},{24,20},{28,24},{1,29},{... | collective-permute-start | bytes 1179656 | tf_op jit(solution)/shard_map/ppermute | solution.py:16
  94.1 2.4 %couple.12.refs_2_ = f32[8,128,384]{2,1,0:T(8,128)S(1)} custom-call(bf16[7,8,256,512]{3,2,1,0:T(8,128)(2,1)S(1)} %spread.1.dense_ref, f32[1,128]{1,0:T(1,128)S(1)} %bitcast.7, bf16[512,384]{1,0:T(8,128)(2,1)S(1)} %get-tuple-element.51.refs_0_), custom_call_target="tpu_custom_call" | custom-call | flops 805306368 | bytes 4194304 | tf_op jit(solution)/shard_map/couple/pallas_call | solution.py:219
  96.5 0.7 collective-permute-done.11.refs_1_
  97.1 3.4 %couple.13.refs_2_ = f32[8,128,384]{2,1,0:T(8,128)S(1)} custom-call(bf16[7,8,256,512]{3,2,1,0:T(8,128)(2,1)S(1)} %spread.1.dense_ref, f32[1,128]{1,0:T(1,128)S(1)} %bitcast.8, bf16[512,384]{1,0:T(8,128)(2,1)S(1)} %collective-permute-done.10.refs_0_, bf16[512,384]{1,0:T(8,128)(2,1)S(1)} %collective-permute-done.11.refs_1_, f32[8,128,384]{2,1,0:T(8,128)S(1)} %couple.12.refs_2_), custom_call_target="tpu_custom_call" | custom-call | flops 1610612736 | bytes 4194304 | tf_op jit(solution)/shard_map/couple/pallas_call | solution.py:219
  100.6 5.0 %collective-permute-done.8.refs_0_ = bf16[512,384]{1,0:T(8,128)(2,1)S(1)} collective-permute-done((bf16[512,384]{1,0:T(8,128)(2,1)S(1)}, bf16[512,384]{1,0:T(8,128)(2,1)S(1)}, u32[]{:S(2)}, u32[]{:S(2)}) %collective-permute-start.8) | collective-permute-done | bytes 393248 | tf_op jit(solution)/shard_map/ppermute | solution.py:16
  105.6 8.5 %collective-permute-done.9.refs_1_ = bf16[512,384]{1,0:T(8,128)(2,1)S(1)} collective-permute-done((bf16[512,384]{1,0:T(8,128)(2,1)S(1)}, bf16[512,384]{1,0:T(8,128)(2,1)S(1)}, u32[]{:S(2)}, u32[]{:S(2)}) %collective-permute-start.9) | collective-permute-done | bytes 393248 | tf_op jit(solution)/shard_map/ppermute | solution.py:16
  114.0 3.5 %couple.14.refs_1_ = f32[8,128,384]{2,1,0:T(8,128)S(1)} custom-call(bf16[7,8,256,512]{3,2,1,0:T(8,128)(2,1)S(1)} %spread.1.dense_ref, f32[1,128]{1,0:T(1,128)S(1)} %bitcast.9, bf16[512,384]{1,0:T(8,128)(2,1)S(1)} %collective-permute-done.8.refs_0_, bf16[512,384]{1,0:T(8,128)(2,1)S(1)} %collective-permute-done.9.refs_1_, f32[8,128,384]{2,1,0:T(8,128)S(1)} %couple.13.refs_2_), custom_call_target="tpu_custom_call" | custom-call | flops 1610612736 | bytes 4194304 | tf_op jit(solution)/shard_map/couple/pallas_call | solution.py:219
  117.6 2.0 %collective-permute-done.7.refs_0_ = bf16[512,384]{1,0:T(8,128)(2,1)S(1)} collective-permute-done((bf16[512,384]{1,0:T(8,128)(2,1)S(1)}, bf16[512,384]{1,0:T(8,128)(2,1)S(1)}, u32[]{:S(2)}, u32[]{:S(2)}) %collective-permute-start.7) | collective-permute-done | bytes 393248 | tf_op jit(solution)/shard_map/ppermute | solution.py:16
  119.6 2.4 %couple.15.refs_1_ = f32[8,128,384]{2,1,0:T(8,128)S(1)} custom-call(bf16[7,8,256,512]{3,2,1,0:T(8,128)(2,1)S(1)} %spread.1.dense_ref, f32[1,128]{1,0:T(1,128)S(1)} %bitcast.10, bf16[512,384]{1,0:T(8,128)(2,1)S(1)} %collective-permute-done.7.refs_0_, f32[8,128,384]{2,1,0:T(8,128)S(1)} %couple.14.refs_1_), custom_call_target="tpu_custom_call" | custom-call | flops 805306368 | bytes 4194304 | tf_op jit(solution)/shard_map/couple/pallas_call | solution.py:219
  122.0 3.9 %finish_second.1 = (f32[8,128,384]{2,1,0:T(8,128)S(1)}, f32[48,128]{1,0:T(8,128)S(1)}) custom-call(bf16[7,8,256,512]{3,2,1,0:T(8,128)(2,1)S(1)} %spread.1.dense_ref, f32[1,128]{1,0:T(1,128)S(1)} %bitcast.11, bf16[512,384]{1,0:T(8,128)(2,1)S(1)} %collective-permute-done.6.refs_0_, f32[8,128,384]{2,1,0:T(8,128)S(1)} %couple.15.refs_1_, ...), custom_call_target="tpu_custom_call" | custom-call | flops 805306368 | bytes 8388608 | tf_op jit(solution)/shard_map/finish_second/pallas_call | solution.py:356
  126.0 1.5 %collective-permute-start.13 = (f32[48,128]{1,0:T(8,128)S(1)}, f32[48,128]{1,0:T(8,128)S(1)}, u32[]{:S(2)}, u32[]{:S(2)}) collective-permute-start(f32[48,128]{1,0:T(8,128)S(1)} %get-tuple-element.55), channel_id=1, source_target_pairs={{0,2},{1,3},{2,0},{3,1},{4,6},{5,7},{6,4},{7,5},{8,10},{9,11},{10,... | collective-permute-start | bytes 73736 | tf_op jit(solution)/shard_map/ppermute | solution.py:38
  127.5 0.3 collective-permute-start.12
  127.8 1.6 %collective-permute-done.14 = f32[48,128]{1,0:T(8,128)S(1)} collective-permute-done((f32[48,128]{1,0:T(8,128)S(1)}, f32[48,128]{1,0:T(8,128)S(1)}, u32[]{:S(2)}, u32[]{:S(2)}) %collective-permute-start.14) | collective-permute-done | bytes 24608 | tf_op jit(solution)/shard_map/ppermute | solution.py:38
  129.5 0.4 collective-permute-done.13
  130.0 3.8 %collective-permute-done.15 = f32[48,128]{1,0:T(8,128)S(1)} collective-permute-done((f32[48,128]{1,0:T(8,128)S(1)}, f32[48,128]{1,0:T(8,128)S(1)}, u32[]{:S(2)}, u32[]{:S(2)}) %collective-permute-start.15) | collective-permute-done | bytes 24608 | tf_op jit(solution)/shard_map/ppermute | solution.py:38
  133.8 2.7 %collective-permute-start.18 = (f32[48,128]{1,0:T(8,128)S(1)}, f32[48,128]{1,0:T(8,128)S(1)}, u32[]{:S(2)}, u32[]{:S(2)}) collective-permute-start(f32[48,128]{1,0:T(8,128)S(1)} %add.24), channel_id=1, source_target_pairs={{0,24},{4,28},{8,16},{12,20},{16,8},{20,12},{24,0},{28,4},{1,25},{... | collective-permute-start | bytes 73736 | tf_op jit(solution)/shard_map/ppermute | solution.py:38
  136.5 6.1 %collective-permute-start.17 = (f32[48,128]{1,0:T(8,128)S(1)}, f32[48,128]{1,0:T(8,128)S(1)}, u32[]{:S(2)}, u32[]{:S(2)}) collective-permute-start(f32[48,128]{1,0:T(8,128)S(1)} %add.24), channel_id=1, source_target_pairs={{0,16},{4,20},{8,24},{12,28},{16,0},{20,4},{24,8},{28,12},{1,17},{... | collective-permute-start | bytes 73736 | tf_op jit(solution)/shard_map/ppermute | solution.py:38
  142.5 0.5 collective-permute-start.16
  143.0 1.5 collective-permute-done.17
  144.5 1.8 %collective-permute-done.16 = f32[48,128]{1,0:T(8,128)S(1)} collective-permute-done((f32[48,128]{1,0:T(8,128)S(1)}, f32[48,128]{1,0:T(8,128)S(1)}, u32[]{:S(2)}, u32[]{:S(2)}) %collective-permute-start.16) | collective-permute-done | bytes 24608 | tf_op jit(solution)/shard_map/ppermute | solution.py:38
  146.4 3.3 %final.1 = (f32[3,1024,128]{2,1,0:T(8,128)}, f32[3,1024,128]{2,1,0:T(8,128)}) custom-call(f32[3,1024,128]{2,1,0:T(8,128)S(1)} %copy-done.1, f32[8,128,384]{2,1,0:T(8,128)S(1)} %get-tuple-element.44.refs_4_.image_ref, f32[8,128,384]{2,1,0:T(8,128)S(1)} %get-tuple-element.54.later_ref, f32[48,128]{1,0:T(8,128)S(1)} %add_add_fusion.gathered_ref), custom_call_target="tpu_custom_call" | custom-call | tf_op jit(solution)/shard_map/final/pallas_call | solution.py:419
  (24 shorter events, 0.2 us)
Async XLA Ops:
  0.6 15.7 %copy-start.7 = (s32[8,24]{1,0:T(8,128)S(1)}, s32[8,24]{1,0:T(8,128)}, u32[]{:S(2)}) copy-start(s32[8,24]{1,0:T(8,128)} %slot_ref.1) | copy-start | bytes 2308
  1.4 1.4 copy-start
  2.8 0.7 copy-start.5
  4.8 24.0 %collective-permute-start.4 = (bf16[528,384]{1,0:T(8,128)(2,1)S(1)}, bf16[528,384]{1,0:T(8,128)(2,1)S(1)}, u32[]{:S(2)}, u32[]{:S(2)}) collective-permute-start(bf16[528,384]{1,0:T(8,128)(2,1)S(1)} %get-tuple-element.33), channel_id=1, source_target_pairs={{0,12},{4,16},{8,20},{12,24},{16,28},{20,0},{24,4},{28,8},{1,13},{... | collective-permute-start | bytes 1216520 | tf_op jit(solution)/shard_map/ppermute | solution.py:16
  8.8 22.6 %collective-permute-start.5 = (bf16[528,384]{1,0:T(8,128)(2,1)S(1)}, bf16[528,384]{1,0:T(8,128)(2,1)S(1)}, u32[]{:S(2)}, u32[]{:S(2)}) collective-permute-start(bf16[528,384]{1,0:T(8,128)(2,1)S(1)} %get-tuple-element.34), channel_id=1, source_target_pairs={{0,20},{4,24},{8,28},{12,0},{16,4},{20,8},{24,12},{28,16},{1,21},{... | collective-permute-start | bytes 1216520 | tf_op jit(solution)/shard_map/ppermute | solution.py:16
  9.9 29.0 %collective-permute-start.2 = (bf16[528,384]{1,0:T(8,128)(2,1)S(1)}, bf16[528,384]{1,0:T(8,128)(2,1)S(1)}, u32[]{:S(2)}, u32[]{:S(2)}) collective-permute-start(bf16[528,384]{1,0:T(8,128)(2,1)S(1)} %get-tuple-element.31), channel_id=1, source_target_pairs={{0,8},{4,12},{8,16},{12,20},{16,24},{20,28},{24,0},{28,4},{1,9},{5... | collective-permute-start | bytes 1216520 | tf_op jit(solution)/shard_map/ppermute | solution.py:16
  11.7 33.1 %collective-permute-start.3 = (bf16[528,384]{1,0:T(8,128)(2,1)S(1)}, bf16[528,384]{1,0:T(8,128)(2,1)S(1)}, u32[]{:S(2)}, u32[]{:S(2)}) collective-permute-start(bf16[528,384]{1,0:T(8,128)(2,1)S(1)} %get-tuple-element.32), channel_id=1, source_target_pairs={{0,24},{4,28},{8,0},{12,4},{16,8},{20,12},{24,16},{28,20},{1,25},{... | collective-permute-start | bytes 1216520 | tf_op jit(solution)/shard_map/ppermute | solution.py:16
  13.7 42.5 %collective-permute-start.1 = (bf16[528,384]{1,0:T(8,128)(2,1)S(1)}, bf16[528,384]{1,0:T(8,128)(2,1)S(1)}, u32[]{:S(2)}, u32[]{:S(2)}) collective-permute-start(bf16[528,384]{1,0:T(8,128)(2,1)S(1)} %get-tuple-element.30), channel_id=1, source_target_pairs={{0,4},{4,8},{8,12},{12,16},{16,20},{20,24},{24,28},{28,0},{1,5},{5... | collective-permute-start | bytes 1216520 | tf_op jit(solution)/shard_map/ppermute | solution.py:16
  16.3 2.8 %copy-start.2 = (bf16[8,24,128,128]{3,2,1,0:T(8,128)(2,1)S(1)}, bf16[8,24,128,128]{3,2,1,0:T(8,128)(2,1)}, u32[]{:S(2)}) copy-start(bf16[8,24,128,128]{3,2,1,0:T(8,128)(2,1)} %ks_ref.1) | copy-start | bytes 18874372
  19.1 1.6 %copy-start.3 = (bf16[8,8,128,128]{3,2,1,0:T(8,128)(2,1)S(1)}, bf16[8,8,128,128]{3,2,1,0:T(8,128)(2,1)}, u32[]{:S(2)}) copy-start(bf16[8,8,128,128]{3,2,1,0:T(8,128)(2,1)} %correlation_ref.1) | copy-start | bytes 6291460
  20.7 8.0 %copy-start.4 = (f32[128]{0:T(128)S(1)}, f32[128]{0:T(128)}, u32[]{:S(2)}) copy-start(f32[128]{0:T(128)} %param.9) | copy-start | bytes 1540
  28.8 29.9 %collective-permute-start = (bf16[528,384]{1,0:T(8,128)(2,1)S(1)}, bf16[528,384]{1,0:T(8,128)(2,1)S(1)}, u32[]{:S(2)}, u32[]{:S(2)}) collective-permute-start(bf16[528,384]{1,0:T(8,128)(2,1)S(1)} %get-tuple-element.29), channel_id=1, source_target_pairs={{0,28},{4,0},{8,4},{12,8},{16,12},{20,16},{24,20},{28,24},{1,29},{... | collective-permute-start | bytes 1216520 | tf_op jit(solution)/shard_map/ppermute | solution.py:16
  28.8 2.4 %copy-start.6 = (f32[1024]{0:T(1024)S(1)}, f32[1024]{0:T(1024)}, u32[]{:S(2)}) copy-start(f32[1024]{0:T(1024)} %param.8) | copy-start | bytes 12292
  56.2 2.5 %copy-start.1 = (f32[3,1024,128]{2,1,0:T(8,128)S(1)}, f32[3,1024,128]{2,1,0:T(8,128)}, u32[]{:S(2)}) copy-start(f32[3,1024,128]{2,1,0:T(8,128)} %right_ref.3) | copy-start | bytes 4718596
  62.5 28.2 %collective-permute-start.10 = (bf16[512,384]{1,0:T(8,128)(2,1)S(1)}, bf16[512,384]{1,0:T(8,128)(2,1)S(1)}, u32[]{:S(2)}, u32[]{:S(2)}) collective-permute-start(bf16[512,384]{1,0:T(8,128)(2,1)S(1)} %get-tuple-element.49), channel_id=1, source_target_pairs={{0,12},{4,16},{8,20},{12,24},{16,28},{20,0},{24,4},{28,8},{1,13},{... | collective-permute-start | bytes 1179656 | tf_op jit(solution)/shard_map/ppermute | solution.py:16
  73.2 24.0 %collective-permute-start.11 = (bf16[512,384]{1,0:T(8,128)(2,1)S(1)}, bf16[512,384]{1,0:T(8,128)(2,1)S(1)}, u32[]{:S(2)}, u32[]{:S(2)}) collective-permute-start(bf16[512,384]{1,0:T(8,128)(2,1)S(1)} %get-tuple-element.50), channel_id=1, source_target_pairs={{0,20},{4,24},{8,28},{12,0},{16,4},{20,8},{24,12},{28,16},{1,21},{... | collective-permute-start | bytes 1179656 | tf_op jit(solution)/shard_map/ppermute | solution.py:16
  73.2 32.4 %collective-permute-start.8 = (bf16[512,384]{1,0:T(8,128)(2,1)S(1)}, bf16[512,384]{1,0:T(8,128)(2,1)S(1)}, u32[]{:S(2)}, u32[]{:S(2)}) collective-permute-start(bf16[512,384]{1,0:T(8,128)(2,1)S(1)} %get-tuple-element.47), channel_id=1, source_target_pairs={{0,8},{4,12},{8,16},{12,20},{16,24},{20,28},{24,0},{28,4},{1,9},{5... | collective-permute-start | bytes 1179656 | tf_op jit(solution)/shard_map/ppermute | solution.py:16
  76.3 37.8 %collective-permute-start.9 = (bf16[512,384]{1,0:T(8,128)(2,1)S(1)}, bf16[512,384]{1,0:T(8,128)(2,1)S(1)}, u32[]{:S(2)}, u32[]{:S(2)}) collective-permute-start(bf16[512,384]{1,0:T(8,128)(2,1)S(1)} %get-tuple-element.48), channel_id=1, source_target_pairs={{0,24},{4,28},{8,0},{12,4},{16,8},{20,12},{24,16},{28,20},{1,25},{... | collective-permute-start | bytes 1179656 | tf_op jit(solution)/shard_map/ppermute | solution.py:16
  77.0 42.6 %collective-permute-start.7 = (bf16[512,384]{1,0:T(8,128)(2,1)S(1)}, bf16[512,384]{1,0:T(8,128)(2,1)S(1)}, u32[]{:S(2)}, u32[]{:S(2)}) collective-permute-start(bf16[512,384]{1,0:T(8,128)(2,1)S(1)} %get-tuple-element.46), channel_id=1, source_target_pairs={{0,4},{4,8},{8,12},{12,16},{16,20},{20,24},{24,28},{28,0},{1,5},{5... | collective-permute-start | bytes 1179656 | tf_op jit(solution)/shard_map/ppermute | solution.py:16
  90.7 31.3 %collective-permute-start.6 = (bf16[512,384]{1,0:T(8,128)(2,1)S(1)}, bf16[512,384]{1,0:T(8,128)(2,1)S(1)}, u32[]{:S(2)}, u32[]{:S(2)}) collective-permute-start(bf16[512,384]{1,0:T(8,128)(2,1)S(1)} %get-tuple-element.45), channel_id=1, source_target_pairs={{0,28},{4,0},{8,4},{12,8},{16,12},{20,16},{24,20},{28,24},{1,29},{... | collective-permute-start | bytes 1179656 | tf_op jit(solution)/shard_map/ppermute | solution.py:16
  125.9 3.6 %collective-permute-start.14 = (f32[48,128]{1,0:T(8,128)S(1)}, f32[48,128]{1,0:T(8,128)S(1)}, u32[]{:S(2)}, u32[]{:S(2)}) collective-permute-start(f32[48,128]{1,0:T(8,128)S(1)} %get-tuple-element.55), channel_id=1, source_target_pairs={{0,3},{1,2},{2,1},{3,0},{4,7},{5,6},{6,5},{7,4},{8,11},{9,10},{10,... | collective-permute-start | bytes 73736 | tf_op jit(solution)/shard_map/ppermute | solution.py:38
  126.0 3.9 %collective-permute-start.13 = (f32[48,128]{1,0:T(8,128)S(1)}, f32[48,128]{1,0:T(8,128)S(1)}, u32[]{:S(2)}, u32[]{:S(2)}) collective-permute-start(f32[48,128]{1,0:T(8,128)S(1)} %get-tuple-element.55), channel_id=1, source_target_pairs={{0,2},{1,3},{2,0},{3,1},{4,6},{5,7},{6,4},{7,5},{8,10},{9,11},{10,... | collective-permute-start | bytes 73736 | tf_op jit(solution)/shard_map/ppermute | solution.py:38
  127.5 2.4 %collective-permute-start.12 = (f32[48,128]{1,0:T(8,128)S(1)}, f32[48,128]{1,0:T(8,128)S(1)}, u32[]{:S(2)}, u32[]{:S(2)}) collective-permute-start(f32[48,128]{1,0:T(8,128)S(1)} %get-tuple-element.55), channel_id=1, source_target_pairs={{0,1},{1,0},{2,3},{3,2},{4,5},{5,4},{6,7},{7,6},{8,9},{9,8},{10,11... | collective-permute-start | bytes 73736 | tf_op jit(solution)/shard_map/ppermute | solution.py:38
  129.9 3.9 %collective-permute-start.15 = (f32[48,128]{1,0:T(8,128)S(1)}, f32[48,128]{1,0:T(8,128)S(1)}, u32[]{:S(2)}, u32[]{:S(2)}) collective-permute-start(f32[48,128]{1,0:T(8,128)S(1)} %add_add_fusion.1), channel_id=1, source_target_pairs={{0,4},{4,0},{8,12},{12,8},{16,20},{20,16},{24,28},{28,24},{1,5},{5... | collective-permute-start | bytes 73736 | tf_op jit(solution)/shard_map/ppermute | solution.py:38
  133.8 9.2 %collective-permute-start.18 = (f32[48,128]{1,0:T(8,128)S(1)}, f32[48,128]{1,0:T(8,128)S(1)}, u32[]{:S(2)}, u32[]{:S(2)}) collective-permute-start(f32[48,128]{1,0:T(8,128)S(1)} %add.24), channel_id=1, source_target_pairs={{0,24},{4,28},{8,16},{12,20},{16,8},{20,12},{24,0},{28,4},{1,25},{... | collective-permute-start | bytes 73736 | tf_op jit(solution)/shard_map/ppermute | solution.py:38
  136.5 8.1 %collective-permute-start.17 = (f32[48,128]{1,0:T(8,128)S(1)}, f32[48,128]{1,0:T(8,128)S(1)}, u32[]{:S(2)}, u32[]{:S(2)}) collective-permute-start(f32[48,128]{1,0:T(8,128)S(1)} %add.24), channel_id=1, source_target_pairs={{0,16},{4,20},{8,24},{12,28},{16,0},{20,4},{24,8},{28,12},{1,17},{... | collective-permute-start | bytes 73736 | tf_op jit(solution)/shard_map/ppermute | solution.py:38
  142.5 3.8 %collective-permute-start.16 = (f32[48,128]{1,0:T(8,128)S(1)}, f32[48,128]{1,0:T(8,128)S(1)}, u32[]{:S(2)}, u32[]{:S(2)}) collective-permute-start(f32[48,128]{1,0:T(8,128)S(1)} %add.24), channel_id=1, source_target_pairs={{0,8},{4,12},{8,0},{12,4},{16,24},{20,28},{24,16},{28,20},{1,9},{5... | collective-permute-start | bytes 73736 | tf_op jit(solution)/shard_map/ppermute | solution.py:38

commit v4 on v3

--- a/solution.py
+++ b/solution.py
@@ -9,6 +9,7 @@
 
 MIB = 2**20
 EXTRA = 16
+BATCH = 2
 
 
 def shifted(array, axis, by):
@@ -92,19 +93,56 @@
     ]
 
 
-def pack(readers, right_side, onsite):
+class Plan:
+    def __init__(self, count, span, relayed):
+        self.count, self.span, self.middle, self.relayed = count, span, (span - 1) // 2, relayed
+
+    def offset(self, source, reader):
+        value = lax.rem(source - reader + (self.middle + self.count), self.count)
+        return jnp.minimum(value, self.span - 1) if self.relayed else value
+
+    def direct(self):
+        if self.relayed:
+            return [1, 2, 3, 7, 6, 5]
+        far = range(self.middle, 0, -1)
+        return [by for f in far for by in (f, -f)]
+
+    def reader(self, key, me):
+        return me ^ key if self.relayed else lax.rem(me + key + self.count, self.count)
+
+    def source(self, key, me):
+        return me ^ key if self.relayed else lax.rem(me - key + self.count, self.count)
+
+    def pairs(self, key):
+        if not self.relayed:
+            return [(i, (i + key) % self.count) for i in range(self.count)]
+        return [(i, i ^ key) for i in range(self.count) if key < 4 or i not in INNER]
+
+
+INNER = (2, 3, 4, 5)
+
+
+def is_inner(me):
+    return (me >= INNER[0]) & (me <= INNER[-1])
+
+
+def pack(plan, readers, right_side, onsite):
     fields, rows, orbitals = right_side.shape
-    span, served = readers.shape[1:]
+    served = readers.shape[2]
     clusters, width = onsite.shape
-    base = served * width
-
-    def kernel(readers_ref, right_ref, onsite_ref, *messages):
+    lanes = fields * orbitals
+    keys = plan.direct()
+
+    def kernel(readers_ref, right_ref, onsite_ref, *refs):
+        messages, rounded = refs[:-1], refs[-1]
         norm = [jnp.zeros((8, orbitals), jnp.float32)] * fields
         heavy = [jnp.zeros((8, orbitals), jnp.float32)] * fields
         for cluster in range(clusters):
             weight = jnp.broadcast_to(onsite_ref[cluster : cluster + 1, :], (8, width))
+            here = slice(cluster * width, (cluster + 1) * width)
             for field in range(fields):
-                right = right_ref[field, cluster * width : (cluster + 1) * width, :]
+                right = right_ref[field, here, :]
+                rounded[here, field * orbitals : (field + 1) * orbitals] = right.astype(jnp.bfloat16)
                 square = right * right
                 norm[field] += folded(square)
                 heavy[field] += jnp.dot(weight, square, preferred_element_type=jnp.float32)
@@ -113,21 +151,110 @@
             / jnp.maximum(jnp.sum(jnp.sum(n, axis=0, keepdims=True), axis=1, keepdims=True), 1e-30)
             for h, n in zip(heavy, norm)
         ]
-        center = jnp.broadcast_to(per_field(centers, orbitals), (EXTRA, fields * orbitals))
-        center = center.astype(jnp.bfloat16)
-        for offset, message in enumerate(messages):
-            message[base : base + EXTRA, :] = center
-            for slot in range(served):
-                start = pl.multiple_of(readers_ref[0, offset, slot] * width, width)
-                for field in range(fields):
-                    message[
-                        slot * width : (slot + 1) * width, field * orbitals : (field + 1) * orbitals
-                    ] = right_ref[field, pl.ds(start, width), :].astype(jnp.bfloat16)
-
-    shape = jax.ShapeDtypeStruct((base + EXTRA, fields * orbitals), jnp.bfloat16)
-    return call(kernel, "pack", [shape] * span, [smem(), vmem(), vmem()])(
-        readers, right_side, onsite
-    )
+        center = jnp.broadcast_to(per_field(centers, orbitals), (EXTRA, lanes)).astype(jnp.bfloat16)
+        rounded[clusters * width :, :] = center
+        fill(plan, keys, readers_ref, rounded, messages, width)
+
+    message = jax.ShapeDtypeStruct((served * width + EXTRA, lanes), jnp.bfloat16)
+    full = jax.ShapeDtypeStruct((clusters * width + EXTRA, lanes), jnp.bfloat16)
+    *messages, own, full = call(
+        kernel, "pack", [message] * (len(keys) + 1) + [full], [smem(), vmem(), vmem()]
+    )(readers, right_side, onsite)
+    return dict(zip(keys, messages)), own, full
+
+
+def fill(plan, keys, readers_ref, rounded, messages, width):
+    served = readers_ref.shape[2]
+    me = lax.axis_index("row")
+    offsets = [plan.offset(me, plan.reader(key, me)) for key in keys] + [plan.middle]
+    pick(readers_ref, offsets, rounded, messages, width)
+
+
+def pick(readers_ref, offsets, rounded, messages, width):
+    served = readers_ref.shape[2]
+    for offset, message in zip(offsets, messages):
+        for slot in range(served):
+            start = pl.multiple_of(readers_ref[0, offset, slot] * width, width)
+            message[slot * width : (slot + 1) * width, :] = rounded[pl.ds(start, width), :]
+        rest = message.shape[0] - served * width
+        if rest:
+            message[served * width :, :] = rounded[rounded.shape[0] - rest :, :]
+
+
+def relay(plan, readers, full, served, width):
+    rest = full.shape[0] % (served * width)
+
+    def kernel(readers_ref, full_ref, *messages):
+        me = lax.axis_index("row")
+        pick(
+            readers_ref,
+            [plan.offset(me ^ 6, reader) for reader in (me, me ^ 1, me ^ 3)],
+            full_ref,
+            messages,
+            width,
+        )
+
+    message = jax.ShapeDtypeStruct((served * width + rest, full.shape[1]), jnp.bfloat16)
+    return call(kernel, "relay", [message] * 3, [smem(), vmem()])(readers, full)
+
+
+def exchange(plan, direct, own, full, readers, served, width):
+    sent = {k: lax.ppermute(m, "row", plan.pairs(k)) for k, m in direct.items()}
+    if not plan.relayed:
+        return [(own, 0)] + [(sent[k], k) for k in plan.direct()]
+    mine, beside, beyond = relay(plan, readers, full, served, width)
+    beside = lax.ppermute(beside, "row", [(i, i ^ 1) for i in INNER])
+    beyond = lax.ppermute(beyond, "row", [(i, i ^ 3) for i in INNER])
+    return [
+        (own, 0),
+        (sent[1], 1),
+        (sent[2], 2),
+        (sent[3], 3),
+        ((mine, sent[7]), (6, 7)),
+        ((beside, sent[6]), (7, 6)),
+        ((sent[5], beyond), (5, 5)),
+    ]
+
+
+def across(plan, full):
+    return lax.ppermute(full, "row", [(i, i ^ 6) for i in INNER]) if plan.relayed else full
+
+
+class Vectors:
+    def __init__(self, plan, items):
+        self.plan, self.items = plan, items
+        self.arrays, self.scratch = [], []
+        for value, _ in items:
+            many = isinstance(value, tuple)
+            self.arrays += list(value) if many else [value]
+            if many:
+                self.scratch.append(pltpu.VMEM(value[0].shape, value[0].dtype))
+        self.lanes = self.arrays[0].shape[1]
+        self.rows = self.arrays[0].shape[0]
+
+    def open(self, refs, scratch):
+        refs, scratch = list(refs), list(scratch)
+        me = lax.axis_index("row")
+        opened = []
+        for value, key in self.items:
+            if isinstance(value, tuple):
+                inner, outer, held = refs.pop(0), refs.pop(0), scratch.pop(0)
+
+                @pl.when(is_inner(me))
+                def _():
+                    held[...] = inner[...]
+
+                @pl.when(jnp.logical_not(is_inner(me)))
+                def _():
+                    held[...] = outer[...]
+
+                source = jnp.where(is_inner(me), me ^ key[0], me ^ key[1])
+                opened.append((self.plan.offset(source, me), held))
+            elif self.plan.relayed:
+                opened.append((self.plan.offset(me ^ key, me), refs.pop(0)))
+            else:
+                opened.append((self.plan.middle - key, refs.pop(0)))
+        return opened
 
 
 def levels(onsite):
@@ -175,108 +302,121 @@
     )(tile_slot, ks_tiles, correlation_tiles)
 
 
-def products(dense_ref, offsets, vectors, cluster, energy):
+def products(dense_ref, opened, clusters, energy):
     depth = dense_ref.shape[-1]
-    for offset, vector in zip(offsets, vectors):
+    for offset, vector in opened:
+        left = dense_ref[offset, clusters]
+        count, height, _ = left.shape
         value = jnp.dot(
-            dense_ref[offset, cluster], vector[0:depth, :], preferred_element_type=jnp.float32
+            left.reshape(count * height, depth), vector[0:depth, :], preferred_element_type=jnp.float32
         )
-        half = value.shape[0] // 2
-        yield value[:half] - energy * value[half:]
-
-
-def centers(vectors, depth):
-    return [vector[depth : depth + EXTRA, :].astype(jnp.float32)[:1] for vector in vectors]
-
-
-def work(dense, offsets, lanes):
-    return 2 * len(offsets) * dense.shape[1] * dense.shape[2] * dense.shape[3] * lanes
-
-
-def couple(dense, offsets, vectors, energies, sums):
+        value = value.reshape(count, 2, height // 2, value.shape[1])
+        yield value[:, 0] - energy * value[:, 1]
+
+
+def centers(opened, depth):
+    return [vector[depth : depth + EXTRA, :].astype(jnp.float32)[:1] for _, vector in opened]
+
+
+def work(dense, items, lanes):
+    return 2 * len(items) * dense.shape[1] * dense.shape[2] * dense.shape[3] * lanes
+
+
+def couple(dense, vectors, energies, sums):
     _, clusters, height, depth = dense.shape
-    lanes = vectors[0].shape[1]
-    count = len(offsets)
-    outs = 2 if vectors[0].shape[0] > depth else 1
+    lanes = vectors.lanes
+    count = len(vectors.arrays)
+    outs = 2 if vectors.rows > depth else 1
+    had = len(sums)
 
     def kernel(dense_ref, energies_ref, *refs):
-        vector_refs, sum_refs, out_refs = refs[:count], refs[count:-outs], refs[-outs:]
+        refs = list(refs)
+        vector_refs, sum_refs = refs[:count], refs[count : count + had]
+        out_refs, scratch = refs[count + had : count + had + outs], refs[count + had + outs :]
         energy = wide([energies_ref[...]] * (lanes // energies_ref.shape[1]))
-        weights = centers(vector_refs, depth) if outs == 2 else [None] * count
-
-        @pl.loop(0, clusters)
-        def _(cluster):
-            values = [ref[cluster] for ref in sum_refs]
-            parts = products(dense_ref, offsets, vector_refs, cluster, energy)
-            for weight, part in zip(weights, parts):
+        opened = vectors.open(vector_refs, scratch)
+        weights = centers(opened, depth) if outs == 2 else [None] * len(opened)
+
+        @pl.loop(0, clusters // BATCH)
+        def _(batch):
+            here = pl.ds(batch * BATCH, BATCH)
+            values = [ref[here] for ref in sum_refs]
+            for weight, part in zip(weights, products(dense_ref, opened, here, energy)):
                 terms = [part] if weight is None else [part, weight * part]
                 values = [v + t for v, t in zip(values, terms)] if values else terms
             for ref, value in zip(out_refs, values):
-                ref[cluster] = value
-
-    inputs = [dense, energies, *vectors, *sums]
+                ref[here] = value
+
+    inputs = [dense, energies, *vectors.arrays, *sums]
     shape = jax.ShapeDtypeStruct((clusters, height // 2, lanes), jnp.float32)
     return call(
         kernel,
         "couple",
         [shape] * outs,
         [vmem()] * len(inputs),
-        flops=work(dense, offsets, lanes),
+        vectors.scratch,
+        flops=work(dense, vectors.items, lanes),
         moved=4 * MIB,
     )(*inputs)
 
 
-def finish_first(dense, offsets, vectors, energies, sums, right_side, level, own, readers):
+def finish_first(plan, dense, vectors, energies, sums, right_side, level, own, readers):
     _, clusters, height, depth = dense.shape
-    lanes = vectors[0].shape[1]
+    lanes = vectors.lanes
     fields = right_side.shape[0]
     width = height // 2
-    count = len(offsets)
-    span, served = readers.shape[1:]
+    count = len(vectors.arrays)
+    keys = plan.direct()
 
     def kernel(dense_ref, energies_ref, *refs):
         vector_refs, refs = refs[:count], refs[count:]
         sum_ref, weighted_ref, right_ref, level_ref, own_ref, readers_ref = refs[:6]
         image_ref, shifted_ref, lines_ref = refs[6:9]
-        messages, (norm, bend, square, outgoing) = refs[9 : 9 + span], refs[9 + span :]
+        messages, outgoing = refs[9 : 10 + len(keys)], refs[10 + len(keys)]
+        norm, bend, square, *scratch = refs[11 + len(keys) :]
         energy = wide([energies_ref[...]] * fields)
-        weights = centers(vector_refs, depth)
-        (center,) = centers([own_ref], depth)
+        opened = vectors.open(vector_refs, scratch)
+        weights = centers(opened, depth)
+        (center,) = centers([(0, own_ref)], depth)
         for ref in (norm, bend, square):
             ref[...] = jnp.zeros_like(ref)
 
-        @pl.loop(0, clusters)
-        def _(cluster):
-            value, weighted = sum_ref[cluster], weighted_ref[cluster]
-            for weight, part in zip(weights, products(dense_ref, offsets, vector_refs, cluster, energy)):
+        @pl.loop(0, clusters // BATCH)
+        def _(batch):
+            here = pl.ds(batch * BATCH, BATCH)
+            value, weighted = sum_ref[here], weighted_ref[here]
+            for weight, part in zip(weights, products(dense_ref, opened, here, energy)):
                 value, weighted = value + part, weighted + weight * part
-            shifted_ref[cluster] = weighted
-            rows = pl.ds(pl.multiple_of(cluster * width, width), width)
-            right = wide([right_ref[f, rows, :] for f in range(fields)])
-            image = wide([level_ref[cluster]] * fields) * right + value
-            image_ref[cluster] = image
-            outgoing[cluster] = (image - center * right).astype(jnp.bfloat16)
-            norm[...] += folded(right * right)
-            bend[...] += folded(right * image)
-            square[...] += folded(image * image)
-
-        for offset, message in enumerate(messages):
-            for slot in range(served):
-                message[slot * width : (slot + 1) * width, :] = outgoing[readers_ref[0, offset, slot]]
+            shifted_ref[here] = weighted
+            for local in range(BATCH):
+                cluster = batch * BATCH + local
+                rows = pl.ds(pl.multiple_of(cluster * width, width), width)
+                right = wide([right_ref[f, rows, :] for f in range(fields)])
+                image = wide([level_ref[cluster]] * fields) * right + value[local]
+                image_ref[cluster] = image
+                outgoing[rows, :] = (image - center * right).astype(jnp.bfloat16)
+                norm[...] += folded(right * right)
+                bend[...] += folded(right * image)
+                square[...] += folded(image * image)
+
+        fill(plan, keys, readers_ref, outgoing, messages, width)
         lines_ref[...] = lined([norm[...], bend[...], square[...]], 8)
 
     message = jax.ShapeDtypeStruct((depth, lanes), jnp.bfloat16)
+    full = jax.ShapeDtypeStruct((clusters * width, lanes), jnp.bfloat16)
     vector = jax.ShapeDtypeStruct((clusters, width, lanes), jnp.float32)
-    return call(
+    image, weighted, lines, *messages, own, full = call(
         kernel,
         "finish_first",
-        [vector, vector, jax.ShapeDtypeStruct((8, lanes), jnp.float32)] + [message] * span,
+        [vector, vector, jax.ShapeDtypeStruct((8, lanes), jnp.float32)]
+        + [message] * (len(keys) + 1)
+        + [full],
         [vmem()] * (2 + count + 5) + [smem()],
-        [pltpu.VMEM((8, lanes), jnp.float32)] * 3
-        + [pltpu.VMEM((clusters, width, lanes), jnp.bfloat16)],
-        flops=work(dense, offsets, lanes),
+        [pltpu.VMEM((8, lanes), jnp.float32)] * 3 + vectors.scratch,
+        flops=work(dense, vectors.items, lanes),
         moved=8 * MIB,
-    )(dense, energies, *vectors, *sums, right_side, level, own, readers)
+    )(dense, energies, *vectors.arrays, *sums, right_side, level, own, readers)
+    return image, weighted, lines, dict(zip(keys, messages)), own, full
 
 
 def guesses(lines, fields):
@@ -291,47 +431,52 @@
     return per_field(alphas, orbitals), per_field(growths, orbitals)
 
 
-def finish_second(dense, offsets, vectors, energies, sums, right_side, level, image, weighted, lines, devices):
+def finish_second(dense, vectors, energies, sums, right_side, level, image, weighted, lines, devices):
     _, clusters, height, _ = dense.shape
-    lanes = vectors[0].shape[1]
+    lanes = vectors.lanes
     fields = right_side.shape[0]
     width = height // 2
-    count = len(offsets)
+    count = len(vectors.arrays)
     spots = -(-devices // 128) * 128
 
     def kernel(dense_ref, energies_ref, *refs):
         vector_refs, refs = refs[:count], refs[count:]
         sum_ref, right_ref, level_ref, image_ref, weighted_ref, lines_ref = refs[:6]
-        later_ref, out_ref, kept = refs[6], refs[7], refs[8]
+        later_ref, out_ref, kept, *scratch = refs[6:]
         energy = wide([energies_ref[...]] * fields)
         alpha, growth = guesses(lines_ref[...], fields)
         kept[...] = jnp.zeros_like(kept)
 
-        @pl.loop(0, clusters)
-        def _(cluster):
-            value = sum_ref[cluster] + weighted_ref[cluster]
-            for part in products(dense_ref, offsets, vector_refs, cluster, energy):
+        opened = vectors.open(vector_refs, scratch)
+
+        @pl.loop(0, clusters // BATCH)
+        def _(batch):
+            here = pl.ds(batch * BATCH, BATCH)
+            value = sum_ref[here] + weighted_ref[here]
+            for part in products(dense_ref, opened, here, energy):
                 value = value + part
-            rows = pl.ds(pl.multiple_of(cluster * width, width), width)
-            right = wide([right_ref[f, rows, :] for f in range(fields)])
-            first = image_ref[cluster]
-            later = wide([level_ref[cluster]] * fields) * first + value
-            later_ref[cluster] = later
-            step = alpha * first
-            residual = right - step
-            direction = growth * right - step
-            bent = growth * first - alpha * later
-            terms = (
-                residual * residual,
-                residual * first,
-                direction * bent,
-                direction * first + right * bent,
-                direction * later + first * bent,
-                right * later + first * first,
-                first * later,
-            )
-            for index, term in enumerate(terms):
-                kept[index] += folded(term)
+            for local in range(BATCH):
+                cluster = batch * BATCH + local
+                rows = pl.ds(pl.multiple_of(cluster * width, width), width)
+                right = wide([right_ref[f, rows, :] for f in range(fields)])
+                first = image_ref[cluster]
+                later = wide([level_ref[cluster]] * fields) * first + value[local]
+                later_ref[cluster] = later
+                step = alpha * first
+                residual = right - step
+                direction = growth * right - step
+                bent = growth * first - alpha * later
+                terms = (
+                    residual * residual,
+                    residual * first,
+                    direction * bent,
+                    direction * first + right * bent,
+                    direction * later + first * bent,
+                    right * later + first * first,
+                    first * later,
+                )
+                for index, term in enumerate(terms):
+                    kept[index] += folded(term)
 
         count_terms = kept.shape[0]
         block = jnp.concatenate(
@@ -361,10 +506,10 @@
             jax.ShapeDtypeStruct((16 * fields, spots), jnp.float32),
         ],
         [vmem()] * (2 + count + 6),
-        [pltpu.VMEM((7, 8, lanes), jnp.float32)],
-        flops=work(dense, offsets, lanes),
+        [pltpu.VMEM((7, 8, lanes), jnp.float32)] + vectors.scratch,
+        flops=work(dense, vectors.items, lanes),
         moved=8 * MIB,
-    )(dense, energies, *vectors, *sums, right_side, level, image, weighted, lines)
+    )(dense, energies, *vectors.arrays, *sums, right_side, level, image, weighted, lines)
 
 
 def step_sizes(gathered, fields, orbitals):
@@ -429,34 +574,30 @@
 
 def body(right_side, onsite, energies, ks_tiles, correlation_tiles, tile_slot, readers):
     span, served = readers.shape[1:]
-    width = ks_tiles.shape[2]
-    middle = (span - 1) // 2
-    devices = lax.axis_size("row") * lax.axis_size("col")
+    clusters, _, width, _ = ks_tiles.shape
+    rows = lax.axis_size("row")
+    devices = rows * lax.axis_size("col")
     onsite = onsite.reshape(-1, width)
     energies = energies.reshape(1, -1)
-
-    order = [middle]
-    for far in range(middle, 0, -1):
-        order += [middle - far, middle + far]
-    groups = [order[:1], order[1:3], order[3:5], order[5:6], order[6:]]
-
-    def exchange(messages):
-        return [shifted(m, "row", middle - o) if o != middle else m for o, m in enumerate(messages)]
-
-    def partial(vectors):
+    plan = Plan(rows, span, rows == 8 and span == 7)
+    theirs = across(plan, readers)
+
+    def partial(items):
         sums = []
-        for group in groups[:-1]:
-            sums = couple(dense, group, [vectors[o] for o in group], energies, sums)
-        return dense, groups[-1], [vectors[o] for o in groups[-1]], energies, sums
-
-    vectors = exchange(pack(readers, right_side, onsite))
-    own = vectors[middle]
+        for group in (items[:1], items[1:3], items[3:-2]):
+            sums = couple(dense, Vectors(plan, group), energies, sums)
+        return dense, Vectors(plan, items[-2:]), energies, sums
+
+    direct, own, full = pack(plan, readers, right_side, onsite)
+    items = exchange(plan, direct, own, across(plan, full), theirs, served, width)
     level = levels(onsite)
     dense = spread(tile_slot, ks_tiles, correlation_tiles, span, served)
-    image, weighted, lines, *messages = finish_first(*partial(vectors), right_side, level, own, readers)
-    vectors = exchange(messages)
+    image, weighted, lines, direct, out, full = finish_first(
+        plan, *partial(items), right_side, level, own, readers
+    )
+    items = exchange(plan, direct, out, across(plan, full), theirs, served, width)
     later, gathered = finish_second(
-        *partial(vectors), right_side, level, image, weighted, lines, devices
+        *partial(items), right_side, level, image, weighted, lines, devices
     )
     return tuple(final(right_side, image, later, summed(gathered)))
 

time: 150 us -> 134 us (0.89)
  waiting for transfers between devices: 57.3 us -> 24.4 us
  starting transfers between devices: 43.3 us -> 67.1 us
  Pallas kernels: 41 us -> 35.6 us
  local copies, waits for them, and re-layouts: 7.26 us -> 5.67 us
    ppermute x12 -> x19, waiting for transfers between devices: 48.2 us -> 16 us  [the longest x12 12.1 us: exchange(): sent = {k: lax.ppermute(m, 'row', plan.pairs(k)) for k, m in direct.items()}]
    ppermute x12 -> x19, starting transfers between devices: 32.1 us -> 59.3 us  [the longest x12 53.3 us: exchange(): sent = {k: lax.ppermute(m, 'row', plan.pairs(k)) for k, m in direct.items()}]
    pallas_call x9, Pallas kernels: 24.9 us -> 18.1 us  [the longest x6 15.4 us: couple(): call(kernel, 'couple', [shape] * outs, [vmem()] * len(inputs), vectors.sc...]
    ppermute x7, starting transfers between devices: 11.2 us -> 7.71 us  [summed(): lax.ppermute(array, axis, [(i, i ^ hop * k) for i in range(count)])]
    unnamed x17, local copies, waits for them, and re-layouts: 7.26 us -> 5.67 us
  transfers between devices with their start and end apart: 19 -> 26, of which waited for: 14 -> 12; matrix products, arithmetic and copies ran while one was open for 0% -> 0% of each run, Pallas kernels for 19% -> 16%
where the time goes in v4:
time: 134 us
  starting transfers between devices  67.1 us (50%)
  Pallas kernels  35.6 us (27%)
  waiting for transfers between devices  24.4 us (18%)
  local copies, waits for them, and re-layouts  5.67 us (4%)
    ppermute x12, starting transfers between devices, exchange(): sent = {k: lax.ppermute(m, 'row', plan.pairs(k)) for k, m in direct.items()}  53.3 us
    pallas_call x6, Pallas kernels, couple(): call(kernel, 'couple', [shape] * outs, [vmem()] * len(inputs), vectors.sc...  15.4 us
    ppermute x12, waiting for transfers between devices, exchange(): sent = {k: lax.ppermute(m, 'row', plan.pairs(k)) for k, m in direct.items()}  12.1 us
    ppermute x7, waiting for transfers between devices, summed(): lax.ppermute(array, axis, [(i, i ^ hop * k) for i in range(count)])  8.39 us
    ppermute x7, starting transfers between devices, summed(): lax.ppermute(array, axis, [(i, i ^ hop * k) for i in range(count)])  7.71 us
    unnamed x17, local copies, waits for them, and re-layouts  5.67 us
    pallas_call x1, Pallas kernels, spread(): call(kernel, 'spread', jax.ShapeDtypeStruct((span, clusters, 2 * width, s...  4.86 us
    pallas_call x1, Pallas kernels, finish_second(): call(kernel, 'finish_second', [jax.ShapeDtypeStruct((clusters, width, lan...  4.67 us
  transfers between devices with their start and end apart: 26, of which 12 were waited for; matrix products, arithmetic and copies ran while one was open for 0% of the time, Pallas kernels for 16%

profile of v4, /device:TPU:0, one launch (start us, length us, event | category | flops | bytes accessed | tf_op | source)
XLA Modules:
  0.0 133.7 jit_solution(11050690346271634917)
XLA Ops:
  0.6 0.8 copy.9.readers_ref.refs_9_
  1.4 1.4 %copy-done = f32[3,1024,128]{2,1,0:T(8,128)S(1)} copy-done((f32[3,1024,128]{2,1,0:T(8,128)S(1)}, f32[3,1024,128]{2,1,0:T(8,128)}, u32[]{:S(2)}) %copy-start) | copy-done | bytes 1572888
  2.8 0.7 copy-done.5
  3.5 1.3 pack.1
  4.8 0.7 collective-permute-start.1
  5.5 6.8 %collective-permute-start.6 = (bf16[528,384]{1,0:T(8,128)(2,1)S(1)}, bf16[528,384]{1,0:T(8,128)(2,1)S(1)}, u32[]{:S(2)}, u32[]{:S(2)}) collective-permute-start(bf16[528,384]{1,0:T(8,128)(2,1)S(1)} %get-tuple-element.40), channel_id=1, source_target_pairs={{0,12},{4,8},{8,4},{12,0},{16,28},{20,24},{24,20},{28,16},{1,13},{... | collective-permute-start | bytes 1216520 | tf_op jit(solution)/shard_map/ppermute | solution.py:202
  12.3 0.5 collective-permute-start.8
  13.0 0.6 collective-permute-start
  13.6 4.1 %collective-permute-start.7 = (bf16[528,384]{1,0:T(8,128)(2,1)S(1)}, bf16[528,384]{1,0:T(8,128)(2,1)S(1)}, u32[]{:S(2)}, u32[]{:S(2)}) collective-permute-start(bf16[528,384]{1,0:T(8,128)(2,1)S(1)} %get-tuple-element.42), channel_id=1, source_target_pairs={{0,28},{4,24},{24,4},{28,0},{1,29},{5,25},{25,5},{29,1},{2,30},{6,... | collective-permute-start | bytes 1216520 | tf_op jit(solution)/shard_map/ppermute | solution.py:202
  17.7 4.4 %collective-permute-start.3 = (bf16[528,384]{1,0:T(8,128)(2,1)S(1)}, bf16[528,384]{1,0:T(8,128)(2,1)S(1)}, u32[]{:S(2)}, u32[]{:S(2)}) collective-permute-start(bf16[528,384]{1,0:T(8,128)(2,1)S(1)} %get-tuple-element.37), channel_id=1, source_target_pairs={{0,24},{4,28},{24,0},{28,4},{1,25},{5,29},{25,1},{29,5},{2,26},{6,... | collective-permute-start | bytes 1216520 | tf_op jit(solution)/shard_map/ppermute | solution.py:202
  22.1 0.7 relay.2
  22.9 12.5 %collective-permute-start.4 = (bf16[528,384]{1,0:T(8,128)(2,1)S(1)}, bf16[528,384]{1,0:T(8,128)(2,1)S(1)}, u32[]{:S(2)}, u32[]{:S(2)}) collective-permute-start(bf16[528,384]{1,0:T(8,128)(2,1)S(1)} %get-tuple-element.38), channel_id=1, source_target_pairs={{0,20},{4,16},{24,12},{28,8},{1,21},{5,17},{25,13},{29,9},{2,22},{... | collective-permute-start | bytes 1216520 | tf_op jit(solution)/shard_map/ppermute | solution.py:202
  35.4 0.7 collective-permute-start.2
  36.1 1.3 collective-permute-start.5
  37.6 2.8 %copy-done.2 = bf16[8,24,128,128]{3,2,1,0:T(8,128)(2,1)S(1)} copy-done((bf16[8,24,128,128]{3,2,1,0:T(8,128)(2,1)S(1)}, bf16[8,24,128,128]{3,2,1,0:T(8,128)(2,1)}, u32[]{:S(2)}) %copy-start.2) | copy-done | bytes 6291480
  40.4 4.9 %spread.1.dense_ref = bf16[7,8,256,512]{3,2,1,0:T(8,128)(2,1)S(1)} custom-call(s32[8,24]{1,0:T(8,128)S(1)} %copy-done.7, bf16[8,24,128,128]{3,2,1,0:T(8,128)(2,1)S(1)} %copy-done.2, bf16[8,8,128,128]{3,2,1,0:T(8,128)(2,1)S(1)} %copy-done.3), custom_call_target="tpu_custom_call" | custom-call | bytes 16777216 | tf_op jit(solution)/shard_map/spread/pallas_call | solution.py:295
  45.3 1.8 %couple.6 = (f32[8,128,384]{2,1,0:T(8,128)S(1)}, f32[8,128,384]{2,1,0:T(8,128)S(1)}) custom-call(bf16[7,8,256,512]{3,2,1,0:T(8,128)(2,1)S(1)} %spread.1.dense_ref, f32[1,128]{1,0:T(1,128)S(1)} %bitcast.2, bf16[528,384]{1,0:T(8,128)(2,1)S(1)} %get-tuple-element.45.refs_0_.refs_8_), custom_call_target="tpu_custom_call" | custom-call | flops 805306368 | bytes 4194304 | tf_op jit(solution)/shard_map/couple/pallas_call | solution.py:352
  47.1 3.0 %couple.7 = (f32[8,128,384]{2,1,0:T(8,128)S(1)}, f32[8,128,384]{2,1,0:T(8,128)S(1)}) custom-call(bf16[7,8,256,512]{3,2,1,0:T(8,128)(2,1)S(1)} %spread.1.dense_ref, f32[1,128]{1,0:T(1,128)S(1)} %bitcast.3, bf16[528,384]{1,0:T(8,128)(2,1)S(1)} %collective-permute-done.8.refs_0_, bf16[528,384]{1,0:T(8,128)(2,1)S(1)} %collective-permute-done.9.refs_1_, ...), custom_call_target="tpu_custom_call" | custom-call | flops 1610612736 | bytes 4194304 | tf_op jit(solution)/shard_map/couple/pallas_call | solution.py:352
  50.1 3.0 %couple.8 = (f32[8,128,384]{2,1,0:T(8,128)S(1)}, f32[8,128,384]{2,1,0:T(8,128)S(1)}) custom-call(bf16[7,8,256,512]{3,2,1,0:T(8,128)(2,1)S(1)} %spread.1.dense_ref, f32[1,128]{1,0:T(1,128)S(1)} %bitcast.4, bf16[528,384]{1,0:T(8,128)(2,1)S(1)} %collective-permute-done.6.refs_0_, bf16[528,384]{1,0:T(8,128)(2,1)S(1)} %get-tuple-element.41.refs_1_, ...), custom_call_target="tpu_custom_call" | custom-call | flops 1610612736 | bytes 4194304 | tf_op jit(solution)/shard_map/couple/pallas_call | solution.py:352
  53.2 2.3 %collective-permute-done.4.refs_2_ = bf16[528,384]{1,0:T(8,128)(2,1)S(1)} collective-permute-done((bf16[528,384]{1,0:T(8,128)(2,1)S(1)}, bf16[528,384]{1,0:T(8,128)(2,1)S(1)}, u32[]{:S(2)}, u32[]{:S(2)}) %collective-permute-start.4) | collective-permute-done | bytes 405536 | tf_op jit(solution)/shard_map/ppermute | solution.py:202
  55.5 1.7 %collective-permute-done.5.refs_3_ = bf16[528,384]{1,0:T(8,128)(2,1)S(1)} collective-permute-done((bf16[528,384]{1,0:T(8,128)(2,1)S(1)}, bf16[528,384]{1,0:T(8,128)(2,1)S(1)}, u32[]{:S(2)}, u32[]{:S(2)}) %collective-permute-start.5) | collective-permute-done | bytes 405536 | tf_op jit(solution)/shard_map/ppermute | solution.py:207
  57.2 4.4 %finish_first.1 = (f32[8,128,384]{2,1,0:T(8,128)S(1)}, f32[8,128,384]{2,1,0:T(8,128)S(1)}, f32[8,384]{1,0:T(8,128)S(1)}, bf16[512,384]{1,0:T(8,128)(2,1)S(1)}, b...) custom-call(bf16[7,8,256,512]{3,2,1,0:T(8,128)(2,1)S(1)} %spread.1.d, ...), custom_call_target="tpu_custom_call" | custom-call | flops 1610612736 | bytes 8388608 | tf_op jit(solution)/shard_map/finish_first/pallas_call | solution.py:408
  61.7 0.7 collective-permute-start.10
  62.4 4.4 %collective-permute-start.15 = (bf16[512,384]{1,0:T(8,128)(2,1)S(1)}, bf16[512,384]{1,0:T(8,128)(2,1)S(1)}, u32[]{:S(2)}, u32[]{:S(2)}) collective-permute-start(bf16[512,384]{1,0:T(8,128)(2,1)S(1)} %get-tuple-element.58), channel_id=1, source_target_pairs={{0,12},{4,8},{8,4},{12,0},{16,28},{20,24},{24,20},{28,16},{1,13},{... | collective-permute-start | bytes 1179656 | tf_op jit(solution)/shard_map/ppermute | solution.py:202
  67.5 4.1 %collective-permute-start.16 = (bf16[512,384]{1,0:T(8,128)(2,1)S(1)}, bf16[512,384]{1,0:T(8,128)(2,1)S(1)}, u32[]{:S(2)}, u32[]{:S(2)}) collective-permute-start(bf16[512,384]{1,0:T(8,128)(2,1)S(1)} %get-tuple-element.60), channel_id=1, source_target_pairs={{0,28},{4,24},{24,4},{28,0},{1,29},{5,25},{25,5},{29,1},{2,30},{6,... | collective-permute-start | bytes 1179656 | tf_op jit(solution)/shard_map/ppermute | solution.py:202
  71.5 4.4 %collective-permute-start.12 = (bf16[512,384]{1,0:T(8,128)(2,1)S(1)}, bf16[512,384]{1,0:T(8,128)(2,1)S(1)}, u32[]{:S(2)}, u32[]{:S(2)}) collective-permute-start(bf16[512,384]{1,0:T(8,128)(2,1)S(1)} %get-tuple-element.55), channel_id=1, source_target_pairs={{0,24},{4,28},{24,0},{28,4},{1,25},{5,29},{25,1},{29,5},{2,26},{6,... | collective-permute-start | bytes 1179656 | tf_op jit(solution)/shard_map/ppermute | solution.py:202
  75.9 0.7 relay.3
  76.9 11.4 %collective-permute-start.13 = (bf16[512,384]{1,0:T(8,128)(2,1)S(1)}, bf16[512,384]{1,0:T(8,128)(2,1)S(1)}, u32[]{:S(2)}, u32[]{:S(2)}) collective-permute-start(bf16[512,384]{1,0:T(8,128)(2,1)S(1)} %get-tuple-element.56), channel_id=1, source_target_pairs={{0,20},{4,16},{24,12},{28,8},{1,21},{5,17},{25,13},{29,9},{2,22},{... | collective-permute-start | bytes 1179656 | tf_op jit(solution)/shard_map/ppermute | solution.py:202
  88.3 0.7 collective-permute-start.11
  89.0 1.3 collective-permute-start.14
  90.3 1.8 %couple.9.refs_2_ = f32[8,128,384]{2,1,0:T(8,128)S(1)} custom-call(bf16[7,8,256,512]{3,2,1,0:T(8,128)(2,1)S(1)} %spread.1.dense_ref, f32[1,128]{1,0:T(1,128)S(1)} %bitcast.6, bf16[512,384]{1,0:T(8,128)(2,1)S(1)} %get-tuple-element.63.refs_0_), custom_call_target="tpu_custom_call" | custom-call | flops 805306368 | bytes 4194304 | tf_op jit(solution)/shard_map/couple/pallas_call | solution.py:352
  92.1 2.9 %couple.10.refs_3_ = f32[8,128,384]{2,1,0:T(8,128)S(1)} custom-call(bf16[7,8,256,512]{3,2,1,0:T(8,128)(2,1)S(1)} %spread.1.dense_ref, f32[1,128]{1,0:T(1,128)S(1)} %bitcast.7, bf16[512,384]{1,0:T(8,128)(2,1)S(1)} %collective-permute-done.17.refs_0_, bf16[512,384]{1,0:T(8,128)(2,1)S(1)} %collective-permute-done.18.refs_1_, f32[8,128,384]{2,1,0:T(8,128)S(1)} %couple.9.refs_2_), custom_call_target="tpu_custom_call" | custom-call | flops 1610612736 | bytes 4194304 | tf_op jit(solution)/shard_map/couple/pallas_call | solution.py:352
  95.0 2.9 %couple.11.refs_4_ = f32[8,128,384]{2,1,0:T(8,128)S(1)} custom-call(bf16[7,8,256,512]{3,2,1,0:T(8,128)(2,1)S(1)} %spread.1.dense_ref, f32[1,128]{1,0:T(1,128)S(1)} %bitcast.8, bf16[512,384]{1,0:T(8,128)(2,1)S(1)} %collective-permute-done.15.refs_0_, bf16[512,384]{1,0:T(8,128)(2,1)S(1)} %get-tuple-element.59.refs_1_, ...), custom_call_target="tpu_custom_call" | custom-call | flops 1610612736 | bytes 4194304 | tf_op jit(solution)/shard_map/couple/pallas_call | solution.py:352
  98.0 5.5 %collective-permute-done.12.refs_1_ = bf16[512,384]{1,0:T(8,128)(2,1)S(1)} collective-permute-done((bf16[512,384]{1,0:T(8,128)(2,1)S(1)}, bf16[512,384]{1,0:T(8,128)(2,1)S(1)}, u32[]{:S(2)}, u32[]{:S(2)}) %collective-permute-start.12) | collective-permute-done | bytes 393248 | tf_op jit(solution)/shard_map/ppermute | solution.py:202
  103.5 4.0 %collective-permute-done.13.refs_2_ = bf16[512,384]{1,0:T(8,128)(2,1)S(1)} collective-permute-done((bf16[512,384]{1,0:T(8,128)(2,1)S(1)}, bf16[512,384]{1,0:T(8,128)(2,1)S(1)}, u32[]{:S(2)}, u32[]{:S(2)}) %collective-permute-start.13) | collective-permute-done | bytes 393248 | tf_op jit(solution)/shard_map/ppermute | solution.py:202
  107.5 2.1 %collective-permute-done.14.refs_3_ = bf16[512,384]{1,0:T(8,128)(2,1)S(1)} collective-permute-done((bf16[512,384]{1,0:T(8,128)(2,1)S(1)}, bf16[512,384]{1,0:T(8,128)(2,1)S(1)}, u32[]{:S(2)}, u32[]{:S(2)}) %collective-permute-start.14) | collective-permute-done | bytes 393248 | tf_op jit(solution)/shard_map/ppermute | solution.py:207
  109.6 4.7 %finish_second.1 = (f32[8,128,384]{2,1,0:T(8,128)S(1)}, f32[48,128]{1,0:T(8,128)S(1)}) custom-call(bf16[7,8,256,512]{3,2,1,0:T(8,128)(2,1)S(1)} %spread.1.dense_ref, f32[1,128]{1,0:T(1,128)S(1)} %bitcast.9, bf16[512,384]{1,0:T(8,128)(2,1)S(1)} %collective-permute-done.11.refs_0_, bf16[512,384]{1,0:T(8,128)(2,1)S(1)} %collective-permute-done.12.refs_1_, ...), custom_call_target="tpu_custom_call" | custom-call | flops 1610612736 | bytes 8388608 | tf_op jit(solution)/shard_map/finish_second/pallas_call | solution.py:501
  114.2 1.2 collective-permute-start.21
  115.4 0.6 collective-permute-start.20
  116.2 1.4 %collective-permute-done.21 = f32[48,128]{1,0:T(8,128)S(1)} collective-permute-done((f32[48,128]{1,0:T(8,128)S(1)}, f32[48,128]{1,0:T(8,128)S(1)}, u32[]{:S(2)}, u32[]{:S(2)}) %collective-permute-start.21) | collective-permute-done | bytes 24608 | tf_op jit(solution)/shard_map/ppermute | solution.py:39
  117.5 1.7 %collective-permute-done.20 = f32[48,128]{1,0:T(8,128)S(1)} collective-permute-done((f32[48,128]{1,0:T(8,128)S(1)}, f32[48,128]{1,0:T(8,128)S(1)}, u32[]{:S(2)}, u32[]{:S(2)}) %collective-permute-start.20) | collective-permute-done | bytes 24608 | tf_op jit(solution)/shard_map/ppermute | solution.py:39
  119.3 1.4 %collective-permute-start.22 = (f32[48,128]{1,0:T(8,128)S(1)}, f32[48,128]{1,0:T(8,128)S(1)}, u32[]{:S(2)}, u32[]{:S(2)}) collective-permute-start(f32[48,128]{1,0:T(8,128)S(1)} %add_add_fusion.1), channel_id=1, source_target_pairs={{0,4},{4,0},{8,12},{12,8},{16,20},{20,16},{24,28},{28,24},{1,5},{5... | collective-permute-start | bytes 73736 | tf_op jit(solution)/shard_map/ppermute | solution.py:39
  120.6 2.5 %collective-permute-done.22 = f32[48,128]{1,0:T(8,128)S(1)} collective-permute-done((f32[48,128]{1,0:T(8,128)S(1)}, f32[48,128]{1,0:T(8,128)S(1)}, u32[]{:S(2)}, u32[]{:S(2)}) %collective-permute-start.22) | collective-permute-done | bytes 24608 | tf_op jit(solution)/shard_map/ppermute | solution.py:39
  123.1 2.5 %collective-permute-start.25 = (f32[48,128]{1,0:T(8,128)S(1)}, f32[48,128]{1,0:T(8,128)S(1)}, u32[]{:S(2)}, u32[]{:S(2)}) collective-permute-start(f32[48,128]{1,0:T(8,128)S(1)} %add.24), channel_id=1, source_target_pairs={{0,24},{4,28},{8,16},{12,20},{16,8},{20,12},{24,0},{28,4},{1,25},{... | collective-permute-start | bytes 73736 | tf_op jit(solution)/shard_map/ppermute | solution.py:39
  125.6 1.9 %collective-permute-start.23 = (f32[48,128]{1,0:T(8,128)S(1)}, f32[48,128]{1,0:T(8,128)S(1)}, u32[]{:S(2)}, u32[]{:S(2)}) collective-permute-start(f32[48,128]{1,0:T(8,128)S(1)} %add.24), channel_id=1, source_target_pairs={{0,8},{4,12},{8,0},{12,4},{16,24},{20,28},{24,16},{28,20},{1,9},{5... | collective-permute-start | bytes 73736 | tf_op jit(solution)/shard_map/ppermute | solution.py:39
  127.5 1.2 collective-permute-done.25
  128.8 1.6 %collective-permute-done.24 = f32[48,128]{1,0:T(8,128)S(1)} collective-permute-done((f32[48,128]{1,0:T(8,128)S(1)}, f32[48,128]{1,0:T(8,128)S(1)}, u32[]{:S(2)}, u32[]{:S(2)}) %collective-permute-start.24) | collective-permute-done | bytes 24608 | tf_op jit(solution)/shard_map/ppermute | solution.py:39
  130.4 3.3 %final.1 = (f32[3,1024,128]{2,1,0:T(8,128)}, f32[3,1024,128]{2,1,0:T(8,128)}) custom-call(f32[3,1024,128]{2,1,0:T(8,128)S(1)} %copy-done.1, f32[8,128,384]{2,1,0:T(8,128)S(1)} %get-tuple-element.52.refs_7_.image_ref, f32[8,128,384]{2,1,0:T(8,128)S(1)} %get-tuple-element.66.later_ref, f32[48,128]{1,0:T(8,128)S(1)} %add_add_fusion.gathered_ref), custom_call_target="tpu_custom_call" | custom-call | tf_op jit(solution)/shard_map/final/pallas_call | solution.py:564
  (38 shorter events, 1.5 us)
Async XLA Ops:
  0.6 36.8 %copy-start.6 = (f32[1024]{0:T(1024)S(1)}, f32[1024]{0:T(1024)}, u32[]{:S(2)}) copy-start(f32[1024]{0:T(1024)} %param.8) | copy-start | bytes 12292
  1.4 1.4 %copy-start = (f32[3,1024,128]{2,1,0:T(8,128)S(1)}, f32[3,1024,128]{2,1,0:T(8,128)}, u32[]{:S(2)}) copy-start(f32[3,1024,128]{2,1,0:T(8,128)} %right_ref.3) | copy-start | bytes 4718596
  2.8 0.7 copy-start.5
  3.5 34.1 %copy-start.3 = (bf16[8,8,128,128]{3,2,1,0:T(8,128)(2,1)S(1)}, bf16[8,8,128,128]{3,2,1,0:T(8,128)(2,1)}, u32[]{:S(2)}) copy-start(bf16[8,8,128,128]{3,2,1,0:T(8,128)(2,1)} %correlation_ref.1) | copy-start | bytes 6291460
  3.5 34.1 %copy-start.7 = (s32[8,24]{1,0:T(8,128)S(1)}, s32[8,24]{1,0:T(8,128)}, u32[]{:S(2)}) copy-start(s32[8,24]{1,0:T(8,128)} %slot_ref.1) | copy-start | bytes 2308
  4.8 12.9 %collective-permute-start.1 = (bf16[1040,384]{1,0:T(8,128)(2,1)S(1)}, bf16[1040,384]{1,0:T(8,128)(2,1)S(1)}, u32[]{:S(2)}, u32[]{:S(2)}) collective-permute-start(bf16[1040,384]{1,0:T(8,128)(2,1)S(1)} %get-tuple-element.35), channel_id=1, source_target_pairs={{8,16},{12,20},{16,8},{20,12},{9,17},{13,21},{17,9},{21,13},{10,18... | collective-permute-start | bytes 2396168 | tf_op jit(solution)/shard_map/ppermute | solution.py:220
  5.5 17.4 %collective-permute-start.6 = (bf16[528,384]{1,0:T(8,128)(2,1)S(1)}, bf16[528,384]{1,0:T(8,128)(2,1)S(1)}, u32[]{:S(2)}, u32[]{:S(2)}) collective-permute-start(bf16[528,384]{1,0:T(8,128)(2,1)S(1)} %get-tuple-element.40), channel_id=1, source_target_pairs={{0,12},{4,8},{8,4},{12,0},{16,28},{20,24},{24,20},{28,16},{1,13},{... | collective-permute-start | bytes 1216520 | tf_op jit(solution)/shard_map/ppermute | solution.py:202
  12.3 23.1 %collective-permute-start.8 = (bf16[528,384]{1,0:T(8,128)(2,1)S(1)}, bf16[528,384]{1,0:T(8,128)(2,1)S(1)}, u32[]{:S(2)}, u32[]{:S(2)}) collective-permute-start(bf16[528,384]{1,0:T(8,128)(2,1)S(1)} %get-tuple-element.43), channel_id=1, source_target_pairs={{0,4},{4,0},{8,12},{12,8},{16,20},{20,16},{24,28},{28,24},{1,5},{5... | collective-permute-start | bytes 1216520 | tf_op jit(solution)/shard_map/ppermute | solution.py:202
  12.8 23.3 %collective-permute-start.9 = (bf16[528,384]{1,0:T(8,128)(2,1)S(1)}, bf16[528,384]{1,0:T(8,128)(2,1)S(1)}, u32[]{:S(2)}, u32[]{:S(2)}) collective-permute-start(bf16[528,384]{1,0:T(8,128)(2,1)S(1)} %get-tuple-element.44), channel_id=1, source_target_pairs={{0,8},{4,12},{8,0},{12,4},{16,24},{20,28},{24,16},{28,20},{1,9},{5... | collective-permute-start | bytes 1216520 | tf_op jit(solution)/shard_map/ppermute | solution.py:202
  13.0 0.7 collective-permute-start
  13.6 36.5 %collective-permute-start.7 = (bf16[528,384]{1,0:T(8,128)(2,1)S(1)}, bf16[528,384]{1,0:T(8,128)(2,1)S(1)}, u32[]{:S(2)}, u32[]{:S(2)}) collective-permute-start(bf16[528,384]{1,0:T(8,128)(2,1)S(1)} %get-tuple-element.42), channel_id=1, source_target_pairs={{0,28},{4,24},{24,4},{28,0},{1,29},{5,25},{25,5},{29,1},{2,30},{6,... | collective-permute-start | bytes 1216520 | tf_op jit(solution)/shard_map/ppermute | solution.py:202
  17.7 35.4 %collective-permute-start.3 = (bf16[528,384]{1,0:T(8,128)(2,1)S(1)}, bf16[528,384]{1,0:T(8,128)(2,1)S(1)}, u32[]{:S(2)}, u32[]{:S(2)}) collective-permute-start(bf16[528,384]{1,0:T(8,128)(2,1)S(1)} %get-tuple-element.37), channel_id=1, source_target_pairs={{0,24},{4,28},{24,0},{28,4},{1,25},{5,29},{25,1},{29,5},{2,26},{6,... | collective-permute-start | bytes 1216520 | tf_op jit(solution)/shard_map/ppermute | solution.py:202
  22.9 32.6 %collective-permute-start.4 = (bf16[528,384]{1,0:T(8,128)(2,1)S(1)}, bf16[528,384]{1,0:T(8,128)(2,1)S(1)}, u32[]{:S(2)}, u32[]{:S(2)}) collective-permute-start(bf16[528,384]{1,0:T(8,128)(2,1)S(1)} %get-tuple-element.38), channel_id=1, source_target_pairs={{0,20},{4,16},{24,12},{28,8},{1,21},{5,17},{25,13},{29,9},{2,22},{... | collective-permute-start | bytes 1216520 | tf_op jit(solution)/shard_map/ppermute | solution.py:202
  35.4 20.1 %collective-permute-start.2 = (bf16[528,384]{1,0:T(8,128)(2,1)S(1)}, bf16[528,384]{1,0:T(8,128)(2,1)S(1)}, u32[]{:S(2)}, u32[]{:S(2)}) collective-permute-start(bf16[528,384]{1,0:T(8,128)(2,1)S(1)} %get-tuple-element.36), channel_id=1, source_target_pairs={{8,12},{12,8},{16,20},{20,16},{9,13},{13,9},{17,21},{21,17},{10,14... | collective-permute-start | bytes 1216520 | tf_op jit(solution)/shard_map/ppermute | solution.py:206
  36.1 21.1 %collective-permute-start.5 = (bf16[528,384]{1,0:T(8,128)(2,1)S(1)}, bf16[528,384]{1,0:T(8,128)(2,1)S(1)}, u32[]{:S(2)}, u32[]{:S(2)}) collective-permute-start(bf16[528,384]{1,0:T(8,128)(2,1)S(1)} %get-tuple-element.39), channel_id=1, source_target_pairs={{8,4},{12,0},{16,28},{20,24},{9,5},{13,1},{17,29},{21,25},{10,6},{... | collective-permute-start | bytes 1216520 | tf_op jit(solution)/shard_map/ppermute | solution.py:207
  37.6 2.8 %copy-start.2 = (bf16[8,24,128,128]{3,2,1,0:T(8,128)(2,1)S(1)}, bf16[8,24,128,128]{3,2,1,0:T(8,128)(2,1)}, u32[]{:S(2)}) copy-start(bf16[8,24,128,128]{3,2,1,0:T(8,128)(2,1)} %ks_ref.1) | copy-start | bytes 18874372
  40.4 4.9 %copy-start.4 = (f32[128]{0:T(128)S(1)}, f32[128]{0:T(128)}, u32[]{:S(2)}) copy-start(f32[128]{0:T(128)} %param.9) | copy-start | bytes 1540
  50.1 7.1 %copy-start.1 = (f32[3,1024,128]{2,1,0:T(8,128)S(1)}, f32[3,1024,128]{2,1,0:T(8,128)}, u32[]{:S(2)}) copy-start(f32[3,1024,128]{2,1,0:T(8,128)} %right_ref.3) | copy-start | bytes 4718596
  61.7 9.9 %collective-permute-start.10 = (bf16[1024,384]{1,0:T(8,128)(2,1)S(1)}, bf16[1024,384]{1,0:T(8,128)(2,1)S(1)}, u32[]{:S(2)}, u32[]{:S(2)}) collective-permute-start(bf16[1024,384]{1,0:T(8,128)(2,1)S(1)} %get-tuple-element.53), channel_id=1, source_target_pairs={{8,16},{12,20},{16,8},{20,12},{9,17},{13,21},{17,9},{21,13},{10,18... | collective-permute-start | bytes 2359304 | tf_op jit(solution)/shard_map/ppermute | solution.py:220
  62.4 14.5 %collective-permute-start.15 = (bf16[512,384]{1,0:T(8,128)(2,1)S(1)}, bf16[512,384]{1,0:T(8,128)(2,1)S(1)}, u32[]{:S(2)}, u32[]{:S(2)}) collective-permute-start(bf16[512,384]{1,0:T(8,128)(2,1)S(1)} %get-tuple-element.58), channel_id=1, source_target_pairs={{0,12},{4,8},{8,4},{12,0},{16,28},{20,24},{24,20},{28,16},{1,13},{... | collective-permute-start | bytes 1179656 | tf_op jit(solution)/shard_map/ppermute | solution.py:202
  66.8 21.5 %collective-permute-start.17 = (bf16[512,384]{1,0:T(8,128)(2,1)S(1)}, bf16[512,384]{1,0:T(8,128)(2,1)S(1)}, u32[]{:S(2)}, u32[]{:S(2)}) collective-permute-start(bf16[512,384]{1,0:T(8,128)(2,1)S(1)} %get-tuple-element.61), channel_id=1, source_target_pairs={{0,4},{4,0},{8,12},{12,8},{16,20},{20,16},{24,28},{28,24},{1,5},{5... | collective-permute-start | bytes 1179656 | tf_op jit(solution)/shard_map/ppermute | solution.py:202
  67.3 21.7 %collective-permute-start.18 = (bf16[512,384]{1,0:T(8,128)(2,1)S(1)}, bf16[512,384]{1,0:T(8,128)(2,1)S(1)}, u32[]{:S(2)}, u32[]{:S(2)}) collective-permute-start(bf16[512,384]{1,0:T(8,128)(2,1)S(1)} %get-tuple-element.62), channel_id=1, source_target_pairs={{0,8},{4,12},{8,0},{12,4},{16,24},{20,28},{24,16},{28,20},{1,9},{5... | collective-permute-start | bytes 1179656 | tf_op jit(solution)/shard_map/ppermute | solution.py:202
  67.5 27.6 %collective-permute-start.16 = (bf16[512,384]{1,0:T(8,128)(2,1)S(1)}, bf16[512,384]{1,0:T(8,128)(2,1)S(1)}, u32[]{:S(2)}, u32[]{:S(2)}) collective-permute-start(bf16[512,384]{1,0:T(8,128)(2,1)S(1)} %get-tuple-element.60), channel_id=1, source_target_pairs={{0,28},{4,24},{24,4},{28,0},{1,29},{5,25},{25,5},{29,1},{2,30},{6,... | collective-permute-start | bytes 1179656 | tf_op jit(solution)/shard_map/ppermute | solution.py:202
  71.5 31.9 %collective-permute-start.12 = (bf16[512,384]{1,0:T(8,128)(2,1)S(1)}, bf16[512,384]{1,0:T(8,128)(2,1)S(1)}, u32[]{:S(2)}, u32[]{:S(2)}) collective-permute-start(bf16[512,384]{1,0:T(8,128)(2,1)S(1)} %get-tuple-element.55), channel_id=1, source_target_pairs={{0,24},{4,28},{24,0},{28,4},{1,25},{5,29},{25,1},{29,5},{2,26},{6,... | collective-permute-start | bytes 1179656 | tf_op jit(solution)/shard_map/ppermute | solution.py:202
  76.9 30.6 %collective-permute-start.13 = (bf16[512,384]{1,0:T(8,128)(2,1)S(1)}, bf16[512,384]{1,0:T(8,128)(2,1)S(1)}, u32[]{:S(2)}, u32[]{:S(2)}) collective-permute-start(bf16[512,384]{1,0:T(8,128)(2,1)S(1)} %get-tuple-element.56), channel_id=1, source_target_pairs={{0,20},{4,16},{24,12},{28,8},{1,21},{5,17},{25,13},{29,9},{2,22},{... | collective-permute-start | bytes 1179656 | tf_op jit(solution)/shard_map/ppermute | solution.py:202
  88.3 19.2 %collective-permute-start.11 = (bf16[512,384]{1,0:T(8,128)(2,1)S(1)}, bf16[512,384]{1,0:T(8,128)(2,1)S(1)}, u32[]{:S(2)}, u32[]{:S(2)}) collective-permute-start(bf16[512,384]{1,0:T(8,128)(2,1)S(1)} %get-tuple-element.54), channel_id=1, source_target_pairs={{8,12},{12,8},{16,20},{20,16},{9,13},{13,9},{17,21},{21,17},{10,14... | collective-permute-start | bytes 1179656 | tf_op jit(solution)/shard_map/ppermute | solution.py:206
  89.0 20.6 %collective-permute-start.14 = (bf16[512,384]{1,0:T(8,128)(2,1)S(1)}, bf16[512,384]{1,0:T(8,128)(2,1)S(1)}, u32[]{:S(2)}, u32[]{:S(2)}) collective-permute-start(bf16[512,384]{1,0:T(8,128)(2,1)S(1)} %get-tuple-element.57), channel_id=1, source_target_pairs={{8,4},{12,0},{16,28},{20,24},{9,5},{13,1},{17,29},{21,25},{10,6},{... | collective-permute-start | bytes 1179656 | tf_op jit(solution)/shard_map/ppermute | solution.py:207
  114.2 3.3 %collective-permute-start.21 = (f32[48,128]{1,0:T(8,128)S(1)}, f32[48,128]{1,0:T(8,128)S(1)}, u32[]{:S(2)}, u32[]{:S(2)}) collective-permute-start(f32[48,128]{1,0:T(8,128)S(1)} %get-tuple-element.67), channel_id=1, source_target_pairs={{0,3},{1,2},{2,1},{3,0},{4,7},{5,6},{6,5},{7,4},{8,11},{9,10},{10,... | collective-permute-start | bytes 73736 | tf_op jit(solution)/shard_map/ppermute | solution.py:39
  115.4 3.8 %collective-permute-start.20 = (f32[48,128]{1,0:T(8,128)S(1)}, f32[48,128]{1,0:T(8,128)S(1)}, u32[]{:S(2)}, u32[]{:S(2)}) collective-permute-start(f32[48,128]{1,0:T(8,128)S(1)} %get-tuple-element.67), channel_id=1, source_target_pairs={{0,2},{1,3},{2,0},{3,1},{4,6},{5,7},{6,4},{7,5},{8,10},{9,11},{10,... | collective-permute-start | bytes 73736 | tf_op jit(solution)/shard_map/ppermute | solution.py:39
  116.0 3.2 %collective-permute-start.19 = (f32[48,128]{1,0:T(8,128)S(1)}, f32[48,128]{1,0:T(8,128)S(1)}, u32[]{:S(2)}, u32[]{:S(2)}) collective-permute-start(f32[48,128]{1,0:T(8,128)S(1)} %get-tuple-element.67), channel_id=1, source_target_pairs={{0,1},{1,0},{2,3},{3,2},{4,5},{5,4},{6,7},{7,6},{8,9},{9,8},{10,11... | collective-permute-start | bytes 73736 | tf_op jit(solution)/shard_map/ppermute | solution.py:39
  119.3 3.9 %collective-permute-start.22 = (f32[48,128]{1,0:T(8,128)S(1)}, f32[48,128]{1,0:T(8,128)S(1)}, u32[]{:S(2)}, u32[]{:S(2)}) collective-permute-start(f32[48,128]{1,0:T(8,128)S(1)} %add_add_fusion.1), channel_id=1, source_target_pairs={{0,4},{4,0},{8,12},{12,8},{16,20},{20,16},{24,28},{28,24},{1,5},{5... | collective-permute-start | bytes 73736 | tf_op jit(solution)/shard_map/ppermute | solution.py:39
  123.1 5.6 %collective-permute-start.25 = (f32[48,128]{1,0:T(8,128)S(1)}, f32[48,128]{1,0:T(8,128)S(1)}, u32[]{:S(2)}, u32[]{:S(2)}) collective-permute-start(f32[48,128]{1,0:T(8,128)S(1)} %add.24), channel_id=1, source_target_pairs={{0,24},{4,28},{8,16},{12,20},{16,8},{20,12},{24,0},{28,4},{1,25},{... | collective-permute-start | bytes 73736 | tf_op jit(solution)/shard_map/ppermute | solution.py:39
  125.6 4.7 %collective-permute-start.24 = (f32[48,128]{1,0:T(8,128)S(1)}, f32[48,128]{1,0:T(8,128)S(1)}, u32[]{:S(2)}, u32[]{:S(2)}) collective-permute-start(f32[48,128]{1,0:T(8,128)S(1)} %add.24), channel_id=1, source_target_pairs={{0,16},{4,20},{8,24},{12,28},{16,0},{20,4},{24,8},{28,12},{1,17},{... | collective-permute-start | bytes 73736 | tf_op jit(solution)/shard_map/ppermute | solution.py:39
  125.6 4.7 %collective-permute-start.23 = (f32[48,128]{1,0:T(8,128)S(1)}, f32[48,128]{1,0:T(8,128)S(1)}, u32[]{:S(2)}, u32[]{:S(2)}) collective-permute-start(f32[48,128]{1,0:T(8,128)S(1)} %add.24), channel_id=1, source_target_pairs={{0,8},{4,12},{8,0},{12,4},{16,24},{20,28},{24,16},{28,20},{1,9},{5... | collective-permute-start | bytes 73736 | tf_op jit(solution)/shard_map/ppermute | solution.py:39

commit v5 on v4

--- a/solution.py
+++ b/solution.py
@@ -151,8 +151,13 @@
             / jnp.maximum(jnp.sum(jnp.sum(n, axis=0, keepdims=True), axis=1, keepdims=True), 1e-30)
             for h, n in zip(heavy, norm)
         ]
-        center = jnp.broadcast_to(per_field(centers, orbitals), (EXTRA, lanes)).astype(jnp.bfloat16)
-        rounded[clusters * width :, :] = center
+        rest = jnp.broadcast_to(per_field(centers, orbitals), (EXTRA, lanes))
+        line, lane = (lax.broadcasted_iota(jnp.int32, (EXTRA, lanes), d) for d in (0, 1))
+        for offset in range(readers_ref.shape[1]):
+            for slot in range(served):
+                here = (line == offset + 1) & (lane == slot)
+                rest = jnp.where(here, readers_ref[0, offset, slot].astype(jnp.float32), rest)
+        rounded[clusters * width :, :] = rest.astype(jnp.bfloat16)
         fill(plan, keys, readers_ref, rounded, messages, width)
 
     message = jax.ShapeDtypeStruct((served * width + EXTRA, lanes), jnp.bfloat16)
@@ -164,60 +169,77 @@
 
 
 def fill(plan, keys, readers_ref, rounded, messages, width):
-    served = readers_ref.shape[2]
     me = lax.axis_index("row")
     offsets = [plan.offset(me, plan.reader(key, me)) for key in keys] + [plan.middle]
-    pick(readers_ref, offsets, rounded, messages, width)
-
-
-def pick(readers_ref, offsets, rounded, messages, width):
-    served = readers_ref.shape[2]
     for offset, message in zip(offsets, messages):
-        for slot in range(served):
-            start = pl.multiple_of(readers_ref[0, offset, slot] * width, width)
-            message[slot * width : (slot + 1) * width, :] = rounded[pl.ds(start, width), :]
-        rest = message.shape[0] - served * width
-        if rest:
-            message[served * width :, :] = rounded[rounded.shape[0] - rest :, :]
-
-
-def relay(plan, readers, full, served, width):
-    rest = full.shape[0] % (served * width)
-
-    def kernel(readers_ref, full_ref, *messages):
-        me = lax.axis_index("row")
-        pick(
-            readers_ref,
-            [plan.offset(me ^ 6, reader) for reader in (me, me ^ 1, me ^ 3)],
-            full_ref,
-            messages,
-            width,
-        )
-
-    message = jax.ShapeDtypeStruct((served * width + rest, full.shape[1]), jnp.bfloat16)
-    return call(kernel, "relay", [message] * 3, [smem(), vmem()])(readers, full)
-
-
-def exchange(plan, direct, own, full, readers, served, width):
+        served = readers_ref.shape[2]
+        gather([readers_ref[0, offset, slot] for slot in range(served)], rounded, message, width)
+
+
+def gather(clusters, rounded, message, width):
+    for slot, cluster in enumerate(clusters):
+        start = pl.multiple_of(cluster * width, width)
+        message[slot * width : (slot + 1) * width, :] = rounded[pl.ds(start, width), :]
+    used = len(clusters) * width
+    if message.shape[0] > used:
+        message[used:, :] = rounded[rounded.shape[0] - EXTRA :, :]
+
+
+def relay(plan, full, chosen, served, width):
+    lanes = full.shape[1]
+    extra = EXTRA if chosen is None else 0
+    message = jax.ShapeDtypeStruct((served * width + extra, lanes), jnp.bfloat16)
+
+    def kernel(*refs):
+        if chosen is None:
+            full_ref, *messages, chosen_ref = refs
+            me = lax.axis_index("row")
+            base = full_ref.shape[0] - EXTRA
+            table = full_ref[base : base + EXTRA, 0:width].astype(jnp.float32)
+            line, lane = (lax.broadcasted_iota(jnp.int32, table.shape, d) for d in (0, 1))
+            for index, reader in enumerate((me, me ^ 1, me ^ 3)):
+                offset = plan.offset(me ^ 6, reader)
+                for slot in range(served):
+                    here = (line == offset + 1) & (lane == slot)
+                    chosen_ref[index, slot] = jnp.sum(jnp.where(here, table, 0.0)).astype(jnp.int32)
+        else:
+            chosen_ref, full_ref, *messages = refs
+        for index, out in enumerate(messages):
+            gather([chosen_ref[index, slot] for slot in range(served)], full_ref, out, width)
+
+    if chosen is not None:
+        return call(kernel, "relay", [message] * 3, [smem(), vmem()])(chosen, full), chosen
+    *messages, chosen = pl.pallas_call(
+        kernel,
+        out_shape=[message] * 3 + [jax.ShapeDtypeStruct((3, served), jnp.int32)],
+        in_specs=[vmem()],
+        out_specs=[vmem()] * 3 + [smem()],
+        compiler_params=pltpu.CompilerParams(vmem_limit_bytes=12 * MIB),
+        cost_estimate=pl.CostEstimate(flops=0, bytes_accessed=MIB, transcendentals=0),
+        name="relay",
+    )(full)
+    return messages, chosen
+
+
+def exchange(plan, direct, own, full, chosen, served, width):
+    if plan.relayed:
+        full = lax.ppermute(full, "row", [(i, i ^ 6) for i in INNER])
     sent = {k: lax.ppermute(m, "row", plan.pairs(k)) for k, m in direct.items()}
     if not plan.relayed:
-        return [(own, 0)] + [(sent[k], k) for k in plan.direct()]
-    mine, beside, beyond = relay(plan, readers, full, served, width)
+        return [(own, 0)] + [(sent[k], k) for k in plan.direct()], None
+    (mine, beside, beyond), chosen = relay(plan, full, chosen, served, width)
     beside = lax.ppermute(beside, "row", [(i, i ^ 1) for i in INNER])
     beyond = lax.ppermute(beyond, "row", [(i, i ^ 3) for i in INNER])
-    return [
+    items = [
         (own, 0),
         (sent[1], 1),
         (sent[2], 2),
         (sent[3], 3),
-        ((mine, sent[7]), (6, 7)),
-        ((beside, sent[6]), (7, 6)),
-        ((sent[5], beyond), (5, 5)),
+        ((sent[5], sent[7]), (5, 7)),
+        ((mine, sent[6]), (6, 6)),
+        ((beside, beyond), (7, 5)),
     ]
-
-
-def across(plan, full):
-    return lax.ppermute(full, "row", [(i, i ^ 6) for i in INNER]) if plan.relayed else full
+    return items, chosen
 
 
 class Vectors:
@@ -542,22 +564,27 @@
     blocks = 4
     each = clusters // blocks
 
-    def kernel(right_ref, image_ref, later_ref, gathered_ref, solution_ref, residual_ref):
+    def kernel(right_ref, image_ref, later_ref, gathered_ref, solution_ref, residual_ref, steps):
         step = pl.program_id(0)
-        alpha, growth, gain = step_sizes(gathered_ref[...], fields, orbitals)
+
+        @pl.when(step == 0)
+        def _():
+            alpha, growth, gain = step_sizes(gathered_ref[...], fields, orbitals)
+            steps[0:1, :] = alpha + gain * growth
+            steps[1:2, :] = gain * alpha
+
         for local in range(each):
             cluster = step * each + local
             rows = pl.ds(pl.multiple_of(cluster * width, width), width)
             here = slice(local * width, (local + 1) * width)
             for field in range(fields):
                 part = slice(field * orbitals, (field + 1) * orbitals)
+                one, two = steps[0:1, part], steps[1:2, part]
                 right = right_ref[field, rows, :]
                 first = image_ref[cluster, :, part]
-                moved = alpha[:, part] * first
-                direction = growth[:, part] * right - moved
-                bent = growth[:, part] * first - alpha[:, part] * later_ref[cluster, :, part]
-                solution_ref[field, here, :] = alpha[:, part] * right + gain[:, part] * direction
-                residual_ref[field, here, :] = (right - moved) - gain[:, part] * bent
+                later = later_ref[cluster, :, part]
+                solution_ref[field, here, :] = one * right - two * first
+                residual_ref[field, here, :] = (right - one * first) + two * later
 
     vector = pl.BlockSpec((fields, each * width, orbitals), lambda i: (0, i, 0))
     shape = jax.ShapeDtypeStruct(right_side.shape, jnp.float32)
@@ -567,6 +594,7 @@
         out_shape=[shape, shape],
         in_specs=[vmem()] * 4,
         out_specs=[vector, vector],
+        scratch_shapes=[pltpu.VMEM((8, lanes), jnp.float32)],
         compiler_params=pltpu.CompilerParams(vmem_limit_bytes=12 * MIB),
         name="final",
     )(right_side, image, later, gathered)
@@ -580,7 +608,6 @@
     onsite = onsite.reshape(-1, width)
     energies = energies.reshape(1, -1)
     plan = Plan(rows, span, rows == 8 and span == 7)
-    theirs = across(plan, readers)
 
     def partial(items):
         sums = []
@@ -589,13 +616,13 @@
         return dense, Vectors(plan, items[-2:]), energies, sums
 
     direct, own, full = pack(plan, readers, right_side, onsite)
-    items = exchange(plan, direct, own, across(plan, full), theirs, served, width)
+    items, chosen = exchange(plan, direct, own, full, None, served, width)
     level = levels(onsite)
     dense = spread(tile_slot, ks_tiles, correlation_tiles, span, served)
     image, weighted, lines, direct, out, full = finish_first(
         plan, *partial(items), right_side, level, own, readers
     )
-    items = exchange(plan, direct, out, across(plan, full), theirs, served, width)
+    items, _ = exchange(plan, direct, out, full, chosen, served, width)
     later, gathered = finish_second(
         *partial(items), right_side, level, image, weighted, lines, devices
     )

time: 134 us -> 141 us (1.052)
  waiting for transfers between devices: 24.4 us -> 49.4 us
  starting transfers between devices: 67.1 us -> 49.9 us
    ppermute x12, waiting for transfers between devices: 12.1 us -> 31.5 us  [exchange(): sent = {k: lax.ppermute(m, 'row', plan.pairs(k)) for k, m in direct.items()}]
    ppermute x12, starting transfers between devices: 53.3 us -> 36.3 us  [exchange(): sent = {k: lax.ppermute(m, 'row', plan.pairs(k)) for k, m in direct.items()}]
    ppermute x2, waiting for transfers between devices: 3.82 us -> 10.9 us  [exchange(): beyond = lax.ppermute(beyond, 'row', [(i, i ^ 3) for i in INNER])]
    ppermute x7, waiting for transfers between devices: 8.39 us -> 6.91 us  [summed(): lax.ppermute(array, axis, [(i, i ^ hop * k) for i in range(count)])]
    unnamed x17 -> x15, local copies, waits for them, and re-layouts: 5.67 us -> 5.66 us
  transfers between devices with their start and end apart: 26 -> 25, of which waited for: 12 -> 15; matrix products, arithmetic and copies ran while one was open for 0% -> 0% of each run, Pallas kernels for 16% -> 16%
where the time goes in v5:
time: 141 us
  starting transfers between devices  49.9 us (35%)
  waiting for transfers between devices  49.4 us (35%)
  Pallas kernels  34.9 us (25%)
  local copies, waits for them, and re-layouts  5.66 us (4%)
    ppermute x12, starting transfers between devices, exchange(): sent = {k: lax.ppermute(m, 'row', plan.pairs(k)) for k, m in direct.items()}  36.3 us
    ppermute x12, waiting for transfers between devices, exchange(): sent = {k: lax.ppermute(m, 'row', plan.pairs(k)) for k, m in direct.items()}  31.5 us
    pallas_call x6, Pallas kernels, couple(): call(kernel, 'couple', [shape] * outs, [vmem()] * len(inputs), vectors.sc...  15.4 us
    ppermute x2, waiting for transfers between devices, exchange(): beyond = lax.ppermute(beyond, 'row', [(i, i ^ 3) for i in INNER])  10.9 us
    ppermute x7, starting transfers between devices, summed(): lax.ppermute(array, axis, [(i, i ^ hop * k) for i in range(count)])  8.34 us
    ppermute x7, waiting for transfers between devices, summed(): lax.ppermute(array, axis, [(i, i ^ hop * k) for i in range(count)])  6.91 us
    unnamed x15, local copies, waits for them, and re-layouts  5.66 us
    pallas_call x1, Pallas kernels, spread(): call(kernel, 'spread', jax.ShapeDtypeStruct((span, clusters, 2 * width, s...  4.86 us
  transfers between devices with their start and end apart: 25, of which 15 were waited for; matrix products, arithmetic and copies ran while one was open for 0% of the time, Pallas kernels for 16%

profile of v5, /device:TPU:0, one launch (start us, length us, event | category | flops | bytes accessed | tf_op | source)
XLA Modules:
  0.0 140.8 jit_solution(10870697083091775325)
XLA Ops:
  0.6 0.8 copy.9.readers_ref.refs_9_
  1.4 1.4 copy-done
  2.8 0.7 copy-done.5
  3.5 1.3 pack.1
  4.8 0.7 collective-permute-start
  5.5 6.8 %collective-permute-start.4 = (bf16[528,384]{1,0:T(8,128)(2,1)S(1)}, bf16[528,384]{1,0:T(8,128)(2,1)S(1)}, u32[]{:S(2)}, u32[]{:S(2)}) collective-permute-start(bf16[528,384]{1,0:T(8,128)(2,1)S(1)} %get-tuple-element.41), channel_id=1, source_target_pairs={{0,12},{4,8},{8,4},{12,0},{16,28},{20,24},{24,20},{28,16},{1,13},{... | collective-permute-start | bytes 1216520 | tf_op jit(solution)/shard_map/ppermute | solution.py:227
  13.0 4.6 %collective-permute-start.5 = (bf16[528,384]{1,0:T(8,128)(2,1)S(1)}, bf16[528,384]{1,0:T(8,128)(2,1)S(1)}, u32[]{:S(2)}, u32[]{:S(2)}) collective-permute-start(bf16[528,384]{1,0:T(8,128)(2,1)S(1)} %get-tuple-element.42), channel_id=1, source_target_pairs={{0,20},{4,16},{24,12},{28,8},{1,21},{5,17},{25,13},{29,9},{2,22},{... | collective-permute-start | bytes 1216520 | tf_op jit(solution)/shard_map/ppermute | solution.py:227
  17.6 4.3 %collective-permute-start.6 = (bf16[528,384]{1,0:T(8,128)(2,1)S(1)}, bf16[528,384]{1,0:T(8,128)(2,1)S(1)}, u32[]{:S(2)}, u32[]{:S(2)}) collective-permute-start(bf16[528,384]{1,0:T(8,128)(2,1)S(1)} %get-tuple-element.43), channel_id=1, source_target_pairs={{0,28},{4,24},{24,4},{28,0},{1,29},{5,25},{25,5},{29,1},{2,30},{6,... | collective-permute-start | bytes 1216520 | tf_op jit(solution)/shard_map/ppermute | solution.py:227
  22.0 0.8 relay.2
  22.8 3.3 %collective-permute-start.1 = (bf16[528,384]{1,0:T(8,128)(2,1)S(1)}, bf16[528,384]{1,0:T(8,128)(2,1)S(1)}, u32[]{:S(2)}, u32[]{:S(2)}) collective-permute-start(bf16[528,384]{1,0:T(8,128)(2,1)S(1)} %get-tuple-element.38), channel_id=1, source_target_pairs={{0,24},{4,28},{24,0},{28,4},{1,25},{5,29},{25,1},{29,5},{2,26},{6,... | collective-permute-start | bytes 1216520 | tf_op jit(solution)/shard_map/ppermute | solution.py:227
  26.1 4.0 %collective-permute-done.7.refs_0_ = bf16[528,384]{1,0:T(8,128)(2,1)S(1)} collective-permute-done((bf16[528,384]{1,0:T(8,128)(2,1)S(1)}, bf16[528,384]{1,0:T(8,128)(2,1)S(1)}, u32[]{:S(2)}, u32[]{:S(2)}) %collective-permute-start.7) | collective-permute-done | bytes 405536 | tf_op jit(solution)/shard_map/ppermute | solution.py:227
  30.9 1.3 collective-permute-start.3
  32.4 2.8 %copy-done.2 = bf16[8,24,128,128]{3,2,1,0:T(8,128)(2,1)S(1)} copy-done((bf16[8,24,128,128]{3,2,1,0:T(8,128)(2,1)S(1)}, bf16[8,24,128,128]{3,2,1,0:T(8,128)(2,1)}, u32[]{:S(2)}) %copy-start.2) | copy-done | bytes 6291480
  35.1 4.9 %spread.1.dense_ref = bf16[7,8,256,512]{3,2,1,0:T(8,128)(2,1)S(1)} custom-call(s32[8,24]{1,0:T(8,128)S(1)} %copy-done.6, bf16[8,24,128,128]{3,2,1,0:T(8,128)(2,1)S(1)} %copy-done.2, bf16[8,8,128,128]{3,2,1,0:T(8,128)(2,1)S(1)} %copy-done.3), custom_call_target="tpu_custom_call" | custom-call | bytes 16777216 | tf_op jit(solution)/shard_map/spread/pallas_call | solution.py:317
  40.0 1.8 %couple.6 = (f32[8,128,384]{2,1,0:T(8,128)S(1)}, f32[8,128,384]{2,1,0:T(8,128)S(1)}) custom-call(bf16[7,8,256,512]{3,2,1,0:T(8,128)(2,1)S(1)} %spread.1.dense_ref, f32[1,128]{1,0:T(1,128)S(1)} %bitcast.2, bf16[528,384]{1,0:T(8,128)(2,1)S(1)} %get-tuple-element.46.refs_0_.refs_8_), custom_call_target="tpu_custom_call" | custom-call | flops 805306368 | bytes 4194304 | tf_op jit(solution)/shard_map/couple/pallas_call | solution.py:374
  41.8 3.0 %couple.7 = (f32[8,128,384]{2,1,0:T(8,128)S(1)}, f32[8,128,384]{2,1,0:T(8,128)S(1)}) custom-call(bf16[7,8,256,512]{3,2,1,0:T(8,128)(2,1)S(1)} %spread.1.dense_ref, f32[1,128]{1,0:T(1,128)S(1)} %bitcast.3, bf16[528,384]{1,0:T(8,128)(2,1)S(1)} %collective-permute-done.7.refs_0_, bf16[528,384]{1,0:T(8,128)(2,1)S(1)} %collective-permute-done.8.refs_1_, ...), custom_call_target="tpu_custom_call" | custom-call | flops 1610612736 | bytes 4194304 | tf_op jit(solution)/shard_map/couple/pallas_call | solution.py:374
  44.8 5.3 %collective-permute-done.6.refs_2_ = bf16[528,384]{1,0:T(8,128)(2,1)S(1)} collective-permute-done((bf16[528,384]{1,0:T(8,128)(2,1)S(1)}, bf16[528,384]{1,0:T(8,128)(2,1)S(1)}, u32[]{:S(2)}, u32[]{:S(2)}) %collective-permute-start.6) | collective-permute-done | bytes 405536 | tf_op jit(solution)/shard_map/ppermute | solution.py:227
  50.1 3.0 %couple.8 = (f32[8,128,384]{2,1,0:T(8,128)S(1)}, f32[8,128,384]{2,1,0:T(8,128)S(1)}) custom-call(bf16[7,8,256,512]{3,2,1,0:T(8,128)(2,1)S(1)} %spread.1.dense_ref, f32[1,128]{1,0:T(1,128)S(1)} %bitcast.4, bf16[528,384]{1,0:T(8,128)(2,1)S(1)} %collective-permute-done.4.refs_0_, bf16[528,384]{1,0:T(8,128)(2,1)S(1)} %collective-permute-done.5.refs_1_, ...), custom_call_target="tpu_custom_call" | custom-call | flops 1610612736 | bytes 4194304 | tf_op jit(solution)/shard_map/couple/pallas_call | solution.py:374
  53.2 4.3 %collective-permute-done.1.refs_1_ = bf16[528,384]{1,0:T(8,128)(2,1)S(1)} collective-permute-done((bf16[528,384]{1,0:T(8,128)(2,1)S(1)}, bf16[528,384]{1,0:T(8,128)(2,1)S(1)}, u32[]{:S(2)}, u32[]{:S(2)}) %collective-permute-start.1) | collective-permute-done | bytes 405536 | tf_op jit(solution)/shard_map/ppermute | solution.py:227
  57.4 4.8 %collective-permute-done.3.refs_3_ = bf16[528,384]{1,0:T(8,128)(2,1)S(1)} collective-permute-done((bf16[528,384]{1,0:T(8,128)(2,1)S(1)}, bf16[528,384]{1,0:T(8,128)(2,1)S(1)}, u32[]{:S(2)}, u32[]{:S(2)}) %collective-permute-start.3) | collective-permute-done | bytes 405536 | tf_op jit(solution)/shard_map/ppermute | solution.py:232
  62.3 4.4 %finish_first.1 = (f32[8,128,384]{2,1,0:T(8,128)S(1)}, f32[8,128,384]{2,1,0:T(8,128)S(1)}, f32[8,384]{1,0:T(8,128)S(1)}, bf16[512,384]{1,0:T(8,128)(2,1)S(1)}, b...) custom-call(bf16[7,8,256,512]{3,2,1,0:T(8,128)(2,1)S(1)} %spread.1.d, ...), custom_call_target="tpu_custom_call" | custom-call | flops 1610612736 | bytes 8388608 | tf_op jit(solution)/shard_map/finish_first/pallas_call | solution.py:430
  66.7 0.7 collective-permute-start.9
  67.4 2.3 %collective-permute-start.13 = (bf16[512,384]{1,0:T(8,128)(2,1)S(1)}, bf16[512,384]{1,0:T(8,128)(2,1)S(1)}, u32[]{:S(2)}, u32[]{:S(2)}) collective-permute-start(bf16[512,384]{1,0:T(8,128)(2,1)S(1)} %get-tuple-element.60), channel_id=1, source_target_pairs={{0,12},{4,8},{8,4},{12,0},{16,28},{20,24},{24,20},{28,16},{1,13},{... | collective-permute-start | bytes 1179656 | tf_op jit(solution)/shard_map/ppermute | solution.py:227
  69.7 1.1 collective-permute-start.16
  71.0 4.1 %collective-permute-start.14 = (bf16[512,384]{1,0:T(8,128)(2,1)S(1)}, bf16[512,384]{1,0:T(8,128)(2,1)S(1)}, u32[]{:S(2)}, u32[]{:S(2)}) collective-permute-start(bf16[512,384]{1,0:T(8,128)(2,1)S(1)} %get-tuple-element.61), channel_id=1, source_target_pairs={{0,20},{4,16},{24,12},{28,8},{1,21},{5,17},{25,13},{29,9},{2,22},{... | collective-permute-start | bytes 1179656 | tf_op jit(solution)/shard_map/ppermute | solution.py:227
  75.1 4.8 %collective-permute-start.15 = (bf16[512,384]{1,0:T(8,128)(2,1)S(1)}, bf16[512,384]{1,0:T(8,128)(2,1)S(1)}, u32[]{:S(2)}, u32[]{:S(2)}) collective-permute-start(bf16[512,384]{1,0:T(8,128)(2,1)S(1)} %get-tuple-element.62), channel_id=1, source_target_pairs={{0,28},{4,24},{24,4},{28,0},{1,29},{5,25},{25,5},{29,1},{2,30},{6,... | collective-permute-start | bytes 1179656 | tf_op jit(solution)/shard_map/ppermute | solution.py:227
  79.9 0.7 relay.3
  80.6 4.1 %collective-permute-start.10 = (bf16[512,384]{1,0:T(8,128)(2,1)S(1)}, bf16[512,384]{1,0:T(8,128)(2,1)S(1)}, u32[]{:S(2)}, u32[]{:S(2)}) collective-permute-start(bf16[512,384]{1,0:T(8,128)(2,1)S(1)} %get-tuple-element.57), channel_id=1, source_target_pairs={{0,24},{4,28},{24,0},{28,4},{1,25},{5,29},{25,1},{29,5},{2,26},{6,... | collective-permute-start | bytes 1179656 | tf_op jit(solution)/shard_map/ppermute | solution.py:227
  84.7 1.5 %collective-permute-done.16.refs_0_ = bf16[512,384]{1,0:T(8,128)(2,1)S(1)} collective-permute-done((bf16[512,384]{1,0:T(8,128)(2,1)S(1)}, bf16[512,384]{1,0:T(8,128)(2,1)S(1)}, u32[]{:S(2)}, u32[]{:S(2)}) %collective-permute-start.16) | collective-permute-done | bytes 393248 | tf_op jit(solution)/shard_map/ppermute | solution.py:227
  87.0 0.8 collective-permute-done.17.refs_1_
  87.7 1.3 collective-permute-start.12
  89.0 1.8 %couple.9.refs_2_ = f32[8,128,384]{2,1,0:T(8,128)S(1)} custom-call(bf16[7,8,256,512]{3,2,1,0:T(8,128)(2,1)S(1)} %spread.1.dense_ref, f32[1,128]{1,0:T(1,128)S(1)} %bitcast.6, bf16[512,384]{1,0:T(8,128)(2,1)S(1)} %get-tuple-element.65.refs_0_), custom_call_target="tpu_custom_call" | custom-call | flops 805306368 | bytes 4194304 | tf_op jit(solution)/shard_map/couple/pallas_call | solution.py:374
  90.8 2.9 %couple.10.refs_3_ = f32[8,128,384]{2,1,0:T(8,128)S(1)} custom-call(bf16[7,8,256,512]{3,2,1,0:T(8,128)(2,1)S(1)} %spread.1.dense_ref, f32[1,128]{1,0:T(1,128)S(1)} %bitcast.7, bf16[512,384]{1,0:T(8,128)(2,1)S(1)} %collective-permute-done.16.refs_0_, bf16[512,384]{1,0:T(8,128)(2,1)S(1)} %collective-permute-done.17.refs_1_, f32[8,128,384]{2,1,0:T(8,128)S(1)} %couple.9.refs_2_), custom_call_target="tpu_custom_call" | custom-call | flops 1610612736 | bytes 4194304 | tf_op jit(solution)/shard_map/couple/pallas_call | solution.py:374
  93.7 2.5 %collective-permute-done.14.refs_1_ = bf16[512,384]{1,0:T(8,128)(2,1)S(1)} collective-permute-done((bf16[512,384]{1,0:T(8,128)(2,1)S(1)}, bf16[512,384]{1,0:T(8,128)(2,1)S(1)}, u32[]{:S(2)}, u32[]{:S(2)}) %collective-permute-start.14) | collective-permute-done | bytes 393248 | tf_op jit(solution)/shard_map/ppermute | solution.py:227
  96.2 10.8 %collective-permute-done.15.refs_2_ = bf16[512,384]{1,0:T(8,128)(2,1)S(1)} collective-permute-done((bf16[512,384]{1,0:T(8,128)(2,1)S(1)}, bf16[512,384]{1,0:T(8,128)(2,1)S(1)}, u32[]{:S(2)}, u32[]{:S(2)}) %collective-permute-start.15) | collective-permute-done | bytes 393248 | tf_op jit(solution)/shard_map/ppermute | solution.py:227
  107.0 2.9 %couple.11.refs_4_ = f32[8,128,384]{2,1,0:T(8,128)S(1)} custom-call(bf16[7,8,256,512]{3,2,1,0:T(8,128)(2,1)S(1)} %spread.1.dense_ref, f32[1,128]{1,0:T(1,128)S(1)} %bitcast.8, bf16[512,384]{1,0:T(8,128)(2,1)S(1)} %collective-permute-done.13.refs_0_, bf16[512,384]{1,0:T(8,128)(2,1)S(1)} %collective-permute-done.14.refs_1_, ...), custom_call_target="tpu_custom_call" | custom-call | flops 1610612736 | bytes 4194304 | tf_op jit(solution)/shard_map/couple/pallas_call | solution.py:374
  109.9 2.2 %collective-permute-done.10.refs_1_ = bf16[512,384]{1,0:T(8,128)(2,1)S(1)} collective-permute-done((bf16[512,384]{1,0:T(8,128)(2,1)S(1)}, bf16[512,384]{1,0:T(8,128)(2,1)S(1)}, u32[]{:S(2)}, u32[]{:S(2)}) %collective-permute-start.10) | collective-permute-done | bytes 393248 | tf_op jit(solution)/shard_map/ppermute | solution.py:227
  112.2 6.1 %collective-permute-done.12.refs_3_ = bf16[512,384]{1,0:T(8,128)(2,1)S(1)} collective-permute-done((bf16[512,384]{1,0:T(8,128)(2,1)S(1)}, bf16[512,384]{1,0:T(8,128)(2,1)S(1)}, u32[]{:S(2)}, u32[]{:S(2)}) %collective-permute-start.12) | collective-permute-done | bytes 393248 | tf_op jit(solution)/shard_map/ppermute | solution.py:232
  118.3 4.7 %finish_second.1 = (f32[8,128,384]{2,1,0:T(8,128)S(1)}, f32[48,128]{1,0:T(8,128)S(1)}) custom-call(bf16[7,8,256,512]{3,2,1,0:T(8,128)(2,1)S(1)} %spread.1.dense_ref, f32[1,128]{1,0:T(1,128)S(1)} %bitcast.9, bf16[512,384]{1,0:T(8,128)(2,1)S(1)} %get-tuple-element.56.refs_0_, bf16[512,384]{1,0:T(8,128)(2,1)S(1)} %collective-permute-done.10.refs_1_, ...), custom_call_target="tpu_custom_call" | custom-call | flops 1610612736 | bytes 8388608 | tf_op jit(solution)/shard_map/finish_second/pallas_call | solution.py:523
  123.1 1.5 %collective-permute-start.19 = (f32[48,128]{1,0:T(8,128)S(1)}, f32[48,128]{1,0:T(8,128)S(1)}, u32[]{:S(2)}, u32[]{:S(2)}) collective-permute-start(f32[48,128]{1,0:T(8,128)S(1)} %get-tuple-element.69), channel_id=1, source_target_pairs={{0,2},{1,3},{2,0},{3,1},{4,6},{5,7},{6,4},{7,5},{8,10},{9,11},{10,... | collective-permute-start | bytes 73736 | tf_op jit(solution)/shard_map/ppermute | solution.py:39
  124.9 1.6 %collective-permute-done.20 = f32[48,128]{1,0:T(8,128)S(1)} collective-permute-done((f32[48,128]{1,0:T(8,128)S(1)}, f32[48,128]{1,0:T(8,128)S(1)}, u32[]{:S(2)}, u32[]{:S(2)}) %collective-permute-start.20) | collective-permute-done | bytes 24608 | tf_op jit(solution)/shard_map/ppermute | solution.py:39
  126.9 2.0 %collective-permute-start.21 = (f32[48,128]{1,0:T(8,128)S(1)}, f32[48,128]{1,0:T(8,128)S(1)}, u32[]{:S(2)}, u32[]{:S(2)}) collective-permute-start(f32[48,128]{1,0:T(8,128)S(1)} %add_add_fusion.1), channel_id=1, source_target_pairs={{0,4},{4,0},{8,12},{12,8},{16,20},{20,16},{24,28},{28,24},{1,5},{5... | collective-permute-start | bytes 73736 | tf_op jit(solution)/shard_map/ppermute | solution.py:39
  129.0 1.9 %collective-permute-done.21 = f32[48,128]{1,0:T(8,128)S(1)} collective-permute-done((f32[48,128]{1,0:T(8,128)S(1)}, f32[48,128]{1,0:T(8,128)S(1)}, u32[]{:S(2)}, u32[]{:S(2)}) %collective-permute-start.21) | collective-permute-done | bytes 24608 | tf_op jit(solution)/shard_map/ppermute | solution.py:39
  130.8 2.6 %collective-permute-start.24 = (f32[48,128]{1,0:T(8,128)S(1)}, f32[48,128]{1,0:T(8,128)S(1)}, u32[]{:S(2)}, u32[]{:S(2)}) collective-permute-start(f32[48,128]{1,0:T(8,128)S(1)} %add.24), channel_id=1, source_target_pairs={{0,24},{4,28},{8,16},{12,20},{16,8},{20,12},{24,0},{28,4},{1,25},{... | collective-permute-start | bytes 73736 | tf_op jit(solution)/shard_map/ppermute | solution.py:39
  133.5 1.8 %collective-permute-start.22 = (f32[48,128]{1,0:T(8,128)S(1)}, f32[48,128]{1,0:T(8,128)S(1)}, u32[]{:S(2)}, u32[]{:S(2)}) collective-permute-start(f32[48,128]{1,0:T(8,128)S(1)} %add.24), channel_id=1, source_target_pairs={{0,8},{4,12},{8,0},{12,4},{16,24},{20,28},{24,16},{28,20},{1,9},{5... | collective-permute-start | bytes 73736 | tf_op jit(solution)/shard_map/ppermute | solution.py:39
  135.2 1.2 collective-permute-done.24
  136.5 1.7 %collective-permute-done.23 = f32[48,128]{1,0:T(8,128)S(1)} collective-permute-done((f32[48,128]{1,0:T(8,128)S(1)}, f32[48,128]{1,0:T(8,128)S(1)}, u32[]{:S(2)}, u32[]{:S(2)}) %collective-permute-start.23) | collective-permute-done | bytes 24608 | tf_op jit(solution)/shard_map/ppermute | solution.py:39
  138.2 2.6 %final.1 = (f32[3,1024,128]{2,1,0:T(8,128)}, f32[3,1024,128]{2,1,0:T(8,128)}) custom-call(f32[3,1024,128]{2,1,0:T(8,128)S(1)} %copy-done.1, f32[8,128,384]{2,1,0:T(8,128)S(1)} %get-tuple-element.53.refs_7_.image_ref, f32[8,128,384]{2,1,0:T(8,128)S(1)} %get-tuple-element.68.later_ref, f32[48,128]{1,0:T(8,128)S(1)} %add_add_fusion.gathered_ref), custom_call_target="tpu_custom_call" | custom-call | tf_op jit(solution)/shard_map/final/pallas_call | solution.py:591
  (34 shorter events, 3.4 us)
Async XLA Ops:
  0.6 31.7 %copy-start.6 = (s32[8,24]{1,0:T(8,128)S(1)}, s32[8,24]{1,0:T(8,128)}, u32[]{:S(2)}) copy-start(s32[8,24]{1,0:T(8,128)} %slot_ref.1) | copy-start | bytes 2308
  1.4 1.4 copy-start
  2.8 0.7 copy-start.5
  3.5 28.8 %copy-start.3 = (bf16[8,8,128,128]{3,2,1,0:T(8,128)(2,1)S(1)}, bf16[8,8,128,128]{3,2,1,0:T(8,128)(2,1)}, u32[]{:S(2)}) copy-start(bf16[8,8,128,128]{3,2,1,0:T(8,128)(2,1)} %correlation_ref.1) | copy-start | bytes 6291460
  4.8 12.8 %collective-permute-start = (bf16[1040,384]{1,0:T(8,128)(2,1)S(1)}, bf16[1040,384]{1,0:T(8,128)(2,1)S(1)}, u32[]{:S(2)}, u32[]{:S(2)}) collective-permute-start(bf16[1040,384]{1,0:T(8,128)(2,1)S(1)} %get-tuple-element.36), channel_id=1, source_target_pairs={{8,16},{12,20},{16,8},{20,12},{9,17},{13,21},{17,9},{21,13},{10,18... | collective-permute-start | bytes 2396168 | tf_op jit(solution)/shard_map/ppermute | solution.py:226
  5.5 17.3 %collective-permute-start.4 = (bf16[528,384]{1,0:T(8,128)(2,1)S(1)}, bf16[528,384]{1,0:T(8,128)(2,1)S(1)}, u32[]{:S(2)}, u32[]{:S(2)}) collective-permute-start(bf16[528,384]{1,0:T(8,128)(2,1)S(1)} %get-tuple-element.41), channel_id=1, source_target_pairs={{0,12},{4,8},{8,4},{12,0},{16,28},{20,24},{24,20},{28,16},{1,13},{... | collective-permute-start | bytes 1216520 | tf_op jit(solution)/shard_map/ppermute | solution.py:227
  12.3 17.8 %collective-permute-start.7 = (bf16[528,384]{1,0:T(8,128)(2,1)S(1)}, bf16[528,384]{1,0:T(8,128)(2,1)S(1)}, u32[]{:S(2)}, u32[]{:S(2)}) collective-permute-start(bf16[528,384]{1,0:T(8,128)(2,1)S(1)} %get-tuple-element.44), channel_id=1, source_target_pairs={{0,4},{4,0},{8,12},{12,8},{16,20},{20,16},{24,28},{28,24},{1,5},{5... | collective-permute-start | bytes 1216520 | tf_op jit(solution)/shard_map/ppermute | solution.py:227
  12.8 18.0 %collective-permute-start.8 = (bf16[528,384]{1,0:T(8,128)(2,1)S(1)}, bf16[528,384]{1,0:T(8,128)(2,1)S(1)}, u32[]{:S(2)}, u32[]{:S(2)}) collective-permute-start(bf16[528,384]{1,0:T(8,128)(2,1)S(1)} %get-tuple-element.45), channel_id=1, source_target_pairs={{0,8},{4,12},{8,0},{12,4},{16,24},{20,28},{24,16},{28,20},{1,9},{5... | collective-permute-start | bytes 1216520 | tf_op jit(solution)/shard_map/ppermute | solution.py:227
  13.0 31.8 %collective-permute-start.5 = (bf16[528,384]{1,0:T(8,128)(2,1)S(1)}, bf16[528,384]{1,0:T(8,128)(2,1)S(1)}, u32[]{:S(2)}, u32[]{:S(2)}) collective-permute-start(bf16[528,384]{1,0:T(8,128)(2,1)S(1)} %get-tuple-element.42), channel_id=1, source_target_pairs={{0,20},{4,16},{24,12},{28,8},{1,21},{5,17},{25,13},{29,9},{2,22},{... | collective-permute-start | bytes 1216520 | tf_op jit(solution)/shard_map/ppermute | solution.py:227
  17.6 32.5 %collective-permute-start.6 = (bf16[528,384]{1,0:T(8,128)(2,1)S(1)}, bf16[528,384]{1,0:T(8,128)(2,1)S(1)}, u32[]{:S(2)}, u32[]{:S(2)}) collective-permute-start(bf16[528,384]{1,0:T(8,128)(2,1)S(1)} %get-tuple-element.43), channel_id=1, source_target_pairs={{0,28},{4,24},{24,4},{28,0},{1,29},{5,25},{25,5},{29,1},{2,30},{6,... | collective-permute-start | bytes 1216520 | tf_op jit(solution)/shard_map/ppermute | solution.py:227
  22.8 34.6 %collective-permute-start.1 = (bf16[528,384]{1,0:T(8,128)(2,1)S(1)}, bf16[528,384]{1,0:T(8,128)(2,1)S(1)}, u32[]{:S(2)}, u32[]{:S(2)}) collective-permute-start(bf16[528,384]{1,0:T(8,128)(2,1)S(1)} %get-tuple-element.38), channel_id=1, source_target_pairs={{0,24},{4,28},{24,0},{28,4},{1,25},{5,29},{25,1},{29,5},{2,26},{6,... | collective-permute-start | bytes 1216520 | tf_op jit(solution)/shard_map/ppermute | solution.py:227
  30.1 27.3 %collective-permute-start.2 = (bf16[528,384]{1,0:T(8,128)(2,1)S(1)}, bf16[528,384]{1,0:T(8,128)(2,1)S(1)}, u32[]{:S(2)}, u32[]{:S(2)}) collective-permute-start(bf16[528,384]{1,0:T(8,128)(2,1)S(1)} %get-tuple-element.39), channel_id=1, source_target_pairs={{8,12},{12,8},{16,20},{20,16},{9,13},{13,9},{17,21},{21,17},{10,14... | collective-permute-start | bytes 1216520 | tf_op jit(solution)/shard_map/ppermute | solution.py:231
  30.9 31.4 %collective-permute-start.3 = (bf16[528,384]{1,0:T(8,128)(2,1)S(1)}, bf16[528,384]{1,0:T(8,128)(2,1)S(1)}, u32[]{:S(2)}, u32[]{:S(2)}) collective-permute-start(bf16[528,384]{1,0:T(8,128)(2,1)S(1)} %get-tuple-element.40), channel_id=1, source_target_pairs={{8,4},{12,0},{16,28},{20,24},{9,5},{13,1},{17,29},{21,25},{10,6},{... | collective-permute-start | bytes 1216520 | tf_op jit(solution)/shard_map/ppermute | solution.py:232
  32.4 2.8 %copy-start.2 = (bf16[8,24,128,128]{3,2,1,0:T(8,128)(2,1)S(1)}, bf16[8,24,128,128]{3,2,1,0:T(8,128)(2,1)}, u32[]{:S(2)}) copy-start(bf16[8,24,128,128]{3,2,1,0:T(8,128)(2,1)} %ks_ref.1) | copy-start | bytes 18874372
  35.1 4.9 %copy-start.4 = (f32[128]{0:T(128)S(1)}, f32[128]{0:T(128)}, u32[]{:S(2)}) copy-start(f32[128]{0:T(128)} %param.9) | copy-start | bytes 1540
  50.1 12.2 %copy-start.1 = (f32[3,1024,128]{2,1,0:T(8,128)S(1)}, f32[3,1024,128]{2,1,0:T(8,128)}, u32[]{:S(2)}) copy-start(f32[3,1024,128]{2,1,0:T(8,128)} %right_ref.3) | copy-start | bytes 4718596
  66.7 8.4 %collective-permute-start.9 = (bf16[1024,384]{1,0:T(8,128)(2,1)S(1)}, bf16[1024,384]{1,0:T(8,128)(2,1)S(1)}, u32[]{:S(2)}, u32[]{:S(2)}) collective-permute-start(bf16[1024,384]{1,0:T(8,128)(2,1)S(1)} %get-tuple-element.55), channel_id=1, source_target_pairs={{8,16},{12,20},{16,8},{20,12},{9,17},{13,21},{17,9},{21,13},{10,18... | collective-permute-start | bytes 2359304 | tf_op jit(solution)/shard_map/ppermute | solution.py:226
  67.4 13.2 %collective-permute-start.13 = (bf16[512,384]{1,0:T(8,128)(2,1)S(1)}, bf16[512,384]{1,0:T(8,128)(2,1)S(1)}, u32[]{:S(2)}, u32[]{:S(2)}) collective-permute-start(bf16[512,384]{1,0:T(8,128)(2,1)S(1)} %get-tuple-element.60), channel_id=1, source_target_pairs={{0,12},{4,8},{8,4},{12,0},{16,28},{20,24},{24,20},{28,16},{1,13},{... | collective-permute-start | bytes 1179656 | tf_op jit(solution)/shard_map/ppermute | solution.py:227
  69.7 16.5 %collective-permute-start.16 = (bf16[512,384]{1,0:T(8,128)(2,1)S(1)}, bf16[512,384]{1,0:T(8,128)(2,1)S(1)}, u32[]{:S(2)}, u32[]{:S(2)}) collective-permute-start(bf16[512,384]{1,0:T(8,128)(2,1)S(1)} %get-tuple-element.63), channel_id=1, source_target_pairs={{0,4},{4,0},{8,12},{12,8},{16,20},{20,16},{24,28},{28,24},{1,5},{5... | collective-permute-start | bytes 1179656 | tf_op jit(solution)/shard_map/ppermute | solution.py:227
  70.8 16.9 %collective-permute-start.17 = (bf16[512,384]{1,0:T(8,128)(2,1)S(1)}, bf16[512,384]{1,0:T(8,128)(2,1)S(1)}, u32[]{:S(2)}, u32[]{:S(2)}) collective-permute-start(bf16[512,384]{1,0:T(8,128)(2,1)S(1)} %get-tuple-element.64), channel_id=1, source_target_pairs={{0,8},{4,12},{8,0},{12,4},{16,24},{20,28},{24,16},{28,20},{1,9},{5... | collective-permute-start | bytes 1179656 | tf_op jit(solution)/shard_map/ppermute | solution.py:227
  71.0 25.2 %collective-permute-start.14 = (bf16[512,384]{1,0:T(8,128)(2,1)S(1)}, bf16[512,384]{1,0:T(8,128)(2,1)S(1)}, u32[]{:S(2)}, u32[]{:S(2)}) collective-permute-start(bf16[512,384]{1,0:T(8,128)(2,1)S(1)} %get-tuple-element.61), channel_id=1, source_target_pairs={{0,20},{4,16},{24,12},{28,8},{1,21},{5,17},{25,13},{29,9},{2,22},{... | collective-permute-start | bytes 1179656 | tf_op jit(solution)/shard_map/ppermute | solution.py:227
  75.1 31.9 %collective-permute-start.15 = (bf16[512,384]{1,0:T(8,128)(2,1)S(1)}, bf16[512,384]{1,0:T(8,128)(2,1)S(1)}, u32[]{:S(2)}, u32[]{:S(2)}) collective-permute-start(bf16[512,384]{1,0:T(8,128)(2,1)S(1)} %get-tuple-element.62), channel_id=1, source_target_pairs={{0,28},{4,24},{24,4},{28,0},{1,29},{5,25},{25,5},{29,1},{2,30},{6,... | collective-permute-start | bytes 1179656 | tf_op jit(solution)/shard_map/ppermute | solution.py:227
  80.6 31.5 %collective-permute-start.10 = (bf16[512,384]{1,0:T(8,128)(2,1)S(1)}, bf16[512,384]{1,0:T(8,128)(2,1)S(1)}, u32[]{:S(2)}, u32[]{:S(2)}) collective-permute-start(bf16[512,384]{1,0:T(8,128)(2,1)S(1)} %get-tuple-element.57), channel_id=1, source_target_pairs={{0,24},{4,28},{24,0},{28,4},{1,25},{5,29},{25,1},{29,5},{2,26},{6,... | collective-permute-start | bytes 1179656 | tf_op jit(solution)/shard_map/ppermute | solution.py:227
  86.3 25.9 %collective-permute-start.11 = (bf16[512,384]{1,0:T(8,128)(2,1)S(1)}, bf16[512,384]{1,0:T(8,128)(2,1)S(1)}, u32[]{:S(2)}, u32[]{:S(2)}) collective-permute-start(bf16[512,384]{1,0:T(8,128)(2,1)S(1)} %get-tuple-element.58), channel_id=1, source_target_pairs={{8,12},{12,8},{16,20},{20,16},{9,13},{13,9},{17,21},{21,17},{10,14... | collective-permute-start | bytes 1179656 | tf_op jit(solution)/shard_map/ppermute | solution.py:231
  87.7 30.5 %collective-permute-start.12 = (bf16[512,384]{1,0:T(8,128)(2,1)S(1)}, bf16[512,384]{1,0:T(8,128)(2,1)S(1)}, u32[]{:S(2)}, u32[]{:S(2)}) collective-permute-start(bf16[512,384]{1,0:T(8,128)(2,1)S(1)} %get-tuple-element.59), channel_id=1, source_target_pairs={{8,4},{12,0},{16,28},{20,24},{9,5},{13,1},{17,29},{21,25},{10,6},{... | collective-permute-start | bytes 1179656 | tf_op jit(solution)/shard_map/ppermute | solution.py:232
  122.9 3.5 %collective-permute-start.20 = (f32[48,128]{1,0:T(8,128)S(1)}, f32[48,128]{1,0:T(8,128)S(1)}, u32[]{:S(2)}, u32[]{:S(2)}) collective-permute-start(f32[48,128]{1,0:T(8,128)S(1)} %get-tuple-element.69), channel_id=1, source_target_pairs={{0,3},{1,2},{2,1},{3,0},{4,7},{5,6},{6,5},{7,4},{8,11},{9,10},{10,... | collective-permute-start | bytes 73736 | tf_op jit(solution)/shard_map/ppermute | solution.py:39
  123.1 3.8 %collective-permute-start.19 = (f32[48,128]{1,0:T(8,128)S(1)}, f32[48,128]{1,0:T(8,128)S(1)}, u32[]{:S(2)}, u32[]{:S(2)}) collective-permute-start(f32[48,128]{1,0:T(8,128)S(1)} %get-tuple-element.69), channel_id=1, source_target_pairs={{0,2},{1,3},{2,0},{3,1},{4,6},{5,7},{6,4},{7,5},{8,10},{9,11},{10,... | collective-permute-start | bytes 73736 | tf_op jit(solution)/shard_map/ppermute | solution.py:39
  124.6 2.4 %collective-permute-start.18 = (f32[48,128]{1,0:T(8,128)S(1)}, f32[48,128]{1,0:T(8,128)S(1)}, u32[]{:S(2)}, u32[]{:S(2)}) collective-permute-start(f32[48,128]{1,0:T(8,128)S(1)} %get-tuple-element.69), channel_id=1, source_target_pairs={{0,1},{1,0},{2,3},{3,2},{4,5},{5,4},{6,7},{7,6},{8,9},{9,8},{10,11... | collective-permute-start | bytes 73736 | tf_op jit(solution)/shard_map/ppermute | solution.py:39
  126.9 3.9 %collective-permute-start.21 = (f32[48,128]{1,0:T(8,128)S(1)}, f32[48,128]{1,0:T(8,128)S(1)}, u32[]{:S(2)}, u32[]{:S(2)}) collective-permute-start(f32[48,128]{1,0:T(8,128)S(1)} %add_add_fusion.1), channel_id=1, source_target_pairs={{0,4},{4,0},{8,12},{12,8},{16,20},{20,16},{24,28},{28,24},{1,5},{5... | collective-permute-start | bytes 73736 | tf_op jit(solution)/shard_map/ppermute | solution.py:39
  130.8 5.6 %collective-permute-start.24 = (f32[48,128]{1,0:T(8,128)S(1)}, f32[48,128]{1,0:T(8,128)S(1)}, u32[]{:S(2)}, u32[]{:S(2)}) collective-permute-start(f32[48,128]{1,0:T(8,128)S(1)} %add.24), channel_id=1, source_target_pairs={{0,24},{4,28},{8,16},{12,20},{16,8},{20,12},{24,0},{28,4},{1,25},{... | collective-permute-start | bytes 73736 | tf_op jit(solution)/shard_map/ppermute | solution.py:39
  133.5 4.7 %collective-permute-start.23 = (f32[48,128]{1,0:T(8,128)S(1)}, f32[48,128]{1,0:T(8,128)S(1)}, u32[]{:S(2)}, u32[]{:S(2)}) collective-permute-start(f32[48,128]{1,0:T(8,128)S(1)} %add.24), channel_id=1, source_target_pairs={{0,16},{4,20},{8,24},{12,28},{16,0},{20,4},{24,8},{28,12},{1,17},{... | collective-permute-start | bytes 73736 | tf_op jit(solution)/shard_map/ppermute | solution.py:39
  133.5 4.7 %collective-permute-start.22 = (f32[48,128]{1,0:T(8,128)S(1)}, f32[48,128]{1,0:T(8,128)S(1)}, u32[]{:S(2)}, u32[]{:S(2)}) collective-permute-start(f32[48,128]{1,0:T(8,128)S(1)} %add.24), channel_id=1, source_target_pairs={{0,8},{4,12},{8,0},{12,4},{16,24},{20,28},{24,16},{28,20},{1,9},{5... | collective-permute-start | bytes 73736 | tf_op jit(solution)/shard_map/ppermute | solution.py:39

commit v6 on v5

--- a/solution.py
+++ b/solution.py
@@ -15,35 +15,6 @@
 def shifted(array, axis, by):
     count = lax.axis_size(axis)
     return lax.ppermute(array, axis, [(i, (i + by) % count) for i in range(count)])
-
-
-def rounds(axis):
-    left, radices = lax.axis_size(axis), []
-    if left % 2 == 0 and left > 4:
-        radices, left = [2], left // 2
-    while left > 1:
-        radix = 4 if left % 4 == 0 else 2
-        radices, left = radices + [radix], left // radix
-    return radices
-
-
-def summed(array):
-    for axis in ("col", "row"):
-        count = lax.axis_size(axis)
-        if count & (count - 1):
-            array = lax.psum(array, axis)
-            continue
-        hop = 1
-        for radix in rounds(axis):
-            others = [
-                lax.ppermute(array, axis, [(i, i ^ (hop * k)) for i in range(count)])
-                for k in range(1, radix)
-            ]
-            array = array + others[0]
-            if radix == 4:
-                array = array + (others[1] + others[2])
-            hop *= radix
-    return array
 
 
 def vmem():
@@ -235,9 +206,9 @@
         (sent[1], 1),
         (sent[2], 2),
         (sent[3], 3),
-        ((sent[5], sent[7]), (5, 7)),
-        ((mine, sent[6]), (6, 6)),
-        ((beside, beyond), (7, 5)),
+        ((mine, sent[7]), (6, 7)),
+        ((beside, sent[6]), (7, 6)),
+        ((sent[5], beyond), (5, 5)),
     ]
     return items, chosen
 
@@ -459,7 +430,6 @@
     fields = right_side.shape[0]
     width = height // 2
     count = len(vectors.arrays)
-    spots = -(-devices // 128) * 128
 
     def kernel(dense_ref, energies_ref, *refs):
         vector_refs, refs = refs[:count], refs[count:]
@@ -510,22 +480,23 @@
         )
         block = jnp.concatenate([block, jnp.zeros((16 - 3 - count_terms, lanes), jnp.float32)], axis=0)
         orbitals = lanes // fields
-        place = lax.axis_index("row") * lax.axis_size("col") + lax.axis_index("col")
-        here = lax.broadcasted_iota(jnp.int32, (16, spots), 1) == place
-        line = lax.broadcasted_iota(jnp.int32, (16, spots), 0)
+        line, lane = (lax.broadcasted_iota(jnp.int32, (16, 128), d) for d in (0, 1))
+        rows = []
         for f, column in enumerate(field_sums(block, fields)):
-            spread_out = jnp.broadcast_to(column, (16, spots))
             first_lane = slice(f * orbitals, f * orbitals + 1)
-            spread_out = jnp.where(line == 10, jnp.broadcast_to(alpha[:, first_lane], (16, spots)), spread_out)
-            spread_out = jnp.where(line == 11, jnp.broadcast_to(growth[:, first_lane], (16, spots)), spread_out)
-            out_ref[f * 16 : (f + 1) * 16, :] = jnp.where(here, spread_out, 0.0)
+            filled = jnp.broadcast_to(column, (16, 128))
+            filled = jnp.where(line == 10, jnp.broadcast_to(alpha[:, first_lane], (16, 128)), filled)
+            filled = jnp.where(line == 11, jnp.broadcast_to(growth[:, first_lane], (16, 128)), filled)
+            rows.append(jnp.sum(jnp.where(line == lane, filled, 0.0), axis=0, keepdims=True))
+        rows.append(jnp.zeros((8 - fields, 128), jnp.float32))
+        out_ref[...] = jnp.broadcast_to(jnp.concatenate(rows, axis=0)[None], out_ref.shape)
 
     return call(
         kernel,
         "finish_second",
         [
             jax.ShapeDtypeStruct((clusters, width, lanes), jnp.float32),
-            jax.ShapeDtypeStruct((16 * fields, spots), jnp.float32),
+            jax.ShapeDtypeStruct((devices, 8, 128), jnp.float32),
         ],
         [vmem()] * (2 + count + 6),
         [pltpu.VMEM((7, 8, lanes), jnp.float32)] + vectors.scratch,
@@ -535,27 +506,35 @@
 
 
 def step_sizes(gathered, fields, orbitals):
-    alphas, growths, gains = [], [], []
-    whole = lambda v: jnp.sum(v, axis=1, keepdims=True)
-    for f in range(fields):
-        line = [gathered[f * 16 + i : f * 16 + i + 1, :] for i in range(12)]
-        norm = whole(line[0])
-        alpha = norm / whole(line[1])
-        growth = alpha * alpha * whole(line[2]) / norm
-        off, more = alpha - line[10], growth - line[11]
-        after = whole(line[3] - 2.0 * off * line[4] + off * off * line[2])
-        bend = whole(
-            line[5]
-            + more * line[6]
-            - off * line[7]
-            + more * more * line[1]
-            - more * off * line[8]
-            + off * off * line[9]
-        )
-        alphas.append(alpha)
-        growths.append(growth)
-        gains.append(after / bend)
-    return [per_field(v, orbitals) for v in (alphas, growths, gains)]
+    rows = gathered.reshape(-1, 128)
+    flat = wide([jnp.transpose(rows[i : i + 128]) for i in range(0, rows.shape[0], 128)])
+    line = [flat[i : i + 1, :] for i in range(12)]
+    place = lax.broadcasted_iota(jnp.int32, line[0].shape, 1) & 7
+    whole = lambda v: [
+        jnp.sum(jnp.where(place == f, v, 0.0), axis=1, keepdims=True) for f in range(fields)
+    ]
+
+    def back(values):
+        row = jnp.zeros_like(line[0])
+        for f, value in enumerate(values):
+            row = jnp.where(place == f, jnp.broadcast_to(value, row.shape), row)
+        return row
+
+    norm = whole(line[0])
+    alpha = [n / b for n, b in zip(norm, whole(line[1]))]
+    growth = [a * a * s / n for a, s, n in zip(alpha, whole(line[2]), norm)]
+    off, more = back(alpha) - line[10], back(growth) - line[11]
+    after = whole(line[3] - 2.0 * off * line[4] + off * off * line[2])
+    bend = whole(
+        line[5]
+        + more * line[6]
+        - off * line[7]
+        + more * more * line[1]
+        - more * off * line[8]
+        + off * off * line[9]
+    )
+    gain = [a / b for a, b in zip(after, bend)]
+    return [per_field(v, orbitals) for v in (alpha, growth, gain)]
 
 
 def final(right_side, image, later, gathered):
@@ -626,7 +605,8 @@
     later, gathered = finish_second(
         *partial(items), right_side, level, image, weighted, lines, devices
     )
-    return tuple(final(right_side, image, later, summed(gathered)))
+    gathered = lax.all_to_all(gathered, ("row", "col"), 0, 0)
+    return tuple(final(right_side, image, later, gathered))
 
 
 def solution(mesh):

time: 141 us -> 130 us (0.922)
  waiting for transfers between devices: 49.4 us -> 17.1 us
  blocking collectives: 0 us -> 12.4 us
  starting transfers between devices: 49.9 us -> 58.2 us
    ppermute x12, waiting for transfers between devices: 31.5 us -> 13.3 us  [exchange(): sent = {k: lax.ppermute(m, 'row', plan.pairs(k)) for k, m in direct.items()}]
    ppermute x12, starting transfers between devices: 36.3 us -> 52.8 us  [exchange(): sent = {k: lax.ppermute(m, 'row', plan.pairs(k)) for k, m in direct.items()}]
    all_to_all x0 -> x1, blocking collectives: none -> 12.4 us  [body(): gathered = lax.all_to_all(gathered, ('row', 'col'), 0, 0)]
    ppermute x7 -> x0, starting transfers between devices: 8.34 us -> none  [summed(): lax.ppermute(array, axis, [(i, i ^ hop * k) for i in range(count)])]
    ppermute x2, waiting for transfers between devices: 10.9 us -> 3.82 us  [exchange(): beyond = lax.ppermute(beyond, 'row', [(i, i ^ 3) for i in INNER])]
    ppermute x7 -> x0, waiting for transfers between devices: 6.91 us -> none  [summed(): lax.ppermute(array, axis, [(i, i ^ hop * k) for i in range(count)])]
  transfers between devices with their start and end apart: 25 -> 18, of which waited for: 15 -> 8; matrix products, arithmetic and copies ran while one was open for 0% -> 0% of each run, Pallas kernels for 16% -> 17%
where the time goes in v6:
time: 130 us; the launch traced here: 129 us
  starting transfers between devices  58.2 us (45%)
  Pallas kernels  34.8 us (27%)
  waiting for transfers between devices  17.1 us (13%)
  blocking collectives  12.4 us (10%)
  local copies, waits for them, and re-layouts  5.67 us (4%)
    ppermute x12, starting transfers between devices, exchange(): sent = {k: lax.ppermute(m, 'row', plan.pairs(k)) for k, m in direct.items()}  52.8 us
    pallas_call x6, Pallas kernels, couple(): call(kernel, 'couple', [shape] * outs, [vmem()] * len(inputs), vectors.sc...  15.4 us
    ppermute x12, waiting for transfers between devices, exchange(): sent = {k: lax.ppermute(m, 'row', plan.pairs(k)) for k, m in direct.items()}  13.3 us
    all_to_all x1, blocking collectives, body(): gathered = lax.all_to_all(gathered, ('row', 'col'), 0, 0)  12.4 us
    unnamed x15, local copies, waits for them, and re-layouts  5.67 us
    pallas_call x1, Pallas kernels, spread(): call(kernel, 'spread', jax.ShapeDtypeStruct((span, clusters, 2 * width, s...  4.86 us
    pallas_call x1, Pallas kernels, finish_second(): call(kernel, 'finish_second', [jax.ShapeDtypeStruct((clusters, width, lan...  4.62 us
    pallas_call x1, Pallas kernels, finish_first(): call(kernel, 'finish_first', [vector, vector, jax.ShapeDtypeStruct((8, la...  4.39 us
  transfers between devices with their start and end apart: 18, of which 8 were waited for; matrix products, arithmetic and copies ran while one was open for 0% of the time, Pallas kernels for 17%

profile of v6, /device:TPU:0, one launch (start us, length us, event | category | flops | bytes accessed | tf_op | source)
XLA Modules:
  0.0 129.2 jit_solution(7034477387937274386)
XLA Ops:
  0.6 0.8 copy.9.readers_ref.refs_9_
  1.4 1.4 %copy-done = f32[3,1024,128]{2,1,0:T(8,128)S(1)} copy-done((f32[3,1024,128]{2,1,0:T(8,128)S(1)}, f32[3,1024,128]{2,1,0:T(8,128)}, u32[]{:S(2)}) %copy-start) | copy-done | bytes 1572888
  2.8 0.7 copy-done.5
  3.5 1.3 pack.1
  4.8 0.7 collective-permute-start
  5.5 6.8 %collective-permute-start.5 = (bf16[528,384]{1,0:T(8,128)(2,1)S(1)}, bf16[528,384]{1,0:T(8,128)(2,1)S(1)}, u32[]{:S(2)}, u32[]{:S(2)}) collective-permute-start(bf16[528,384]{1,0:T(8,128)(2,1)S(1)} %get-tuple-element.41), channel_id=1, source_target_pairs={{0,12},{4,8},{8,4},{12,0},{16,28},{20,24},{24,20},{28,16},{1,13},{... | collective-permute-start | bytes 1216520 | tf_op jit(solution)/shard_map/ppermute | solution.py:198
  12.3 0.5 collective-permute-start.7
  12.8 0.1 collective-permute-start.8
  13.0 4.1 %collective-permute-start.6 = (bf16[528,384]{1,0:T(8,128)(2,1)S(1)}, bf16[528,384]{1,0:T(8,128)(2,1)S(1)}, u32[]{:S(2)}, u32[]{:S(2)}) collective-permute-start(bf16[528,384]{1,0:T(8,128)(2,1)S(1)} %get-tuple-element.43), channel_id=1, source_target_pairs={{0,28},{4,24},{24,4},{28,0},{1,29},{5,25},{25,5},{29,1},{2,30},{6,... | collective-permute-start | bytes 1216520 | tf_op jit(solution)/shard_map/ppermute | solution.py:198
  17.1 4.4 %collective-permute-start.2 = (bf16[528,384]{1,0:T(8,128)(2,1)S(1)}, bf16[528,384]{1,0:T(8,128)(2,1)S(1)}, u32[]{:S(2)}, u32[]{:S(2)}) collective-permute-start(bf16[528,384]{1,0:T(8,128)(2,1)S(1)} %get-tuple-element.38), channel_id=1, source_target_pairs={{0,24},{4,28},{24,0},{28,4},{1,25},{5,29},{25,1},{29,5},{2,26},{6,... | collective-permute-start | bytes 1216520 | tf_op jit(solution)/shard_map/ppermute | solution.py:198
  21.5 0.8 relay.2
  22.3 0.3 collective-permute-done.5.refs_0_
  22.6 12.0 %collective-permute-start.3 = (bf16[528,384]{1,0:T(8,128)(2,1)S(1)}, bf16[528,384]{1,0:T(8,128)(2,1)S(1)}, u32[]{:S(2)}, u32[]{:S(2)}) collective-permute-start(bf16[528,384]{1,0:T(8,128)(2,1)S(1)} %get-tuple-element.39), channel_id=1, source_target_pairs={{0,20},{4,16},{24,12},{28,8},{1,21},{5,17},{25,13},{29,9},{2,22},{... | collective-permute-start | bytes 1216520 | tf_op jit(solution)/shard_map/ppermute | solution.py:198
  34.7 0.0 collective-permute-done.7.refs_0_
  34.7 0.7 collective-permute-start.1
  35.4 1.3 %collective-permute-start.4 = (bf16[528,384]{1,0:T(8,128)(2,1)S(1)}, bf16[528,384]{1,0:T(8,128)(2,1)S(1)}, u32[]{:S(2)}, u32[]{:S(2)}) collective-permute-start(bf16[528,384]{1,0:T(8,128)(2,1)S(1)} %get-tuple-element.40), channel_id=1, source_target_pairs={{8,4},{12,0},{16,28},{20,24},{9,5},{13,1},{17,29},{21,25},{10,6},{... | collective-permute-start | bytes 1216520 | tf_op jit(solution)/shard_map/ppermute | solution.py:203
  36.7 0.2 levels.1.refs_7_.refs_6_
  36.9 0.0 copy-start.2
  36.9 2.8 %copy-done.2 = bf16[8,24,128,128]{3,2,1,0:T(8,128)(2,1)S(1)} copy-done((bf16[8,24,128,128]{3,2,1,0:T(8,128)(2,1)S(1)}, bf16[8,24,128,128]{3,2,1,0:T(8,128)(2,1)}, u32[]{:S(2)}) %copy-start.2) | copy-done | bytes 6291480
  39.7 4.9 %spread.1.dense_ref = bf16[7,8,256,512]{3,2,1,0:T(8,128)(2,1)S(1)} custom-call(s32[8,24]{1,0:T(8,128)S(1)} %copy-done.6, bf16[8,24,128,128]{3,2,1,0:T(8,128)(2,1)S(1)} %copy-done.2, bf16[8,8,128,128]{3,2,1,0:T(8,128)(2,1)S(1)} %copy-done.3), custom_call_target="tpu_custom_call" | custom-call | bytes 16777216 | tf_op jit(solution)/shard_map/spread/pallas_call | solution.py:288
  44.6 1.8 %couple.6 = (f32[8,128,384]{2,1,0:T(8,128)S(1)}, f32[8,128,384]{2,1,0:T(8,128)S(1)}) custom-call(bf16[7,8,256,512]{3,2,1,0:T(8,128)(2,1)S(1)} %spread.1.dense_ref, f32[1,128]{1,0:T(1,128)S(1)} %bitcast.2, bf16[528,384]{1,0:T(8,128)(2,1)S(1)} %get-tuple-element.46.refs_0_.refs_8_), custom_call_target="tpu_custom_call" | custom-call | flops 805306368 | bytes 4194304 | tf_op jit(solution)/shard_map/couple/pallas_call | solution.py:345
  46.4 3.0 %couple.7 = (f32[8,128,384]{2,1,0:T(8,128)S(1)}, f32[8,128,384]{2,1,0:T(8,128)S(1)}) custom-call(bf16[7,8,256,512]{3,2,1,0:T(8,128)(2,1)S(1)} %spread.1.dense_ref, f32[1,128]{1,0:T(1,128)S(1)} %bitcast.3, bf16[528,384]{1,0:T(8,128)(2,1)S(1)} %collective-permute-done.7.refs_0_, bf16[528,384]{1,0:T(8,128)(2,1)S(1)} %collective-permute-done.8.refs_1_, ...), custom_call_target="tpu_custom_call" | custom-call | flops 1610612736 | bytes 4194304 | tf_op jit(solution)/shard_map/couple/pallas_call | solution.py:345
  49.4 0.0 copy-start.1
  49.4 3.0 %couple.8 = (f32[8,128,384]{2,1,0:T(8,128)S(1)}, f32[8,128,384]{2,1,0:T(8,128)S(1)}) custom-call(bf16[7,8,256,512]{3,2,1,0:T(8,128)(2,1)S(1)} %spread.1.dense_ref, f32[1,128]{1,0:T(1,128)S(1)} %bitcast.4, bf16[528,384]{1,0:T(8,128)(2,1)S(1)} %collective-permute-done.5.refs_0_, bf16[528,384]{1,0:T(8,128)(2,1)S(1)} %get-tuple-element.42.refs_1_, ...), custom_call_target="tpu_custom_call" | custom-call | flops 1610612736 | bytes 4194304 | tf_op jit(solution)/shard_map/couple/pallas_call | solution.py:345
  52.5 3.0 %collective-permute-done.3.refs_2_ = bf16[528,384]{1,0:T(8,128)(2,1)S(1)} collective-permute-done((bf16[528,384]{1,0:T(8,128)(2,1)S(1)}, bf16[528,384]{1,0:T(8,128)(2,1)S(1)}, u32[]{:S(2)}, u32[]{:S(2)}) %collective-permute-start.3) | collective-permute-done | bytes 405536 | tf_op jit(solution)/shard_map/ppermute | solution.py:198
  55.5 1.7 %collective-permute-done.4.refs_3_ = bf16[528,384]{1,0:T(8,128)(2,1)S(1)} collective-permute-done((bf16[528,384]{1,0:T(8,128)(2,1)S(1)}, bf16[528,384]{1,0:T(8,128)(2,1)S(1)}, u32[]{:S(2)}, u32[]{:S(2)}) %collective-permute-start.4) | collective-permute-done | bytes 405536 | tf_op jit(solution)/shard_map/ppermute | solution.py:203
  57.2 4.4 %finish_first.1 = (f32[8,128,384]{2,1,0:T(8,128)S(1)}, f32[8,128,384]{2,1,0:T(8,128)S(1)}, f32[8,384]{1,0:T(8,128)S(1)}, bf16[512,384]{1,0:T(8,128)(2,1)S(1)}, b...) custom-call(bf16[7,8,256,512]{3,2,1,0:T(8,128)(2,1)S(1)} %spread.1.d, ...), custom_call_target="tpu_custom_call" | custom-call | flops 1610612736 | bytes 8388608 | tf_op jit(solution)/shard_map/finish_first/pallas_call | solution.py:401
  61.6 0.7 collective-permute-start.9
  62.4 4.4 %collective-permute-start.14 = (bf16[512,384]{1,0:T(8,128)(2,1)S(1)}, bf16[512,384]{1,0:T(8,128)(2,1)S(1)}, u32[]{:S(2)}, u32[]{:S(2)}) collective-permute-start(bf16[512,384]{1,0:T(8,128)(2,1)S(1)} %get-tuple-element.60), channel_id=1, source_target_pairs={{0,12},{4,8},{8,4},{12,0},{16,28},{20,24},{24,20},{28,16},{1,13},{... | collective-permute-start | bytes 1179656 | tf_op jit(solution)/shard_map/ppermute | solution.py:198
  66.8 0.5 collective-permute-start.16
  67.3 0.1 collective-permute-start.17
  67.4 4.1 %collective-permute-start.15 = (bf16[512,384]{1,0:T(8,128)(2,1)S(1)}, bf16[512,384]{1,0:T(8,128)(2,1)S(1)}, u32[]{:S(2)}, u32[]{:S(2)}) collective-permute-start(bf16[512,384]{1,0:T(8,128)(2,1)S(1)} %get-tuple-element.62), channel_id=1, source_target_pairs={{0,28},{4,24},{24,4},{28,0},{1,29},{5,25},{25,5},{29,1},{2,30},{6,... | collective-permute-start | bytes 1179656 | tf_op jit(solution)/shard_map/ppermute | solution.py:198
  71.5 4.4 %collective-permute-start.11 = (bf16[512,384]{1,0:T(8,128)(2,1)S(1)}, bf16[512,384]{1,0:T(8,128)(2,1)S(1)}, u32[]{:S(2)}, u32[]{:S(2)}) collective-permute-start(bf16[512,384]{1,0:T(8,128)(2,1)S(1)} %get-tuple-element.57), channel_id=1, source_target_pairs={{0,24},{4,28},{24,0},{28,4},{1,25},{5,29},{25,1},{29,5},{2,26},{6,... | collective-permute-start | bytes 1179656 | tf_op jit(solution)/shard_map/ppermute | solution.py:198
  75.9 0.7 relay.3
  76.6 0.3 collective-permute-done.14.refs_0_
  76.9 11.3 %collective-permute-start.12 = (bf16[512,384]{1,0:T(8,128)(2,1)S(1)}, bf16[512,384]{1,0:T(8,128)(2,1)S(1)}, u32[]{:S(2)}, u32[]{:S(2)}) collective-permute-start(bf16[512,384]{1,0:T(8,128)(2,1)S(1)} %get-tuple-element.58), channel_id=1, source_target_pairs={{0,20},{4,16},{24,12},{28,8},{1,21},{5,17},{25,13},{29,9},{2,22},{... | collective-permute-start | bytes 1179656 | tf_op jit(solution)/shard_map/ppermute | solution.py:198
  88.2 0.7 collective-permute-start.10
  88.9 1.3 %collective-permute-start.13 = (bf16[512,384]{1,0:T(8,128)(2,1)S(1)}, bf16[512,384]{1,0:T(8,128)(2,1)S(1)}, u32[]{:S(2)}, u32[]{:S(2)}) collective-permute-start(bf16[512,384]{1,0:T(8,128)(2,1)S(1)} %get-tuple-element.59), channel_id=1, source_target_pairs={{8,4},{12,0},{16,28},{20,24},{9,5},{13,1},{17,29},{21,25},{10,6},{... | collective-permute-start | bytes 1179656 | tf_op jit(solution)/shard_map/ppermute | solution.py:203
  90.2 1.8 %couple.9.refs_2_ = f32[8,128,384]{2,1,0:T(8,128)S(1)} custom-call(bf16[7,8,256,512]{3,2,1,0:T(8,128)(2,1)S(1)} %spread.1.dense_ref, f32[1,128]{1,0:T(1,128)S(1)} %bitcast.6, bf16[512,384]{1,0:T(8,128)(2,1)S(1)} %get-tuple-element.65.refs_0_), custom_call_target="tpu_custom_call" | custom-call | flops 805306368 | bytes 4194304 | tf_op jit(solution)/shard_map/couple/pallas_call | solution.py:345
  92.0 2.9 %couple.10.refs_3_ = f32[8,128,384]{2,1,0:T(8,128)S(1)} custom-call(bf16[7,8,256,512]{3,2,1,0:T(8,128)(2,1)S(1)} %spread.1.dense_ref, f32[1,128]{1,0:T(1,128)S(1)} %bitcast.7, bf16[512,384]{1,0:T(8,128)(2,1)S(1)} %collective-permute-done.16.refs_0_, bf16[512,384]{1,0:T(8,128)(2,1)S(1)} %collective-permute-done.17.refs_1_, f32[8,128,384]{2,1,0:T(8,128)S(1)} %couple.9.refs_2_), custom_call_target="tpu_custom_call" | custom-call | flops 1610612736 | bytes 4194304 | tf_op jit(solution)/shard_map/couple/pallas_call | solution.py:345
  94.9 0.1 collective-permute-done.15.refs_2_
  95.0 2.9 %couple.11.refs_4_ = f32[8,128,384]{2,1,0:T(8,128)S(1)} custom-call(bf16[7,8,256,512]{3,2,1,0:T(8,128)(2,1)S(1)} %spread.1.dense_ref, f32[1,128]{1,0:T(1,128)S(1)} %bitcast.8, bf16[512,384]{1,0:T(8,128)(2,1)S(1)} %collective-permute-done.14.refs_0_, bf16[512,384]{1,0:T(8,128)(2,1)S(1)} %get-tuple-element.61.refs_1_, ...), custom_call_target="tpu_custom_call" | custom-call | flops 1610612736 | bytes 4194304 | tf_op jit(solution)/shard_map/couple/pallas_call | solution.py:345
  97.9 5.5 %collective-permute-done.11.refs_1_ = bf16[512,384]{1,0:T(8,128)(2,1)S(1)} collective-permute-done((bf16[512,384]{1,0:T(8,128)(2,1)S(1)}, bf16[512,384]{1,0:T(8,128)(2,1)S(1)}, u32[]{:S(2)}, u32[]{:S(2)}) %collective-permute-start.11) | collective-permute-done | bytes 393248 | tf_op jit(solution)/shard_map/ppermute | solution.py:198
  103.4 4.0 %collective-permute-done.12.refs_2_ = bf16[512,384]{1,0:T(8,128)(2,1)S(1)} collective-permute-done((bf16[512,384]{1,0:T(8,128)(2,1)S(1)}, bf16[512,384]{1,0:T(8,128)(2,1)S(1)}, u32[]{:S(2)}, u32[]{:S(2)}) %collective-permute-start.12) | collective-permute-done | bytes 393248 | tf_op jit(solution)/shard_map/ppermute | solution.py:198
  107.4 2.1 %collective-permute-done.13.refs_3_ = bf16[512,384]{1,0:T(8,128)(2,1)S(1)} collective-permute-done((bf16[512,384]{1,0:T(8,128)(2,1)S(1)}, bf16[512,384]{1,0:T(8,128)(2,1)S(1)}, u32[]{:S(2)}, u32[]{:S(2)}) %collective-permute-start.13) | collective-permute-done | bytes 393248 | tf_op jit(solution)/shard_map/ppermute | solution.py:203
  109.5 4.6 %finish_second.1 = (f32[8,128,384]{2,1,0:T(8,128)S(1)}, f32[32,8,128]{2,1,0:T(8,128)S(1)}) custom-call(bf16[7,8,256,512]{3,2,1,0:T(8,128)(2,1)S(1)} %spread.1.dense_ref, f32[1,128]{1,0:T(1,128)S(1)} %bitcast.9, bf16[512,384]{1,0:T(8,128)(2,1)S(1)} %collective-permute-done.10.refs_0_, bf16[512,384]{1,0:T(8,128)(2,1)S(1)} %collective-permute-done.11.refs_1_, ...), custom_call_target="tpu_custom_call" | custom-call | flops 1610612736 | bytes 8388608 | tf_op jit(solution)/shard_map/finish_second/pallas_call | solution.py:494
  114.1 12.4 %all_to_all.5.gathered_ref = f32[32,8,128]{2,1,0:T(8,128)S(1)} all-to-all(f32[32,8,128]{2,1,0:T(8,128)S(1)} %get-tuple-element.69), channel_id=1, replica_groups=mesh['row'=8,'col'=4] {'row','col'}, dimensions={0} | all-to-all | bytes 262144 | tf_op jit(solution)/shard_map/all_to_all | solution.py:608
  126.6 2.6 %final.1 = (f32[3,1024,128]{2,1,0:T(8,128)}, f32[3,1024,128]{2,1,0:T(8,128)}) custom-call(f32[3,1024,128]{2,1,0:T(8,128)S(1)} %copy-done.1, f32[8,128,384]{2,1,0:T(8,128)S(1)} %get-tuple-element.53.refs_7_.image_ref, f32[8,128,384]{2,1,0:T(8,128)S(1)} %get-tuple-element.68.later_ref, f32[32,8,128]{2,1,0:T(8,128)S(1)} %all_to_all.5.gathered_ref), custom_call_target="tpu_custom_call" | custom-call | tf_op jit(solution)/shard_map/final/pallas_call | solution.py:570
  (18 shorter events, 0.0 us)
Async XLA Ops:
  0.6 36.3 %copy-start.6 = (s32[8,24]{1,0:T(8,128)S(1)}, s32[8,24]{1,0:T(8,128)}, u32[]{:S(2)}) copy-start(s32[8,24]{1,0:T(8,128)} %slot_ref.1) | copy-start | bytes 2308
  1.4 1.4 %copy-start = (f32[3,1024,128]{2,1,0:T(8,128)S(1)}, f32[3,1024,128]{2,1,0:T(8,128)}, u32[]{:S(2)}) copy-start(f32[3,1024,128]{2,1,0:T(8,128)} %right_ref.3) | copy-start | bytes 4718596
  2.8 0.7 copy-start.5
  3.5 33.4 %copy-start.3 = (bf16[8,8,128,128]{3,2,1,0:T(8,128)(2,1)S(1)}, bf16[8,8,128,128]{3,2,1,0:T(8,128)(2,1)}, u32[]{:S(2)}) copy-start(bf16[8,8,128,128]{3,2,1,0:T(8,128)(2,1)} %correlation_ref.1) | copy-start | bytes 6291460
  4.8 12.3 %collective-permute-start = (bf16[1040,384]{1,0:T(8,128)(2,1)S(1)}, bf16[1040,384]{1,0:T(8,128)(2,1)S(1)}, u32[]{:S(2)}, u32[]{:S(2)}) collective-permute-start(bf16[1040,384]{1,0:T(8,128)(2,1)S(1)} %get-tuple-element.36), channel_id=1, source_target_pairs={{8,16},{12,20},{16,8},{20,12},{9,17},{13,21},{17,9},{21,13},{10,18... | collective-permute-start | bytes 2396168 | tf_op jit(solution)/shard_map/ppermute | solution.py:197
  5.5 17.1 %collective-permute-start.5 = (bf16[528,384]{1,0:T(8,128)(2,1)S(1)}, bf16[528,384]{1,0:T(8,128)(2,1)S(1)}, u32[]{:S(2)}, u32[]{:S(2)}) collective-permute-start(bf16[528,384]{1,0:T(8,128)(2,1)S(1)} %get-tuple-element.41), channel_id=1, source_target_pairs={{0,12},{4,8},{8,4},{12,0},{16,28},{20,24},{24,20},{28,16},{1,13},{... | collective-permute-start | bytes 1216520 | tf_op jit(solution)/shard_map/ppermute | solution.py:198
  12.3 22.3 %collective-permute-start.7 = (bf16[528,384]{1,0:T(8,128)(2,1)S(1)}, bf16[528,384]{1,0:T(8,128)(2,1)S(1)}, u32[]{:S(2)}, u32[]{:S(2)}) collective-permute-start(bf16[528,384]{1,0:T(8,128)(2,1)S(1)} %get-tuple-element.44), channel_id=1, source_target_pairs={{0,4},{4,0},{8,12},{12,8},{16,20},{20,16},{24,28},{28,24},{1,5},{5... | collective-permute-start | bytes 1216520 | tf_op jit(solution)/shard_map/ppermute | solution.py:198
  12.8 22.5 %collective-permute-start.8 = (bf16[528,384]{1,0:T(8,128)(2,1)S(1)}, bf16[528,384]{1,0:T(8,128)(2,1)S(1)}, u32[]{:S(2)}, u32[]{:S(2)}) collective-permute-start(bf16[528,384]{1,0:T(8,128)(2,1)S(1)} %get-tuple-element.45), channel_id=1, source_target_pairs={{0,8},{4,12},{8,0},{12,4},{16,24},{20,28},{24,16},{28,20},{1,9},{5... | collective-permute-start | bytes 1216520 | tf_op jit(solution)/shard_map/ppermute | solution.py:198
  13.0 36.4 %collective-permute-start.6 = (bf16[528,384]{1,0:T(8,128)(2,1)S(1)}, bf16[528,384]{1,0:T(8,128)(2,1)S(1)}, u32[]{:S(2)}, u32[]{:S(2)}) collective-permute-start(bf16[528,384]{1,0:T(8,128)(2,1)S(1)} %get-tuple-element.43), channel_id=1, source_target_pairs={{0,28},{4,24},{24,4},{28,0},{1,29},{5,25},{25,5},{29,1},{2,30},{6,... | collective-permute-start | bytes 1216520 | tf_op jit(solution)/shard_map/ppermute | solution.py:198
  17.1 35.4 %collective-permute-start.2 = (bf16[528,384]{1,0:T(8,128)(2,1)S(1)}, bf16[528,384]{1,0:T(8,128)(2,1)S(1)}, u32[]{:S(2)}, u32[]{:S(2)}) collective-permute-start(bf16[528,384]{1,0:T(8,128)(2,1)S(1)} %get-tuple-element.38), channel_id=1, source_target_pairs={{0,24},{4,28},{24,0},{28,4},{1,25},{5,29},{25,1},{29,5},{2,26},{6,... | collective-permute-start | bytes 1216520 | tf_op jit(solution)/shard_map/ppermute | solution.py:198
  22.6 32.9 %collective-permute-start.3 = (bf16[528,384]{1,0:T(8,128)(2,1)S(1)}, bf16[528,384]{1,0:T(8,128)(2,1)S(1)}, u32[]{:S(2)}, u32[]{:S(2)}) collective-permute-start(bf16[528,384]{1,0:T(8,128)(2,1)S(1)} %get-tuple-element.39), channel_id=1, source_target_pairs={{0,20},{4,16},{24,12},{28,8},{1,21},{5,17},{25,13},{29,9},{2,22},{... | collective-permute-start | bytes 1216520 | tf_op jit(solution)/shard_map/ppermute | solution.py:198
  34.7 20.8 %collective-permute-start.1 = (bf16[528,384]{1,0:T(8,128)(2,1)S(1)}, bf16[528,384]{1,0:T(8,128)(2,1)S(1)}, u32[]{:S(2)}, u32[]{:S(2)}) collective-permute-start(bf16[528,384]{1,0:T(8,128)(2,1)S(1)} %get-tuple-element.37), channel_id=1, source_target_pairs={{8,12},{12,8},{16,20},{20,16},{9,13},{13,9},{17,21},{21,17},{10,14... | collective-permute-start | bytes 1216520 | tf_op jit(solution)/shard_map/ppermute | solution.py:202
  35.4 21.8 %collective-permute-start.4 = (bf16[528,384]{1,0:T(8,128)(2,1)S(1)}, bf16[528,384]{1,0:T(8,128)(2,1)S(1)}, u32[]{:S(2)}, u32[]{:S(2)}) collective-permute-start(bf16[528,384]{1,0:T(8,128)(2,1)S(1)} %get-tuple-element.40), channel_id=1, source_target_pairs={{8,4},{12,0},{16,28},{20,24},{9,5},{13,1},{17,29},{21,25},{10,6},{... | collective-permute-start | bytes 1216520 | tf_op jit(solution)/shard_map/ppermute | solution.py:203
  36.9 2.8 %copy-start.2 = (bf16[8,24,128,128]{3,2,1,0:T(8,128)(2,1)S(1)}, bf16[8,24,128,128]{3,2,1,0:T(8,128)(2,1)}, u32[]{:S(2)}) copy-start(bf16[8,24,128,128]{3,2,1,0:T(8,128)(2,1)} %ks_ref.1) | copy-start | bytes 18874372
  39.7 4.9 %copy-start.4 = (f32[128]{0:T(128)S(1)}, f32[128]{0:T(128)}, u32[]{:S(2)}) copy-start(f32[128]{0:T(128)} %param.9) | copy-start | bytes 1540
  49.4 7.9 %copy-start.1 = (f32[3,1024,128]{2,1,0:T(8,128)S(1)}, f32[3,1024,128]{2,1,0:T(8,128)}, u32[]{:S(2)}) copy-start(f32[3,1024,128]{2,1,0:T(8,128)} %right_ref.3) | copy-start | bytes 4718596
  61.6 9.9 %collective-permute-start.9 = (bf16[1024,384]{1,0:T(8,128)(2,1)S(1)}, bf16[1024,384]{1,0:T(8,128)(2,1)S(1)}, u32[]{:S(2)}, u32[]{:S(2)}) collective-permute-start(bf16[1024,384]{1,0:T(8,128)(2,1)S(1)} %get-tuple-element.55), channel_id=1, source_target_pairs={{8,16},{12,20},{16,8},{20,12},{9,17},{13,21},{17,9},{21,13},{10,18... | collective-permute-start | bytes 2359304 | tf_op jit(solution)/shard_map/ppermute | solution.py:197
  62.4 14.5 %collective-permute-start.14 = (bf16[512,384]{1,0:T(8,128)(2,1)S(1)}, bf16[512,384]{1,0:T(8,128)(2,1)S(1)}, u32[]{:S(2)}, u32[]{:S(2)}) collective-permute-start(bf16[512,384]{1,0:T(8,128)(2,1)S(1)} %get-tuple-element.60), channel_id=1, source_target_pairs={{0,12},{4,8},{8,4},{12,0},{16,28},{20,24},{24,20},{28,16},{1,13},{... | collective-permute-start | bytes 1179656 | tf_op jit(solution)/shard_map/ppermute | solution.py:198
  66.8 21.4 %collective-permute-start.16 = (bf16[512,384]{1,0:T(8,128)(2,1)S(1)}, bf16[512,384]{1,0:T(8,128)(2,1)S(1)}, u32[]{:S(2)}, u32[]{:S(2)}) collective-permute-start(bf16[512,384]{1,0:T(8,128)(2,1)S(1)} %get-tuple-element.63), channel_id=1, source_target_pairs={{0,4},{4,0},{8,12},{12,8},{16,20},{20,16},{24,28},{28,24},{1,5},{5... | collective-permute-start | bytes 1179656 | tf_op jit(solution)/shard_map/ppermute | solution.py:198
  67.3 21.6 %collective-permute-start.17 = (bf16[512,384]{1,0:T(8,128)(2,1)S(1)}, bf16[512,384]{1,0:T(8,128)(2,1)S(1)}, u32[]{:S(2)}, u32[]{:S(2)}) collective-permute-start(bf16[512,384]{1,0:T(8,128)(2,1)S(1)} %get-tuple-element.64), channel_id=1, source_target_pairs={{0,8},{4,12},{8,0},{12,4},{16,24},{20,28},{24,16},{28,20},{1,9},{5... | collective-permute-start | bytes 1179656 | tf_op jit(solution)/shard_map/ppermute | solution.py:198
  67.4 27.6 %collective-permute-start.15 = (bf16[512,384]{1,0:T(8,128)(2,1)S(1)}, bf16[512,384]{1,0:T(8,128)(2,1)S(1)}, u32[]{:S(2)}, u32[]{:S(2)}) collective-permute-start(bf16[512,384]{1,0:T(8,128)(2,1)S(1)} %get-tuple-element.62), channel_id=1, source_target_pairs={{0,28},{4,24},{24,4},{28,0},{1,29},{5,25},{25,5},{29,1},{2,30},{6,... | collective-permute-start | bytes 1179656 | tf_op jit(solution)/shard_map/ppermute | solution.py:198
  71.5 31.9 %collective-permute-start.11 = (bf16[512,384]{1,0:T(8,128)(2,1)S(1)}, bf16[512,384]{1,0:T(8,128)(2,1)S(1)}, u32[]{:S(2)}, u32[]{:S(2)}) collective-permute-start(bf16[512,384]{1,0:T(8,128)(2,1)S(1)} %get-tuple-element.57), channel_id=1, source_target_pairs={{0,24},{4,28},{24,0},{28,4},{1,25},{5,29},{25,1},{29,5},{2,26},{6,... | collective-permute-start | bytes 1179656 | tf_op jit(solution)/shard_map/ppermute | solution.py:198
  76.9 30.6 %collective-permute-start.12 = (bf16[512,384]{1,0:T(8,128)(2,1)S(1)}, bf16[512,384]{1,0:T(8,128)(2,1)S(1)}, u32[]{:S(2)}, u32[]{:S(2)}) collective-permute-start(bf16[512,384]{1,0:T(8,128)(2,1)S(1)} %get-tuple-element.58), channel_id=1, source_target_pairs={{0,20},{4,16},{24,12},{28,8},{1,21},{5,17},{25,13},{29,9},{2,22},{... | collective-permute-start | bytes 1179656 | tf_op jit(solution)/shard_map/ppermute | solution.py:198
  88.2 19.2 %collective-permute-start.10 = (bf16[512,384]{1,0:T(8,128)(2,1)S(1)}, bf16[512,384]{1,0:T(8,128)(2,1)S(1)}, u32[]{:S(2)}, u32[]{:S(2)}) collective-permute-start(bf16[512,384]{1,0:T(8,128)(2,1)S(1)} %get-tuple-element.56), channel_id=1, source_target_pairs={{8,12},{12,8},{16,20},{20,16},{9,13},{13,9},{17,21},{21,17},{10,14... | collective-permute-start | bytes 1179656 | tf_op jit(solution)/shard_map/ppermute | solution.py:202
  88.9 20.6 %collective-permute-start.13 = (bf16[512,384]{1,0:T(8,128)(2,1)S(1)}, bf16[512,384]{1,0:T(8,128)(2,1)S(1)}, u32[]{:S(2)}, u32[]{:S(2)}) collective-permute-start(bf16[512,384]{1,0:T(8,128)(2,1)S(1)} %get-tuple-element.59), channel_id=1, source_target_pairs={{8,4},{12,0},{16,28},{20,24},{9,5},{13,1},{17,29},{21,25},{10,6},{... | collective-permute-start | bytes 1179656 | tf_op jit(solution)/shard_map/ppermute | solution.py:203

commit v7 on v6

--- a/solution.py
+++ b/solution.py
@@ -74,7 +74,7 @@
 
     def direct(self):
         if self.relayed:
-            return [1, 2, 3, 7, 6, 5]
+            return [1, 2, 3, 7]
         far = range(self.middle, 0, -1)
         return [by for f in far for by in (f, -f)]
 
@@ -99,16 +99,33 @@
 
 def pack(plan, readers, right_side, onsite):
     fields, rows, orbitals = right_side.shape
-    served = readers.shape[2]
+    served = readers.shape[1]
     clusters, width = onsite.shape
     lanes = fields * orbitals
     keys = plan.direct()
 
-    def kernel(readers_ref, right_ref, onsite_ref, *refs):
-        messages, rounded = refs[:-1], refs[-1]
+    def kernel(readers_hbm, right_hbm, onsite_hbm, *refs):
+        messages, rounded = refs[: len(keys) + 1], refs[len(keys) + 1]
+        readers_ref, right_ref, onsite_ref, sems, more = refs[len(keys) + 2 :]
+        copies = []
+        for cluster in range(clusters):
+            here = pl.ds(cluster * width, width)
+            copies.append(
+                pltpu.make_async_copy(
+                    right_hbm.at[:, here, :], right_ref.at[:, here, :], sems.at[cluster]
+                )
+            )
+        others = [
+            pltpu.make_async_copy(onsite_hbm, onsite_ref, more.at[0]),
+            pltpu.make_async_copy(readers_hbm, readers_ref, more.at[1]),
+        ]
+        for copy in copies[:1] + others + copies[1:]:
+            copy.start()
+        others[0].wait()
         norm = [jnp.zeros((8, orbitals), jnp.float32)] * fields
         heavy = [jnp.zeros((8, orbitals), jnp.float32)] * fields
         for cluster in range(clusters):
+            copies[cluster].wait()
             weight = jnp.broadcast_to(onsite_ref[cluster : cluster + 1, :], (8, width))
             here = slice(cluster * width, (cluster + 1) * width)
             for field in range(fields):
@@ -122,29 +139,54 @@
             / jnp.maximum(jnp.sum(jnp.sum(n, axis=0, keepdims=True), axis=1, keepdims=True), 1e-30)
             for h, n in zip(heavy, norm)
         ]
+        others[1].wait()
         rest = jnp.broadcast_to(per_field(centers, orbitals), (EXTRA, lanes))
         line, lane = (lax.broadcasted_iota(jnp.int32, (EXTRA, lanes), d) for d in (0, 1))
-        for offset in range(readers_ref.shape[1]):
+        for offset in range(readers_ref.shape[2]):
             for slot in range(served):
                 here = (line == offset + 1) & (lane == slot)
-                rest = jnp.where(here, readers_ref[0, offset, slot].astype(jnp.float32), rest)
+                rest = jnp.where(here, readers_ref[0, slot, offset].astype(jnp.float32), rest)
         rounded[clusters * width :, :] = rest.astype(jnp.bfloat16)
         fill(plan, keys, readers_ref, rounded, messages, width)
 
     message = jax.ShapeDtypeStruct((served * width + EXTRA, lanes), jnp.bfloat16)
     full = jax.ShapeDtypeStruct((clusters * width + EXTRA, lanes), jnp.bfloat16)
     *messages, own, full = call(
-        kernel, "pack", [message] * (len(keys) + 1) + [full], [smem(), vmem(), vmem()]
+        kernel,
+        "pack",
+        [message] * (len(keys) + 1) + [full],
+        [pl.BlockSpec(memory_space=pltpu.HBM)] * 3,
+        [
+            pltpu.SMEM(readers.shape, readers.dtype),
+            pltpu.VMEM(right_side.shape, jnp.float32),
+            pltpu.VMEM(onsite.shape, jnp.float32),
+            pltpu.SemaphoreType.DMA((clusters,)),
+            pltpu.SemaphoreType.DMA((2,)),
+        ],
+        limit=51,
     )(readers, right_side, onsite)
     return dict(zip(keys, messages)), own, full
+
+
+def deal(plan, readers, full, served, width):
+    keys = plan.direct()
+
+    def kernel(readers_ref, full_ref, *messages):
+        fill(plan, keys, readers_ref, full_ref, messages, width)
+
+    message = jax.ShapeDtypeStruct((served * width, full.shape[1]), jnp.bfloat16)
+    *messages, own = call(kernel, "deal", [message] * (len(keys) + 1), [smem(), vmem()])(
+        readers, full
+    )
+    return dict(zip(keys, messages)), own
 
 
 def fill(plan, keys, readers_ref, rounded, messages, width):
     me = lax.axis_index("row")
     offsets = [plan.offset(me, plan.reader(key, me)) for key in keys] + [plan.middle]
     for offset, message in zip(offsets, messages):
-        served = readers_ref.shape[2]
-        gather([readers_ref[0, offset, slot] for slot in range(served)], rounded, message, width)
+        served = readers_ref.shape[1]
+        gather([readers_ref[0, slot, offset] for slot in range(served)], rounded, message, width)
 
 
 def gather(clusters, rounded, message, width):
@@ -156,15 +198,16 @@
         message[used:, :] = rounded[rounded.shape[0] - EXTRA :, :]
 
 
-def relay(plan, full, chosen, served, width):
+def relay(plan, readers, mine, full, chosen, after, served, width):
     lanes = full.shape[1]
     extra = EXTRA if chosen is None else 0
     message = jax.ShapeDtypeStruct((served * width + extra, lanes), jnp.bfloat16)
 
     def kernel(*refs):
+        readers_ref, mine_ref, full_ref, given_ref, *messages = refs[:7]
+        me = lax.axis_index("row")
+        chosen_ref = given_ref if chosen is not None else refs[7]
         if chosen is None:
-            full_ref, *messages, chosen_ref = refs
-            me = lax.axis_index("row")
             base = full_ref.shape[0] - EXTRA
             table = full_ref[base : base + EXTRA, 0:width].astype(jnp.float32)
             line, lane = (lax.broadcasted_iota(jnp.int32, table.shape, d) for d in (0, 1))
@@ -173,42 +216,53 @@
                 for slot in range(served):
                     here = (line == offset + 1) & (lane == slot)
                     chosen_ref[index, slot] = jnp.sum(jnp.where(here, table, 0.0)).astype(jnp.int32)
-        else:
-            chosen_ref, full_ref, *messages = refs
-        for index, out in enumerate(messages):
-            gather([chosen_ref[index, slot] for slot in range(served)], full_ref, out, width)
-
-    if chosen is not None:
-        return call(kernel, "relay", [message] * 3, [smem(), vmem()])(chosen, full), chosen
-    *messages, chosen = pl.pallas_call(
-        kernel,
-        out_shape=[message] * 3 + [jax.ShapeDtypeStruct((3, served), jnp.int32)],
-        in_specs=[vmem()],
-        out_specs=[vmem()] * 3 + [smem()],
+
+        @pl.when(is_inner(me))
+        def _():
+            for index, out in enumerate(messages):
+                gather([chosen_ref[index, slot] for slot in range(served)], full_ref, out, width)
+
+        @pl.when(jnp.logical_not(is_inner(me)))
+        def _():
+            for key, out in zip((6, 5), messages[1:]):
+                offset = plan.offset(me, me ^ key)
+                clusters = [readers_ref[0, slot, offset] for slot in range(served)]
+                gather(clusters, mine_ref, out, width)
+
+    inputs = [readers, mine, full, after if chosen is None else chosen]
+    specs = [smem(), vmem(), vmem(), pl.BlockSpec(memory_space=pl.ANY) if chosen is None else smem()]
+    shapes, outs = [message] * 3, [vmem()] * 3
+    if chosen is None:
+        shapes.append(jax.ShapeDtypeStruct((3, served), jnp.int32))
+        outs.append(smem())
+    *messages, last = pl.pallas_call(
+        kernel,
+        out_shape=shapes,
+        in_specs=specs,
+        out_specs=outs,
         compiler_params=pltpu.CompilerParams(vmem_limit_bytes=12 * MIB),
         cost_estimate=pl.CostEstimate(flops=0, bytes_accessed=MIB, transcendentals=0),
         name="relay",
-    )(full)
-    return messages, chosen
-
-
-def exchange(plan, direct, own, full, chosen, served, width):
-    if plan.relayed:
-        full = lax.ppermute(full, "row", [(i, i ^ 6) for i in INNER])
+    )(*inputs)
+    return (messages, last) if chosen is None else (messages + [last], chosen)
+
+
+def exchange(plan, readers, direct, own, full, chosen, after, served, width):
     sent = {k: lax.ppermute(m, "row", plan.pairs(k)) for k, m in direct.items()}
     if not plan.relayed:
         return [(own, 0)] + [(sent[k], k) for k in plan.direct()], None
-    (mine, beside, beyond), chosen = relay(plan, full, chosen, served, width)
-    beside = lax.ppermute(beside, "row", [(i, i ^ 1) for i in INNER])
-    beyond = lax.ppermute(beyond, "row", [(i, i ^ 3) for i in INNER])
+    theirs = lax.ppermute(full, "row", [(i, i ^ 6) for i in INNER])
+    (mine, near, far), chosen = relay(plan, readers, full, theirs, chosen, after, served, width)
+    near = lax.ppermute(near, "row", [(i, i ^ (1 if i in INNER else 6)) for i in range(plan.count)])
+    far = lax.ppermute(far, "row", [(i, i ^ (3 if i in INNER else 5)) for i in range(plan.count)])
     items = [
         (own, 0),
         (sent[1], 1),
         (sent[2], 2),
         (sent[3], 3),
         ((mine, sent[7]), (6, 7)),
-        ((beside, sent[6]), (7, 6)),
-        ((sent[5], beyond), (5, 5)),
+        (near, (7, 6)),
+        (far, 5),
     ]
     return items, chosen
 
@@ -230,23 +284,24 @@
         me = lax.axis_index("row")
         opened = []
         for value, key in self.items:
+            if not self.plan.relayed:
+                opened.append((self.plan.middle - key, refs.pop(0)))
+                continue
+            inner, outer = key if isinstance(key, tuple) else (key, key)
+            held = refs.pop(0)
             if isinstance(value, tuple):
-                inner, outer, held = refs.pop(0), refs.pop(0), scratch.pop(0)
+                kept, held, other = held, scratch.pop(0), refs.pop(0)
 
                 @pl.when(is_inner(me))
                 def _():
-                    held[...] = inner[...]
+                    held[...] = kept[...]
 
                 @pl.when(jnp.logical_not(is_inner(me)))
                 def _():
-                    held[...] = outer[...]
-
-                source = jnp.where(is_inner(me), me ^ key[0], me ^ key[1])
-                opened.append((self.plan.offset(source, me), held))
-            elif self.plan.relayed:
-                opened.append((self.plan.offset(me ^ key, me), refs.pop(0)))
-            else:
-                opened.append((self.plan.middle - key, refs.pop(0)))
+                    held[...] = other[...]
+
+            source = jnp.where(is_inner(me), me ^ inner, me ^ outer)
+            opened.append((self.plan.offset(source, me), held))
         return opened
 
 
@@ -315,7 +370,7 @@
     return 2 * len(items) * dense.shape[1] * dense.shape[2] * dense.shape[3] * lanes
 
 
-def couple(dense, vectors, energies, sums):
+def couple(dense, vectors, energies, sums, after=None):
     _, clusters, height, depth = dense.shape
     lanes = vectors.lanes
     count = len(vectors.arrays)
@@ -323,7 +378,7 @@
     had = len(sums)
 
     def kernel(dense_ref, energies_ref, *refs):
-        refs = list(refs)
+        refs = list(refs[1:] if after is not None else refs)
         vector_refs, sum_refs = refs[:count], refs[count : count + had]
         out_refs, scratch = refs[count + had : count + had + outs], refs[count + had + outs :]
         energy = wide([energies_ref[...]] * (lanes // energies_ref.shape[1]))
@@ -340,47 +395,42 @@
             for ref, value in zip(out_refs, values):
                 ref[here] = value
 
-    inputs = [dense, energies, *vectors.arrays, *sums]
+    order = [] if after is None else [after]
+    inputs = [dense, energies, *order, *vectors.arrays, *sums]
     shape = jax.ShapeDtypeStruct((clusters, height // 2, lanes), jnp.float32)
     return call(
         kernel,
         "couple",
         [shape] * outs,
-        [vmem()] * len(inputs),
+        [vmem()] * 2
+        + [pl.BlockSpec(memory_space=pl.ANY)] * len(order)
+        + [vmem()] * (len(vectors.arrays) + had),
         vectors.scratch,
         flops=work(dense, vectors.items, lanes),
         moved=4 * MIB,
     )(*inputs)
 
 
-def finish_first(plan, dense, vectors, energies, sums, right_side, level, own, readers):
+def finish_first(dense, vectors, energies, value_sum, right_side, level, own):
     _, clusters, height, depth = dense.shape
     lanes = vectors.lanes
     fields = right_side.shape[0]
     width = height // 2
     count = len(vectors.arrays)
-    keys = plan.direct()
 
     def kernel(dense_ref, energies_ref, *refs):
         vector_refs, refs = refs[:count], refs[count:]
-        sum_ref, weighted_ref, right_ref, level_ref, own_ref, readers_ref = refs[:6]
-        image_ref, shifted_ref, lines_ref = refs[6:9]
-        messages, outgoing = refs[9 : 10 + len(keys)], refs[10 + len(keys)]
-        norm, bend, square, *scratch = refs[11 + len(keys) :]
+        sum_ref, right_ref, level_ref, own_ref, image_ref, outgoing, *scratch = refs
         energy = wide([energies_ref[...]] * fields)
         opened = vectors.open(vector_refs, scratch)
-        weights = centers(opened, depth)
         (center,) = centers([(0, own_ref)], depth)
-        for ref in (norm, bend, square):
-            ref[...] = jnp.zeros_like(ref)
 
         @pl.loop(0, clusters // BATCH)
         def _(batch):
             here = pl.ds(batch * BATCH, BATCH)
-            value, weighted = sum_ref[here], weighted_ref[here]
-            for weight, part in zip(weights, products(dense_ref, opened, here, energy)):
-                value, weighted = value + part, weighted + weight * part
-            shifted_ref[here] = weighted
+            value = sum_ref[here]
+            for part in products(dense_ref, opened, here, energy):
+                value = value + part
             for local in range(BATCH):
                 cluster = batch * BATCH + local
                 rows = pl.ds(pl.multiple_of(cluster * width, width), width)
@@ -388,28 +438,19 @@
                 image = wide([level_ref[cluster]] * fields) * right + value[local]
                 image_ref[cluster] = image
                 outgoing[rows, :] = (image - center * right).astype(jnp.bfloat16)
-                norm[...] += folded(right * right)
-                bend[...] += folded(right * image)
-                square[...] += folded(image * image)
-
-        fill(plan, keys, readers_ref, outgoing, messages, width)
-        lines_ref[...] = lined([norm[...], bend[...], square[...]], 8)
-
-    message = jax.ShapeDtypeStruct((depth, lanes), jnp.bfloat16)
-    full = jax.ShapeDtypeStruct((clusters * width, lanes), jnp.bfloat16)
-    vector = jax.ShapeDtypeStruct((clusters, width, lanes), jnp.float32)
-    image, weighted, lines, *messages, own, full = call(
+
+    return call(
         kernel,
         "finish_first",
-        [vector, vector, jax.ShapeDtypeStruct((8, lanes), jnp.float32)]
-        + [message] * (len(keys) + 1)
-        + [full],
-        [vmem()] * (2 + count + 5) + [smem()],
-        [pltpu.VMEM((8, lanes), jnp.float32)] * 3 + vectors.scratch,
+        [
+            jax.ShapeDtypeStruct((clusters, width, lanes), jnp.float32),
+            jax.ShapeDtypeStruct((clusters * width, lanes), jnp.bfloat16),
+        ],
+        [vmem()] * (2 + count + 4),
+        vectors.scratch,
         flops=work(dense, vectors.items, lanes),
         moved=8 * MIB,
-    )(dense, energies, *vectors.arrays, *sums, right_side, level, own, readers)
-    return image, weighted, lines, dict(zip(keys, messages)), own, full
+    )(dense, energies, *vectors.arrays, value_sum, right_side, level, own)
 
 
 def guesses(lines, fields):
@@ -424,7 +465,46 @@
     return per_field(alphas, orbitals), per_field(growths, orbitals)
 
 
-def finish_second(dense, vectors, energies, sums, right_side, level, image, weighted, lines, devices):
+def prepare(right_side, image, after):
+    fields, rows, orbitals = right_side.shape
+    clusters, width, lanes = image.shape
+
+    def kernel(right_ref, image_ref, _, lines_ref, kept):
+        kept[...] = jnp.zeros_like(kept)
+
+        def sweep(base, terms):
+            @pl.loop(0, clusters)
+            def _(cluster):
+                here = pl.ds(pl.multiple_of(cluster * width, width), width)
+                right = wide([right_ref[f, here, :] for f in range(fields)])
+                for index, term in enumerate(terms(right, image_ref[cluster])):
+                    kept[base + index] += folded(term)
+
+        sweep(0, lambda right, first: (right * right, right * first, first * first))
+        alpha, growth = guesses(lined([kept[i] for i in range(3)], 8), fields)
+
+        def later_terms(right, first):
+            step = alpha * first
+            residual = right - step
+            return residual * residual, residual * first, (growth * right - step) * first
+
+        sweep(3, later_terms)
+        lines_ref[...] = lined([kept[i] for i in range(6)], 8)
+        lines_ref[6:7, :] = alpha
+        lines_ref[7:8, :] = growth
+
+    return call(
+        kernel,
+        "prepare",
+        jax.ShapeDtypeStruct((8, lanes), jnp.float32),
+        [vmem(), vmem(), pl.BlockSpec(memory_space=pl.ANY)],
+        [pltpu.VMEM((6, 8, lanes), jnp.float32)],
+        flops=8 * MIB,
+        moved=4 * MIB,
+    )(right_side, image, after)
+
+
+def finish_second(dense, vectors, energies, value_sum, right_side, level, image, weighted, lines, devices):
     _, clusters, height, _ = dense.shape
     lanes = vectors.lanes
     fields = right_side.shape[0]
@@ -436,9 +516,8 @@
         sum_ref, right_ref, level_ref, image_ref, weighted_ref, lines_ref = refs[:6]
         later_ref, out_ref, kept, *scratch = refs[6:]
         energy = wide([energies_ref[...]] * fields)
-        alpha, growth = guesses(lines_ref[...], fields)
+        alpha, growth = lines_ref[6:7, :], lines_ref[7:8, :]
         kept[...] = jnp.zeros_like(kept)
-
         opened = vectors.open(vector_refs, scratch)
 
         @pl.loop(0, clusters // BATCH)
@@ -454,39 +533,19 @@
                 first = image_ref[cluster]
                 later = wide([level_ref[cluster]] * fields) * first + value[local]
                 later_ref[cluster] = later
-                step = alpha * first
-                residual = right - step
-                direction = growth * right - step
-                bent = growth * first - alpha * later
-                terms = (
-                    residual * residual,
-                    residual * first,
-                    direction * bent,
-                    direction * first + right * bent,
-                    direction * later + first * bent,
-                    right * later + first * first,
-                    first * later,
-                )
-                for index, term in enumerate(terms):
-                    kept[index] += folded(term)
-
-        count_terms = kept.shape[0]
-        block = jnp.concatenate(
-            [
-                lines_ref[0:3, :],
-                lined([kept[i] for i in range(count_terms)], count_terms + 1)[:count_terms],
-            ],
-            axis=0,
-        )
-        block = jnp.concatenate([block, jnp.zeros((16 - 3 - count_terms, lanes), jnp.float32)], axis=0)
+                direction = growth * right - alpha * first
+                for index, left in enumerate((direction, right, first)):
+                    kept[index] += folded(left * later)
+
+        block = jnp.concatenate([lines_ref[0:6, :], lined([kept[i] for i in range(3)], 10)], axis=0)
         orbitals = lanes // fields
         line, lane = (lax.broadcasted_iota(jnp.int32, (16, 128), d) for d in (0, 1))
         rows = []
         for f, column in enumerate(field_sums(block, fields)):
             first_lane = slice(f * orbitals, f * orbitals + 1)
             filled = jnp.broadcast_to(column, (16, 128))
-            filled = jnp.where(line == 10, jnp.broadcast_to(alpha[:, first_lane], (16, 128)), filled)
-            filled = jnp.where(line == 11, jnp.broadcast_to(growth[:, first_lane], (16, 128)), filled)
+            filled = jnp.where(line == 9, jnp.broadcast_to(alpha[:, first_lane], (16, 128)), filled)
+            filled = jnp.where(line == 10, jnp.broadcast_to(growth[:, first_lane], (16, 128)), filled)
             rows.append(jnp.sum(jnp.where(line == lane, filled, 0.0), axis=0, keepdims=True))
         rows.append(jnp.zeros((8 - fields, 128), jnp.float32))
         out_ref[...] = jnp.broadcast_to(jnp.concatenate(rows, axis=0)[None], out_ref.shape)
@@ -499,16 +558,16 @@
             jax.ShapeDtypeStruct((devices, 8, 128), jnp.float32),
         ],
         [vmem()] * (2 + count + 6),
-        [pltpu.VMEM((7, 8, lanes), jnp.float32)] + vectors.scratch,
+        [pltpu.VMEM((3, 8, lanes), jnp.float32)] + vectors.scratch,
         flops=work(dense, vectors.items, lanes),
         moved=8 * MIB,
-    )(dense, energies, *vectors.arrays, *sums, right_side, level, image, weighted, lines)
+    )(dense, energies, *vectors.arrays, value_sum, right_side, level, image, weighted, lines)
 
 
 def step_sizes(gathered, fields, orbitals):
     rows = gathered.reshape(-1, 128)
     flat = wide([jnp.transpose(rows[i : i + 128]) for i in range(0, rows.shape[0], 128)])
-    line = [flat[i : i + 1, :] for i in range(12)]
+    line = [flat[i : i + 1, :] for i in range(11)]
     place = lax.broadcasted_iota(jnp.int32, line[0].shape, 1) & 7
     whole = lambda v: [
         jnp.sum(jnp.where(place == f, v, 0.0), axis=1, keepdims=True) for f in range(fields)
@@ -523,15 +582,15 @@
     norm = whole(line[0])
     alpha = [n / b for n, b in zip(norm, whole(line[1]))]
     growth = [a * a * s / n for a, s, n in zip(alpha, whole(line[2]), norm)]
-    off, more = back(alpha) - line[10], back(growth) - line[11]
+    off, more = back(alpha) - line[9], back(growth) - line[10]
     after = whole(line[3] - 2.0 * off * line[4] + off * off * line[2])
     bend = whole(
-        line[5]
-        + more * line[6]
-        - off * line[7]
+        (line[10] * line[5] - line[9] * line[6])
+        + more * (line[5] + line[10] * line[1] - line[9] * line[7])
+        - off * (line[6] + line[10] * line[2] - line[9] * line[8])
         + more * more * line[1]
-        - more * off * line[8]
-        + off * off * line[9]
+        - more * off * (line[7] + line[2])
+        + off * off * line[8]
     )
     gain = [a / b for a, b in zip(after, bend)]
     return [per_field(v, orbitals) for v in (alpha, growth, gain)]
@@ -540,7 +599,7 @@
 def final(right_side, image, later, gathered):
     fields, rows, orbitals = right_side.shape
     clusters, width, lanes = image.shape
-    blocks = 4
+    blocks = 8
     each = clusters // blocks
 
     def kernel(right_ref, image_ref, later_ref, gathered_ref, solution_ref, residual_ref, steps):
@@ -587,23 +646,30 @@
     onsite = onsite.reshape(-1, width)
     energies = energies.reshape(1, -1)
     plan = Plan(rows, span, rows == 8 and span == 7)
+    readers = jnp.swapaxes(readers, 1, 2)
 
     def partial(items):
-        sums = []
-        for group in (items[:1], items[1:3], items[3:-2]):
-            sums = couple(dense, Vectors(plan, group), energies, sums)
-        return dense, Vectors(plan, items[-2:]), energies, sums
+        sums = [[]]
+        for group in (items[:3], items[3:-2], items[-2:-1]):
+            sums.append(couple(dense, Vectors(plan, group), energies, sums[-1]))
+        return sums[-1], sums[1][0]
 
     direct, own, full = pack(plan, readers, right_side, onsite)
-    items, chosen = exchange(plan, direct, own, full, None, served, width)
+    dense = spread(tile_slot, ks_tiles, correlation_tiles, span, served)
+    items, chosen = exchange(plan, readers, direct, own, full, None, dense, served, width)
     level = levels(onsite)
-    dense = spread(tile_slot, ks_tiles, correlation_tiles, span, served)
-    image, weighted, lines, direct, out, full = finish_first(
-        plan, *partial(items), right_side, level, own, readers
-    )
-    items, _ = exchange(plan, direct, out, full, chosen, served, width)
+    sums, _ = partial(items)
+    last = Vectors(plan, items[-1:])
+    image, full = finish_first(dense, last, energies, sums[0], right_side, level, own)
+
+    direct, out = deal(plan, readers, full, served, width)
+    items, _ = exchange(plan, readers, direct, out, full, chosen, None, served, width)
+    (value,), begun = partial(items)
+    lines = prepare(right_side, image, begun)
+    _, weighted = couple(dense, last, energies, sums, begun)
+    last = Vectors(plan, items[-1:])
     later, gathered = finish_second(
-        *partial(items), right_side, level, image, weighted, lines, devices
+        dense, last, energies, value, right_side, level, image, weighted, lines, devices
     )
     gathered = lax.all_to_all(gathered, ("row", "col"), 0, 0)
     return tuple(final(right_side, image, later, gathered))

time: 130 us -> 125 us (0.962)
  starting transfers between devices: 58.2 us -> 40.7 us
  waiting for transfers between devices: 17.1 us -> 24.8 us
  Pallas kernels: 34.8 us -> 39.7 us
    ppermute x12 -> x8, starting transfers between devices: 52.8 us -> 21 us  [exchange(): sent = {k: lax.ppermute(m, 'row', plan.pairs(k)) for k, m in direct.items()}]
    ppermute x6, starting transfers between devices: 5.38 us -> 19.7 us  [the longest x2 13.2 us: exchange(): lax.ppermute(far, 'row', [(i, i ^ (3 if i in INNER else 5)) for i in rang...]
    ppermute x6, waiting for transfers between devices: 3.83 us -> 15 us  [the longest x2 8.11 us: exchange(): lax.ppermute(near, 'row', [(i, i ^ (1 if i in INNER else 6)) for i in ran...]
    pallas_call x10 -> x13, Pallas kernels: 22.6 us -> 28.6 us  [the longest x7 20.5 us: couple(): call(kernel, 'couple', [shape] * outs, [vmem()] * 2 + [pl.BlockSpec(memor...]
    ppermute x12 -> x8, waiting for transfers between devices: 13.3 us -> 9.82 us  [exchange(): sent = {k: lax.ppermute(m, 'row', plan.pairs(k)) for k, m in direct.items()}]
    pallas_call x1, Pallas kernels: 4.62 us -> 2.31 us  [finish_second(): call(kernel, 'finish_second', [jax.ShapeDtypeStruct((clusters, width, lan...]
    unnamed x15 -> x16, local copies, waits for them, and re-layouts: 5.67 us -> 5.75 us
  transfers between devices with their start and end apart: 18 -> 14, of which waited for: 8 -> 6; matrix products, arithmetic and copies ran while one was open for 0% -> 0% of each run, Pallas kernels for 17% -> 24%
where the time goes in v7:
time: 125 us
  starting transfers between devices  40.7 us (33%)
  Pallas kernels  39.7 us (32%)
  waiting for transfers between devices  24.8 us (20%)
  blocking collectives  13 us (10%)
  local copies, waits for them, and re-layouts  5.75 us (5%)
    ppermute x8, starting transfers between devices, exchange(): sent = {k: lax.ppermute(m, 'row', plan.pairs(k)) for k, m in direct.items()}  21 us
    pallas_call x7, Pallas kernels, couple(): call(kernel, 'couple', [shape] * outs, [vmem()] * 2 + [pl.BlockSpec(memor...  20.5 us
    ppermute x2, starting transfers between devices, exchange(): lax.ppermute(far, 'row', [(i, i ^ (3 if i in INNER else 5)) for i in rang...  13.2 us
    all_to_all x1, blocking collectives, body(): gathered = lax.all_to_all(gathered, ('row', 'col'), 0, 0)  13 us
    ppermute x8, waiting for transfers between devices, exchange(): sent = {k: lax.ppermute(m, 'row', plan.pairs(k)) for k, m in direct.items()}  9.82 us
    ppermute x2, waiting for transfers between devices, exchange(): lax.ppermute(near, 'row', [(i, i ^ (1 if i in INNER else 6)) for i in ran...  8.11 us
    ppermute x2, waiting for transfers between devices, exchange(): lax.ppermute(far, 'row', [(i, i ^ (3 if i in INNER else 5)) for i in rang...  6.87 us
    unnamed x16, local copies, waits for them, and re-layouts  5.75 us
  transfers between devices with their start and end apart: 14, of which 6 were waited for; matrix products, arithmetic and copies ran while one was open for 0% of the time, Pallas kernels for 24%

profile of v7, /device:TPU:0, one launch (start us, length us, event | category | flops | bytes accessed | tf_op | source)
XLA Modules:
  0.0 124.8 jit_solution(4348261678958860865)
XLA Ops:
  0.6 0.0 copy-start.4
  0.6 0.7 copy-done.4
  1.3 0.7 copy-done.6
  2.0 2.0 %pack.1 = (bf16[528,384]{1,0:T(8,128)(2,1)S(1)}, bf16[528,384]{1,0:T(8,128)(2,1)S(1)}, bf16[528,384]{1,0:T(8,128)(2,1)S(1)}, bf16[528,384]{1,0:T(8,128)(2,1)S(1)...) custom-call(s32[1,4,7]{2,1,0:T(4,128)S(1)} %bitcast.12, f32[3,1024,128]{2,1,0:T(8,128)} %right_ref.3, ...), custom_call_target="tpu_custom_call" | custom-call | bytes 1048576 | tf_op jit(solution)/shard_map/pack/pallas_call | solution.py:154
  4.0 0.7 collective-permute-start
  4.7 3.0 %collective-permute-start.5 = (bf16[528,384]{1,0:T(8,128)(2,1)S(1)}, bf16[528,384]{1,0:T(8,128)(2,1)S(1)}, u32[]{:S(2)}, u32[]{:S(2)}) collective-permute-start(bf16[528,384]{1,0:T(8,128)(2,1)S(1)} %get-tuple-element.38), channel_id=1, source_target_pairs={{0,4},{4,0},{8,12},{12,8},{16,20},{20,16},{24,28},{28,24},{1,5},{5... | collective-permute-start | bytes 1216520 | tf_op jit(solution)/shard_map/ppermute | solution.py:251
  7.8 4.3 %collective-permute-start.6 = (bf16[528,384]{1,0:T(8,128)(2,1)S(1)}, bf16[528,384]{1,0:T(8,128)(2,1)S(1)}, u32[]{:S(2)}, u32[]{:S(2)}) collective-permute-start(bf16[528,384]{1,0:T(8,128)(2,1)S(1)} %get-tuple-element.39), channel_id=1, source_target_pairs={{0,8},{4,12},{8,0},{12,4},{16,24},{20,28},{24,16},{28,20},{1,9},{5... | collective-permute-start | bytes 1216520 | tf_op jit(solution)/shard_map/ppermute | solution.py:251
  12.1 0.0 collective-permute-start.3
  12.1 4.1 %collective-permute-start.4 = (bf16[528,384]{1,0:T(8,128)(2,1)S(1)}, bf16[528,384]{1,0:T(8,128)(2,1)S(1)}, u32[]{:S(2)}, u32[]{:S(2)}) collective-permute-start(bf16[528,384]{1,0:T(8,128)(2,1)S(1)} %get-tuple-element.36), channel_id=1, source_target_pairs={{0,28},{4,24},{24,4},{28,0},{1,29},{5,25},{25,5},{29,1},{2,30},{6,... | collective-permute-start | bytes 1216520 | tf_op jit(solution)/shard_map/ppermute | solution.py:251
  16.3 0.0 copy-start.1
  16.3 2.8 %copy-done.1 = bf16[8,24,128,128]{3,2,1,0:T(8,128)(2,1)S(1)} copy-done((bf16[8,24,128,128]{3,2,1,0:T(8,128)(2,1)S(1)}, bf16[8,24,128,128]{3,2,1,0:T(8,128)(2,1)}, u32[]{:S(2)}) %copy-start.1) | copy-done | bytes 6291480
  19.1 1.6 %copy-done.2 = bf16[8,8,128,128]{3,2,1,0:T(8,128)(2,1)S(1)} copy-done((bf16[8,8,128,128]{3,2,1,0:T(8,128)(2,1)S(1)}, bf16[8,8,128,128]{3,2,1,0:T(8,128)(2,1)}, u32[]{:S(2)}) %copy-start.2) | copy-done | bytes 2097176
  20.7 4.9 %spread.1.refs_3_.dense_ref = bf16[7,8,256,512]{3,2,1,0:T(8,128)(2,1)S(1)} custom-call(s32[8,24]{1,0:T(8,128)S(1)} %copy-done.7, bf16[8,24,128,128]{3,2,1,0:T(8,128)(2,1)S(1)} %copy-done.1, bf16[8,8,128,128]{3,2,1,0:T(8,128)(2,1)S(1)} %copy-done.2), custom_call_target="tpu_custom_call" | custom-call | bytes 16777216 | tf_op jit(solution)/shard_map/spread/pallas_call | solution.py:343
  25.5 0.0 copy-start.3
  25.6 1.4 %relay.2 = (bf16[528,384]{1,0:T(8,128)(2,1)S(1)}, bf16[528,384]{1,0:T(8,128)(2,1)S(1)}, bf16[528,384]{1,0:T(8,128)(2,1)S(1)}, s32[3,4]{1,0:T(4,128)S(1)}) custom-call(s32[1,4,7]{2,1,0:T(4,128)S(1)} %bitcast.13, bf16[1040,384]{1,0:T(8,128)(2,1)S(1)} %get-tuple-element.31.refs_1_, bf16[1040,384]{1,0:T(8,128)(2,1)S(1)} %collective-permute-done.refs_2_, ...), custom_call_target="tpu_custom_call" | custom-call | bytes 1048576 | tf_op jit(solution)/shard_map/relay/pallas_call | solution.py:238
  27.0 2.5 %collective-permute-start.2 = (bf16[528,384]{1,0:T(8,128)(2,1)S(1)}, bf16[528,384]{1,0:T(8,128)(2,1)S(1)}, u32[]{:S(2)}, u32[]{:S(2)}) collective-permute-start(bf16[528,384]{1,0:T(8,128)(2,1)S(1)} %get-tuple-element.33), channel_id=1, source_target_pairs={{0,24},{4,28},{8,12},{12,8},{16,20},{20,16},{24,0},{28,4},{1,25},{... | collective-permute-start | bytes 1216520 | tf_op jit(solution)/shard_map/ppermute | solution.py:256
  29.5 0.2 levels.1.refs_3_
  29.7 3.0 %collective-permute-start.1 = (bf16[528,384]{1,0:T(8,128)(2,1)S(1)}, bf16[528,384]{1,0:T(8,128)(2,1)S(1)}, u32[]{:S(2)}, u32[]{:S(2)}) collective-permute-start(bf16[528,384]{1,0:T(8,128)(2,1)S(1)} %get-tuple-element.32), channel_id=1, source_target_pairs={{0,20},{4,16},{8,4},{12,0},{16,28},{20,24},{24,12},{28,8},{1,21},{... | collective-permute-start | bytes 1216520 | tf_op jit(solution)/shard_map/ppermute | solution.py:257
  32.7 0.0 collective-permute-done.6.refs_2_
  32.7 4.0 %couple.7 = (f32[8,128,384]{2,1,0:T(8,128)S(1)}, f32[8,128,384]{2,1,0:T(8,128)S(1)}) custom-call(bf16[7,8,256,512]{3,2,1,0:T(8,128)(2,1)S(1)} %spread.1.refs_3_.dense_ref, f32[1,128]{1,0:T(1,128)S(1)} %bitcast.3, bf16[528,384]{1,0:T(8,128)(2,1)S(1)} %get-tuple-element.37.refs_0_.refs_4_, bf16[528,384]{1,0:T(8,128)(2,1)S(1)} %collective-permute-done.5.refs_1_, ...), custom_call_target="tpu_custom_call" | custom-call | flops 2415919104 | bytes 4194304 | tf_op jit(solution)/shard_map/couple/pallas_call | solution.py:401
  36.8 0.0 collective-permute-done.3.refs_0_
  36.8 4.4 %collective-permute-done.4.refs_2_ = bf16[528,384]{1,0:T(8,128)(2,1)S(1)} collective-permute-done((bf16[528,384]{1,0:T(8,128)(2,1)S(1)}, bf16[528,384]{1,0:T(8,128)(2,1)S(1)}, u32[]{:S(2)}, u32[]{:S(2)}) %collective-permute-start.4) | collective-permute-done | bytes 405536 | tf_op jit(solution)/shard_map/ppermute | solution.py:251
  41.2 3.0 %couple.8 = (f32[8,128,384]{2,1,0:T(8,128)S(1)}, f32[8,128,384]{2,1,0:T(8,128)S(1)}) custom-call(bf16[7,8,256,512]{3,2,1,0:T(8,128)(2,1)S(1)} %spread.1.refs_3_.dense_ref, f32[1,128]{1,0:T(1,128)S(1)} %bitcast.4, bf16[528,384]{1,0:T(8,128)(2,1)S(1)} %collective-permute-done.3.refs_0_, bf16[528,384]{1,0:T(8,128)(2,1)S(1)} %get-tuple-element.35.refs_1_, ...), custom_call_target="tpu_custom_call" | custom-call | flops 1610612736 | bytes 4194304 | tf_op jit(solution)/shard_map/couple/pallas_call | solution.py:401
  44.2 5.6 %collective-permute-done.2.refs_0_ = bf16[528,384]{1,0:T(8,128)(2,1)S(1)} collective-permute-done((bf16[528,384]{1,0:T(8,128)(2,1)S(1)}, bf16[528,384]{1,0:T(8,128)(2,1)S(1)}, u32[]{:S(2)}, u32[]{:S(2)}) %collective-permute-start.2) | collective-permute-done | bytes 405536 | tf_op jit(solution)/shard_map/ppermute | solution.py:256
  49.9 1.8 %couple.9 = (f32[8,128,384]{2,1,0:T(8,128)S(1)}, f32[8,128,384]{2,1,0:T(8,128)S(1)}) custom-call(bf16[7,8,256,512]{3,2,1,0:T(8,128)(2,1)S(1)} %spread.1.refs_3_.dense_ref, f32[1,128]{1,0:T(1,128)S(1)} %bitcast.5, bf16[528,384]{1,0:T(8,128)(2,1)S(1)} %collective-permute-done.2.refs_0_, f32[8,128,384]{2,1,0:T(8,128)S(1)} %get-tuple-element.42.refs_1_, ...), custom_call_target="tpu_custom_call" | custom-call | flops 805306368 | bytes 4194304 | tf_op jit(solution)/shard_map/couple/pallas_call | solution.py:401
  51.7 4.7 %collective-permute-done.1.refs_0_.refs_1_ = bf16[528,384]{1,0:T(8,128)(2,1)S(1)} collective-permute-done((bf16[528,384]{1,0:T(8,128)(2,1)S(1)}, bf16[528,384]{1,0:T(8,128)(2,1)S(1)}, u32[]{:S(2)}, u32[]{:S(2)}) %collective-permute-start.1) | collective-permute-done | bytes 405536 | tf_op jit(solution)/shard_map/ppermute | solution.py:257
  56.4 1.9 %finish_first.1 = (f32[8,128,384]{2,1,0:T(8,128)S(1)}, bf16[1024,384]{1,0:T(8,128)(2,1)S(1)}) custom-call(bf16[7,8,256,512]{3,2,1,0:T(8,128)(2,1)S(1)} %spread.1.refs_3_.dense_ref, f32[1,128]{1,0:T(1,128)S(1)} %bitcast.6, bf16[528,384]{1,0:T(8,128)(2,1)S(1)} %collective-permute-done.1.refs_0_.refs_1_, f32[8,128,384]{2,1,0:T(8,128)S(1)} %get-tuple-element.44.refs_1_.refs_2_, ...), custom_call_target="tpu_custom_call" | custom-call | flops 805306368 | bytes 8388608 | tf_op jit(solution)/shard_map/finish_first/pallas_call | solution.py:442
  58.3 0.7 collective-permute-start.7
  59.0 0.8 deal.1
  59.8 1.4 %collective-permute-start.12 = (bf16[512,384]{1,0:T(8,128)(2,1)S(1)}, bf16[512,384]{1,0:T(8,128)(2,1)S(1)}, u32[]{:S(2)}, u32[]{:S(2)}) collective-permute-start(bf16[512,384]{1,0:T(8,128)(2,1)S(1)} %get-tuple-element.54), channel_id=1, source_target_pairs={{0,4},{4,0},{8,12},{12,8},{16,20},{20,16},{24,28},{28,24},{1,5},{5... | collective-permute-start | bytes 1179656 | tf_op jit(solution)/shard_map/ppermute | solution.py:251
  61.2 3.9 %collective-permute-start.13 = (bf16[512,384]{1,0:T(8,128)(2,1)S(1)}, bf16[512,384]{1,0:T(8,128)(2,1)S(1)}, u32[]{:S(2)}, u32[]{:S(2)}) collective-permute-start(bf16[512,384]{1,0:T(8,128)(2,1)S(1)} %get-tuple-element.55), channel_id=1, source_target_pairs={{0,8},{4,12},{8,0},{12,4},{16,24},{20,28},{24,16},{28,20},{1,9},{5... | collective-permute-start | bytes 1179656 | tf_op jit(solution)/shard_map/ppermute | solution.py:251
  65.1 0.0 collective-permute-start.10
  65.1 4.1 %collective-permute-start.11 = (bf16[512,384]{1,0:T(8,128)(2,1)S(1)}, bf16[512,384]{1,0:T(8,128)(2,1)S(1)}, u32[]{:S(2)}, u32[]{:S(2)}) collective-permute-start(bf16[512,384]{1,0:T(8,128)(2,1)S(1)} %get-tuple-element.52), channel_id=1, source_target_pairs={{0,28},{4,24},{24,4},{28,0},{1,29},{5,25},{25,5},{29,1},{2,30},{6,... | collective-permute-start | bytes 1179656 | tf_op jit(solution)/shard_map/ppermute | solution.py:251
  69.3 0.7 relay.3
  70.0 2.5 %collective-permute-start.9 = (bf16[512,384]{1,0:T(8,128)(2,1)S(1)}, bf16[512,384]{1,0:T(8,128)(2,1)S(1)}, u32[]{:S(2)}, u32[]{:S(2)}) collective-permute-start(bf16[512,384]{1,0:T(8,128)(2,1)S(1)} %get-tuple-element.49), channel_id=1, source_target_pairs={{0,24},{4,28},{8,12},{12,8},{16,20},{20,16},{24,0},{28,4},{1,25},{... | collective-permute-start | bytes 1179656 | tf_op jit(solution)/shard_map/ppermute | solution.py:256
  72.5 0.0 collective-permute-done.12.refs_1_
  72.5 10.2 %collective-permute-start.8 = (bf16[512,384]{1,0:T(8,128)(2,1)S(1)}, bf16[512,384]{1,0:T(8,128)(2,1)S(1)}, u32[]{:S(2)}, u32[]{:S(2)}) collective-permute-start(bf16[512,384]{1,0:T(8,128)(2,1)S(1)} %get-tuple-element.48), channel_id=1, source_target_pairs={{0,20},{4,16},{8,4},{12,0},{16,28},{20,24},{24,12},{28,8},{1,21},{... | collective-permute-start | bytes 1179656 | tf_op jit(solution)/shard_map/ppermute | solution.py:257
  82.7 4.0 %couple.10.refs_3_.refs_0_._ = f32[8,128,384]{2,1,0:T(8,128)S(1)} custom-call(bf16[7,8,256,512]{3,2,1,0:T(8,128)(2,1)S(1)} %spread.1.refs_3_.dense_ref, f32[1,128]{1,0:T(1,128)S(1)} %bitcast.7, bf16[512,384]{1,0:T(8,128)(2,1)S(1)} %get-tuple-element.53.refs_0_, bf16[512,384]{1,0:T(8,128)(2,1)S(1)} %collective-permute-done.12.refs_1_, ...), custom_call_target="tpu_custom_call" | custom-call | flops 2415919104 | bytes 4194304 | tf_op jit(solution)/shard_map/couple/pallas_call | solution.py:401
  86.7 1.3 %prepare.1.refs_6_ = f32[8,384]{1,0:T(8,128)S(1)} custom-call(f32[3,1024,128]{2,1,0:T(8,128)S(1)} %copy-done, f32[8,128,384]{2,1,0:T(8,128)S(1)} %get-tuple-element.45.image_ref.refs_4_, f32[8,128,384]{2,1,0:T(8,128)S(1)} %couple.10.refs_3_.refs_0_._), custom_call_target="tpu_custom_call" | custom-call | flops 8388608 | bytes 4194304 | tf_op jit(solution)/shard_map/prepare/pallas_call | solution.py:496
  88.1 3.0 %couple.13 = (f32[8,128,384]{2,1,0:T(8,128)}, f32[8,128,384]{2,1,0:T(8,128)S(1)}) custom-call(bf16[7,8,256,512]{3,2,1,0:T(8,128)(2,1)S(1)} %spread.1.refs_3_.dense_ref, f32[1,128]{1,0:T(1,128)S(1)} %bitcast.8, f32[8,128,384]{2,1,0:T(8,128)S(1)} %couple.10.refs_3_.refs_0_._, bf16[528,384]{1,0:T(8,128)(2,1)S(1)} %collective-permute-done.1.refs_0_.refs_1_, ...), custom_call_target="tpu_custom_call" | custom-call | flops 805306368 | bytes 4194304 | tf_op jit(solution)/shard_map/couple/pallas_call | solution.py:401
  91.0 5.4 %collective-permute-done.10.refs_0_ = bf16[512,384]{1,0:T(8,128)(2,1)S(1)} collective-permute-done((bf16[512,384]{1,0:T(8,128)(2,1)S(1)}, bf16[512,384]{1,0:T(8,128)(2,1)S(1)}, u32[]{:S(2)}, u32[]{:S(2)}) %collective-permute-start.10) | collective-permute-done | bytes 393248 | tf_op jit(solution)/shard_map/ppermute | solution.py:251
  96.4 2.9 %couple.11.refs_1_ = f32[8,128,384]{2,1,0:T(8,128)S(1)} custom-call(bf16[7,8,256,512]{3,2,1,0:T(8,128)(2,1)S(1)} %spread.1.refs_3_.dense_ref, f32[1,128]{1,0:T(1,128)S(1)} %bitcast.9, bf16[512,384]{1,0:T(8,128)(2,1)S(1)} %collective-permute-done.10.refs_0_, bf16[512,384]{1,0:T(8,128)(2,1)S(1)} %get-tuple-element.51.refs_1_, ...), custom_call_target="tpu_custom_call" | custom-call | flops 1610612736 | bytes 4194304 | tf_op jit(solution)/shard_map/couple/pallas_call | solution.py:401
  99.3 2.5 %collective-permute-done.9.refs_0_ = bf16[512,384]{1,0:T(8,128)(2,1)S(1)} collective-permute-done((bf16[512,384]{1,0:T(8,128)(2,1)S(1)}, bf16[512,384]{1,0:T(8,128)(2,1)S(1)}, u32[]{:S(2)}, u32[]{:S(2)}) %collective-permute-start.9) | collective-permute-done | bytes 393248 | tf_op jit(solution)/shard_map/ppermute | solution.py:256
  101.8 1.8 %couple.12.refs_1_ = f32[8,128,384]{2,1,0:T(8,128)S(1)} custom-call(bf16[7,8,256,512]{3,2,1,0:T(8,128)(2,1)S(1)} %spread.1.refs_3_.dense_ref, f32[1,128]{1,0:T(1,128)S(1)} %bitcast.10, bf16[512,384]{1,0:T(8,128)(2,1)S(1)} %collective-permute-done.9.refs_0_, f32[8,128,384]{2,1,0:T(8,128)S(1)} %couple.11.refs_1_), custom_call_target="tpu_custom_call" | custom-call | flops 805306368 | bytes 4194304 | tf_op jit(solution)/shard_map/couple/pallas_call | solution.py:401
  103.6 2.2 %collective-permute-done.8.refs_0_ = bf16[512,384]{1,0:T(8,128)(2,1)S(1)} collective-permute-done((bf16[512,384]{1,0:T(8,128)(2,1)S(1)}, bf16[512,384]{1,0:T(8,128)(2,1)S(1)}, u32[]{:S(2)}, u32[]{:S(2)}) %collective-permute-start.8) | collective-permute-done | bytes 393248 | tf_op jit(solution)/shard_map/ppermute | solution.py:257
  105.8 2.3 %finish_second.1 = (f32[8,128,384]{2,1,0:T(8,128)S(1)}, f32[32,8,128]{2,1,0:T(8,128)S(1)}) custom-call(bf16[7,8,256,512]{3,2,1,0:T(8,128)(2,1)S(1)} %spread.1.refs_3_.dense_ref, f32[1,128]{1,0:T(1,128)S(1)} %bitcast.11, bf16[512,384]{1,0:T(8,128)(2,1)S(1)} %collective-permute-done.8.refs_0_, f32[8,128,384]{2,1,0:T(8,128)S(1)} %couple.12.refs_1_, ...), custom_call_target="tpu_custom_call" | custom-call | flops 805306368 | bytes 8388608 | tf_op jit(solution)/shard_map/finish_second/pallas_call | solution.py:553
  108.1 13.0 %all_to_all.5.gathered_ref = f32[32,8,128]{2,1,0:T(8,128)S(1)} all-to-all(f32[32,8,128]{2,1,0:T(8,128)S(1)} %get-tuple-element.59), channel_id=1, replica_groups=mesh['row'=8,'col'=4] {'row','col'}, dimensions={0} | all-to-all | bytes 262144 | tf_op jit(solution)/shard_map/all_to_all | solution.py:674
  121.1 3.7 %final.1 = (f32[3,1024,128]{2,1,0:T(8,128)}, f32[3,1024,128]{2,1,0:T(8,128)}) custom-call(f32[3,1024,128]{2,1,0:T(8,128)S(1)} %copy-done, f32[8,128,384]{2,1,0:T(8,128)S(1)} %get-tuple-element.45.image_ref.refs_4_, f32[8,128,384]{2,1,0:T(8,128)S(1)} %get-tuple-element.58.later_ref, f32[32,8,128]{2,1,0:T(8,128)S(1)} %all_to_all.5.gathered_ref), custom_call_target="tpu_custom_call" | custom-call | tf_op jit(solution)/shard_map/final/pallas_call | solution.py:629
  (14 shorter events, 0.0 us)
Async XLA Ops:
  0.6 0.7 copy-start.4
  1.3 0.7 copy-start.6
  2.0 14.3 %copy-start.7 = (s32[8,24]{1,0:T(8,128)S(1)}, s32[8,24]{1,0:T(8,128)}, u32[]{:S(2)}) copy-start(s32[8,24]{1,0:T(8,128)} %slot_ref.1) | copy-start | bytes 2308
  4.0 21.5 %collective-permute-start = (bf16[1040,384]{1,0:T(8,128)(2,1)S(1)}, bf16[1040,384]{1,0:T(8,128)(2,1)S(1)}, u32[]{:S(2)}, u32[]{:S(2)}) collective-permute-start(bf16[1040,384]{1,0:T(8,128)(2,1)S(1)} %get-tuple-element.31.refs_1_), channel_id=1, source_target_pairs={{8,16},{12,20},{16,8},{20,12},{9,17},{13,21},{17,9},{21,13},{10,18... | collective-permute-start | bytes 2396168 | tf_op jit(solution)/shard_map/ppermute | solution.py:254
  4.7 25.0 %collective-permute-start.5 = (bf16[528,384]{1,0:T(8,128)(2,1)S(1)}, bf16[528,384]{1,0:T(8,128)(2,1)S(1)}, u32[]{:S(2)}, u32[]{:S(2)}) collective-permute-start(bf16[528,384]{1,0:T(8,128)(2,1)S(1)} %get-tuple-element.38), channel_id=1, source_target_pairs={{0,4},{4,0},{8,12},{12,8},{16,20},{20,16},{24,28},{28,24},{1,5},{5... | collective-permute-start | bytes 1216520 | tf_op jit(solution)/shard_map/ppermute | solution.py:251
  7.8 25.0 %collective-permute-start.6 = (bf16[528,384]{1,0:T(8,128)(2,1)S(1)}, bf16[528,384]{1,0:T(8,128)(2,1)S(1)}, u32[]{:S(2)}, u32[]{:S(2)}) collective-permute-start(bf16[528,384]{1,0:T(8,128)(2,1)S(1)} %get-tuple-element.39), channel_id=1, source_target_pairs={{0,8},{4,12},{8,0},{12,4},{16,24},{20,28},{24,16},{28,20},{1,9},{5... | collective-permute-start | bytes 1216520 | tf_op jit(solution)/shard_map/ppermute | solution.py:251
  12.1 24.7 %collective-permute-start.3 = (bf16[528,384]{1,0:T(8,128)(2,1)S(1)}, bf16[528,384]{1,0:T(8,128)(2,1)S(1)}, u32[]{:S(2)}, u32[]{:S(2)}) collective-permute-start(bf16[528,384]{1,0:T(8,128)(2,1)S(1)} %get-tuple-element.34), channel_id=1, source_target_pairs={{0,12},{4,8},{8,4},{12,0},{16,28},{20,24},{24,20},{28,16},{1,13},{... | collective-permute-start | bytes 1216520 | tf_op jit(solution)/shard_map/ppermute | solution.py:251
  12.1 29.1 %collective-permute-start.4 = (bf16[528,384]{1,0:T(8,128)(2,1)S(1)}, bf16[528,384]{1,0:T(8,128)(2,1)S(1)}, u32[]{:S(2)}, u32[]{:S(2)}) collective-permute-start(bf16[528,384]{1,0:T(8,128)(2,1)S(1)} %get-tuple-element.36), channel_id=1, source_target_pairs={{0,28},{4,24},{24,4},{28,0},{1,29},{5,25},{25,5},{29,1},{2,30},{6,... | collective-permute-start | bytes 1216520 | tf_op jit(solution)/shard_map/ppermute | solution.py:251
  16.3 2.8 %copy-start.1 = (bf16[8,24,128,128]{3,2,1,0:T(8,128)(2,1)S(1)}, bf16[8,24,128,128]{3,2,1,0:T(8,128)(2,1)}, u32[]{:S(2)}) copy-start(bf16[8,24,128,128]{3,2,1,0:T(8,128)(2,1)} %ks_ref.1) | copy-start | bytes 18874372
  19.1 1.6 %copy-start.2 = (bf16[8,8,128,128]{3,2,1,0:T(8,128)(2,1)S(1)}, bf16[8,8,128,128]{3,2,1,0:T(8,128)(2,1)}, u32[]{:S(2)}) copy-start(bf16[8,8,128,128]{3,2,1,0:T(8,128)(2,1)} %correlation_ref.1) | copy-start | bytes 6291460
  25.5 7.2 %copy-start.3 = (f32[128]{0:T(128)S(1)}, f32[128]{0:T(128)}, u32[]{:S(2)}) copy-start(f32[128]{0:T(128)} %param.9) | copy-start | bytes 1540
  27.0 22.9 %collective-permute-start.2 = (bf16[528,384]{1,0:T(8,128)(2,1)S(1)}, bf16[528,384]{1,0:T(8,128)(2,1)S(1)}, u32[]{:S(2)}, u32[]{:S(2)}) collective-permute-start(bf16[528,384]{1,0:T(8,128)(2,1)S(1)} %get-tuple-element.33), channel_id=1, source_target_pairs={{0,24},{4,28},{8,12},{12,8},{16,20},{20,16},{24,0},{28,4},{1,25},{... | collective-permute-start | bytes 1216520 | tf_op jit(solution)/shard_map/ppermute | solution.py:256
  29.7 26.6 %collective-permute-start.1 = (bf16[528,384]{1,0:T(8,128)(2,1)S(1)}, bf16[528,384]{1,0:T(8,128)(2,1)S(1)}, u32[]{:S(2)}, u32[]{:S(2)}) collective-permute-start(bf16[528,384]{1,0:T(8,128)(2,1)S(1)} %get-tuple-element.32), channel_id=1, source_target_pairs={{0,20},{4,16},{8,4},{12,0},{16,28},{20,24},{24,12},{28,8},{1,21},{... | collective-permute-start | bytes 1216520 | tf_op jit(solution)/shard_map/ppermute | solution.py:257
  49.9 6.5 %copy-start = (f32[3,1024,128]{2,1,0:T(8,128)S(1)}, f32[3,1024,128]{2,1,0:T(8,128)}, u32[]{:S(2)}) copy-start(f32[3,1024,128]{2,1,0:T(8,128)} %right_ref.3) | copy-start | bytes 4718596
  56.4 2.6 %copy-start.5 = (s32[1,7,4]{1,2,0:T(4,128)S(1)}, s32[1,7,4]{1,2,0:T(4,128)}, u32[]{:S(2)}) copy-start(s32[1,7,4]{1,2,0:T(4,128)} %param.13) | copy-start | bytes 340
  58.3 11.0 %collective-permute-start.7 = (bf16[1024,384]{1,0:T(8,128)(2,1)S(1)}, bf16[1024,384]{1,0:T(8,128)(2,1)S(1)}, u32[]{:S(2)}, u32[]{:S(2)}) collective-permute-start(bf16[1024,384]{1,0:T(8,128)(2,1)S(1)} %get-tuple-element.46.refs_1_.full_ref), channel_id=1, source_target_pairs={{8,16},{12,20},{16,8},{20,12},{9,17},{13,21},{17,9},{21,13},{10,18... | collective-permute-start | bytes 2359304 | tf_op jit(solution)/shard_map/ppermute | solution.py:254
  59.8 12.7 %collective-permute-start.12 = (bf16[512,384]{1,0:T(8,128)(2,1)S(1)}, bf16[512,384]{1,0:T(8,128)(2,1)S(1)}, u32[]{:S(2)}, u32[]{:S(2)}) collective-permute-start(bf16[512,384]{1,0:T(8,128)(2,1)S(1)} %get-tuple-element.54), channel_id=1, source_target_pairs={{0,4},{4,0},{8,12},{12,8},{16,20},{20,16},{24,28},{28,24},{1,5},{5... | collective-permute-start | bytes 1179656 | tf_op jit(solution)/shard_map/ppermute | solution.py:251
  61.2 21.6 %collective-permute-start.13 = (bf16[512,384]{1,0:T(8,128)(2,1)S(1)}, bf16[512,384]{1,0:T(8,128)(2,1)S(1)}, u32[]{:S(2)}, u32[]{:S(2)}) collective-permute-start(bf16[512,384]{1,0:T(8,128)(2,1)S(1)} %get-tuple-element.55), channel_id=1, source_target_pairs={{0,8},{4,12},{8,0},{12,4},{16,24},{20,28},{24,16},{28,20},{1,9},{5... | collective-permute-start | bytes 1179656 | tf_op jit(solution)/shard_map/ppermute | solution.py:251
  65.1 31.3 %collective-permute-start.10 = (bf16[512,384]{1,0:T(8,128)(2,1)S(1)}, bf16[512,384]{1,0:T(8,128)(2,1)S(1)}, u32[]{:S(2)}, u32[]{:S(2)}) collective-permute-start(bf16[512,384]{1,0:T(8,128)(2,1)S(1)} %get-tuple-element.50), channel_id=1, source_target_pairs={{0,12},{4,8},{8,4},{12,0},{16,28},{20,24},{24,20},{28,16},{1,13},{... | collective-permute-start | bytes 1179656 | tf_op jit(solution)/shard_map/ppermute | solution.py:251
  65.1 31.3 %collective-permute-start.11 = (bf16[512,384]{1,0:T(8,128)(2,1)S(1)}, bf16[512,384]{1,0:T(8,128)(2,1)S(1)}, u32[]{:S(2)}, u32[]{:S(2)}) collective-permute-start(bf16[512,384]{1,0:T(8,128)(2,1)S(1)} %get-tuple-element.52), channel_id=1, source_target_pairs={{0,28},{4,24},{24,4},{28,0},{1,29},{5,25},{25,5},{29,1},{2,30},{6,... | collective-permute-start | bytes 1179656 | tf_op jit(solution)/shard_map/ppermute | solution.py:251
  70.0 31.8 %collective-permute-start.9 = (bf16[512,384]{1,0:T(8,128)(2,1)S(1)}, bf16[512,384]{1,0:T(8,128)(2,1)S(1)}, u32[]{:S(2)}, u32[]{:S(2)}) collective-permute-start(bf16[512,384]{1,0:T(8,128)(2,1)S(1)} %get-tuple-element.49), channel_id=1, source_target_pairs={{0,24},{4,28},{8,12},{12,8},{16,20},{20,16},{24,0},{28,4},{1,25},{... | collective-permute-start | bytes 1179656 | tf_op jit(solution)/shard_map/ppermute | solution.py:256
  72.5 33.3 %collective-permute-start.8 = (bf16[512,384]{1,0:T(8,128)(2,1)S(1)}, bf16[512,384]{1,0:T(8,128)(2,1)S(1)}, u32[]{:S(2)}, u32[]{:S(2)}) collective-permute-start(bf16[512,384]{1,0:T(8,128)(2,1)S(1)} %get-tuple-element.48), channel_id=1, source_target_pairs={{0,20},{4,16},{8,4},{12,0},{16,28},{20,24},{24,12},{28,8},{1,21},{... | collective-permute-start | bytes 1179656 | tf_op jit(solution)/shard_map/ppermute | solution.py:257

commit v8 on v7

--- a/solution.py
+++ b/solution.py
@@ -168,19 +168,6 @@
     return dict(zip(keys, messages)), own, full
 
 
-def deal(plan, readers, full, served, width):
-    keys = plan.direct()
-
-    def kernel(readers_ref, full_ref, *messages):
-        fill(plan, keys, readers_ref, full_ref, messages, width)
-
-    message = jax.ShapeDtypeStruct((served * width, full.shape[1]), jnp.bfloat16)
-    *messages, own = call(kernel, "deal", [message] * (len(keys) + 1), [smem(), vmem()])(
-        readers, full
-    )
-    return dict(zip(keys, messages)), own
-
-
 def fill(plan, keys, readers_ref, rounded, messages, width):
     me = lax.axis_index("row")
     offsets = [plan.offset(me, plan.reader(key, me)) for key in keys] + [plan.middle]
@@ -257,12 +244,12 @@
     far = lax.ppermute(far, "row", [(i, i ^ (3 if i in INNER else 5)) for i in range(plan.count)])
     items = [
         (own, 0),
+        ((mine, sent[7]), (6, 7)),
         (sent[1], 1),
         (sent[2], 2),
         (sent[3], 3),
-        ((mine, sent[7]), (6, 7)),
+        (far, 5),
         (near, (7, 6)),
-        (far, 5),
     ]
     return items, chosen
 
@@ -411,16 +398,19 @@
     )(*inputs)
 
 
-def finish_first(dense, vectors, energies, value_sum, right_side, level, own):
+def finish_first(plan, dense, vectors, energies, value_sum, right_side, level, own, readers):
     _, clusters, height, depth = dense.shape
     lanes = vectors.lanes
     fields = right_side.shape[0]
     width = height // 2
     count = len(vectors.arrays)
+    keys = plan.direct()
+    outs = len(keys) + 1
 
     def kernel(dense_ref, energies_ref, *refs):
         vector_refs, refs = refs[:count], refs[count:]
-        sum_ref, right_ref, level_ref, own_ref, image_ref, outgoing, *scratch = refs
+        sum_ref, right_ref, level_ref, own_ref, readers_ref, image_ref, outgoing = refs[:7]
+        messages, scratch = refs[7 : 7 + outs], refs[7 + outs :]
         energy = wide([energies_ref[...]] * fields)
         opened = vectors.open(vector_refs, scratch)
         (center,) = centers([(0, own_ref)], depth)
@@ -439,18 +429,22 @@
                 image_ref[cluster] = image
                 outgoing[rows, :] = (image - center * right).astype(jnp.bfloat16)
 
-    return call(
+        fill(plan, keys, readers_ref, outgoing, messages, width)
+
+    image, full, *messages, out = call(
         kernel,
         "finish_first",
         [
             jax.ShapeDtypeStruct((clusters, width, lanes), jnp.float32),
             jax.ShapeDtypeStruct((clusters * width, lanes), jnp.bfloat16),
-        ],
-        [vmem()] * (2 + count + 4),
+        ]
+        + [jax.ShapeDtypeStruct((depth, lanes), jnp.bfloat16)] * outs,
+        [vmem()] * (2 + count + 4) + [smem()],
         vectors.scratch,
         flops=work(dense, vectors.items, lanes),
         moved=8 * MIB,
-    )(dense, energies, *vectors.arrays, value_sum, right_side, level, own)
+    )(dense, energies, *vectors.arrays, value_sum, right_side, level, own, readers)
+    return image, full, dict(zip(keys, messages)), out
 
 
 def guesses(lines, fields):
@@ -599,7 +593,7 @@
 def final(right_side, image, later, gathered):
     fields, rows, orbitals = right_side.shape
     clusters, width, lanes = image.shape
-    blocks = 8
+    blocks = 4
     each = clusters // blocks
 
     def kernel(right_ref, image_ref, later_ref, gathered_ref, solution_ref, residual_ref, steps):
@@ -650,7 +644,7 @@
 
     def partial(items):
         sums = [[]]
-        for group in (items[:3], items[3:-2], items[-2:-1]):
+        for group in (items[:2], items[2:-2], items[-2:-1]):
             sums.append(couple(dense, Vectors(plan, group), energies, sums[-1]))
         return sums[-1], sums[1][0]
 
@@ -660,9 +654,10 @@
     level = levels(onsite)
     sums, _ = partial(items)
     last = Vectors(plan, items[-1:])
-    image, full = finish_first(dense, last, energies, sums[0], right_side, level, own)
-
-    direct, out = deal(plan, readers, full, served, width)
+    image, full, direct, out = finish_first(
+        plan, dense, last, energies, sums[0], right_side, level, own, readers
+    )
+
     items, _ = exchange(plan, readers, direct, out, full, chosen, None, served, width)
     (value,), begun = partial(items)
     lines = prepare(right_side, image, begun)

time: 125 us -> 129 us (1.032)
  starting transfers between devices: 40.7 us -> 50.3 us
  waiting for transfers between devices: 24.8 us -> 20.9 us
  blocking collectives: 13 us -> 11.7 us
    ppermute x2, starting transfers between devices: 13.2 us -> 26.7 us  [exchange(): lax.ppermute(far, 'row', [(i, i ^ (3 if i in INNER else 5)) for i in rang...]
    ppermute x8, waiting for transfers between devices: 9.82 us -> 6.7 us  [exchange(): sent = {k: lax.ppermute(m, 'row', plan.pairs(k)) for k, m in direct.items()}]
    ppermute x2, starting transfers between devices: 5.08 us -> 2.83 us  [exchange(): lax.ppermute(near, 'row', [(i, i ^ (1 if i in INNER else 6)) for i in ran...]
    ppermute x8, starting transfers between devices: 21 us -> 19.3 us  [exchange(): sent = {k: lax.ppermute(m, 'row', plan.pairs(k)) for k, m in direct.items()}]
    ppermute x2, waiting for transfers between devices: 8.11 us -> 6.68 us  [exchange(): lax.ppermute(near, 'row', [(i, i ^ (1 if i in INNER else 6)) for i in ran...]
  transfers between devices with their start and end apart: 14 -> 14, of which waited for: 6 -> 4; matrix products, arithmetic and copies ran while one was open for 0% -> 0% of each run, Pallas kernels for 24% -> 23%
where the time goes in v8:
time: 129 us; the launch traced here: 128 us
  starting transfers between devices  50.3 us (39%)
  Pallas kernels  38.7 us (30%)
  waiting for transfers between devices  20.9 us (16%)
  blocking collectives  11.7 us (9%)
  local copies, waits for them, and re-layouts  5.76 us (4%)
    ppermute x2, starting transfers between devices, exchange(): lax.ppermute(far, 'row', [(i, i ^ (3 if i in INNER else 5)) for i in rang...  26.7 us
    pallas_call x7, Pallas kernels, couple(): call(kernel, 'couple', [shape] * outs, [vmem()] * 2 + [pl.BlockSpec(memor...  20.6 us
    ppermute x8, starting transfers between devices, exchange(): sent = {k: lax.ppermute(m, 'row', plan.pairs(k)) for k, m in direct.items()}  19.3 us
    all_to_all x1, blocking collectives, body(): gathered = lax.all_to_all(gathered, ('row', 'col'), 0, 0)  11.7 us
    ppermute x2, waiting for transfers between devices, exchange(): lax.ppermute(far, 'row', [(i, i ^ (3 if i in INNER else 5)) for i in rang...  7.49 us
    ppermute x8, waiting for transfers between devices, exchange(): sent = {k: lax.ppermute(m, 'row', plan.pairs(k)) for k, m in direct.items()}  6.7 us
    ppermute x2, waiting for transfers between devices, exchange(): lax.ppermute(near, 'row', [(i, i ^ (1 if i in INNER else 6)) for i in ran...  6.68 us
    unnamed x16, local copies, waits for them, and re-layouts  5.76 us
  transfers between devices with their start and end apart: 14, of which 4 were waited for; matrix products, arithmetic and copies ran while one was open for 0% of the time, Pallas kernels for 23%

profile of v8, /device:TPU:0, one launch (start us, length us, event | category | flops | bytes accessed | tf_op | source)
XLA Modules:
  0.0 128.3 jit_solution(2659060463909208505)
XLA Ops:
  0.6 0.0 copy-start.4
  0.6 0.7 copy-done.4
  1.3 0.7 copy-done.6
  2.0 2.0 %pack.1 = (bf16[528,384]{1,0:T(8,128)(2,1)S(1)}, bf16[528,384]{1,0:T(8,128)(2,1)S(1)}, bf16[528,384]{1,0:T(8,128)(2,1)S(1)}, bf16[528,384]{1,0:T(8,128)(2,1)S(1)...) custom-call(s32[1,4,7]{2,1,0:T(4,128)S(1)} %bitcast.12, f32[3,1024,128]{2,1,0:T(8,128)} %right_ref.3, ...), custom_call_target="tpu_custom_call" | custom-call | bytes 1048576 | tf_op jit(solution)/shard_map/pack/pallas_call | solution.py:154
  4.0 0.7 collective-permute-start
  4.7 7.9 %collective-permute-start.6 = (bf16[528,384]{1,0:T(8,128)(2,1)S(1)}, bf16[528,384]{1,0:T(8,128)(2,1)S(1)}, u32[]{:S(2)}, u32[]{:S(2)}) collective-permute-start(bf16[528,384]{1,0:T(8,128)(2,1)S(1)} %get-tuple-element.39), channel_id=1, source_target_pairs={{0,28},{4,24},{24,4},{28,0},{1,29},{5,25},{25,5},{29,1},{2,30},{6,... | collective-permute-start | bytes 1216520 | tf_op jit(solution)/shard_map/ppermute | solution.py:238
  12.7 0.6 collective-permute-start.3
  13.2 0.0 collective-permute-start.4
  13.2 3.0 %collective-permute-start.5 = (bf16[528,384]{1,0:T(8,128)(2,1)S(1)}, bf16[528,384]{1,0:T(8,128)(2,1)S(1)}, u32[]{:S(2)}, u32[]{:S(2)}) collective-permute-start(bf16[528,384]{1,0:T(8,128)(2,1)S(1)} %get-tuple-element.36), channel_id=1, source_target_pairs={{0,12},{4,8},{8,4},{12,0},{16,28},{20,24},{24,20},{28,16},{1,13},{... | collective-permute-start | bytes 1216520 | tf_op jit(solution)/shard_map/ppermute | solution.py:238
  16.2 2.8 %copy-done.1 = bf16[8,24,128,128]{3,2,1,0:T(8,128)(2,1)S(1)} copy-done((bf16[8,24,128,128]{3,2,1,0:T(8,128)(2,1)S(1)}, bf16[8,24,128,128]{3,2,1,0:T(8,128)(2,1)}, u32[]{:S(2)}) %copy-start.1) | copy-done | bytes 6291480
  19.0 1.6 %copy-done.2 = bf16[8,8,128,128]{3,2,1,0:T(8,128)(2,1)S(1)} copy-done((bf16[8,8,128,128]{3,2,1,0:T(8,128)(2,1)S(1)}, bf16[8,8,128,128]{3,2,1,0:T(8,128)(2,1)}, u32[]{:S(2)}) %copy-start.2) | copy-done | bytes 2097176
  20.6 4.9 %spread.1.refs_3_.dense_ref = bf16[7,8,256,512]{3,2,1,0:T(8,128)(2,1)S(1)} custom-call(s32[8,24]{1,0:T(8,128)S(1)} %copy-done.7, bf16[8,24,128,128]{3,2,1,0:T(8,128)(2,1)S(1)} %copy-done.1, bf16[8,8,128,128]{3,2,1,0:T(8,128)(2,1)S(1)} %copy-done.2), custom_call_target="tpu_custom_call" | custom-call | bytes 16777216 | tf_op jit(solution)/shard_map/spread/pallas_call | solution.py:330
  25.5 0.0 copy-start.3
  25.5 0.0 collective-permute-done.refs_2_
  25.5 1.4 %relay.2 = (bf16[528,384]{1,0:T(8,128)(2,1)S(1)}, bf16[528,384]{1,0:T(8,128)(2,1)S(1)}, bf16[528,384]{1,0:T(8,128)(2,1)S(1)}, s32[3,4]{1,0:T(4,128)S(1)}) custom-call(s32[1,4,7]{2,1,0:T(4,128)S(1)} %bitcast.13, bf16[1040,384]{1,0:T(8,128)(2,1)S(1)} %get-tuple-element.31.refs_1_, bf16[1040,384]{1,0:T(8,128)(2,1)S(1)} %collective-permute-done.refs_2_, ...), custom_call_target="tpu_custom_call" | custom-call | bytes 1048576 | tf_op jit(solution)/shard_map/relay/pallas_call | solution.py:225
  26.9 13.7 %collective-permute-start.2 = (bf16[528,384]{1,0:T(8,128)(2,1)S(1)}, bf16[528,384]{1,0:T(8,128)(2,1)S(1)}, u32[]{:S(2)}, u32[]{:S(2)}) collective-permute-start(bf16[528,384]{1,0:T(8,128)(2,1)S(1)} %get-tuple-element.33), channel_id=1, source_target_pairs={{0,20},{4,16},{8,4},{12,0},{16,28},{20,24},{24,12},{28,8},{1,21},{... | collective-permute-start | bytes 1216520 | tf_op jit(solution)/shard_map/ppermute | solution.py:244
  40.7 0.2 levels.1.refs_3_
  40.8 0.0 collective-permute-done.6.refs_2_
  40.9 1.4 %collective-permute-start.1 = (bf16[528,384]{1,0:T(8,128)(2,1)S(1)}, bf16[528,384]{1,0:T(8,128)(2,1)S(1)}, u32[]{:S(2)}, u32[]{:S(2)}) collective-permute-start(bf16[528,384]{1,0:T(8,128)(2,1)S(1)} %get-tuple-element.32), channel_id=1, source_target_pairs={{0,24},{4,28},{8,12},{12,8},{16,20},{20,16},{24,0},{28,4},{1,25},{... | collective-permute-start | bytes 1216520 | tf_op jit(solution)/shard_map/ppermute | solution.py:243
  42.3 2.9 %couple.7 = (f32[8,128,384]{2,1,0:T(8,128)S(1)}, f32[8,128,384]{2,1,0:T(8,128)S(1)}) custom-call(bf16[7,8,256,512]{3,2,1,0:T(8,128)(2,1)S(1)} %spread.1.refs_3_.dense_ref, f32[1,128]{1,0:T(1,128)S(1)} %bitcast.3, bf16[528,384]{1,0:T(8,128)(2,1)S(1)} %get-tuple-element.37.refs_0_.refs_4_, bf16[528,384]{1,0:T(8,128)(2,1)S(1)} %get-tuple-element.38.refs_1_, ...), custom_call_target="tpu_custom_call" | custom-call | flops 1610612736 | bytes 4194304 | tf_op jit(solution)/shard_map/couple/pallas_call | solution.py:388
  45.2 0.0 collective-permute-done.3.refs_0_
  45.2 0.0 collective-permute-done.4.refs_1_
  45.2 0.0 collective-permute-done.5.refs_2_
  45.2 4.3 %couple.8 = (f32[8,128,384]{2,1,0:T(8,128)S(1)}, f32[8,128,384]{2,1,0:T(8,128)S(1)}) custom-call(bf16[7,8,256,512]{3,2,1,0:T(8,128)(2,1)S(1)} %spread.1.refs_3_.dense_ref, f32[1,128]{1,0:T(1,128)S(1)} %bitcast.4, bf16[528,384]{1,0:T(8,128)(2,1)S(1)} %collective-permute-done.3.refs_0_, bf16[528,384]{1,0:T(8,128)(2,1)S(1)} %collective-permute-done.4.refs_1_, ...), custom_call_target="tpu_custom_call" | custom-call | flops 2415919104 | bytes 4194304 | tf_op jit(solution)/shard_map/couple/pallas_call | solution.py:388
  49.5 1.0 collective-permute-done.2.refs_0_
  50.5 1.8 %couple.9 = (f32[8,128,384]{2,1,0:T(8,128)S(1)}, f32[8,128,384]{2,1,0:T(8,128)S(1)}) custom-call(bf16[7,8,256,512]{3,2,1,0:T(8,128)(2,1)S(1)} %spread.1.refs_3_.dense_ref, f32[1,128]{1,0:T(1,128)S(1)} %bitcast.5, bf16[528,384]{1,0:T(8,128)(2,1)S(1)} %collective-permute-done.2.refs_0_, f32[8,128,384]{2,1,0:T(8,128)S(1)} %get-tuple-element.42.refs_1_, ...), custom_call_target="tpu_custom_call" | custom-call | flops 805306368 | bytes 4194304 | tf_op jit(solution)/shard_map/couple/pallas_call | solution.py:388
  52.3 6.7 %collective-permute-done.1.refs_0_.refs_1_ = bf16[528,384]{1,0:T(8,128)(2,1)S(1)} collective-permute-done((bf16[528,384]{1,0:T(8,128)(2,1)S(1)}, bf16[528,384]{1,0:T(8,128)(2,1)S(1)}, u32[]{:S(2)}, u32[]{:S(2)}) %collective-permute-start.1) | collective-permute-done | bytes 405536 | tf_op jit(solution)/shard_map/ppermute | solution.py:243
  59.0 2.7 %finish_first.1 = (f32[8,128,384]{2,1,0:T(8,128)S(1)}, bf16[1024,384]{1,0:T(8,128)(2,1)S(1)}, bf16[512,384]{1,0:T(8,128)(2,1)S(1)}, bf16[512,384]{1,0:T(8,128)(2...) custom-call(bf16[7,8,256,512]{3,2,1,0:T(8,128)(2,1)S(1)} %spread.1.refs_3_.dense_r, ...), custom_call_target="tpu_custom_call" | custom-call | flops 805306368 | bytes 8388608 | tf_op jit(solution)/shard_map/finish_first/pallas_call | solution.py:434
  61.6 0.7 collective-permute-start.7
  62.4 4.3 %collective-permute-start.13 = (bf16[512,384]{1,0:T(8,128)(2,1)S(1)}, bf16[512,384]{1,0:T(8,128)(2,1)S(1)}, u32[]{:S(2)}, u32[]{:S(2)}) collective-permute-start(bf16[512,384]{1,0:T(8,128)(2,1)S(1)} %get-tuple-element.55), channel_id=1, source_target_pairs={{0,28},{4,24},{24,4},{28,0},{1,29},{5,25},{25,5},{29,1},{2,30},{6,... | collective-permute-start | bytes 1179656 | tf_op jit(solution)/shard_map/ppermute | solution.py:238
  66.7 1.6 %collective-permute-start.10 = (bf16[512,384]{1,0:T(8,128)(2,1)S(1)}, bf16[512,384]{1,0:T(8,128)(2,1)S(1)}, u32[]{:S(2)}, u32[]{:S(2)}) collective-permute-start(bf16[512,384]{1,0:T(8,128)(2,1)S(1)} %get-tuple-element.50), channel_id=1, source_target_pairs={{0,4},{4,0},{8,12},{12,8},{16,20},{20,16},{24,28},{28,24},{1,5},{5... | collective-permute-start | bytes 1179656 | tf_op jit(solution)/shard_map/ppermute | solution.py:238
  68.3 2.0 %collective-permute-start.12 = (bf16[512,384]{1,0:T(8,128)(2,1)S(1)}, bf16[512,384]{1,0:T(8,128)(2,1)S(1)}, u32[]{:S(2)}, u32[]{:S(2)}) collective-permute-start(bf16[512,384]{1,0:T(8,128)(2,1)S(1)} %get-tuple-element.52), channel_id=1, source_target_pairs={{0,12},{4,8},{8,4},{12,0},{16,28},{20,24},{24,20},{28,16},{1,13},{... | collective-permute-start | bytes 1179656 | tf_op jit(solution)/shard_map/ppermute | solution.py:238
  70.3 0.7 relay.3
  71.0 1.4 %collective-permute-start.8 = (bf16[512,384]{1,0:T(8,128)(2,1)S(1)}, bf16[512,384]{1,0:T(8,128)(2,1)S(1)}, u32[]{:S(2)}, u32[]{:S(2)}) collective-permute-start(bf16[512,384]{1,0:T(8,128)(2,1)S(1)} %get-tuple-element.48), channel_id=1, source_target_pairs={{0,24},{4,28},{8,12},{12,8},{16,20},{20,16},{24,0},{28,4},{1,25},{... | collective-permute-start | bytes 1179656 | tf_op jit(solution)/shard_map/ppermute | solution.py:243
  72.4 6.7 %collective-permute-done.13.refs_2_ = bf16[512,384]{1,0:T(8,128)(2,1)S(1)} collective-permute-done((bf16[512,384]{1,0:T(8,128)(2,1)S(1)}, bf16[512,384]{1,0:T(8,128)(2,1)S(1)}, u32[]{:S(2)}, u32[]{:S(2)}) %collective-permute-start.13) | collective-permute-done | bytes 393248 | tf_op jit(solution)/shard_map/ppermute | solution.py:238
  79.1 13.0 %collective-permute-start.9 = (bf16[512,384]{1,0:T(8,128)(2,1)S(1)}, bf16[512,384]{1,0:T(8,128)(2,1)S(1)}, u32[]{:S(2)}, u32[]{:S(2)}) collective-permute-start(bf16[512,384]{1,0:T(8,128)(2,1)S(1)} %get-tuple-element.49), channel_id=1, source_target_pairs={{0,20},{4,16},{8,4},{12,0},{16,28},{20,24},{24,12},{28,8},{1,21},{... | collective-permute-start | bytes 1179656 | tf_op jit(solution)/shard_map/ppermute | solution.py:244
  92.1 2.9 %couple.10.refs_3_.refs_0_._ = f32[8,128,384]{2,1,0:T(8,128)S(1)} custom-call(bf16[7,8,256,512]{3,2,1,0:T(8,128)(2,1)S(1)} %spread.1.refs_3_.dense_ref, f32[1,128]{1,0:T(1,128)S(1)} %bitcast.7, bf16[512,384]{1,0:T(8,128)(2,1)S(1)} %get-tuple-element.53.refs_0_, bf16[512,384]{1,0:T(8,128)(2,1)S(1)} %get-tuple-element.54.refs_1_, ...), custom_call_target="tpu_custom_call" | custom-call | flops 1610612736 | bytes 4194304 | tf_op jit(solution)/shard_map/couple/pallas_call | solution.py:388
  95.0 1.3 %prepare.1.refs_6_ = f32[8,384]{1,0:T(8,128)S(1)} custom-call(f32[3,1024,128]{2,1,0:T(8,128)S(1)} %copy-done, f32[8,128,384]{2,1,0:T(8,128)S(1)} %get-tuple-element.45.image_ref.refs_4_, f32[8,128,384]{2,1,0:T(8,128)S(1)} %couple.10.refs_3_.refs_0_._), custom_call_target="tpu_custom_call" | custom-call | flops 8388608 | bytes 4194304 | tf_op jit(solution)/shard_map/prepare/pallas_call | solution.py:490
  96.3 3.0 %couple.13 = (f32[8,128,384]{2,1,0:T(8,128)}, f32[8,128,384]{2,1,0:T(8,128)S(1)}) custom-call(bf16[7,8,256,512]{3,2,1,0:T(8,128)(2,1)S(1)} %spread.1.refs_3_.dense_ref, f32[1,128]{1,0:T(1,128)S(1)} %bitcast.8, f32[8,128,384]{2,1,0:T(8,128)S(1)} %couple.10.refs_3_.refs_0_._, bf16[528,384]{1,0:T(8,128)(2,1)S(1)} %collective-permute-done.1.refs_0_.refs_1_, ...), custom_call_target="tpu_custom_call" | custom-call | flops 805306368 | bytes 4194304 | tf_op jit(solution)/shard_map/couple/pallas_call | solution.py:388
  99.3 0.0 collective-permute-done.10.refs_0_
  99.3 0.0 collective-permute-done.11.refs_1_
  99.3 0.0 collective-permute-done.12.refs_2_
  99.3 4.0 %couple.11.refs_1_ = f32[8,128,384]{2,1,0:T(8,128)S(1)} custom-call(bf16[7,8,256,512]{3,2,1,0:T(8,128)(2,1)S(1)} %spread.1.refs_3_.dense_ref, f32[1,128]{1,0:T(1,128)S(1)} %bitcast.9, bf16[512,384]{1,0:T(8,128)(2,1)S(1)} %collective-permute-done.10.refs_0_, bf16[512,384]{1,0:T(8,128)(2,1)S(1)} %collective-permute-done.11.refs_1_, ...), custom_call_target="tpu_custom_call" | custom-call | flops 2415919104 | bytes 4194304 | tf_op jit(solution)/shard_map/couple/pallas_call | solution.py:388
  103.3 6.5 %collective-permute-done.9.refs_0_ = bf16[512,384]{1,0:T(8,128)(2,1)S(1)} collective-permute-done((bf16[512,384]{1,0:T(8,128)(2,1)S(1)}, bf16[512,384]{1,0:T(8,128)(2,1)S(1)}, u32[]{:S(2)}, u32[]{:S(2)}) %collective-permute-start.9) | collective-permute-done | bytes 393248 | tf_op jit(solution)/shard_map/ppermute | solution.py:244
  109.8 1.8 %couple.12.refs_1_ = f32[8,128,384]{2,1,0:T(8,128)S(1)} custom-call(bf16[7,8,256,512]{3,2,1,0:T(8,128)(2,1)S(1)} %spread.1.refs_3_.dense_ref, f32[1,128]{1,0:T(1,128)S(1)} %bitcast.10, bf16[512,384]{1,0:T(8,128)(2,1)S(1)} %collective-permute-done.9.refs_0_, f32[8,128,384]{2,1,0:T(8,128)S(1)} %couple.11.refs_1_), custom_call_target="tpu_custom_call" | custom-call | flops 805306368 | bytes 4194304 | tf_op jit(solution)/shard_map/couple/pallas_call | solution.py:388
  111.6 2.4 %finish_second.1 = (f32[8,128,384]{2,1,0:T(8,128)S(1)}, f32[32,8,128]{2,1,0:T(8,128)S(1)}) custom-call(bf16[7,8,256,512]{3,2,1,0:T(8,128)(2,1)S(1)} %spread.1.refs_3_.dense_ref, f32[1,128]{1,0:T(1,128)S(1)} %bitcast.11, bf16[512,384]{1,0:T(8,128)(2,1)S(1)} %collective-permute-done.8.refs_0_, f32[8,128,384]{2,1,0:T(8,128)S(1)} %couple.12.refs_1_, ...), custom_call_target="tpu_custom_call" | custom-call | flops 805306368 | bytes 8388608 | tf_op jit(solution)/shard_map/finish_second/pallas_call | solution.py:547
  113.9 11.7 %all_to_all.5.gathered_ref = f32[32,8,128]{2,1,0:T(8,128)S(1)} all-to-all(f32[32,8,128]{2,1,0:T(8,128)S(1)} %get-tuple-element.59), channel_id=1, replica_groups=mesh['row'=8,'col'=4] {'row','col'}, dimensions={0} | all-to-all | bytes 262144 | tf_op jit(solution)/shard_map/all_to_all | solution.py:669
  125.7 2.6 %final.1 = (f32[3,1024,128]{2,1,0:T(8,128)}, f32[3,1024,128]{2,1,0:T(8,128)}) custom-call(f32[3,1024,128]{2,1,0:T(8,128)S(1)} %copy-done, f32[8,128,384]{2,1,0:T(8,128)S(1)} %get-tuple-element.45.image_ref.refs_4_, f32[8,128,384]{2,1,0:T(8,128)S(1)} %get-tuple-element.58.later_ref, f32[32,8,128]{2,1,0:T(8,128)S(1)} %all_to_all.5.gathered_ref), custom_call_target="tpu_custom_call" | custom-call | tf_op jit(solution)/shard_map/final/pallas_call | solution.py:623
  (13 shorter events, 0.0 us)
Async XLA Ops:
  0.6 0.7 copy-start.4
  1.3 0.7 copy-start.6
  2.0 14.2 %copy-start.7 = (s32[8,24]{1,0:T(8,128)S(1)}, s32[8,24]{1,0:T(8,128)}, u32[]{:S(2)}) copy-start(s32[8,24]{1,0:T(8,128)} %slot_ref.1) | copy-start | bytes 2308
  4.0 21.5 %collective-permute-start = (bf16[1040,384]{1,0:T(8,128)(2,1)S(1)}, bf16[1040,384]{1,0:T(8,128)(2,1)S(1)}, u32[]{:S(2)}, u32[]{:S(2)}) collective-permute-start(bf16[1040,384]{1,0:T(8,128)(2,1)S(1)} %get-tuple-element.31.refs_1_), channel_id=1, source_target_pairs={{8,16},{12,20},{16,8},{20,12},{9,17},{13,21},{17,9},{21,13},{10,18... | collective-permute-start | bytes 2396168 | tf_op jit(solution)/shard_map/ppermute | solution.py:241
  4.7 36.1 %collective-permute-start.6 = (bf16[528,384]{1,0:T(8,128)(2,1)S(1)}, bf16[528,384]{1,0:T(8,128)(2,1)S(1)}, u32[]{:S(2)}, u32[]{:S(2)}) collective-permute-start(bf16[528,384]{1,0:T(8,128)(2,1)S(1)} %get-tuple-element.39), channel_id=1, source_target_pairs={{0,28},{4,24},{24,4},{28,0},{1,29},{5,25},{25,5},{29,1},{2,30},{6,... | collective-permute-start | bytes 1216520 | tf_op jit(solution)/shard_map/ppermute | solution.py:238
  12.7 32.6 %collective-permute-start.3 = (bf16[528,384]{1,0:T(8,128)(2,1)S(1)}, bf16[528,384]{1,0:T(8,128)(2,1)S(1)}, u32[]{:S(2)}, u32[]{:S(2)}) collective-permute-start(bf16[528,384]{1,0:T(8,128)(2,1)S(1)} %get-tuple-element.34), channel_id=1, source_target_pairs={{0,4},{4,0},{8,12},{12,8},{16,20},{20,16},{24,28},{28,24},{1,5},{5... | collective-permute-start | bytes 1216520 | tf_op jit(solution)/shard_map/ppermute | solution.py:238
  13.2 32.0 %collective-permute-start.4 = (bf16[528,384]{1,0:T(8,128)(2,1)S(1)}, bf16[528,384]{1,0:T(8,128)(2,1)S(1)}, u32[]{:S(2)}, u32[]{:S(2)}) collective-permute-start(bf16[528,384]{1,0:T(8,128)(2,1)S(1)} %get-tuple-element.35), channel_id=1, source_target_pairs={{0,8},{4,12},{8,0},{12,4},{16,24},{20,28},{24,16},{28,20},{1,9},{5... | collective-permute-start | bytes 1216520 | tf_op jit(solution)/shard_map/ppermute | solution.py:238
  13.2 32.0 %collective-permute-start.5 = (bf16[528,384]{1,0:T(8,128)(2,1)S(1)}, bf16[528,384]{1,0:T(8,128)(2,1)S(1)}, u32[]{:S(2)}, u32[]{:S(2)}) collective-permute-start(bf16[528,384]{1,0:T(8,128)(2,1)S(1)} %get-tuple-element.36), channel_id=1, source_target_pairs={{0,12},{4,8},{8,4},{12,0},{16,28},{20,24},{24,20},{28,16},{1,13},{... | collective-permute-start | bytes 1216520 | tf_op jit(solution)/shard_map/ppermute | solution.py:238
  16.2 2.8 %copy-start.1 = (bf16[8,24,128,128]{3,2,1,0:T(8,128)(2,1)S(1)}, bf16[8,24,128,128]{3,2,1,0:T(8,128)(2,1)}, u32[]{:S(2)}) copy-start(bf16[8,24,128,128]{3,2,1,0:T(8,128)(2,1)} %ks_ref.1) | copy-start | bytes 18874372
  19.0 1.6 %copy-start.2 = (bf16[8,8,128,128]{3,2,1,0:T(8,128)(2,1)S(1)}, bf16[8,8,128,128]{3,2,1,0:T(8,128)(2,1)}, u32[]{:S(2)}) copy-start(bf16[8,8,128,128]{3,2,1,0:T(8,128)(2,1)} %correlation_ref.1) | copy-start | bytes 6291460
  25.5 16.8 %copy-start.3 = (f32[128]{0:T(128)S(1)}, f32[128]{0:T(128)}, u32[]{:S(2)}) copy-start(f32[128]{0:T(128)} %param.9) | copy-start | bytes 1540
  26.9 23.6 %collective-permute-start.2 = (bf16[528,384]{1,0:T(8,128)(2,1)S(1)}, bf16[528,384]{1,0:T(8,128)(2,1)S(1)}, u32[]{:S(2)}, u32[]{:S(2)}) collective-permute-start(bf16[528,384]{1,0:T(8,128)(2,1)S(1)} %get-tuple-element.33), channel_id=1, source_target_pairs={{0,20},{4,16},{8,4},{12,0},{16,28},{20,24},{24,12},{28,8},{1,21},{... | collective-permute-start | bytes 1216520 | tf_op jit(solution)/shard_map/ppermute | solution.py:244
  40.9 18.1 %collective-permute-start.1 = (bf16[528,384]{1,0:T(8,128)(2,1)S(1)}, bf16[528,384]{1,0:T(8,128)(2,1)S(1)}, u32[]{:S(2)}, u32[]{:S(2)}) collective-permute-start(bf16[528,384]{1,0:T(8,128)(2,1)S(1)} %get-tuple-element.32), channel_id=1, source_target_pairs={{0,24},{4,28},{8,12},{12,8},{16,20},{20,16},{24,0},{28,4},{1,25},{... | collective-permute-start | bytes 1216520 | tf_op jit(solution)/shard_map/ppermute | solution.py:243
  50.5 8.5 %copy-start = (f32[3,1024,128]{2,1,0:T(8,128)S(1)}, f32[3,1024,128]{2,1,0:T(8,128)}, u32[]{:S(2)}) copy-start(f32[3,1024,128]{2,1,0:T(8,128)} %right_ref.3) | copy-start | bytes 4718596
  50.5 8.5 %copy-start.5 = (s32[1,7,4]{1,2,0:T(4,128)S(1)}, s32[1,7,4]{1,2,0:T(4,128)}, u32[]{:S(2)}) copy-start(s32[1,7,4]{1,2,0:T(4,128)} %param.13) | copy-start | bytes 340
  61.6 8.6 %collective-permute-start.7 = (bf16[1024,384]{1,0:T(8,128)(2,1)S(1)}, bf16[1024,384]{1,0:T(8,128)(2,1)S(1)}, u32[]{:S(2)}, u32[]{:S(2)}) collective-permute-start(bf16[1024,384]{1,0:T(8,128)(2,1)S(1)} %get-tuple-element.46.refs_1_), channel_id=1, source_target_pairs={{8,16},{12,20},{16,8},{20,12},{9,17},{13,21},{17,9},{21,13},{10,18... | collective-permute-start | bytes 2359304 | tf_op jit(solution)/shard_map/ppermute | solution.py:241
  62.4 16.7 %collective-permute-start.13 = (bf16[512,384]{1,0:T(8,128)(2,1)S(1)}, bf16[512,384]{1,0:T(8,128)(2,1)S(1)}, u32[]{:S(2)}, u32[]{:S(2)}) collective-permute-start(bf16[512,384]{1,0:T(8,128)(2,1)S(1)} %get-tuple-element.55), channel_id=1, source_target_pairs={{0,28},{4,24},{24,4},{28,0},{1,29},{5,25},{25,5},{29,1},{2,30},{6,... | collective-permute-start | bytes 1179656 | tf_op jit(solution)/shard_map/ppermute | solution.py:238
  66.7 32.6 %collective-permute-start.10 = (bf16[512,384]{1,0:T(8,128)(2,1)S(1)}, bf16[512,384]{1,0:T(8,128)(2,1)S(1)}, u32[]{:S(2)}, u32[]{:S(2)}) collective-permute-start(bf16[512,384]{1,0:T(8,128)(2,1)S(1)} %get-tuple-element.50), channel_id=1, source_target_pairs={{0,4},{4,0},{8,12},{12,8},{16,20},{20,16},{24,28},{28,24},{1,5},{5... | collective-permute-start | bytes 1179656 | tf_op jit(solution)/shard_map/ppermute | solution.py:238
  68.3 31.0 %collective-permute-start.11 = (bf16[512,384]{1,0:T(8,128)(2,1)S(1)}, bf16[512,384]{1,0:T(8,128)(2,1)S(1)}, u32[]{:S(2)}, u32[]{:S(2)}) collective-permute-start(bf16[512,384]{1,0:T(8,128)(2,1)S(1)} %get-tuple-element.51), channel_id=1, source_target_pairs={{0,8},{4,12},{8,0},{12,4},{16,24},{20,28},{24,16},{28,20},{1,9},{5... | collective-permute-start | bytes 1179656 | tf_op jit(solution)/shard_map/ppermute | solution.py:238
  68.3 31.0 %collective-permute-start.12 = (bf16[512,384]{1,0:T(8,128)(2,1)S(1)}, bf16[512,384]{1,0:T(8,128)(2,1)S(1)}, u32[]{:S(2)}, u32[]{:S(2)}) collective-permute-start(bf16[512,384]{1,0:T(8,128)(2,1)S(1)} %get-tuple-element.52), channel_id=1, source_target_pairs={{0,12},{4,8},{8,4},{12,0},{16,28},{20,24},{24,20},{28,16},{1,13},{... | collective-permute-start | bytes 1179656 | tf_op jit(solution)/shard_map/ppermute | solution.py:238
  71.0 40.6 %collective-permute-start.8 = (bf16[512,384]{1,0:T(8,128)(2,1)S(1)}, bf16[512,384]{1,0:T(8,128)(2,1)S(1)}, u32[]{:S(2)}, u32[]{:S(2)}) collective-permute-start(bf16[512,384]{1,0:T(8,128)(2,1)S(1)} %get-tuple-element.48), channel_id=1, source_target_pairs={{0,24},{4,28},{8,12},{12,8},{16,20},{20,16},{24,0},{28,4},{1,25},{... | collective-permute-start | bytes 1179656 | tf_op jit(solution)/shard_map/ppermute | solution.py:243
  79.1 30.7 %collective-permute-start.9 = (bf16[512,384]{1,0:T(8,128)(2,1)S(1)}, bf16[512,384]{1,0:T(8,128)(2,1)S(1)}, u32[]{:S(2)}, u32[]{:S(2)}) collective-permute-start(bf16[512,384]{1,0:T(8,128)(2,1)S(1)} %get-tuple-element.49), channel_id=1, source_target_pairs={{0,20},{4,16},{8,4},{12,0},{16,28},{20,24},{24,12},{28,8},{1,21},{... | collective-permute-start | bytes 1179656 | tf_op jit(solution)/shard_map/ppermute | solution.py:244

commit v9 on v8

--- a/solution.py
+++ b/solution.py
@@ -191,9 +191,9 @@
     message = jax.ShapeDtypeStruct((served * width + extra, lanes), jnp.bfloat16)
 
     def kernel(*refs):
-        readers_ref, mine_ref, full_ref, given_ref, *messages = refs[:7]
+        readers_ref, mine_ref, full_ref, _, *refs = refs
         me = lax.axis_index("row")
-        chosen_ref = given_ref if chosen is not None else refs[7]
+        *messages, chosen_ref = refs if chosen is None else [*refs[1:], refs[0]]
         if chosen is None:
             base = full_ref.shape[0] - EXTRA
             table = full_ref[base : base + EXTRA, 0:width].astype(jnp.float32)
@@ -216,8 +216,9 @@
                 clusters = [readers_ref[0, slot, offset] for slot in range(served)]
                 gather(clusters, mine_ref, out, width)
 
-    inputs = [readers, mine, full, after if chosen is None else chosen]
-    specs = [smem(), vmem(), vmem(), pl.BlockSpec(memory_space=pl.ANY) if chosen is None else smem()]
+    inputs = [readers, mine, full, after] + ([] if chosen is None else [chosen])
+    specs = [smem(), vmem(), vmem(), pl.BlockSpec(memory_space=pl.ANY)]
+    specs += [] if chosen is None else [smem()]
     shapes, outs = [message] * 3, [vmem()] * 3
     if chosen is None:
         shapes.append(jax.ShapeDtypeStruct((3, served), jnp.int32))
@@ -234,24 +235,22 @@
     return (messages, last) if chosen is None else (messages + [last], chosen)
 
 
-def exchange(plan, readers, direct, own, full, chosen, after, served, width):
+def exchange(plan, readers, direct, own, full, chosen, begin, served, width):
     sent = {k: lax.ppermute(m, "row", plan.pairs(k)) for k, m in direct.items()}
     if not plan.relayed:
-        return [(own, 0)] + [(sent[k], k) for k in plan.direct()], None
+        items = [(own, 0)] + [(sent[k], k) for k in plan.direct()]
+        sums = begin(items[:3], None)
+        return items, sums, None, sums[0]
     theirs = lax.ppermute(full, "row", [(i, i ^ 6) for i in INNER])
-    (mine, near, far), chosen = relay(plan, readers, full, theirs, chosen, after, served, width)
+    items = [(own, 0), (sent[1], 1), (sent[2], 2), (sent[3], 3)]
+    sums = begin(items[:3], theirs)
+    (mine, near, far), chosen = relay(
+        plan, readers, full, theirs, chosen, sums[0], served, width
+    )
     near = lax.ppermute(near, "row", [(i, i ^ (1 if i in INNER else 6)) for i in range(plan.count)])
     far = lax.ppermute(far, "row", [(i, i ^ (3 if i in INNER else 5)) for i in range(plan.count)])
-    items = [
-        (own, 0),
-        ((mine, sent[7]), (6, 7)),
-        (sent[1], 1),
-        (sent[2], 2),
-        (sent[3], 3),
-        (far, 5),
-        (near, (7, 6)),
-    ]
-    return items, chosen
+    items += [((mine, sent[7]), (6, 7)), (far, 5), (near, (7, 6))]
+    return items, sums, chosen, mine
 
 
 class Vectors:
@@ -642,27 +641,27 @@
     plan = Plan(rows, span, rows == 8 and span == 7)
     readers = jnp.swapaxes(readers, 1, 2)
 
-    def partial(items):
-        sums = [[]]
-        for group in (items[:2], items[2:-2], items[-2:-1]):
-            sums.append(couple(dense, Vectors(plan, group), energies, sums[-1]))
-        return sums[-1], sums[1][0]
+    def begin(items, after):
+        return couple(dense, Vectors(plan, items), energies, [], after)
+
+    def partial(items, sums):
+        for group in (items[3:-2], items[-2:-1]):
+            sums = couple(dense, Vectors(plan, group), energies, sums)
+        return sums, Vectors(plan, items[-1:])
 
     direct, own, full = pack(plan, readers, right_side, onsite)
     dense = spread(tile_slot, ks_tiles, correlation_tiles, span, served)
-    items, chosen = exchange(plan, readers, direct, own, full, None, dense, served, width)
+    items, sums, chosen, _ = exchange(plan, readers, direct, own, full, None, begin, served, width)
     level = levels(onsite)
-    sums, _ = partial(items)
-    last = Vectors(plan, items[-1:])
+    sums, last = partial(items, sums)
     image, full, direct, out = finish_first(
         plan, dense, last, energies, sums[0], right_side, level, own, readers
     )
 
-    items, _ = exchange(plan, readers, direct, out, full, chosen, None, served, width)
-    (value,), begun = partial(items)
-    lines = prepare(right_side, image, begun)
-    _, weighted = couple(dense, last, energies, sums, begun)
-    last = Vectors(plan, items[-1:])
+    items, begun, _, mark = exchange(plan, readers, direct, out, full, chosen, begin, served, width)
+    lines = prepare(right_side, image, mark)
+    _, weighted = couple(dense, last, energies, sums, mark)
+    (value,), last = partial(items, begun)
     later, gathered = finish_second(
         dense, last, energies, value, right_side, level, image, weighted, lines, devices
     )

time: 129 us -> 123 us (0.953)
  starting transfers between devices: 50.3 us -> 32.8 us
  waiting for transfers between devices: 20.9 us -> 31.4 us
  blocking collectives: 11.7 us -> 13.7 us
    ppermute x2, starting transfers between devices: 26.7 us -> 9.23 us  [exchange(): lax.ppermute(far, 'row', [(i, i ^ (3 if i in INNER else 5)) for i in rang...]
    ppermute x8, waiting for transfers between devices: 6.7 us -> 12 us  [exchange(): sent = {k: lax.ppermute(m, 'row', plan.pairs(k)) for k, m in direct.items()}]
    ppermute x2, waiting for transfers between devices: 6.68 us -> 9.95 us  [exchange(): lax.ppermute(near, 'row', [(i, i ^ (1 if i in INNER else 6)) for i in ran...]
    all_to_all x1, blocking collectives: 11.7 us -> 13.7 us  [body(): gathered = lax.all_to_all(gathered, ('row', 'col'), 0, 0)]
    ppermute x2, waiting for transfers between devices: 7.49 us -> 9.46 us  [exchange(): lax.ppermute(far, 'row', [(i, i ^ (3 if i in INNER else 5)) for i in rang...]
    unnamed x16 -> x14, local copies, waits for them, and re-layouts: 5.76 us -> 5.74 us
  transfers between devices with their start and end apart: 14 -> 14, of which waited for: 4 -> 8; matrix products, arithmetic and copies ran while one was open for 0% -> 0% of each run, Pallas kernels for 23% -> 24%
where the time goes in v9:
time: 123 us
  Pallas kernels  38.5 us (31%)
  starting transfers between devices  32.8 us (27%)
  waiting for transfers between devices  31.4 us (26%)
  blocking collectives  13.7 us (11%)
  local copies, waits for them, and re-layouts  5.74 us (5%)
    pallas_call x7, Pallas kernels, couple(): call(kernel, 'couple', [shape] * outs, [vmem()] * 2 + [pl.BlockSpec(memor...  20.5 us
    ppermute x8, starting transfers between devices, exchange(): sent = {k: lax.ppermute(m, 'row', plan.pairs(k)) for k, m in direct.items()}  19.4 us
    all_to_all x1, blocking collectives, body(): gathered = lax.all_to_all(gathered, ('row', 'col'), 0, 0)  13.7 us
    ppermute x8, waiting for transfers between devices, exchange(): sent = {k: lax.ppermute(m, 'row', plan.pairs(k)) for k, m in direct.items()}  12 us
    ppermute x2, waiting for transfers between devices, exchange(): lax.ppermute(near, 'row', [(i, i ^ (1 if i in INNER else 6)) for i in ran...  9.95 us
    ppermute x2, waiting for transfers between devices, exchange(): lax.ppermute(far, 'row', [(i, i ^ (3 if i in INNER else 5)) for i in rang...  9.46 us
    ppermute x2, starting transfers between devices, exchange(): lax.ppermute(far, 'row', [(i, i ^ (3 if i in INNER else 5)) for i in rang...  9.23 us
    unnamed x14, local copies, waits for them, and re-layouts  5.74 us
  transfers between devices with their start and end apart: 14, of which 8 were waited for; matrix products, arithmetic and copies ran while one was open for 0% of the time, Pallas kernels for 24%

profile of v9, /device:TPU:0, one launch (start us, length us, event | category | flops | bytes accessed | tf_op | source)
XLA Modules:
  0.0 123.0 jit_solution(11672384014546636419)
XLA Ops:
  0.6 0.7 copy-done.4
  1.3 0.7 copy-done.5
  2.0 2.0 %pack.1 = (bf16[528,384]{1,0:T(8,128)(2,1)S(1)}, bf16[528,384]{1,0:T(8,128)(2,1)S(1)}, bf16[528,384]{1,0:T(8,128)(2,1)S(1)}, bf16[528,384]{1,0:T(8,128)(2,1)S(1)...) custom-call(s32[1,4,7]{2,1,0:T(4,128)S(1)} %bitcast.12, f32[3,1024,128]{2,1,0:T(8,128)} %right_ref.3, ...), custom_call_target="tpu_custom_call" | custom-call | bytes 1048576 | tf_op jit(solution)/shard_map/pack/pallas_call | solution.py:154
  4.0 0.7 collective-permute-start
  4.7 3.0 %collective-permute-start.1 = (bf16[528,384]{1,0:T(8,128)(2,1)S(1)}, bf16[528,384]{1,0:T(8,128)(2,1)S(1)}, u32[]{:S(2)}, u32[]{:S(2)}) collective-permute-start(bf16[528,384]{1,0:T(8,128)(2,1)S(1)} %get-tuple-element.33), channel_id=1, source_target_pairs={{0,4},{4,0},{8,12},{12,8},{16,20},{20,16},{24,28},{28,24},{1,5},{5... | collective-permute-start | bytes 1216520 | tf_op jit(solution)/shard_map/ppermute | solution.py:239
  7.8 4.3 %collective-permute-start.2 = (bf16[528,384]{1,0:T(8,128)(2,1)S(1)}, bf16[528,384]{1,0:T(8,128)(2,1)S(1)}, u32[]{:S(2)}, u32[]{:S(2)}) collective-permute-start(bf16[528,384]{1,0:T(8,128)(2,1)S(1)} %get-tuple-element.34), channel_id=1, source_target_pairs={{0,8},{4,12},{8,0},{12,4},{16,24},{20,28},{24,16},{28,20},{1,9},{5... | collective-permute-start | bytes 1216520 | tf_op jit(solution)/shard_map/ppermute | solution.py:239
  12.1 0.0 collective-permute-start.5
  12.1 4.1 %collective-permute-start.6 = (bf16[528,384]{1,0:T(8,128)(2,1)S(1)}, bf16[528,384]{1,0:T(8,128)(2,1)S(1)}, u32[]{:S(2)}, u32[]{:S(2)}) collective-permute-start(bf16[528,384]{1,0:T(8,128)(2,1)S(1)} %get-tuple-element.40), channel_id=1, source_target_pairs={{0,28},{4,24},{24,4},{28,0},{1,29},{5,25},{25,5},{29,1},{2,30},{6,... | collective-permute-start | bytes 1216520 | tf_op jit(solution)/shard_map/ppermute | solution.py:239
  16.3 0.0 copy-start.1
  16.3 2.8 %copy-done.1 = bf16[8,24,128,128]{3,2,1,0:T(8,128)(2,1)S(1)} copy-done((bf16[8,24,128,128]{3,2,1,0:T(8,128)(2,1)S(1)}, bf16[8,24,128,128]{3,2,1,0:T(8,128)(2,1)}, u32[]{:S(2)}) %copy-start.1) | copy-done | bytes 6291480
  19.1 1.6 %copy-done.2 = bf16[8,8,128,128]{3,2,1,0:T(8,128)(2,1)S(1)} copy-done((bf16[8,8,128,128]{3,2,1,0:T(8,128)(2,1)S(1)}, bf16[8,8,128,128]{3,2,1,0:T(8,128)(2,1)}, u32[]{:S(2)}) %copy-start.2) | copy-done | bytes 2097176
  20.7 4.9 %spread.1.dense_ref = bf16[7,8,256,512]{3,2,1,0:T(8,128)(2,1)S(1)} custom-call(s32[8,24]{1,0:T(8,128)S(1)} %copy-done.6, bf16[8,24,128,128]{3,2,1,0:T(8,128)(2,1)S(1)} %copy-done.1, bf16[8,8,128,128]{3,2,1,0:T(8,128)(2,1)S(1)} %copy-done.2), custom_call_target="tpu_custom_call" | custom-call | bytes 16777216 | tf_op jit(solution)/shard_map/spread/pallas_call | solution.py:329
  25.5 0.0 collective-permute-done.1.refs_2_
  25.5 0.0 collective-permute-done.2.refs_3_
  25.6 0.0 collective-permute-done.refs_0_.refs_2_
  25.6 4.1 %couple.7 = (f32[8,128,384]{2,1,0:T(8,128)S(1)}, f32[8,128,384]{2,1,0:T(8,128)S(1)}) custom-call(bf16[7,8,256,512]{3,2,1,0:T(8,128)(2,1)S(1)} %spread.1.dense_ref, f32[1,128]{1,0:T(1,128)S(1)} %bitcast.3, bf16[1040,384]{1,0:T(8,128)(2,1)S(1)} %collective-permute-done.refs_0_.refs_2_, bf16[528,384]{1,0:T(8,128)(2,1)S(1)} %get-tuple-element.32.refs_1_.refs_4_, ...), custom_call_target="tpu_custom_call" | custom-call | flops 2415919104 | bytes 4194304 | tf_op jit(solution)/shard_map/couple/pallas_call | solution.py:387
  29.6 1.4 %relay.2 = (bf16[528,384]{1,0:T(8,128)(2,1)S(1)}, bf16[528,384]{1,0:T(8,128)(2,1)S(1)}, bf16[528,384]{1,0:T(8,128)(2,1)S(1)}, s32[3,4]{1,0:T(4,128)S(1)}) custom-call(s32[1,4,7]{2,1,0:T(4,128)S(1)} %bitcast.13, bf16[1040,384]{1,0:T(8,128)(2,1)S(1)} %get-tuple-element.31.refs_1_, bf16[1040,384]{1,0:T(8,128)(2,1)S(1)} %collective-permute-done.refs_0_.refs_2_, ...), custom_call_target="tpu_custom_call" | custom-call | bytes 1048576 | tf_op jit(solution)/shard_map/relay/pallas_call | solution.py:226
  31.1 4.9 %collective-permute-start.4 = (bf16[528,384]{1,0:T(8,128)(2,1)S(1)}, bf16[528,384]{1,0:T(8,128)(2,1)S(1)}, u32[]{:S(2)}, u32[]{:S(2)}) collective-permute-start(bf16[528,384]{1,0:T(8,128)(2,1)S(1)} %get-tuple-element.37), channel_id=1, source_target_pairs={{0,20},{4,16},{8,4},{12,0},{16,28},{20,24},{24,12},{28,8},{1,21},{... | collective-permute-start | bytes 1216520 | tf_op jit(solution)/shard_map/ppermute | solution.py:251
  36.0 1.3 %collective-permute-start.3 = (bf16[528,384]{1,0:T(8,128)(2,1)S(1)}, bf16[528,384]{1,0:T(8,128)(2,1)S(1)}, u32[]{:S(2)}, u32[]{:S(2)}) collective-permute-start(bf16[528,384]{1,0:T(8,128)(2,1)S(1)} %get-tuple-element.36), channel_id=1, source_target_pairs={{0,24},{4,28},{8,12},{12,8},{16,20},{20,16},{24,0},{28,4},{1,25},{... | collective-permute-start | bytes 1216520 | tf_op jit(solution)/shard_map/ppermute | solution.py:250
  37.4 0.2 levels.1.refs_3_
  37.6 0.0 collective-permute-done.5.refs_0_
  37.6 3.6 %collective-permute-done.6.refs_2_ = bf16[528,384]{1,0:T(8,128)(2,1)S(1)} collective-permute-done((bf16[528,384]{1,0:T(8,128)(2,1)S(1)}, bf16[528,384]{1,0:T(8,128)(2,1)S(1)}, u32[]{:S(2)}, u32[]{:S(2)}) %collective-permute-start.6) | collective-permute-done | bytes 405536 | tf_op jit(solution)/shard_map/ppermute | solution.py:239
  41.1 3.0 %couple.8 = (f32[8,128,384]{2,1,0:T(8,128)S(1)}, f32[8,128,384]{2,1,0:T(8,128)S(1)}) custom-call(bf16[7,8,256,512]{3,2,1,0:T(8,128)(2,1)S(1)} %spread.1.dense_ref, f32[1,128]{1,0:T(1,128)S(1)} %bitcast.4, bf16[528,384]{1,0:T(8,128)(2,1)S(1)} %collective-permute-done.5.refs_0_, bf16[528,384]{1,0:T(8,128)(2,1)S(1)} %get-tuple-element.39.refs_1_, ...), custom_call_target="tpu_custom_call" | custom-call | flops 1610612736 | bytes 4194304 | tf_op jit(solution)/shard_map/couple/pallas_call | solution.py:387
  44.1 5.5 %collective-permute-done.4.refs_0_ = bf16[528,384]{1,0:T(8,128)(2,1)S(1)} collective-permute-done((bf16[528,384]{1,0:T(8,128)(2,1)S(1)}, bf16[528,384]{1,0:T(8,128)(2,1)S(1)}, u32[]{:S(2)}, u32[]{:S(2)}) %collective-permute-start.4) | collective-permute-done | bytes 405536 | tf_op jit(solution)/shard_map/ppermute | solution.py:251
  49.7 1.8 %couple.9 = (f32[8,128,384]{2,1,0:T(8,128)S(1)}, f32[8,128,384]{2,1,0:T(8,128)S(1)}) custom-call(bf16[7,8,256,512]{3,2,1,0:T(8,128)(2,1)S(1)} %spread.1.dense_ref, f32[1,128]{1,0:T(1,128)S(1)} %bitcast.5, bf16[528,384]{1,0:T(8,128)(2,1)S(1)} %collective-permute-done.4.refs_0_, f32[8,128,384]{2,1,0:T(8,128)S(1)} %get-tuple-element.42.refs_1_, ...), custom_call_target="tpu_custom_call" | custom-call | flops 805306368 | bytes 4194304 | tf_op jit(solution)/shard_map/couple/pallas_call | solution.py:387
  51.5 5.3 %collective-permute-done.3.refs_0_.refs_1_ = bf16[528,384]{1,0:T(8,128)(2,1)S(1)} collective-permute-done((bf16[528,384]{1,0:T(8,128)(2,1)S(1)}, bf16[528,384]{1,0:T(8,128)(2,1)S(1)}, u32[]{:S(2)}, u32[]{:S(2)}) %collective-permute-start.3) | collective-permute-done | bytes 405536 | tf_op jit(solution)/shard_map/ppermute | solution.py:250
  56.9 2.6 %finish_first.1 = (f32[8,128,384]{2,1,0:T(8,128)S(1)}, bf16[1024,384]{1,0:T(8,128)(2,1)S(1)}, bf16[512,384]{1,0:T(8,128)(2,1)S(1)}, bf16[512,384]{1,0:T(8,128)(2...) custom-call(bf16[7,8,256,512]{3,2,1,0:T(8,128)(2,1)S(1)} %spread.1.dense_ref, ...), custom_call_target="tpu_custom_call" | custom-call | flops 805306368 | bytes 8388608 | tf_op jit(solution)/shard_map/finish_first/pallas_call | solution.py:433
  59.5 0.7 collective-permute-start.7
  60.2 0.6 collective-permute-start.8
  60.7 3.0 %collective-permute-start.12 = (bf16[512,384]{1,0:T(8,128)(2,1)S(1)}, bf16[512,384]{1,0:T(8,128)(2,1)S(1)}, u32[]{:S(2)}, u32[]{:S(2)}) collective-permute-start(bf16[512,384]{1,0:T(8,128)(2,1)S(1)} %get-tuple-element.53), channel_id=1, source_target_pairs={{0,12},{4,8},{8,4},{12,0},{16,28},{20,24},{24,20},{28,16},{1,13},{... | collective-permute-start | bytes 1179656 | tf_op jit(solution)/shard_map/ppermute | solution.py:239
  63.7 4.3 %collective-permute-start.13 = (bf16[512,384]{1,0:T(8,128)(2,1)S(1)}, bf16[512,384]{1,0:T(8,128)(2,1)S(1)}, u32[]{:S(2)}, u32[]{:S(2)}) collective-permute-start(bf16[512,384]{1,0:T(8,128)(2,1)S(1)} %get-tuple-element.55), channel_id=1, source_target_pairs={{0,28},{4,24},{24,4},{28,0},{1,29},{5,25},{25,5},{29,1},{2,30},{6,... | collective-permute-start | bytes 1179656 | tf_op jit(solution)/shard_map/ppermute | solution.py:239
  68.0 3.3 %collective-permute-done.8.refs_2_ = bf16[512,384]{1,0:T(8,128)(2,1)S(1)} collective-permute-done((bf16[512,384]{1,0:T(8,128)(2,1)S(1)}, bf16[512,384]{1,0:T(8,128)(2,1)S(1)}, u32[]{:S(2)}, u32[]{:S(2)}) %collective-permute-start.8) | collective-permute-done | bytes 393248 | tf_op jit(solution)/shard_map/ppermute | solution.py:239
  71.4 1.4 %collective-permute-done.9.refs_3_ = bf16[512,384]{1,0:T(8,128)(2,1)S(1)} collective-permute-done((bf16[512,384]{1,0:T(8,128)(2,1)S(1)}, bf16[512,384]{1,0:T(8,128)(2,1)S(1)}, u32[]{:S(2)}, u32[]{:S(2)}) %collective-permute-start.9) | collective-permute-done | bytes 393248 | tf_op jit(solution)/shard_map/ppermute | solution.py:239
  72.8 0.0 collective-permute-done.7.refs_0_.refs_2_
  72.8 4.0 %couple.10.refs_3_ = f32[8,128,384]{2,1,0:T(8,128)S(1)} custom-call(bf16[7,8,256,512]{3,2,1,0:T(8,128)(2,1)S(1)} %spread.1.dense_ref, f32[1,128]{1,0:T(1,128)S(1)} %bitcast.7, bf16[1024,384]{1,0:T(8,128)(2,1)S(1)} %collective-permute-done.7.refs_0_.refs_2_, bf16[512,384]{1,0:T(8,128)(2,1)S(1)} %get-tuple-element.47.refs_1_, ...), custom_call_target="tpu_custom_call" | custom-call | flops 2415919104 | bytes 4194304 | tf_op jit(solution)/shard_map/couple/pallas_call | solution.py:387
  76.8 0.7 relay.3
  77.5 4.3 %collective-permute-start.11 = (bf16[512,384]{1,0:T(8,128)(2,1)S(1)}, bf16[512,384]{1,0:T(8,128)(2,1)S(1)}, u32[]{:S(2)}, u32[]{:S(2)}) collective-permute-start(bf16[512,384]{1,0:T(8,128)(2,1)S(1)} %get-tuple-element.52), channel_id=1, source_target_pairs={{0,20},{4,16},{8,4},{12,0},{16,28},{20,24},{24,12},{28,8},{1,21},{... | collective-permute-start | bytes 1179656 | tf_op jit(solution)/shard_map/ppermute | solution.py:251
  81.8 1.4 %collective-permute-start.10 = (bf16[512,384]{1,0:T(8,128)(2,1)S(1)}, bf16[512,384]{1,0:T(8,128)(2,1)S(1)}, u32[]{:S(2)}, u32[]{:S(2)}) collective-permute-start(bf16[512,384]{1,0:T(8,128)(2,1)S(1)} %get-tuple-element.51), channel_id=1, source_target_pairs={{0,24},{4,28},{8,12},{12,8},{16,20},{20,16},{24,0},{28,4},{1,25},{... | collective-permute-start | bytes 1179656 | tf_op jit(solution)/shard_map/ppermute | solution.py:250
  83.2 1.3 %prepare.1.refs_6_ = f32[8,384]{1,0:T(8,128)S(1)} custom-call(f32[3,1024,128]{2,1,0:T(8,128)S(1)} %copy-done, f32[8,128,384]{2,1,0:T(8,128)S(1)} %get-tuple-element.45.image_ref.refs_4_, bf16[512,384]{1,0:T(8,128)(2,1)S(1)} %get-tuple-element.54.refs_1_.refs_0_._), custom_call_target="tpu_custom_call" | custom-call | flops 8388608 | bytes 4194304 | tf_op jit(solution)/shard_map/prepare/pallas_call | solution.py:489
  84.5 2.9 %couple.13 = (f32[8,128,384]{2,1,0:T(8,128)}, f32[8,128,384]{2,1,0:T(8,128)S(1)}) custom-call(bf16[7,8,256,512]{3,2,1,0:T(8,128)(2,1)S(1)} %spread.1.dense_ref, f32[1,128]{1,0:T(1,128)S(1)} %bitcast.8, bf16[512,384]{1,0:T(8,128)(2,1)S(1)} %get-tuple-element.54.refs_1_.refs_0_._, bf16[528,384]{1,0:T(8,128)(2,1)S(1)} %collective-permute-done.3.refs_0_.refs_1_, ...), custom_call_target="tpu_custom_call" | custom-call | flops 805306368 | bytes 4194304 | tf_op jit(solution)/shard_map/couple/pallas_call | solution.py:387
  87.4 3.7 %collective-permute-done.13.refs_2_ = bf16[512,384]{1,0:T(8,128)(2,1)S(1)} collective-permute-done((bf16[512,384]{1,0:T(8,128)(2,1)S(1)}, bf16[512,384]{1,0:T(8,128)(2,1)S(1)}, u32[]{:S(2)}, u32[]{:S(2)}) %collective-permute-start.13) | collective-permute-done | bytes 393248 | tf_op jit(solution)/shard_map/ppermute | solution.py:239
  91.1 2.9 %couple.11.refs_1_ = f32[8,128,384]{2,1,0:T(8,128)S(1)} custom-call(bf16[7,8,256,512]{3,2,1,0:T(8,128)(2,1)S(1)} %spread.1.dense_ref, f32[1,128]{1,0:T(1,128)S(1)} %bitcast.9, bf16[512,384]{1,0:T(8,128)(2,1)S(1)} %collective-permute-done.12.refs_0_, bf16[512,384]{1,0:T(8,128)(2,1)S(1)} %get-tuple-element.54.refs_1_.refs_0_._, ...), custom_call_target="tpu_custom_call" | custom-call | flops 1610612736 | bytes 4194304 | tf_op jit(solution)/shard_map/couple/pallas_call | solution.py:387
  94.0 3.9 %collective-permute-done.11.refs_0_ = bf16[512,384]{1,0:T(8,128)(2,1)S(1)} collective-permute-done((bf16[512,384]{1,0:T(8,128)(2,1)S(1)}, bf16[512,384]{1,0:T(8,128)(2,1)S(1)}, u32[]{:S(2)}, u32[]{:S(2)}) %collective-permute-start.11) | collective-permute-done | bytes 393248 | tf_op jit(solution)/shard_map/ppermute | solution.py:251
  97.9 1.8 %couple.12.refs_1_ = f32[8,128,384]{2,1,0:T(8,128)S(1)} custom-call(bf16[7,8,256,512]{3,2,1,0:T(8,128)(2,1)S(1)} %spread.1.dense_ref, f32[1,128]{1,0:T(1,128)S(1)} %bitcast.10, bf16[512,384]{1,0:T(8,128)(2,1)S(1)} %collective-permute-done.11.refs_0_, f32[8,128,384]{2,1,0:T(8,128)S(1)} %couple.11.refs_1_), custom_call_target="tpu_custom_call" | custom-call | flops 805306368 | bytes 4194304 | tf_op jit(solution)/shard_map/couple/pallas_call | solution.py:387
  99.7 4.6 %collective-permute-done.10.refs_0_ = bf16[512,384]{1,0:T(8,128)(2,1)S(1)} collective-permute-done((bf16[512,384]{1,0:T(8,128)(2,1)S(1)}, bf16[512,384]{1,0:T(8,128)(2,1)S(1)}, u32[]{:S(2)}, u32[]{:S(2)}) %collective-permute-start.10) | collective-permute-done | bytes 393248 | tf_op jit(solution)/shard_map/ppermute | solution.py:250
  104.3 2.4 %finish_second.1 = (f32[8,128,384]{2,1,0:T(8,128)S(1)}, f32[32,8,128]{2,1,0:T(8,128)S(1)}) custom-call(bf16[7,8,256,512]{3,2,1,0:T(8,128)(2,1)S(1)} %spread.1.dense_ref, f32[1,128]{1,0:T(1,128)S(1)} %bitcast.11, bf16[512,384]{1,0:T(8,128)(2,1)S(1)} %collective-permute-done.10.refs_0_, f32[8,128,384]{2,1,0:T(8,128)S(1)} %couple.12.refs_1_, ...), custom_call_target="tpu_custom_call" | custom-call | flops 805306368 | bytes 8388608 | tf_op jit(solution)/shard_map/finish_second/pallas_call | solution.py:546
  106.7 13.7 %all_to_all.5.gathered_ref = f32[32,8,128]{2,1,0:T(8,128)S(1)} all-to-all(f32[32,8,128]{2,1,0:T(8,128)S(1)} %get-tuple-element.59), channel_id=1, replica_groups=mesh['row'=8,'col'=4] {'row','col'}, dimensions={0} | all-to-all | bytes 262144 | tf_op jit(solution)/shard_map/all_to_all | solution.py:668
  120.4 2.6 %final.1 = (f32[3,1024,128]{2,1,0:T(8,128)}, f32[3,1024,128]{2,1,0:T(8,128)}) custom-call(f32[3,1024,128]{2,1,0:T(8,128)S(1)} %copy-done, f32[8,128,384]{2,1,0:T(8,128)S(1)} %get-tuple-element.45.image_ref.refs_4_, f32[8,128,384]{2,1,0:T(8,128)S(1)} %get-tuple-element.58.later_ref, f32[32,8,128]{2,1,0:T(8,128)S(1)} %all_to_all.5.gathered_ref), custom_call_target="tpu_custom_call" | custom-call | tf_op jit(solution)/shard_map/final/pallas_call | solution.py:622
  (11 shorter events, 0.0 us)
Async XLA Ops:
  0.6 0.7 copy-start.4
  1.3 0.7 copy-start.5
  2.0 14.3 %copy-start.6 = (s32[8,24]{1,0:T(8,128)S(1)}, s32[8,24]{1,0:T(8,128)}, u32[]{:S(2)}) copy-start(s32[8,24]{1,0:T(8,128)} %slot_ref.1) | copy-start | bytes 2308
  4.0 21.5 %collective-permute-start = (bf16[1040,384]{1,0:T(8,128)(2,1)S(1)}, bf16[1040,384]{1,0:T(8,128)(2,1)S(1)}, u32[]{:S(2)}, u32[]{:S(2)}) collective-permute-start(bf16[1040,384]{1,0:T(8,128)(2,1)S(1)} %get-tuple-element.31.refs_1_), channel_id=1, source_target_pairs={{8,16},{12,20},{16,8},{20,12},{9,17},{13,21},{17,9},{21,13},{10,18... | collective-permute-start | bytes 2396168 | tf_op jit(solution)/shard_map/ppermute | solution.py:244
  4.7 20.8 %collective-permute-start.1 = (bf16[528,384]{1,0:T(8,128)(2,1)S(1)}, bf16[528,384]{1,0:T(8,128)(2,1)S(1)}, u32[]{:S(2)}, u32[]{:S(2)}) collective-permute-start(bf16[528,384]{1,0:T(8,128)(2,1)S(1)} %get-tuple-element.33), channel_id=1, source_target_pairs={{0,4},{4,0},{8,12},{12,8},{16,20},{20,16},{24,28},{28,24},{1,5},{5... | collective-permute-start | bytes 1216520 | tf_op jit(solution)/shard_map/ppermute | solution.py:239
  7.8 17.8 %collective-permute-start.2 = (bf16[528,384]{1,0:T(8,128)(2,1)S(1)}, bf16[528,384]{1,0:T(8,128)(2,1)S(1)}, u32[]{:S(2)}, u32[]{:S(2)}) collective-permute-start(bf16[528,384]{1,0:T(8,128)(2,1)S(1)} %get-tuple-element.34), channel_id=1, source_target_pairs={{0,8},{4,12},{8,0},{12,4},{16,24},{20,28},{24,16},{28,20},{1,9},{5... | collective-permute-start | bytes 1216520 | tf_op jit(solution)/shard_map/ppermute | solution.py:239
  12.1 25.4 %collective-permute-start.5 = (bf16[528,384]{1,0:T(8,128)(2,1)S(1)}, bf16[528,384]{1,0:T(8,128)(2,1)S(1)}, u32[]{:S(2)}, u32[]{:S(2)}) collective-permute-start(bf16[528,384]{1,0:T(8,128)(2,1)S(1)} %get-tuple-element.38), channel_id=1, source_target_pairs={{0,12},{4,8},{8,4},{12,0},{16,28},{20,24},{24,20},{28,16},{1,13},{... | collective-permute-start | bytes 1216520 | tf_op jit(solution)/shard_map/ppermute | solution.py:239
  12.1 29.0 %collective-permute-start.6 = (bf16[528,384]{1,0:T(8,128)(2,1)S(1)}, bf16[528,384]{1,0:T(8,128)(2,1)S(1)}, u32[]{:S(2)}, u32[]{:S(2)}) collective-permute-start(bf16[528,384]{1,0:T(8,128)(2,1)S(1)} %get-tuple-element.40), channel_id=1, source_target_pairs={{0,28},{4,24},{24,4},{28,0},{1,29},{5,25},{25,5},{29,1},{2,30},{6,... | collective-permute-start | bytes 1216520 | tf_op jit(solution)/shard_map/ppermute | solution.py:239
  16.3 2.8 %copy-start.1 = (bf16[8,24,128,128]{3,2,1,0:T(8,128)(2,1)S(1)}, bf16[8,24,128,128]{3,2,1,0:T(8,128)(2,1)}, u32[]{:S(2)}) copy-start(bf16[8,24,128,128]{3,2,1,0:T(8,128)(2,1)} %ks_ref.1) | copy-start | bytes 18874372
  19.1 1.6 %copy-start.2 = (bf16[8,8,128,128]{3,2,1,0:T(8,128)(2,1)S(1)}, bf16[8,8,128,128]{3,2,1,0:T(8,128)(2,1)}, u32[]{:S(2)}) copy-start(bf16[8,8,128,128]{3,2,1,0:T(8,128)(2,1)} %correlation_ref.1) | copy-start | bytes 6291460
  20.7 4.9 %copy-start.3 = (f32[128]{0:T(128)S(1)}, f32[128]{0:T(128)}, u32[]{:S(2)}) copy-start(f32[128]{0:T(128)} %param.9) | copy-start | bytes 1540
  31.1 18.6 %collective-permute-start.4 = (bf16[528,384]{1,0:T(8,128)(2,1)S(1)}, bf16[528,384]{1,0:T(8,128)(2,1)S(1)}, u32[]{:S(2)}, u32[]{:S(2)}) collective-permute-start(bf16[528,384]{1,0:T(8,128)(2,1)S(1)} %get-tuple-element.37), channel_id=1, source_target_pairs={{0,20},{4,16},{8,4},{12,0},{16,28},{20,24},{24,12},{28,8},{1,21},{... | collective-permute-start | bytes 1216520 | tf_op jit(solution)/shard_map/ppermute | solution.py:251
  36.0 20.8 %collective-permute-start.3 = (bf16[528,384]{1,0:T(8,128)(2,1)S(1)}, bf16[528,384]{1,0:T(8,128)(2,1)S(1)}, u32[]{:S(2)}, u32[]{:S(2)}) collective-permute-start(bf16[528,384]{1,0:T(8,128)(2,1)S(1)} %get-tuple-element.36), channel_id=1, source_target_pairs={{0,24},{4,28},{8,12},{12,8},{16,20},{20,16},{24,0},{28,4},{1,25},{... | collective-permute-start | bytes 1216520 | tf_op jit(solution)/shard_map/ppermute | solution.py:250
  49.7 7.2 %copy-start = (f32[3,1024,128]{2,1,0:T(8,128)S(1)}, f32[3,1024,128]{2,1,0:T(8,128)}, u32[]{:S(2)}) copy-start(f32[3,1024,128]{2,1,0:T(8,128)} %right_ref.3) | copy-start | bytes 4718596
  59.5 13.3 %collective-permute-start.7 = (bf16[1024,384]{1,0:T(8,128)(2,1)S(1)}, bf16[1024,384]{1,0:T(8,128)(2,1)S(1)}, u32[]{:S(2)}, u32[]{:S(2)}) collective-permute-start(bf16[1024,384]{1,0:T(8,128)(2,1)S(1)} %get-tuple-element.46.refs_1_), channel_id=1, source_target_pairs={{8,16},{12,20},{16,8},{20,12},{9,17},{13,21},{17,9},{21,13},{10,18... | collective-permute-start | bytes 2359304 | tf_op jit(solution)/shard_map/ppermute | solution.py:244
  60.2 11.2 %collective-permute-start.8 = (bf16[512,384]{1,0:T(8,128)(2,1)S(1)}, bf16[512,384]{1,0:T(8,128)(2,1)S(1)}, u32[]{:S(2)}, u32[]{:S(2)}) collective-permute-start(bf16[512,384]{1,0:T(8,128)(2,1)S(1)} %get-tuple-element.48), channel_id=1, source_target_pairs={{0,4},{4,0},{8,12},{12,8},{16,20},{20,16},{24,28},{28,24},{1,5},{5... | collective-permute-start | bytes 1179656 | tf_op jit(solution)/shard_map/ppermute | solution.py:239
  60.7 12.1 %collective-permute-start.9 = (bf16[512,384]{1,0:T(8,128)(2,1)S(1)}, bf16[512,384]{1,0:T(8,128)(2,1)S(1)}, u32[]{:S(2)}, u32[]{:S(2)}) collective-permute-start(bf16[512,384]{1,0:T(8,128)(2,1)S(1)} %get-tuple-element.49), channel_id=1, source_target_pairs={{0,8},{4,12},{8,0},{12,4},{16,24},{20,28},{24,16},{28,20},{1,9},{5... | collective-permute-start | bytes 1179656 | tf_op jit(solution)/shard_map/ppermute | solution.py:239
  60.7 26.7 %collective-permute-start.12 = (bf16[512,384]{1,0:T(8,128)(2,1)S(1)}, bf16[512,384]{1,0:T(8,128)(2,1)S(1)}, u32[]{:S(2)}, u32[]{:S(2)}) collective-permute-start(bf16[512,384]{1,0:T(8,128)(2,1)S(1)} %get-tuple-element.53), channel_id=1, source_target_pairs={{0,12},{4,8},{8,4},{12,0},{16,28},{20,24},{24,20},{28,16},{1,13},{... | collective-permute-start | bytes 1179656 | tf_op jit(solution)/shard_map/ppermute | solution.py:239
  63.7 27.4 %collective-permute-start.13 = (bf16[512,384]{1,0:T(8,128)(2,1)S(1)}, bf16[512,384]{1,0:T(8,128)(2,1)S(1)}, u32[]{:S(2)}, u32[]{:S(2)}) collective-permute-start(bf16[512,384]{1,0:T(8,128)(2,1)S(1)} %get-tuple-element.55), channel_id=1, source_target_pairs={{0,28},{4,24},{24,4},{28,0},{1,29},{5,25},{25,5},{29,1},{2,30},{6,... | collective-permute-start | bytes 1179656 | tf_op jit(solution)/shard_map/ppermute | solution.py:239
  77.5 20.4 %collective-permute-start.11 = (bf16[512,384]{1,0:T(8,128)(2,1)S(1)}, bf16[512,384]{1,0:T(8,128)(2,1)S(1)}, u32[]{:S(2)}, u32[]{:S(2)}) collective-permute-start(bf16[512,384]{1,0:T(8,128)(2,1)S(1)} %get-tuple-element.52), channel_id=1, source_target_pairs={{0,20},{4,16},{8,4},{12,0},{16,28},{20,24},{24,12},{28,8},{1,21},{... | collective-permute-start | bytes 1179656 | tf_op jit(solution)/shard_map/ppermute | solution.py:251
  81.8 22.5 %collective-permute-start.10 = (bf16[512,384]{1,0:T(8,128)(2,1)S(1)}, bf16[512,384]{1,0:T(8,128)(2,1)S(1)}, u32[]{:S(2)}, u32[]{:S(2)}) collective-permute-start(bf16[512,384]{1,0:T(8,128)(2,1)S(1)} %get-tuple-element.51), channel_id=1, source_target_pairs={{0,24},{4,28},{8,12},{12,8},{16,20},{20,16},{24,0},{28,4},{1,25},{... | collective-permute-start | bytes 1179656 | tf_op jit(solution)/shard_map/ppermute | solution.py:250

commit v10 on v9

--- a/solution.py
+++ b/solution.py
@@ -72,9 +72,12 @@
         value = lax.rem(source - reader + (self.middle + self.count), self.count)
         return jnp.minimum(value, self.span - 1) if self.relayed else value
 
+    def early(self):
+        return [2, 3] if self.relayed else self.direct()
+
     def direct(self):
         if self.relayed:
-            return [1, 2, 3, 7]
+            return [2, 3, 1, 7]
         far = range(self.middle, 0, -1)
         return [by for f in far for by in (f, -f)]
 
@@ -102,11 +105,11 @@
     served = readers.shape[1]
     clusters, width = onsite.shape
     lanes = fields * orbitals
-    keys = plan.direct()
+    keys = plan.early()
 
     def kernel(readers_hbm, right_hbm, onsite_hbm, *refs):
-        messages, rounded = refs[: len(keys) + 1], refs[len(keys) + 1]
-        readers_ref, right_ref, onsite_ref, sems, more = refs[len(keys) + 2 :]
+        messages, rounded = refs[: len(keys)], refs[len(keys)]
+        readers_ref, right_ref, onsite_ref, sems, more = refs[len(keys) + 1 :]
         copies = []
         for cluster in range(clusters):
             here = pl.ds(cluster * width, width)
@@ -151,10 +154,10 @@
 
     message = jax.ShapeDtypeStruct((served * width + EXTRA, lanes), jnp.bfloat16)
     full = jax.ShapeDtypeStruct((clusters * width + EXTRA, lanes), jnp.bfloat16)
-    *messages, own, full = call(
+    *messages, full = call(
         kernel,
         "pack",
-        [message] * (len(keys) + 1) + [full],
+        [message] * len(keys) + [full],
         [pl.BlockSpec(memory_space=pltpu.HBM)] * 3,
         [
             pltpu.SMEM(readers.shape, readers.dtype),
@@ -163,8 +166,29 @@
             pltpu.SemaphoreType.DMA((clusters,)),
             pltpu.SemaphoreType.DMA((2,)),
         ],
-        limit=51,
+        limit=52,
     )(readers, right_side, onsite)
+    return dict(zip(keys, messages)), full
+
+
+def deal(plan, readers, full, served, width):
+    keys = [key for key in plan.direct() if key not in plan.early()]
+    lanes = full.shape[1]
+
+    def kernel(readers_ref, full_ref, same_ref, *messages):
+        fill(plan, keys, readers_ref, full_ref, messages, width)
+
+    message = jax.ShapeDtypeStruct((served * width + EXTRA, lanes), jnp.bfloat16)
+    full, *messages, own = pl.pallas_call(
+        kernel,
+        out_shape=[jax.ShapeDtypeStruct(full.shape, full.dtype)] + [message] * (len(keys) + 1),
+        in_specs=[smem(), vmem()],
+        out_specs=[vmem()] * (len(keys) + 2),
+        input_output_aliases={1: 0},
+        compiler_params=pltpu.CompilerParams(vmem_limit_bytes=12 * MIB),
+        cost_estimate=pl.CostEstimate(flops=0, bytes_accessed=MIB, transcendentals=0),
+        name="deal",
+    )(readers, full)
     return dict(zip(keys, messages)), own, full
 
 
@@ -239,11 +263,11 @@
     sent = {k: lax.ppermute(m, "row", plan.pairs(k)) for k, m in direct.items()}
     if not plan.relayed:
         items = [(own, 0)] + [(sent[k], k) for k in plan.direct()]
-        sums = begin(items[:3], None)
+        sums = begin(items[:3])
         return items, sums, None, sums[0]
     theirs = lax.ppermute(full, "row", [(i, i ^ 6) for i in INNER])
-    items = [(own, 0), (sent[1], 1), (sent[2], 2), (sent[3], 3)]
-    sums = begin(items[:3], theirs)
+    items = [(own, 0), (sent[2], 2), (sent[3], 3), (sent[1], 1)]
+    sums = begin(items[:3])
     (mine, near, far), chosen = relay(
         plan, readers, full, theirs, chosen, sums[0], served, width
     )
@@ -356,7 +380,7 @@
     return 2 * len(items) * dense.shape[1] * dense.shape[2] * dense.shape[3] * lanes
 
 
-def couple(dense, vectors, energies, sums, after=None):
+def couple(dense, vectors, energies, sums, after=None, weight=1):
     _, clusters, height, depth = dense.shape
     lanes = vectors.lanes
     count = len(vectors.arrays)
@@ -392,7 +416,7 @@
         + [pl.BlockSpec(memory_space=pl.ANY)] * len(order)
         + [vmem()] * (len(vectors.arrays) + had),
         vectors.scratch,
-        flops=work(dense, vectors.items, lanes),
+        flops=weight * work(dense, vectors.items, lanes),
         moved=4 * MIB,
     )(*inputs)
 
@@ -641,24 +665,26 @@
     plan = Plan(rows, span, rows == 8 and span == 7)
     readers = jnp.swapaxes(readers, 1, 2)
 
-    def begin(items, after):
-        return couple(dense, Vectors(plan, items), energies, [], after)
+    def begin(weight):
+        return lambda items: couple(dense, Vectors(plan, items), energies, [], weight=weight)
 
     def partial(items, sums):
         for group in (items[3:-2], items[-2:-1]):
             sums = couple(dense, Vectors(plan, group), energies, sums)
         return sums, Vectors(plan, items[-1:])
 
-    direct, own, full = pack(plan, readers, right_side, onsite)
+    early, full = pack(plan, readers, right_side, onsite)
+    direct, own, full = deal(plan, readers, full, served, width)
+    direct = early | direct
     dense = spread(tile_slot, ks_tiles, correlation_tiles, span, served)
-    items, sums, chosen, _ = exchange(plan, readers, direct, own, full, None, begin, served, width)
+    items, sums, chosen, _ = exchange(plan, readers, direct, own, full, None, begin(8), served, width)
     level = levels(onsite)
     sums, last = partial(items, sums)
     image, full, direct, out = finish_first(
         plan, dense, last, energies, sums[0], right_side, level, own, readers
     )
 
-    items, begun, _, mark = exchange(plan, readers, direct, out, full, chosen, begin, served, width)
+    items, begun, _, mark = exchange(plan, readers, direct, out, full, chosen, begin(1), served, width)
     lines = prepare(right_side, image, mark)
     _, weighted = couple(dense, last, energies, sums, mark)
     (value,), last = partial(items, begun)

time: 123 us -> 126 us (1.024)
  starting transfers between devices: 32.8 us -> 40.1 us
  waiting for transfers between devices: 31.4 us -> 29.2 us
  blocking collectives: 13.7 us -> 11.8 us
  local copies, waits for them, and re-layouts: 5.74 us -> 4.3 us
    ppermute x2, starting transfers between devices: 9.23 us -> 14.3 us  [exchange(): lax.ppermute(far, 'row', [(i, i ^ (3 if i in INNER else 5)) for i in rang...]
    ppermute x2, waiting for transfers between devices: 9.46 us -> 7.01 us  [exchange(): lax.ppermute(far, 'row', [(i, i ^ (3 if i in INNER else 5)) for i in rang...]
    all_to_all x1, blocking collectives: 13.7 us -> 11.8 us  [body(): gathered = lax.all_to_all(gathered, ('row', 'col'), 0, 0)]
    ppermute x8, waiting for transfers between devices: 12 us -> 13.5 us  [exchange(): sent = {k: lax.ppermute(m, 'row', plan.pairs(k)) for k, m in direct.items()}]
    unnamed x14, local copies, waits for them, and re-layouts: 5.74 us -> 4.3 us
    ppermute x2, waiting for transfers between devices: 9.95 us -> 8.63 us  [exchange(): lax.ppermute(near, 'row', [(i, i ^ (1 if i in INNER else 6)) for i in ran...]
    ppermute x2, starting transfers between devices: 2.71 us -> 3.98 us  [exchange(): lax.ppermute(near, 'row', [(i, i ^ (1 if i in INNER else 6)) for i in ran...]
    pallas_call x1 -> x2, Pallas kernels: 2.01 us -> 2.57 us  [the longest x1 1.89 us: pack(): call(kernel, 'pack', [message] * len(keys) + [full], [pl.BlockSpec(memory...]
  transfers between devices with their start and end apart: 14 -> 14, of which waited for: 8 -> 7; matrix products, arithmetic and copies ran while one was open for 0% -> 0% of each run, Pallas kernels for 24% -> 24%
where the time goes in v10:
time: 126 us; the launch traced here: 125 us
  starting transfers between devices  40.1 us (32%)
  Pallas kernels  39.2 us (31%)
  waiting for transfers between devices  29.2 us (23%)
  blocking collectives  11.8 us (9%)
  local copies, waits for them, and re-layouts  4.3 us (3%)
    pallas_call x7, Pallas kernels, couple(): call(kernel, 'couple', [shape] * outs, [vmem()] * 2 + [pl.BlockSpec(memor...  20.5 us
    ppermute x8, starting transfers between devices, exchange(): sent = {k: lax.ppermute(m, 'row', plan.pairs(k)) for k, m in direct.items()}  20.4 us
    ppermute x2, starting transfers between devices, exchange(): lax.ppermute(far, 'row', [(i, i ^ (3 if i in INNER else 5)) for i in rang...  14.3 us
    ppermute x8, waiting for transfers between devices, exchange(): sent = {k: lax.ppermute(m, 'row', plan.pairs(k)) for k, m in direct.items()}  13.5 us
    all_to_all x1, blocking collectives, body(): gathered = lax.all_to_all(gathered, ('row', 'col'), 0, 0)  11.8 us
    ppermute x2, waiting for transfers between devices, exchange(): lax.ppermute(near, 'row', [(i, i ^ (1 if i in INNER else 6)) for i in ran...  8.63 us
    ppermute x2, waiting for transfers between devices, exchange(): lax.ppermute(far, 'row', [(i, i ^ (3 if i in INNER else 5)) for i in rang...  7.01 us
    pallas_call x1, Pallas kernels, spread(): call(kernel, 'spread', jax.ShapeDtypeStruct((span, clusters, 2 * width, s...  4.86 us
  transfers between devices with their start and end apart: 14, of which 7 were waited for; matrix products, arithmetic and copies ran while one was open for 0% of the time, Pallas kernels for 24%

profile of v10, /device:TPU:0, one launch (start us, length us, event | category | flops | bytes accessed | tf_op | source)
XLA Modules:
  0.0 125.4 jit_solution(15750139797799916678)
XLA Ops:
  0.7 0.8 copy-done.3
  1.5 0.7 copy-done.5
  2.2 1.9 %pack.1 = (bf16[528,384]{1,0:T(8,128)(2,1)S(1)}, bf16[528,384]{1,0:T(8,128)(2,1)S(1)}, bf16[1040,384]{1,0:T(8,128)(2,1)S(1)}) custom-call(s32[1,4,7]{2,1,0:T(4,128)S(1)} %bitcast.3, f32[3,1024,128]{2,1,0:T(8,128)} %right_ref.3, f32[8,128]{1,0:T(8,128)S(1)} %bitcast.17), custom_call_target="tpu_custom_call" | custom-call | bytes 1048576 | tf_op jit(solution)/shard_map/pack/pallas_call | solution.py:157
  4.1 3.1 %collective-permute-start.1 = (bf16[528,384]{1,0:T(8,128)(2,1)S(1)}, bf16[528,384]{1,0:T(8,128)(2,1)S(1)}, u32[]{:S(2)}, u32[]{:S(2)}) collective-permute-start(bf16[528,384]{1,0:T(8,128)(2,1)S(1)} %get-tuple-element.35), channel_id=1, source_target_pairs={{0,8},{4,12},{8,0},{12,4},{16,24},{20,28},{24,16},{28,20},{1,9},{5... | collective-permute-start | bytes 1216520 | tf_op jit(solution)/shard_map/ppermute | solution.py:263
  7.2 1.4 %collective-permute-start.2 = (bf16[528,384]{1,0:T(8,128)(2,1)S(1)}, bf16[528,384]{1,0:T(8,128)(2,1)S(1)}, u32[]{:S(2)}, u32[]{:S(2)}) collective-permute-start(bf16[528,384]{1,0:T(8,128)(2,1)S(1)} %get-tuple-element.36), channel_id=1, source_target_pairs={{0,12},{4,8},{8,4},{12,0},{16,28},{20,24},{24,20},{28,16},{1,13},{... | collective-permute-start | bytes 1216520 | tf_op jit(solution)/shard_map/ppermute | solution.py:263
  8.6 0.7 deal.1
  9.2 0.7 collective-permute-start
  10.0 0.2 collective-permute-start.5
  10.2 6.8 %collective-permute-start.6 = (bf16[528,384]{1,0:T(8,128)(2,1)S(1)}, bf16[528,384]{1,0:T(8,128)(2,1)S(1)}, u32[]{:S(2)}, u32[]{:S(2)}) collective-permute-start(bf16[528,384]{1,0:T(8,128)(2,1)S(1)} %get-tuple-element.42), channel_id=1, source_target_pairs={{0,28},{4,24},{24,4},{28,0},{1,29},{5,25},{25,5},{29,1},{2,30},{6,... | collective-permute-start | bytes 1216520 | tf_op jit(solution)/shard_map/ppermute | solution.py:263
  17.0 0.0 copy-start.1
  17.0 2.8 %copy-done.1 = bf16[8,24,128,128]{3,2,1,0:T(8,128)(2,1)S(1)} copy-done((bf16[8,24,128,128]{3,2,1,0:T(8,128)(2,1)S(1)}, bf16[8,24,128,128]{3,2,1,0:T(8,128)(2,1)}, u32[]{:S(2)}) %copy-start.1) | copy-done | bytes 6291480
  19.8 4.9 %spread.1.dense_ref = bf16[7,8,256,512]{3,2,1,0:T(8,128)(2,1)S(1)} custom-call(s32[8,24]{1,0:T(8,128)S(1)} %copy-done.6, bf16[8,24,128,128]{3,2,1,0:T(8,128)(2,1)S(1)} %copy-done.1, bf16[8,8,128,128]{3,2,1,0:T(8,128)(2,1)S(1)} %copy-done.2), custom_call_target="tpu_custom_call" | custom-call | bytes 16777216 | tf_op jit(solution)/shard_map/spread/pallas_call | solution.py:353
  24.7 0.0 collective-permute-done.1.refs_1_
  24.7 1.8 %collective-permute-done.2.refs_2_ = bf16[528,384]{1,0:T(8,128)(2,1)S(1)} collective-permute-done((bf16[528,384]{1,0:T(8,128)(2,1)S(1)}, bf16[528,384]{1,0:T(8,128)(2,1)S(1)}, u32[]{:S(2)}, u32[]{:S(2)}) %collective-permute-start.2) | collective-permute-done | bytes 405536 | tf_op jit(solution)/shard_map/ppermute | solution.py:263
  26.4 4.0 %couple.7 = (f32[8,128,384]{2,1,0:T(8,128)S(1)}, f32[8,128,384]{2,1,0:T(8,128)S(1)}) custom-call(bf16[7,8,256,512]{3,2,1,0:T(8,128)(2,1)S(1)} %spread.1.dense_ref, f32[1,128]{1,0:T(1,128)S(1)} %bitcast.8, bf16[528,384]{1,0:T(8,128)(2,1)S(1)} %get-tuple-element.34.refs_0_.refs_4_, bf16[528,384]{1,0:T(8,128)(2,1)S(1)} %collective-permute-done.1.refs_1_, ...), custom_call_target="tpu_custom_call" | custom-call | flops 19327352832 | bytes 4194304 | tf_op jit(solution)/shard_map/couple/pallas_call | solution.py:411
  30.5 0.0 collective-permute-done.refs_2_
  30.5 1.4 %relay.2 = (bf16[528,384]{1,0:T(8,128)(2,1)S(1)}, bf16[528,384]{1,0:T(8,128)(2,1)S(1)}, bf16[528,384]{1,0:T(8,128)(2,1)S(1)}, s32[3,4]{1,0:T(4,128)S(1)}) custom-call(s32[1,4,7]{2,1,0:T(4,128)S(1)} %bitcast.5, bf16[1040,384]{1,0:T(8,128)(2,1)S(1)} %get-tuple-element.33.refs_1_, bf16[1040,384]{1,0:T(8,128)(2,1)S(1)} %collective-permute-done.refs_2_, ...), custom_call_target="tpu_custom_call" | custom-call | bytes 1048576 | tf_op jit(solution)/shard_map/relay/pallas_call | solution.py:250
  31.9 10.9 %collective-permute-start.4 = (bf16[528,384]{1,0:T(8,128)(2,1)S(1)}, bf16[528,384]{1,0:T(8,128)(2,1)S(1)}, u32[]{:S(2)}, u32[]{:S(2)}) collective-permute-start(bf16[528,384]{1,0:T(8,128)(2,1)S(1)} %get-tuple-element.39), channel_id=1, source_target_pairs={{0,20},{4,16},{8,4},{12,0},{16,28},{20,24},{24,12},{28,8},{1,21},{... | collective-permute-start | bytes 1216520 | tf_op jit(solution)/shard_map/ppermute | solution.py:275
  42.9 1.5 %collective-permute-start.3 = (bf16[528,384]{1,0:T(8,128)(2,1)S(1)}, bf16[528,384]{1,0:T(8,128)(2,1)S(1)}, u32[]{:S(2)}, u32[]{:S(2)}) collective-permute-start(bf16[528,384]{1,0:T(8,128)(2,1)S(1)} %get-tuple-element.38), channel_id=1, source_target_pairs={{0,24},{4,28},{8,12},{12,8},{16,20},{20,16},{24,0},{28,4},{1,25},{... | collective-permute-start | bytes 1216520 | tf_op jit(solution)/shard_map/ppermute | solution.py:274
  44.4 0.2 levels.1.refs_3_
  44.6 0.0 collective-permute-done.5.refs_0_
  44.6 0.0 collective-permute-done.6.refs_2_
  44.6 3.0 %couple.8 = (f32[8,128,384]{2,1,0:T(8,128)S(1)}, f32[8,128,384]{2,1,0:T(8,128)S(1)}) custom-call(bf16[7,8,256,512]{3,2,1,0:T(8,128)(2,1)S(1)} %spread.1.dense_ref, f32[1,128]{1,0:T(1,128)S(1)} %bitcast.9, bf16[528,384]{1,0:T(8,128)(2,1)S(1)} %collective-permute-done.5.refs_0_, bf16[528,384]{1,0:T(8,128)(2,1)S(1)} %get-tuple-element.41.refs_1_, ...), custom_call_target="tpu_custom_call" | custom-call | flops 1610612736 | bytes 4194304 | tf_op jit(solution)/shard_map/couple/pallas_call | solution.py:411
  47.6 5.1 %collective-permute-done.4.refs_0_ = bf16[528,384]{1,0:T(8,128)(2,1)S(1)} collective-permute-done((bf16[528,384]{1,0:T(8,128)(2,1)S(1)}, bf16[528,384]{1,0:T(8,128)(2,1)S(1)}, u32[]{:S(2)}, u32[]{:S(2)}) %collective-permute-start.4) | collective-permute-done | bytes 405536 | tf_op jit(solution)/shard_map/ppermute | solution.py:275
  52.7 1.8 %couple.9 = (f32[8,128,384]{2,1,0:T(8,128)S(1)}, f32[8,128,384]{2,1,0:T(8,128)S(1)}) custom-call(bf16[7,8,256,512]{3,2,1,0:T(8,128)(2,1)S(1)} %spread.1.dense_ref, f32[1,128]{1,0:T(1,128)S(1)} %bitcast.10, bf16[528,384]{1,0:T(8,128)(2,1)S(1)} %collective-permute-done.4.refs_0_, f32[8,128,384]{2,1,0:T(8,128)S(1)} %get-tuple-element.44.refs_1_, ...), custom_call_target="tpu_custom_call" | custom-call | flops 805306368 | bytes 4194304 | tf_op jit(solution)/shard_map/couple/pallas_call | solution.py:411
  54.5 6.0 %collective-permute-done.3.refs_0_.refs_1_ = bf16[528,384]{1,0:T(8,128)(2,1)S(1)} collective-permute-done((bf16[528,384]{1,0:T(8,128)(2,1)S(1)}, bf16[528,384]{1,0:T(8,128)(2,1)S(1)}, u32[]{:S(2)}, u32[]{:S(2)}) %collective-permute-start.3) | collective-permute-done | bytes 405536 | tf_op jit(solution)/shard_map/ppermute | solution.py:274
  60.6 2.6 %finish_first.1 = (f32[8,128,384]{2,1,0:T(8,128)S(1)}, bf16[1024,384]{1,0:T(8,128)(2,1)S(1)}, bf16[512,384]{1,0:T(8,128)(2,1)S(1)}, bf16[512,384]{1,0:T(8,128)(2...) custom-call(bf16[7,8,256,512]{3,2,1,0:T(8,128)(2,1)S(1)} %spread.1.dense_ref, ...), custom_call_target="tpu_custom_call" | custom-call | flops 805306368 | bytes 8388608 | tf_op jit(solution)/shard_map/finish_first/pallas_call | solution.py:457
  63.2 0.7 collective-permute-start.7
  63.9 2.6 %collective-permute-start.8 = (bf16[512,384]{1,0:T(8,128)(2,1)S(1)}, bf16[512,384]{1,0:T(8,128)(2,1)S(1)}, u32[]{:S(2)}, u32[]{:S(2)}) collective-permute-start(bf16[512,384]{1,0:T(8,128)(2,1)S(1)} %get-tuple-element.50), channel_id=1, source_target_pairs={{0,8},{4,12},{8,0},{12,4},{16,24},{20,28},{24,16},{28,20},{1,9},{5... | collective-permute-start | bytes 1179656 | tf_op jit(solution)/shard_map/ppermute | solution.py:263
  66.5 0.5 collective-permute-start.9
  66.9 1.1 collective-permute-start.12
  68.0 4.7 %collective-permute-start.13 = (bf16[512,384]{1,0:T(8,128)(2,1)S(1)}, bf16[512,384]{1,0:T(8,128)(2,1)S(1)}, u32[]{:S(2)}, u32[]{:S(2)}) collective-permute-start(bf16[512,384]{1,0:T(8,128)(2,1)S(1)} %get-tuple-element.57), channel_id=1, source_target_pairs={{0,28},{4,24},{24,4},{28,0},{1,29},{5,25},{25,5},{29,1},{2,30},{6,... | collective-permute-start | bytes 1179656 | tf_op jit(solution)/shard_map/ppermute | solution.py:263
  72.8 3.7 %collective-permute-done.8.refs_1_ = bf16[512,384]{1,0:T(8,128)(2,1)S(1)} collective-permute-done((bf16[512,384]{1,0:T(8,128)(2,1)S(1)}, bf16[512,384]{1,0:T(8,128)(2,1)S(1)}, u32[]{:S(2)}, u32[]{:S(2)}) %collective-permute-start.8) | collective-permute-done | bytes 393248 | tf_op jit(solution)/shard_map/ppermute | solution.py:263
  76.5 8.0 %collective-permute-done.9.refs_2_ = bf16[512,384]{1,0:T(8,128)(2,1)S(1)} collective-permute-done((bf16[512,384]{1,0:T(8,128)(2,1)S(1)}, bf16[512,384]{1,0:T(8,128)(2,1)S(1)}, u32[]{:S(2)}, u32[]{:S(2)}) %collective-permute-start.9) | collective-permute-done | bytes 393248 | tf_op jit(solution)/shard_map/ppermute | solution.py:263
  84.5 4.0 %couple.10.refs_3_ = f32[8,128,384]{2,1,0:T(8,128)S(1)} custom-call(bf16[7,8,256,512]{3,2,1,0:T(8,128)(2,1)S(1)} %spread.1.dense_ref, f32[1,128]{1,0:T(1,128)S(1)} %bitcast.12, bf16[512,384]{1,0:T(8,128)(2,1)S(1)} %get-tuple-element.49.refs_0_, bf16[512,384]{1,0:T(8,128)(2,1)S(1)} %collective-permute-done.8.refs_1_, ...), custom_call_target="tpu_custom_call" | custom-call | flops 2415919104 | bytes 4194304 | tf_op jit(solution)/shard_map/couple/pallas_call | solution.py:411
  88.5 0.0 collective-permute-done.7.refs_2_
  88.5 0.7 relay.3
  89.2 3.3 %collective-permute-start.11 = (bf16[512,384]{1,0:T(8,128)(2,1)S(1)}, bf16[512,384]{1,0:T(8,128)(2,1)S(1)}, u32[]{:S(2)}, u32[]{:S(2)}) collective-permute-start(bf16[512,384]{1,0:T(8,128)(2,1)S(1)} %get-tuple-element.54), channel_id=1, source_target_pairs={{0,20},{4,16},{8,4},{12,0},{16,28},{20,24},{24,12},{28,8},{1,21},{... | collective-permute-start | bytes 1179656 | tf_op jit(solution)/shard_map/ppermute | solution.py:275
  92.6 2.5 %collective-permute-start.10 = (bf16[512,384]{1,0:T(8,128)(2,1)S(1)}, bf16[512,384]{1,0:T(8,128)(2,1)S(1)}, u32[]{:S(2)}, u32[]{:S(2)}) collective-permute-start(bf16[512,384]{1,0:T(8,128)(2,1)S(1)} %get-tuple-element.53), channel_id=1, source_target_pairs={{0,24},{4,28},{8,12},{12,8},{16,20},{20,16},{24,0},{28,4},{1,25},{... | collective-permute-start | bytes 1179656 | tf_op jit(solution)/shard_map/ppermute | solution.py:274
  95.0 1.3 %prepare.1.refs_6_ = f32[8,384]{1,0:T(8,128)S(1)} custom-call(f32[3,1024,128]{2,1,0:T(8,128)S(1)} %copy-done, f32[8,128,384]{2,1,0:T(8,128)S(1)} %get-tuple-element.47.image_ref.refs_4_, bf16[512,384]{1,0:T(8,128)(2,1)S(1)} %get-tuple-element.56.refs_1_.refs_0_._), custom_call_target="tpu_custom_call" | custom-call | flops 8388608 | bytes 4194304 | tf_op jit(solution)/shard_map/prepare/pallas_call | solution.py:513
  96.4 3.0 %couple.13 = (f32[8,128,384]{2,1,0:T(8,128)}, f32[8,128,384]{2,1,0:T(8,128)S(1)}) custom-call(bf16[7,8,256,512]{3,2,1,0:T(8,128)(2,1)S(1)} %spread.1.dense_ref, f32[1,128]{1,0:T(1,128)S(1)} %bitcast.13, bf16[512,384]{1,0:T(8,128)(2,1)S(1)} %get-tuple-element.56.refs_1_.refs_0_._, bf16[528,384]{1,0:T(8,128)(2,1)S(1)} %collective-permute-done.3.refs_0_.refs_1_, ...), custom_call_target="tpu_custom_call" | custom-call | flops 805306368 | bytes 4194304 | tf_op jit(solution)/shard_map/couple/pallas_call | solution.py:411
  99.3 2.9 %couple.11.refs_1_ = f32[8,128,384]{2,1,0:T(8,128)S(1)} custom-call(bf16[7,8,256,512]{3,2,1,0:T(8,128)(2,1)S(1)} %spread.1.dense_ref, f32[1,128]{1,0:T(1,128)S(1)} %bitcast.14, bf16[512,384]{1,0:T(8,128)(2,1)S(1)} %collective-permute-done.12.refs_0_, bf16[512,384]{1,0:T(8,128)(2,1)S(1)} %get-tuple-element.56.refs_1_.refs_0_._, ...), custom_call_target="tpu_custom_call" | custom-call | flops 1610612736 | bytes 4194304 | tf_op jit(solution)/shard_map/couple/pallas_call | solution.py:411
  102.3 2.0 %collective-permute-done.11.refs_0_ = bf16[512,384]{1,0:T(8,128)(2,1)S(1)} collective-permute-done((bf16[512,384]{1,0:T(8,128)(2,1)S(1)}, bf16[512,384]{1,0:T(8,128)(2,1)S(1)}, u32[]{:S(2)}, u32[]{:S(2)}) %collective-permute-start.11) | collective-permute-done | bytes 393248 | tf_op jit(solution)/shard_map/ppermute | solution.py:275
  104.2 1.8 %couple.12.refs_1_ = f32[8,128,384]{2,1,0:T(8,128)S(1)} custom-call(bf16[7,8,256,512]{3,2,1,0:T(8,128)(2,1)S(1)} %spread.1.dense_ref, f32[1,128]{1,0:T(1,128)S(1)} %bitcast.15, bf16[512,384]{1,0:T(8,128)(2,1)S(1)} %collective-permute-done.11.refs_0_, f32[8,128,384]{2,1,0:T(8,128)S(1)} %couple.11.refs_1_), custom_call_target="tpu_custom_call" | custom-call | flops 805306368 | bytes 4194304 | tf_op jit(solution)/shard_map/couple/pallas_call | solution.py:411
  106.0 2.6 %collective-permute-done.10.refs_0_ = bf16[512,384]{1,0:T(8,128)(2,1)S(1)} collective-permute-done((bf16[512,384]{1,0:T(8,128)(2,1)S(1)}, bf16[512,384]{1,0:T(8,128)(2,1)S(1)}, u32[]{:S(2)}, u32[]{:S(2)}) %collective-permute-start.10) | collective-permute-done | bytes 393248 | tf_op jit(solution)/shard_map/ppermute | solution.py:274
  108.6 2.4 %finish_second.1 = (f32[8,128,384]{2,1,0:T(8,128)S(1)}, f32[32,8,128]{2,1,0:T(8,128)S(1)}) custom-call(bf16[7,8,256,512]{3,2,1,0:T(8,128)(2,1)S(1)} %spread.1.dense_ref, f32[1,128]{1,0:T(1,128)S(1)} %bitcast.16, bf16[512,384]{1,0:T(8,128)(2,1)S(1)} %collective-permute-done.10.refs_0_, f32[8,128,384]{2,1,0:T(8,128)S(1)} %couple.12.refs_1_, ...), custom_call_target="tpu_custom_call" | custom-call | flops 805306368 | bytes 8388608 | tf_op jit(solution)/shard_map/finish_second/pallas_call | solution.py:570
  111.0 11.8 %all_to_all.5.gathered_ref = f32[32,8,128]{2,1,0:T(8,128)S(1)} all-to-all(f32[32,8,128]{2,1,0:T(8,128)S(1)} %get-tuple-element.61), channel_id=1, replica_groups=mesh['row'=8,'col'=4] {'row','col'}, dimensions={0} | all-to-all | bytes 262144 | tf_op jit(solution)/shard_map/all_to_all | solution.py:694
  122.8 2.6 %final.1 = (f32[3,1024,128]{2,1,0:T(8,128)}, f32[3,1024,128]{2,1,0:T(8,128)}) custom-call(f32[3,1024,128]{2,1,0:T(8,128)S(1)} %copy-done, f32[8,128,384]{2,1,0:T(8,128)S(1)} %get-tuple-element.47.image_ref.refs_4_, f32[8,128,384]{2,1,0:T(8,128)S(1)} %get-tuple-element.60.later_ref, f32[32,8,128]{2,1,0:T(8,128)S(1)} %all_to_all.5.gathered_ref), custom_call_target="tpu_custom_call" | custom-call | tf_op jit(solution)/shard_map/final/pallas_call | solution.py:646
  (12 shorter events, 0.0 us)
Async XLA Ops:
  0.6 16.4 %copy-start.2 = (bf16[8,8,128,128]{3,2,1,0:T(8,128)(2,1)S(1)}, bf16[8,8,128,128]{3,2,1,0:T(8,128)(2,1)}, u32[]{:S(2)}) copy-start(bf16[8,8,128,128]{3,2,1,0:T(8,128)(2,1)} %correlation_ref.1) | copy-start | bytes 6291460
  0.6 0.8 copy-start.3
  1.5 0.7 copy-start.5
  2.2 14.9 %copy-start.6 = (s32[8,24]{1,0:T(8,128)S(1)}, s32[8,24]{1,0:T(8,128)}, u32[]{:S(2)}) copy-start(s32[8,24]{1,0:T(8,128)} %slot_ref.1) | copy-start | bytes 2308
  4.1 20.6 %collective-permute-start.1 = (bf16[528,384]{1,0:T(8,128)(2,1)S(1)}, bf16[528,384]{1,0:T(8,128)(2,1)S(1)}, u32[]{:S(2)}, u32[]{:S(2)}) collective-permute-start(bf16[528,384]{1,0:T(8,128)(2,1)S(1)} %get-tuple-element.35), channel_id=1, source_target_pairs={{0,8},{4,12},{8,0},{12,4},{16,24},{20,28},{24,16},{28,20},{1,9},{5... | collective-permute-start | bytes 1216520 | tf_op jit(solution)/shard_map/ppermute | solution.py:263
  7.2 19.3 %collective-permute-start.2 = (bf16[528,384]{1,0:T(8,128)(2,1)S(1)}, bf16[528,384]{1,0:T(8,128)(2,1)S(1)}, u32[]{:S(2)}, u32[]{:S(2)}) collective-permute-start(bf16[528,384]{1,0:T(8,128)(2,1)S(1)} %get-tuple-element.36), channel_id=1, source_target_pairs={{0,12},{4,8},{8,4},{12,0},{16,28},{20,24},{24,20},{28,16},{1,13},{... | collective-permute-start | bytes 1216520 | tf_op jit(solution)/shard_map/ppermute | solution.py:263
  9.2 21.3 %collective-permute-start = (bf16[1040,384]{1,0:T(8,128)(2,1)S(1)}, bf16[1040,384]{1,0:T(8,128)(2,1)S(1)}, u32[]{:S(2)}, u32[]{:S(2)}) collective-permute-start(bf16[1040,384]{1,0:T(8,128)(2,1)S(1)} %get-tuple-element.33.refs_1_), channel_id=1, source_target_pairs={{8,16},{12,20},{16,8},{20,12},{9,17},{13,21},{17,9},{21,13},{10,18... | collective-permute-start | bytes 2396168 | tf_op jit(solution)/shard_map/ppermute | solution.py:268
  10.0 34.6 %collective-permute-start.5 = (bf16[528,384]{1,0:T(8,128)(2,1)S(1)}, bf16[528,384]{1,0:T(8,128)(2,1)S(1)}, u32[]{:S(2)}, u32[]{:S(2)}) collective-permute-start(bf16[528,384]{1,0:T(8,128)(2,1)S(1)} %get-tuple-element.40), channel_id=1, source_target_pairs={{0,4},{4,0},{8,12},{12,8},{16,20},{20,16},{24,28},{28,24},{1,5},{5... | collective-permute-start | bytes 1216520 | tf_op jit(solution)/shard_map/ppermute | solution.py:263
  10.2 34.4 %collective-permute-start.6 = (bf16[528,384]{1,0:T(8,128)(2,1)S(1)}, bf16[528,384]{1,0:T(8,128)(2,1)S(1)}, u32[]{:S(2)}, u32[]{:S(2)}) collective-permute-start(bf16[528,384]{1,0:T(8,128)(2,1)S(1)} %get-tuple-element.42), channel_id=1, source_target_pairs={{0,28},{4,24},{24,4},{28,0},{1,29},{5,25},{25,5},{29,1},{2,30},{6,... | collective-permute-start | bytes 1216520 | tf_op jit(solution)/shard_map/ppermute | solution.py:263
  17.0 2.8 %copy-start.1 = (bf16[8,24,128,128]{3,2,1,0:T(8,128)(2,1)S(1)}, bf16[8,24,128,128]{3,2,1,0:T(8,128)(2,1)}, u32[]{:S(2)}) copy-start(bf16[8,24,128,128]{3,2,1,0:T(8,128)(2,1)} %ks_ref.1) | copy-start | bytes 18874372
  19.8 6.6 %copy-start.4 = (f32[128]{0:T(128)S(1)}, f32[128]{0:T(128)}, u32[]{:S(2)}) copy-start(f32[128]{0:T(128)} %param.9) | copy-start | bytes 1540
  31.9 20.8 %collective-permute-start.4 = (bf16[528,384]{1,0:T(8,128)(2,1)S(1)}, bf16[528,384]{1,0:T(8,128)(2,1)S(1)}, u32[]{:S(2)}, u32[]{:S(2)}) collective-permute-start(bf16[528,384]{1,0:T(8,128)(2,1)S(1)} %get-tuple-element.39), channel_id=1, source_target_pairs={{0,20},{4,16},{8,4},{12,0},{16,28},{20,24},{24,12},{28,8},{1,21},{... | collective-permute-start | bytes 1216520 | tf_op jit(solution)/shard_map/ppermute | solution.py:275
  42.9 17.7 %collective-permute-start.3 = (bf16[528,384]{1,0:T(8,128)(2,1)S(1)}, bf16[528,384]{1,0:T(8,128)(2,1)S(1)}, u32[]{:S(2)}, u32[]{:S(2)}) collective-permute-start(bf16[528,384]{1,0:T(8,128)(2,1)S(1)} %get-tuple-element.38), channel_id=1, source_target_pairs={{0,24},{4,28},{8,12},{12,8},{16,20},{20,16},{24,0},{28,4},{1,25},{... | collective-permute-start | bytes 1216520 | tf_op jit(solution)/shard_map/ppermute | solution.py:274
  52.7 7.9 %copy-start = (f32[3,1024,128]{2,1,0:T(8,128)S(1)}, f32[3,1024,128]{2,1,0:T(8,128)}, u32[]{:S(2)}) copy-start(f32[3,1024,128]{2,1,0:T(8,128)} %right_ref.3) | copy-start | bytes 4718596
  63.2 25.4 %collective-permute-start.7 = (bf16[1024,384]{1,0:T(8,128)(2,1)S(1)}, bf16[1024,384]{1,0:T(8,128)(2,1)S(1)}, u32[]{:S(2)}, u32[]{:S(2)}) collective-permute-start(bf16[1024,384]{1,0:T(8,128)(2,1)S(1)} %get-tuple-element.48.refs_1_), channel_id=1, source_target_pairs={{8,16},{12,20},{16,8},{20,12},{9,17},{13,21},{17,9},{21,13},{10,18... | collective-permute-start | bytes 2359304 | tf_op jit(solution)/shard_map/ppermute | solution.py:268
  63.9 12.6 %collective-permute-start.8 = (bf16[512,384]{1,0:T(8,128)(2,1)S(1)}, bf16[512,384]{1,0:T(8,128)(2,1)S(1)}, u32[]{:S(2)}, u32[]{:S(2)}) collective-permute-start(bf16[512,384]{1,0:T(8,128)(2,1)S(1)} %get-tuple-element.50), channel_id=1, source_target_pairs={{0,8},{4,12},{8,0},{12,4},{16,24},{20,28},{24,16},{28,20},{1,9},{5... | collective-permute-start | bytes 1179656 | tf_op jit(solution)/shard_map/ppermute | solution.py:263
  66.5 18.0 %collective-permute-start.9 = (bf16[512,384]{1,0:T(8,128)(2,1)S(1)}, bf16[512,384]{1,0:T(8,128)(2,1)S(1)}, u32[]{:S(2)}, u32[]{:S(2)}) collective-permute-start(bf16[512,384]{1,0:T(8,128)(2,1)S(1)} %get-tuple-element.51), channel_id=1, source_target_pairs={{0,12},{4,8},{8,4},{12,0},{16,28},{20,24},{24,20},{28,16},{1,13},{... | collective-permute-start | bytes 1179656 | tf_op jit(solution)/shard_map/ppermute | solution.py:263
  66.9 32.4 %collective-permute-start.12 = (bf16[512,384]{1,0:T(8,128)(2,1)S(1)}, bf16[512,384]{1,0:T(8,128)(2,1)S(1)}, u32[]{:S(2)}, u32[]{:S(2)}) collective-permute-start(bf16[512,384]{1,0:T(8,128)(2,1)S(1)} %get-tuple-element.55), channel_id=1, source_target_pairs={{0,4},{4,0},{8,12},{12,8},{16,20},{20,16},{24,28},{28,24},{1,5},{5... | collective-permute-start | bytes 1179656 | tf_op jit(solution)/shard_map/ppermute | solution.py:263
  68.0 31.3 %collective-permute-start.13 = (bf16[512,384]{1,0:T(8,128)(2,1)S(1)}, bf16[512,384]{1,0:T(8,128)(2,1)S(1)}, u32[]{:S(2)}, u32[]{:S(2)}) collective-permute-start(bf16[512,384]{1,0:T(8,128)(2,1)S(1)} %get-tuple-element.57), channel_id=1, source_target_pairs={{0,28},{4,24},{24,4},{28,0},{1,29},{5,25},{25,5},{29,1},{2,30},{6,... | collective-permute-start | bytes 1179656 | tf_op jit(solution)/shard_map/ppermute | solution.py:263
  89.2 15.0 %collective-permute-start.11 = (bf16[512,384]{1,0:T(8,128)(2,1)S(1)}, bf16[512,384]{1,0:T(8,128)(2,1)S(1)}, u32[]{:S(2)}, u32[]{:S(2)}) collective-permute-start(bf16[512,384]{1,0:T(8,128)(2,1)S(1)} %get-tuple-element.54), channel_id=1, source_target_pairs={{0,20},{4,16},{8,4},{12,0},{16,28},{20,24},{24,12},{28,8},{1,21},{... | collective-permute-start | bytes 1179656 | tf_op jit(solution)/shard_map/ppermute | solution.py:275
  92.6 16.0 %collective-permute-start.10 = (bf16[512,384]{1,0:T(8,128)(2,1)S(1)}, bf16[512,384]{1,0:T(8,128)(2,1)S(1)}, u32[]{:S(2)}, u32[]{:S(2)}) collective-permute-start(bf16[512,384]{1,0:T(8,128)(2,1)S(1)} %get-tuple-element.53), channel_id=1, source_target_pairs={{0,24},{4,28},{8,12},{12,8},{16,20},{20,16},{24,0},{28,4},{1,25},{... | collective-permute-start | bytes 1179656 | tf_op jit(solution)/shard_map/ppermute | solution.py:274

commit v11 on v10

--- a/solution.py
+++ b/solution.py
@@ -73,7 +73,7 @@
         return jnp.minimum(value, self.span - 1) if self.relayed else value
 
     def early(self):
-        return [2, 3] if self.relayed else self.direct()
+        return [2] if self.relayed else self.direct()
 
     def direct(self):
         if self.relayed:
@@ -263,11 +263,11 @@
     sent = {k: lax.ppermute(m, "row", plan.pairs(k)) for k, m in direct.items()}
     if not plan.relayed:
         items = [(own, 0)] + [(sent[k], k) for k in plan.direct()]
-        sums = begin(items[:3])
+        sums = begin(items[:2])
         return items, sums, None, sums[0]
     theirs = lax.ppermute(full, "row", [(i, i ^ 6) for i in INNER])
     items = [(own, 0), (sent[2], 2), (sent[3], 3), (sent[1], 1)]
-    sums = begin(items[:3])
+    sums = begin(items[:2])
     (mine, near, far), chosen = relay(
         plan, readers, full, theirs, chosen, sums[0], served, width
     )
@@ -669,7 +669,7 @@
         return lambda items: couple(dense, Vectors(plan, items), energies, [], weight=weight)
 
     def partial(items, sums):
-        for group in (items[3:-2], items[-2:-1]):
+        for group in (items[2:-2], items[-2:-1]):
             sums = couple(dense, Vectors(plan, group), energies, sums)
         return sums, Vectors(plan, items[-1:])
 

time: 126 us -> 126 us (level)
  waiting for transfers between devices: 29.2 us -> 25.1 us
  starting transfers between devices: 40.1 us -> 43.3 us
    ppermute x2, waiting for transfers between devices: 7.01 us -> 0.01 us  [exchange(): lax.ppermute(far, 'row', [(i, i ^ (3 if i in INNER else 5)) for i in rang...]
    ppermute x8, waiting for transfers between devices: 13.5 us -> 18.9 us  [exchange(): sent = {k: lax.ppermute(m, 'row', plan.pairs(k)) for k, m in direct.items()}]
    ppermute x2, starting transfers between devices: 14.3 us -> 18.7 us  [exchange(): lax.ppermute(far, 'row', [(i, i ^ (3 if i in INNER else 5)) for i in rang...]
    ppermute x2, waiting for transfers between devices: 8.63 us -> 6.19 us  [exchange(): lax.ppermute(near, 'row', [(i, i ^ (1 if i in INNER else 6)) for i in ran...]
    ppermute x2, starting transfers between devices: 3.98 us -> 2.7 us  [exchange(): lax.ppermute(near, 'row', [(i, i ^ (1 if i in INNER else 6)) for i in ran...]
    unnamed x14 -> x16, local copies, waits for them, and re-layouts: 4.3 us -> 4.31 us
  transfers between devices with their start and end apart: 14 -> 14, of which waited for: 7 -> 5; matrix products, arithmetic and copies ran while one was open for 0% -> 0% of each run, Pallas kernels for 24% -> 24%
where the time goes in v11:
time: 126 us
  starting transfers between devices  43.3 us (34%)
  Pallas kernels  39.2 us (31%)
  waiting for transfers between devices  25.1 us (20%)
  blocking collectives  12.6 us (10%)
  local copies, waits for them, and re-layouts  4.31 us (3%)
    pallas_call x7, Pallas kernels, couple(): call(kernel, 'couple', [shape] * outs, [vmem()] * 2 + [pl.BlockSpec(memor...  20.6 us
    ppermute x8, starting transfers between devices, exchange(): sent = {k: lax.ppermute(m, 'row', plan.pairs(k)) for k, m in direct.items()}  20.4 us
    ppermute x8, waiting for transfers between devices, exchange(): sent = {k: lax.ppermute(m, 'row', plan.pairs(k)) for k, m in direct.items()}  18.9 us
    ppermute x2, starting transfers between devices, exchange(): lax.ppermute(far, 'row', [(i, i ^ (3 if i in INNER else 5)) for i in rang...  18.7 us
    all_to_all x1, blocking collectives, body(): gathered = lax.all_to_all(gathered, ('row', 'col'), 0, 0)  12.6 us
    ppermute x2, waiting for transfers between devices, exchange(): lax.ppermute(near, 'row', [(i, i ^ (1 if i in INNER else 6)) for i in ran...  6.19 us
    pallas_call x1, Pallas kernels, spread(): call(kernel, 'spread', jax.ShapeDtypeStruct((span, clusters, 2 * width, s...  4.86 us
    unnamed x16, local copies, waits for them, and re-layouts  4.31 us
  transfers between devices with their start and end apart: 14, of which 5 were waited for; matrix products, arithmetic and copies ran while one was open for 0% of the time, Pallas kernels for 24%

profile of v11, /device:TPU:0, one launch (start us, length us, event | category | flops | bytes accessed | tf_op | source)
XLA Modules:
  0.0 125.5 jit_solution(8521146786278526825)
XLA Ops:
  0.7 0.8 copy-done.3
  1.5 0.7 copy-done.5
  2.2 1.9 %pack.1 = (bf16[528,384]{1,0:T(8,128)(2,1)S(1)}, bf16[1040,384]{1,0:T(8,128)(2,1)S(1)}) custom-call(s32[1,4,7]{2,1,0:T(4,128)S(1)} %bitcast.3, f32[3,1024,128]{2,1,0:T(8,128)} %right_ref.3, f32[8,128]{1,0:T(8,128)S(1)} %bitcast.17), custom_call_target="tpu_custom_call" | custom-call | bytes 1048576 | tf_op jit(solution)/shard_map/pack/pallas_call | solution.py:157
  4.0 3.1 %collective-permute-start.1 = (bf16[528,384]{1,0:T(8,128)(2,1)S(1)}, bf16[528,384]{1,0:T(8,128)(2,1)S(1)}, u32[]{:S(2)}, u32[]{:S(2)}) collective-permute-start(bf16[528,384]{1,0:T(8,128)(2,1)S(1)} %get-tuple-element.35), channel_id=1, source_target_pairs={{0,8},{4,12},{8,0},{12,4},{16,24},{20,28},{24,16},{28,20},{1,9},{5... | collective-permute-start | bytes 1216520 | tf_op jit(solution)/shard_map/ppermute | solution.py:263
  7.1 0.7 deal.1
  7.9 0.7 collective-permute-start
  8.6 5.4 %collective-permute-start.4 = (bf16[528,384]{1,0:T(8,128)(2,1)S(1)}, bf16[528,384]{1,0:T(8,128)(2,1)S(1)}, u32[]{:S(2)}, u32[]{:S(2)}) collective-permute-start(bf16[528,384]{1,0:T(8,128)(2,1)S(1)} %get-tuple-element.39), channel_id=1, source_target_pairs={{0,12},{4,8},{8,4},{12,0},{16,28},{20,24},{24,20},{28,16},{1,13},{... | collective-permute-start | bytes 1216520 | tf_op jit(solution)/shard_map/ppermute | solution.py:263
  13.9 0.5 collective-permute-start.5
  14.4 3.8 %collective-permute-start.6 = (bf16[528,384]{1,0:T(8,128)(2,1)S(1)}, bf16[528,384]{1,0:T(8,128)(2,1)S(1)}, u32[]{:S(2)}, u32[]{:S(2)}) collective-permute-start(bf16[528,384]{1,0:T(8,128)(2,1)S(1)} %get-tuple-element.42), channel_id=1, source_target_pairs={{0,28},{4,24},{24,4},{28,0},{1,29},{5,25},{25,5},{29,1},{2,30},{6,... | collective-permute-start | bytes 1216520 | tf_op jit(solution)/shard_map/ppermute | solution.py:263
  18.2 0.0 copy-start.1
  18.3 2.8 %copy-done.1 = bf16[8,24,128,128]{3,2,1,0:T(8,128)(2,1)S(1)} copy-done((bf16[8,24,128,128]{3,2,1,0:T(8,128)(2,1)S(1)}, bf16[8,24,128,128]{3,2,1,0:T(8,128)(2,1)}, u32[]{:S(2)}) %copy-start.1) | copy-done | bytes 6291480
  21.0 4.9 %spread.1.dense_ref = bf16[7,8,256,512]{3,2,1,0:T(8,128)(2,1)S(1)} custom-call(s32[8,24]{1,0:T(8,128)S(1)} %copy-done.7, bf16[8,24,128,128]{3,2,1,0:T(8,128)(2,1)S(1)} %copy-done.1, bf16[8,8,128,128]{3,2,1,0:T(8,128)(2,1)S(1)} %copy-done.2), custom_call_target="tpu_custom_call" | custom-call | bytes 16777216 | tf_op jit(solution)/shard_map/spread/pallas_call | solution.py:353
  25.9 0.0 collective-permute-done.1.refs_1_
  25.9 2.9 %couple.7 = (f32[8,128,384]{2,1,0:T(8,128)S(1)}, f32[8,128,384]{2,1,0:T(8,128)S(1)}) custom-call(bf16[7,8,256,512]{3,2,1,0:T(8,128)(2,1)S(1)} %spread.1.dense_ref, f32[1,128]{1,0:T(1,128)S(1)} %bitcast.8, bf16[528,384]{1,0:T(8,128)(2,1)S(1)} %get-tuple-element.34.refs_0_.refs_4_, bf16[528,384]{1,0:T(8,128)(2,1)S(1)} %collective-permute-done.1.refs_1_), custom_call_target="tpu_custom_call" | custom-call | flops 12884901888 | bytes 4194304 | tf_op jit(solution)/shard_map/couple/pallas_call | solution.py:411
  28.8 0.0 collective-permute-done.refs_2_
  28.8 0.0 copy-start.6
  28.9 1.4 %relay.2 = (bf16[528,384]{1,0:T(8,128)(2,1)S(1)}, bf16[528,384]{1,0:T(8,128)(2,1)S(1)}, bf16[528,384]{1,0:T(8,128)(2,1)S(1)}, s32[3,4]{1,0:T(4,128)S(1)}) custom-call(s32[1,4,7]{2,1,0:T(4,128)S(1)} %bitcast.5, bf16[1040,384]{1,0:T(8,128)(2,1)S(1)} %get-tuple-element.33.refs_1_, bf16[1040,384]{1,0:T(8,128)(2,1)S(1)} %collective-permute-done.refs_2_, ...), custom_call_target="tpu_custom_call" | custom-call | bytes 1048576 | tf_op jit(solution)/shard_map/relay/pallas_call | solution.py:250
  30.3 12.5 %collective-permute-start.3 = (bf16[528,384]{1,0:T(8,128)(2,1)S(1)}, bf16[528,384]{1,0:T(8,128)(2,1)S(1)}, u32[]{:S(2)}, u32[]{:S(2)}) collective-permute-start(bf16[528,384]{1,0:T(8,128)(2,1)S(1)} %get-tuple-element.38), channel_id=1, source_target_pairs={{0,20},{4,16},{8,4},{12,0},{16,28},{20,24},{24,12},{28,8},{1,21},{... | collective-permute-start | bytes 1216520 | tf_op jit(solution)/shard_map/ppermute | solution.py:275
  42.8 1.2 collective-permute-start.2
  44.0 0.2 levels.1.refs_3_
  44.2 0.0 collective-permute-done.4.refs_0_
  44.2 6.1 %collective-permute-done.5.refs_1_ = bf16[528,384]{1,0:T(8,128)(2,1)S(1)} collective-permute-done((bf16[528,384]{1,0:T(8,128)(2,1)S(1)}, bf16[528,384]{1,0:T(8,128)(2,1)S(1)}, u32[]{:S(2)}, u32[]{:S(2)}) %collective-permute-start.5) | collective-permute-done | bytes 405536 | tf_op jit(solution)/shard_map/ppermute | solution.py:263
  50.3 4.2 %couple.8 = (f32[8,128,384]{2,1,0:T(8,128)S(1)}, f32[8,128,384]{2,1,0:T(8,128)S(1)}) custom-call(bf16[7,8,256,512]{3,2,1,0:T(8,128)(2,1)S(1)} %spread.1.dense_ref, f32[1,128]{1,0:T(1,128)S(1)} %bitcast.9, bf16[528,384]{1,0:T(8,128)(2,1)S(1)} %collective-permute-done.4.refs_0_, bf16[528,384]{1,0:T(8,128)(2,1)S(1)} %collective-permute-done.5.refs_1_, ...), custom_call_target="tpu_custom_call" | custom-call | flops 2415919104 | bytes 4194304 | tf_op jit(solution)/shard_map/couple/pallas_call | solution.py:411
  54.5 0.0 copy-start
  54.5 1.8 %couple.9 = (f32[8,128,384]{2,1,0:T(8,128)S(1)}, f32[8,128,384]{2,1,0:T(8,128)S(1)}) custom-call(bf16[7,8,256,512]{3,2,1,0:T(8,128)(2,1)S(1)} %spread.1.dense_ref, f32[1,128]{1,0:T(1,128)S(1)} %bitcast.10, bf16[528,384]{1,0:T(8,128)(2,1)S(1)} %collective-permute-done.3.refs_0_, f32[8,128,384]{2,1,0:T(8,128)S(1)} %get-tuple-element.44.refs_1_, ...), custom_call_target="tpu_custom_call" | custom-call | flops 805306368 | bytes 4194304 | tf_op jit(solution)/shard_map/couple/pallas_call | solution.py:411
  56.3 4.6 %collective-permute-done.2.refs_0_.refs_1_ = bf16[528,384]{1,0:T(8,128)(2,1)S(1)} collective-permute-done((bf16[528,384]{1,0:T(8,128)(2,1)S(1)}, bf16[528,384]{1,0:T(8,128)(2,1)S(1)}, u32[]{:S(2)}, u32[]{:S(2)}) %collective-permute-start.2) | collective-permute-done | bytes 405536 | tf_op jit(solution)/shard_map/ppermute | solution.py:274
  60.9 2.6 %finish_first.1 = (f32[8,128,384]{2,1,0:T(8,128)S(1)}, bf16[1024,384]{1,0:T(8,128)(2,1)S(1)}, bf16[512,384]{1,0:T(8,128)(2,1)S(1)}, bf16[512,384]{1,0:T(8,128)(2...) custom-call(bf16[7,8,256,512]{3,2,1,0:T(8,128)(2,1)S(1)} %spread.1.dense_ref, ...), custom_call_target="tpu_custom_call" | custom-call | flops 805306368 | bytes 8388608 | tf_op jit(solution)/shard_map/finish_first/pallas_call | solution.py:457
  63.5 0.7 collective-permute-start.7
  64.2 1.4 %collective-permute-start.8 = (bf16[512,384]{1,0:T(8,128)(2,1)S(1)}, bf16[512,384]{1,0:T(8,128)(2,1)S(1)}, u32[]{:S(2)}, u32[]{:S(2)}) collective-permute-start(bf16[512,384]{1,0:T(8,128)(2,1)S(1)} %get-tuple-element.50), channel_id=1, source_target_pairs={{0,8},{4,12},{8,0},{12,4},{16,24},{20,28},{24,16},{28,20},{1,9},{5... | collective-permute-start | bytes 1179656 | tf_op jit(solution)/shard_map/ppermute | solution.py:263
  65.7 1.0 collective-permute-start.11
  66.7 1.1 collective-permute-start.12
  67.8 4.2 %collective-permute-start.13 = (bf16[512,384]{1,0:T(8,128)(2,1)S(1)}, bf16[512,384]{1,0:T(8,128)(2,1)S(1)}, u32[]{:S(2)}, u32[]{:S(2)}) collective-permute-start(bf16[512,384]{1,0:T(8,128)(2,1)S(1)} %get-tuple-element.57), channel_id=1, source_target_pairs={{0,28},{4,24},{24,4},{28,0},{1,29},{5,25},{25,5},{29,1},{2,30},{6,... | collective-permute-start | bytes 1179656 | tf_op jit(solution)/shard_map/ppermute | solution.py:263
  72.0 4.4 %collective-permute-done.8.refs_1_ = bf16[512,384]{1,0:T(8,128)(2,1)S(1)} collective-permute-done((bf16[512,384]{1,0:T(8,128)(2,1)S(1)}, bf16[512,384]{1,0:T(8,128)(2,1)S(1)}, u32[]{:S(2)}, u32[]{:S(2)}) %collective-permute-start.8) | collective-permute-done | bytes 393248 | tf_op jit(solution)/shard_map/ppermute | solution.py:263
  76.4 2.9 %couple.10.refs_3_.refs_4_ = f32[8,128,384]{2,1,0:T(8,128)S(1)} custom-call(bf16[7,8,256,512]{3,2,1,0:T(8,128)(2,1)S(1)} %spread.1.dense_ref, f32[1,128]{1,0:T(1,128)S(1)} %bitcast.12, bf16[512,384]{1,0:T(8,128)(2,1)S(1)} %get-tuple-element.49.refs_0_, bf16[512,384]{1,0:T(8,128)(2,1)S(1)} %collective-permute-done.8.refs_1_), custom_call_target="tpu_custom_call" | custom-call | flops 1610612736 | bytes 4194304 | tf_op jit(solution)/shard_map/couple/pallas_call | solution.py:411
  79.2 0.0 collective-permute-done.7.refs_2_
  79.2 0.7 relay.3
  79.9 6.2 %collective-permute-start.10 = (bf16[512,384]{1,0:T(8,128)(2,1)S(1)}, bf16[512,384]{1,0:T(8,128)(2,1)S(1)}, u32[]{:S(2)}, u32[]{:S(2)}) collective-permute-start(bf16[512,384]{1,0:T(8,128)(2,1)S(1)} %get-tuple-element.53), channel_id=1, source_target_pairs={{0,20},{4,16},{8,4},{12,0},{16,28},{20,24},{24,12},{28,8},{1,21},{... | collective-permute-start | bytes 1179656 | tf_op jit(solution)/shard_map/ppermute | solution.py:275
  86.2 1.5 %collective-permute-start.9 = (bf16[512,384]{1,0:T(8,128)(2,1)S(1)}, bf16[512,384]{1,0:T(8,128)(2,1)S(1)}, u32[]{:S(2)}, u32[]{:S(2)}) collective-permute-start(bf16[512,384]{1,0:T(8,128)(2,1)S(1)} %get-tuple-element.52), channel_id=1, source_target_pairs={{0,24},{4,28},{8,12},{12,8},{16,20},{20,16},{24,0},{28,4},{1,25},{... | collective-permute-start | bytes 1179656 | tf_op jit(solution)/shard_map/ppermute | solution.py:274
  87.7 1.3 %prepare.1.refs_6_ = f32[8,384]{1,0:T(8,128)S(1)} custom-call(f32[3,1024,128]{2,1,0:T(8,128)S(1)} %copy-done, f32[8,128,384]{2,1,0:T(8,128)S(1)} %get-tuple-element.47.image_ref.refs_4_, bf16[512,384]{1,0:T(8,128)(2,1)S(1)} %get-tuple-element.56.refs_2_.refs_0_._), custom_call_target="tpu_custom_call" | custom-call | flops 8388608 | bytes 4194304 | tf_op jit(solution)/shard_map/prepare/pallas_call | solution.py:513
  89.0 3.0 %couple.13 = (f32[8,128,384]{2,1,0:T(8,128)}, f32[8,128,384]{2,1,0:T(8,128)S(1)}) custom-call(bf16[7,8,256,512]{3,2,1,0:T(8,128)(2,1)S(1)} %spread.1.dense_ref, f32[1,128]{1,0:T(1,128)S(1)} %bitcast.13, bf16[512,384]{1,0:T(8,128)(2,1)S(1)} %get-tuple-element.56.refs_2_.refs_0_._, bf16[528,384]{1,0:T(8,128)(2,1)S(1)} %collective-permute-done.2.refs_0_.refs_1_, ...), custom_call_target="tpu_custom_call" | custom-call | flops 805306368 | bytes 4194304 | tf_op jit(solution)/shard_map/couple/pallas_call | solution.py:411
  92.0 0.0 collective-permute-done.11.refs_0_
  92.0 8.4 %collective-permute-done.12.refs_1_ = bf16[512,384]{1,0:T(8,128)(2,1)S(1)} collective-permute-done((bf16[512,384]{1,0:T(8,128)(2,1)S(1)}, bf16[512,384]{1,0:T(8,128)(2,1)S(1)}, u32[]{:S(2)}, u32[]{:S(2)}) %collective-permute-start.12) | collective-permute-done | bytes 393248 | tf_op jit(solution)/shard_map/ppermute | solution.py:263
  100.4 4.1 %couple.11.refs_1_ = f32[8,128,384]{2,1,0:T(8,128)S(1)} custom-call(bf16[7,8,256,512]{3,2,1,0:T(8,128)(2,1)S(1)} %spread.1.dense_ref, f32[1,128]{1,0:T(1,128)S(1)} %bitcast.14, bf16[512,384]{1,0:T(8,128)(2,1)S(1)} %collective-permute-done.11.refs_0_, bf16[512,384]{1,0:T(8,128)(2,1)S(1)} %collective-permute-done.12.refs_1_, ...), custom_call_target="tpu_custom_call" | custom-call | flops 2415919104 | bytes 4194304 | tf_op jit(solution)/shard_map/couple/pallas_call | solution.py:411
  104.5 1.8 %couple.12.refs_1_ = f32[8,128,384]{2,1,0:T(8,128)S(1)} custom-call(bf16[7,8,256,512]{3,2,1,0:T(8,128)(2,1)S(1)} %spread.1.dense_ref, f32[1,128]{1,0:T(1,128)S(1)} %bitcast.15, bf16[512,384]{1,0:T(8,128)(2,1)S(1)} %collective-permute-done.10.refs_0_, f32[8,128,384]{2,1,0:T(8,128)S(1)} %couple.11.refs_1_), custom_call_target="tpu_custom_call" | custom-call | flops 805306368 | bytes 4194304 | tf_op jit(solution)/shard_map/couple/pallas_call | solution.py:411
  106.3 1.6 %collective-permute-done.9.refs_0_ = bf16[512,384]{1,0:T(8,128)(2,1)S(1)} collective-permute-done((bf16[512,384]{1,0:T(8,128)(2,1)S(1)}, bf16[512,384]{1,0:T(8,128)(2,1)S(1)}, u32[]{:S(2)}, u32[]{:S(2)}) %collective-permute-start.9) | collective-permute-done | bytes 393248 | tf_op jit(solution)/shard_map/ppermute | solution.py:274
  107.9 2.4 %finish_second.1 = (f32[8,128,384]{2,1,0:T(8,128)S(1)}, f32[32,8,128]{2,1,0:T(8,128)S(1)}) custom-call(bf16[7,8,256,512]{3,2,1,0:T(8,128)(2,1)S(1)} %spread.1.dense_ref, f32[1,128]{1,0:T(1,128)S(1)} %bitcast.16, bf16[512,384]{1,0:T(8,128)(2,1)S(1)} %collective-permute-done.9.refs_0_, f32[8,128,384]{2,1,0:T(8,128)S(1)} %couple.12.refs_1_, ...), custom_call_target="tpu_custom_call" | custom-call | flops 805306368 | bytes 8388608 | tf_op jit(solution)/shard_map/finish_second/pallas_call | solution.py:570
  110.3 12.6 %all_to_all.5.gathered_ref = f32[32,8,128]{2,1,0:T(8,128)S(1)} all-to-all(f32[32,8,128]{2,1,0:T(8,128)S(1)} %get-tuple-element.61), channel_id=1, replica_groups=mesh['row'=8,'col'=4] {'row','col'}, dimensions={0} | all-to-all | bytes 262144 | tf_op jit(solution)/shard_map/all_to_all | solution.py:694
  122.9 2.6 %final.1 = (f32[3,1024,128]{2,1,0:T(8,128)}, f32[3,1024,128]{2,1,0:T(8,128)}) custom-call(f32[3,1024,128]{2,1,0:T(8,128)S(1)} %copy-done, f32[8,128,384]{2,1,0:T(8,128)S(1)} %get-tuple-element.47.image_ref.refs_4_, f32[8,128,384]{2,1,0:T(8,128)S(1)} %get-tuple-element.60.later_ref, f32[32,8,128]{2,1,0:T(8,128)S(1)} %all_to_all.5.gathered_ref), custom_call_target="tpu_custom_call" | custom-call | tf_op jit(solution)/shard_map/final/pallas_call | solution.py:646
  (14 shorter events, 0.0 us)
Async XLA Ops:
  0.6 17.6 %copy-start.2 = (bf16[8,8,128,128]{3,2,1,0:T(8,128)(2,1)S(1)}, bf16[8,8,128,128]{3,2,1,0:T(8,128)(2,1)}, u32[]{:S(2)}) copy-start(bf16[8,8,128,128]{3,2,1,0:T(8,128)(2,1)} %correlation_ref.1) | copy-start | bytes 6291460
  0.6 0.8 copy-start.3
  1.5 0.7 copy-start.5
  2.2 16.1 %copy-start.7 = (s32[8,24]{1,0:T(8,128)S(1)}, s32[8,24]{1,0:T(8,128)}, u32[]{:S(2)}) copy-start(s32[8,24]{1,0:T(8,128)} %slot_ref.1) | copy-start | bytes 2308
  4.0 21.9 %collective-permute-start.1 = (bf16[528,384]{1,0:T(8,128)(2,1)S(1)}, bf16[528,384]{1,0:T(8,128)(2,1)S(1)}, u32[]{:S(2)}, u32[]{:S(2)}) collective-permute-start(bf16[528,384]{1,0:T(8,128)(2,1)S(1)} %get-tuple-element.35), channel_id=1, source_target_pairs={{0,8},{4,12},{8,0},{12,4},{16,24},{20,28},{24,16},{28,20},{1,9},{5... | collective-permute-start | bytes 1216520 | tf_op jit(solution)/shard_map/ppermute | solution.py:263
  7.9 21.0 %collective-permute-start = (bf16[1040,384]{1,0:T(8,128)(2,1)S(1)}, bf16[1040,384]{1,0:T(8,128)(2,1)S(1)}, u32[]{:S(2)}, u32[]{:S(2)}) collective-permute-start(bf16[1040,384]{1,0:T(8,128)(2,1)S(1)} %get-tuple-element.33.refs_1_), channel_id=1, source_target_pairs={{8,16},{12,20},{16,8},{20,12},{9,17},{13,21},{17,9},{21,13},{10,18... | collective-permute-start | bytes 2396168 | tf_op jit(solution)/shard_map/ppermute | solution.py:268
  8.6 35.6 %collective-permute-start.4 = (bf16[528,384]{1,0:T(8,128)(2,1)S(1)}, bf16[528,384]{1,0:T(8,128)(2,1)S(1)}, u32[]{:S(2)}, u32[]{:S(2)}) collective-permute-start(bf16[528,384]{1,0:T(8,128)(2,1)S(1)} %get-tuple-element.39), channel_id=1, source_target_pairs={{0,12},{4,8},{8,4},{12,0},{16,28},{20,24},{24,20},{28,16},{1,13},{... | collective-permute-start | bytes 1216520 | tf_op jit(solution)/shard_map/ppermute | solution.py:263
  13.9 36.3 %collective-permute-start.5 = (bf16[528,384]{1,0:T(8,128)(2,1)S(1)}, bf16[528,384]{1,0:T(8,128)(2,1)S(1)}, u32[]{:S(2)}, u32[]{:S(2)}) collective-permute-start(bf16[528,384]{1,0:T(8,128)(2,1)S(1)} %get-tuple-element.40), channel_id=1, source_target_pairs={{0,4},{4,0},{8,12},{12,8},{16,20},{20,16},{24,28},{28,24},{1,5},{5... | collective-permute-start | bytes 1216520 | tf_op jit(solution)/shard_map/ppermute | solution.py:263
  14.4 35.8 %collective-permute-start.6 = (bf16[528,384]{1,0:T(8,128)(2,1)S(1)}, bf16[528,384]{1,0:T(8,128)(2,1)S(1)}, u32[]{:S(2)}, u32[]{:S(2)}) collective-permute-start(bf16[528,384]{1,0:T(8,128)(2,1)S(1)} %get-tuple-element.42), channel_id=1, source_target_pairs={{0,28},{4,24},{24,4},{28,0},{1,29},{5,25},{25,5},{29,1},{2,30},{6,... | collective-permute-start | bytes 1216520 | tf_op jit(solution)/shard_map/ppermute | solution.py:263
  18.2 2.8 %copy-start.1 = (bf16[8,24,128,128]{3,2,1,0:T(8,128)(2,1)S(1)}, bf16[8,24,128,128]{3,2,1,0:T(8,128)(2,1)}, u32[]{:S(2)}) copy-start(bf16[8,24,128,128]{3,2,1,0:T(8,128)(2,1)} %ks_ref.1) | copy-start | bytes 18874372
  21.0 4.9 %copy-start.4 = (f32[128]{0:T(128)S(1)}, f32[128]{0:T(128)}, u32[]{:S(2)}) copy-start(f32[128]{0:T(128)} %param.9) | copy-start | bytes 1540
  28.8 15.1 %copy-start.6 = (f32[1024]{0:T(1024)S(1)}, f32[1024]{0:T(1024)}, u32[]{:S(2)}) copy-start(f32[1024]{0:T(1024)} %param.8) | copy-start | bytes 12292
  30.3 24.2 %collective-permute-start.3 = (bf16[528,384]{1,0:T(8,128)(2,1)S(1)}, bf16[528,384]{1,0:T(8,128)(2,1)S(1)}, u32[]{:S(2)}, u32[]{:S(2)}) collective-permute-start(bf16[528,384]{1,0:T(8,128)(2,1)S(1)} %get-tuple-element.38), channel_id=1, source_target_pairs={{0,20},{4,16},{8,4},{12,0},{16,28},{20,24},{24,12},{28,8},{1,21},{... | collective-permute-start | bytes 1216520 | tf_op jit(solution)/shard_map/ppermute | solution.py:275
  42.8 18.1 %collective-permute-start.2 = (bf16[528,384]{1,0:T(8,128)(2,1)S(1)}, bf16[528,384]{1,0:T(8,128)(2,1)S(1)}, u32[]{:S(2)}, u32[]{:S(2)}) collective-permute-start(bf16[528,384]{1,0:T(8,128)(2,1)S(1)} %get-tuple-element.37), channel_id=1, source_target_pairs={{0,24},{4,28},{8,12},{12,8},{16,20},{20,16},{24,0},{28,4},{1,25},{... | collective-permute-start | bytes 1216520 | tf_op jit(solution)/shard_map/ppermute | solution.py:274
  54.5 6.4 %copy-start = (f32[3,1024,128]{2,1,0:T(8,128)S(1)}, f32[3,1024,128]{2,1,0:T(8,128)}, u32[]{:S(2)}) copy-start(f32[3,1024,128]{2,1,0:T(8,128)} %right_ref.3) | copy-start | bytes 4718596
  63.5 15.7 %collective-permute-start.7 = (bf16[1024,384]{1,0:T(8,128)(2,1)S(1)}, bf16[1024,384]{1,0:T(8,128)(2,1)S(1)}, u32[]{:S(2)}, u32[]{:S(2)}) collective-permute-start(bf16[1024,384]{1,0:T(8,128)(2,1)S(1)} %get-tuple-element.48.refs_1_), channel_id=1, source_target_pairs={{8,16},{12,20},{16,8},{20,12},{9,17},{13,21},{17,9},{21,13},{10,18... | collective-permute-start | bytes 2359304 | tf_op jit(solution)/shard_map/ppermute | solution.py:268
  64.2 12.1 %collective-permute-start.8 = (bf16[512,384]{1,0:T(8,128)(2,1)S(1)}, bf16[512,384]{1,0:T(8,128)(2,1)S(1)}, u32[]{:S(2)}, u32[]{:S(2)}) collective-permute-start(bf16[512,384]{1,0:T(8,128)(2,1)S(1)} %get-tuple-element.50), channel_id=1, source_target_pairs={{0,8},{4,12},{8,0},{12,4},{16,24},{20,28},{24,16},{28,20},{1,9},{5... | collective-permute-start | bytes 1179656 | tf_op jit(solution)/shard_map/ppermute | solution.py:263
  65.7 26.3 %collective-permute-start.11 = (bf16[512,384]{1,0:T(8,128)(2,1)S(1)}, bf16[512,384]{1,0:T(8,128)(2,1)S(1)}, u32[]{:S(2)}, u32[]{:S(2)}) collective-permute-start(bf16[512,384]{1,0:T(8,128)(2,1)S(1)} %get-tuple-element.54), channel_id=1, source_target_pairs={{0,12},{4,8},{8,4},{12,0},{16,28},{20,24},{24,20},{28,16},{1,13},{... | collective-permute-start | bytes 1179656 | tf_op jit(solution)/shard_map/ppermute | solution.py:263
  66.7 33.7 %collective-permute-start.12 = (bf16[512,384]{1,0:T(8,128)(2,1)S(1)}, bf16[512,384]{1,0:T(8,128)(2,1)S(1)}, u32[]{:S(2)}, u32[]{:S(2)}) collective-permute-start(bf16[512,384]{1,0:T(8,128)(2,1)S(1)} %get-tuple-element.55), channel_id=1, source_target_pairs={{0,4},{4,0},{8,12},{12,8},{16,20},{20,16},{24,28},{28,24},{1,5},{5... | collective-permute-start | bytes 1179656 | tf_op jit(solution)/shard_map/ppermute | solution.py:263
  67.8 32.6 %collective-permute-start.13 = (bf16[512,384]{1,0:T(8,128)(2,1)S(1)}, bf16[512,384]{1,0:T(8,128)(2,1)S(1)}, u32[]{:S(2)}, u32[]{:S(2)}) collective-permute-start(bf16[512,384]{1,0:T(8,128)(2,1)S(1)} %get-tuple-element.57), channel_id=1, source_target_pairs={{0,28},{4,24},{24,4},{28,0},{1,29},{5,25},{25,5},{29,1},{2,30},{6,... | collective-permute-start | bytes 1179656 | tf_op jit(solution)/shard_map/ppermute | solution.py:263
  79.9 24.5 %collective-permute-start.10 = (bf16[512,384]{1,0:T(8,128)(2,1)S(1)}, bf16[512,384]{1,0:T(8,128)(2,1)S(1)}, u32[]{:S(2)}, u32[]{:S(2)}) collective-permute-start(bf16[512,384]{1,0:T(8,128)(2,1)S(1)} %get-tuple-element.53), channel_id=1, source_target_pairs={{0,20},{4,16},{8,4},{12,0},{16,28},{20,24},{24,12},{28,8},{1,21},{... | collective-permute-start | bytes 1179656 | tf_op jit(solution)/shard_map/ppermute | solution.py:275
  86.2 21.7 %collective-permute-start.9 = (bf16[512,384]{1,0:T(8,128)(2,1)S(1)}, bf16[512,384]{1,0:T(8,128)(2,1)S(1)}, u32[]{:S(2)}, u32[]{:S(2)}) collective-permute-start(bf16[512,384]{1,0:T(8,128)(2,1)S(1)} %get-tuple-element.52), channel_id=1, source_target_pairs={{0,24},{4,28},{8,12},{12,8},{16,20},{20,16},{24,0},{28,4},{1,25},{... | collective-permute-start | bytes 1179656 | tf_op jit(solution)/shard_map/ppermute | solution.py:274

commit v12 on v9

--- a/solution.py
+++ b/solution.py
@@ -235,15 +235,15 @@
     return (messages, last) if chosen is None else (messages + [last], chosen)
 
 
-def exchange(plan, readers, direct, own, full, chosen, begin, served, width):
+def exchange(plan, readers, direct, own, full, chosen, begin, near, served, width):
     sent = {k: lax.ppermute(m, "row", plan.pairs(k)) for k, m in direct.items()}
     if not plan.relayed:
         items = [(own, 0)] + [(sent[k], k) for k in plan.direct()]
         sums = begin(items[:3], None)
         return items, sums, None, sums[0]
     theirs = lax.ppermute(full, "row", [(i, i ^ 6) for i in INNER])
-    items = [(own, 0), (sent[1], 1), (sent[2], 2), (sent[3], 3)]
-    sums = begin(items[:3], theirs)
+    items = [(own, 0)] + [(sent[k], k) for k in near]
+    sums = begin(items[:3], theirs if chosen is None else None)
     (mine, near, far), chosen = relay(
         plan, readers, full, theirs, chosen, sums[0], served, width
     )
@@ -651,14 +651,14 @@
 
     direct, own, full = pack(plan, readers, right_side, onsite)
     dense = spread(tile_slot, ks_tiles, correlation_tiles, span, served)
-    items, sums, chosen, _ = exchange(plan, readers, direct, own, full, None, begin, served, width)
+    items, sums, chosen, _ = exchange(plan, readers, direct, own, full, None, begin, (1, 2, 3), served, width)
     level = levels(onsite)
     sums, last = partial(items, sums)
     image, full, direct, out = finish_first(
         plan, dense, last, energies, sums[0], right_side, level, own, readers
     )
 
-    items, begun, _, mark = exchange(plan, readers, direct, out, full, chosen, begin, served, width)
+    items, begun, _, mark = exchange(plan, readers, direct, out, full, chosen, begin, (2, 3, 1), served, width)
     lines = prepare(right_side, image, mark)
     _, weighted = couple(dense, last, energies, sums, mark)
     (value,), last = partial(items, begun)

time: 123 us -> 123 us (level)
  waiting for transfers between devices: 31.4 us -> 27.9 us
  starting transfers between devices: 32.8 us -> 36 us
    ppermute x2, waiting for transfers between devices: 9.46 us -> 5.52 us  [exchange(): lax.ppermute(far, 'row', [(i, i ^ (3 if i in INNER else 5)) for i in rang...]
    ppermute x8, waiting for transfers between devices: 12 us -> 15.3 us  [exchange(): sent = {k: lax.ppermute(m, 'row', plan.pairs(k)) for k, m in direct.items()}]
    ppermute x2, waiting for transfers between devices: 9.95 us -> 7.11 us  [exchange(): lax.ppermute(near, 'row', [(i, i ^ (1 if i in INNER else 6)) for i in ran...]
    ppermute x2, starting transfers between devices: 9.23 us -> 11.4 us  [exchange(): lax.ppermute(far, 'row', [(i, i ^ (3 if i in INNER else 5)) for i in rang...]
  transfers between devices with their start and end apart: 14 -> 14, of which waited for: 8 -> 6; matrix products, arithmetic and copies ran while one was open for 0% -> 0% of each run, Pallas kernels for 24% -> 24%
where the time goes in v12:
time: 123 us
  Pallas kernels  38.6 us (31%)
  starting transfers between devices  36 us (29%)
  waiting for transfers between devices  27.9 us (23%)
  blocking collectives  14 us (11%)
  local copies, waits for them, and re-layouts  5.74 us (5%)
    pallas_call x7, Pallas kernels, couple(): call(kernel, 'couple', [shape] * outs, [vmem()] * 2 + [pl.BlockSpec(memor...  20.5 us
    ppermute x8, starting transfers between devices, exchange(): sent = {k: lax.ppermute(m, 'row', plan.pairs(k)) for k, m in direct.items()}  19.4 us
    ppermute x8, waiting for transfers between devices, exchange(): sent = {k: lax.ppermute(m, 'row', plan.pairs(k)) for k, m in direct.items()}  15.3 us
    all_to_all x1, blocking collectives, body(): gathered = lax.all_to_all(gathered, ('row', 'col'), 0, 0)  14 us
    ppermute x2, starting transfers between devices, exchange(): lax.ppermute(far, 'row', [(i, i ^ (3 if i in INNER else 5)) for i in rang...  11.4 us
    ppermute x2, waiting for transfers between devices, exchange(): lax.ppermute(near, 'row', [(i, i ^ (1 if i in INNER else 6)) for i in ran...  7.11 us
    unnamed x14, local copies, waits for them, and re-layouts  5.74 us
    ppermute x2, waiting for transfers between devices, exchange(): lax.ppermute(far, 'row', [(i, i ^ (3 if i in INNER else 5)) for i in rang...  5.52 us
  transfers between devices with their start and end apart: 14, of which 6 were waited for; matrix products, arithmetic and copies ran while one was open for 0% of the time, Pallas kernels for 24%

profile of v12, /device:TPU:0, one launch (start us, length us, event | category | flops | bytes accessed | tf_op | source)
XLA Modules:
  0.0 123.1 jit_solution(16332551319016584671)
XLA Ops:
  0.6 0.7 copy-done.4
  1.3 0.7 copy-done.5
  2.0 2.0 %pack.1 = (bf16[528,384]{1,0:T(8,128)(2,1)S(1)}, bf16[528,384]{1,0:T(8,128)(2,1)S(1)}, bf16[528,384]{1,0:T(8,128)(2,1)S(1)}, bf16[528,384]{1,0:T(8,128)(2,1)S(1)...) custom-call(s32[1,4,7]{2,1,0:T(4,128)S(1)} %bitcast.12, f32[3,1024,128]{2,1,0:T(8,128)} %right_ref.3, ...), custom_call_target="tpu_custom_call" | custom-call | bytes 1048576 | tf_op jit(solution)/shard_map/pack/pallas_call | solution.py:154
  4.0 0.7 collective-permute-start
  4.7 3.0 %collective-permute-start.1 = (bf16[528,384]{1,0:T(8,128)(2,1)S(1)}, bf16[528,384]{1,0:T(8,128)(2,1)S(1)}, u32[]{:S(2)}, u32[]{:S(2)}) collective-permute-start(bf16[528,384]{1,0:T(8,128)(2,1)S(1)} %get-tuple-element.33), channel_id=1, source_target_pairs={{0,4},{4,0},{8,12},{12,8},{16,20},{20,16},{24,28},{28,24},{1,5},{5... | collective-permute-start | bytes 1216520 | tf_op jit(solution)/shard_map/ppermute | solution.py:239
  7.8 4.3 %collective-permute-start.2 = (bf16[528,384]{1,0:T(8,128)(2,1)S(1)}, bf16[528,384]{1,0:T(8,128)(2,1)S(1)}, u32[]{:S(2)}, u32[]{:S(2)}) collective-permute-start(bf16[528,384]{1,0:T(8,128)(2,1)S(1)} %get-tuple-element.34), channel_id=1, source_target_pairs={{0,8},{4,12},{8,0},{12,4},{16,24},{20,28},{24,16},{28,20},{1,9},{5... | collective-permute-start | bytes 1216520 | tf_op jit(solution)/shard_map/ppermute | solution.py:239
  12.1 0.0 collective-permute-start.5
  12.1 4.1 %collective-permute-start.6 = (bf16[528,384]{1,0:T(8,128)(2,1)S(1)}, bf16[528,384]{1,0:T(8,128)(2,1)S(1)}, u32[]{:S(2)}, u32[]{:S(2)}) collective-permute-start(bf16[528,384]{1,0:T(8,128)(2,1)S(1)} %get-tuple-element.40), channel_id=1, source_target_pairs={{0,28},{4,24},{24,4},{28,0},{1,29},{5,25},{25,5},{29,1},{2,30},{6,... | collective-permute-start | bytes 1216520 | tf_op jit(solution)/shard_map/ppermute | solution.py:239
  16.3 0.0 copy-start.1
  16.3 2.8 %copy-done.1 = bf16[8,24,128,128]{3,2,1,0:T(8,128)(2,1)S(1)} copy-done((bf16[8,24,128,128]{3,2,1,0:T(8,128)(2,1)S(1)}, bf16[8,24,128,128]{3,2,1,0:T(8,128)(2,1)}, u32[]{:S(2)}) %copy-start.1) | copy-done | bytes 6291480
  19.1 1.6 %copy-done.2 = bf16[8,8,128,128]{3,2,1,0:T(8,128)(2,1)S(1)} copy-done((bf16[8,8,128,128]{3,2,1,0:T(8,128)(2,1)S(1)}, bf16[8,8,128,128]{3,2,1,0:T(8,128)(2,1)}, u32[]{:S(2)}) %copy-start.2) | copy-done | bytes 2097176
  20.7 4.9 %spread.1.dense_ref = bf16[7,8,256,512]{3,2,1,0:T(8,128)(2,1)S(1)} custom-call(s32[8,24]{1,0:T(8,128)S(1)} %copy-done.6, bf16[8,24,128,128]{3,2,1,0:T(8,128)(2,1)S(1)} %copy-done.1, bf16[8,8,128,128]{3,2,1,0:T(8,128)(2,1)S(1)} %copy-done.2), custom_call_target="tpu_custom_call" | custom-call | bytes 16777216 | tf_op jit(solution)/shard_map/spread/pallas_call | solution.py:329
  25.5 0.0 collective-permute-done.1.refs_2_
  25.5 0.0 collective-permute-done.2.refs_3_
  25.6 0.0 collective-permute-done.refs_0_.refs_2_
  25.6 4.1 %couple.7 = (f32[8,128,384]{2,1,0:T(8,128)S(1)}, f32[8,128,384]{2,1,0:T(8,128)S(1)}) custom-call(bf16[7,8,256,512]{3,2,1,0:T(8,128)(2,1)S(1)} %spread.1.dense_ref, f32[1,128]{1,0:T(1,128)S(1)} %bitcast.3, bf16[1040,384]{1,0:T(8,128)(2,1)S(1)} %collective-permute-done.refs_0_.refs_2_, bf16[528,384]{1,0:T(8,128)(2,1)S(1)} %get-tuple-element.32.refs_1_.refs_4_, ...), custom_call_target="tpu_custom_call" | custom-call | flops 2415919104 | bytes 4194304 | tf_op jit(solution)/shard_map/couple/pallas_call | solution.py:387
  29.6 1.4 %relay.2 = (bf16[528,384]{1,0:T(8,128)(2,1)S(1)}, bf16[528,384]{1,0:T(8,128)(2,1)S(1)}, bf16[528,384]{1,0:T(8,128)(2,1)S(1)}, s32[3,4]{1,0:T(4,128)S(1)}) custom-call(s32[1,4,7]{2,1,0:T(4,128)S(1)} %bitcast.13, bf16[1040,384]{1,0:T(8,128)(2,1)S(1)} %get-tuple-element.31.refs_1_, bf16[1040,384]{1,0:T(8,128)(2,1)S(1)} %collective-permute-done.refs_0_.refs_2_, ...), custom_call_target="tpu_custom_call" | custom-call | bytes 1048576 | tf_op jit(solution)/shard_map/relay/pallas_call | solution.py:226
  31.1 4.9 %collective-permute-start.4 = (bf16[528,384]{1,0:T(8,128)(2,1)S(1)}, bf16[528,384]{1,0:T(8,128)(2,1)S(1)}, u32[]{:S(2)}, u32[]{:S(2)}) collective-permute-start(bf16[528,384]{1,0:T(8,128)(2,1)S(1)} %get-tuple-element.37), channel_id=1, source_target_pairs={{0,20},{4,16},{8,4},{12,0},{16,28},{20,24},{24,12},{28,8},{1,21},{... | collective-permute-start | bytes 1216520 | tf_op jit(solution)/shard_map/ppermute | solution.py:251
  36.0 1.3 %collective-permute-start.3 = (bf16[528,384]{1,0:T(8,128)(2,1)S(1)}, bf16[528,384]{1,0:T(8,128)(2,1)S(1)}, u32[]{:S(2)}, u32[]{:S(2)}) collective-permute-start(bf16[528,384]{1,0:T(8,128)(2,1)S(1)} %get-tuple-element.36), channel_id=1, source_target_pairs={{0,24},{4,28},{8,12},{12,8},{16,20},{20,16},{24,0},{28,4},{1,25},{... | collective-permute-start | bytes 1216520 | tf_op jit(solution)/shard_map/ppermute | solution.py:250
  37.4 0.2 levels.1.refs_3_
  37.6 0.0 collective-permute-done.5.refs_0_
  37.6 3.6 %collective-permute-done.6.refs_2_ = bf16[528,384]{1,0:T(8,128)(2,1)S(1)} collective-permute-done((bf16[528,384]{1,0:T(8,128)(2,1)S(1)}, bf16[528,384]{1,0:T(8,128)(2,1)S(1)}, u32[]{:S(2)}, u32[]{:S(2)}) %collective-permute-start.6) | collective-permute-done | bytes 405536 | tf_op jit(solution)/shard_map/ppermute | solution.py:239
  41.1 3.0 %couple.8 = (f32[8,128,384]{2,1,0:T(8,128)S(1)}, f32[8,128,384]{2,1,0:T(8,128)S(1)}) custom-call(bf16[7,8,256,512]{3,2,1,0:T(8,128)(2,1)S(1)} %spread.1.dense_ref, f32[1,128]{1,0:T(1,128)S(1)} %bitcast.4, bf16[528,384]{1,0:T(8,128)(2,1)S(1)} %collective-permute-done.5.refs_0_, bf16[528,384]{1,0:T(8,128)(2,1)S(1)} %get-tuple-element.39.refs_1_, ...), custom_call_target="tpu_custom_call" | custom-call | flops 1610612736 | bytes 4194304 | tf_op jit(solution)/shard_map/couple/pallas_call | solution.py:387
  44.2 5.5 %collective-permute-done.4.refs_0_ = bf16[528,384]{1,0:T(8,128)(2,1)S(1)} collective-permute-done((bf16[528,384]{1,0:T(8,128)(2,1)S(1)}, bf16[528,384]{1,0:T(8,128)(2,1)S(1)}, u32[]{:S(2)}, u32[]{:S(2)}) %collective-permute-start.4) | collective-permute-done | bytes 405536 | tf_op jit(solution)/shard_map/ppermute | solution.py:251
  49.7 1.8 %couple.9 = (f32[8,128,384]{2,1,0:T(8,128)S(1)}, f32[8,128,384]{2,1,0:T(8,128)S(1)}) custom-call(bf16[7,8,256,512]{3,2,1,0:T(8,128)(2,1)S(1)} %spread.1.dense_ref, f32[1,128]{1,0:T(1,128)S(1)} %bitcast.5, bf16[528,384]{1,0:T(8,128)(2,1)S(1)} %collective-permute-done.4.refs_0_, f32[8,128,384]{2,1,0:T(8,128)S(1)} %get-tuple-element.42.refs_1_, ...), custom_call_target="tpu_custom_call" | custom-call | flops 805306368 | bytes 4194304 | tf_op jit(solution)/shard_map/couple/pallas_call | solution.py:387
  51.5 5.4 %collective-permute-done.3.refs_0_.refs_1_ = bf16[528,384]{1,0:T(8,128)(2,1)S(1)} collective-permute-done((bf16[528,384]{1,0:T(8,128)(2,1)S(1)}, bf16[528,384]{1,0:T(8,128)(2,1)S(1)}, u32[]{:S(2)}, u32[]{:S(2)}) %collective-permute-start.3) | collective-permute-done | bytes 405536 | tf_op jit(solution)/shard_map/ppermute | solution.py:250
  56.9 2.6 %finish_first.1 = (f32[8,128,384]{2,1,0:T(8,128)S(1)}, bf16[1024,384]{1,0:T(8,128)(2,1)S(1)}, bf16[512,384]{1,0:T(8,128)(2,1)S(1)}, bf16[512,384]{1,0:T(8,128)(2...) custom-call(bf16[7,8,256,512]{3,2,1,0:T(8,128)(2,1)S(1)} %spread.1.dense_ref, ...), custom_call_target="tpu_custom_call" | custom-call | flops 805306368 | bytes 8388608 | tf_op jit(solution)/shard_map/finish_first/pallas_call | solution.py:433
  59.5 0.7 collective-permute-start.7
  60.2 0.1 collective-permute-start.8
  60.3 2.0 %collective-permute-start.9 = (bf16[512,384]{1,0:T(8,128)(2,1)S(1)}, bf16[512,384]{1,0:T(8,128)(2,1)S(1)}, u32[]{:S(2)}, u32[]{:S(2)}) collective-permute-start(bf16[512,384]{1,0:T(8,128)(2,1)S(1)} %get-tuple-element.49), channel_id=1, source_target_pairs={{0,12},{4,8},{8,4},{12,0},{16,28},{20,24},{24,20},{28,16},{1,13},{... | collective-permute-start | bytes 1179656 | tf_op jit(solution)/shard_map/ppermute | solution.py:239
  62.2 1.5 %collective-permute-start.12 = (bf16[512,384]{1,0:T(8,128)(2,1)S(1)}, bf16[512,384]{1,0:T(8,128)(2,1)S(1)}, u32[]{:S(2)}, u32[]{:S(2)}) collective-permute-start(bf16[512,384]{1,0:T(8,128)(2,1)S(1)} %get-tuple-element.53), channel_id=1, source_target_pairs={{0,4},{4,0},{8,12},{12,8},{16,20},{20,16},{24,28},{28,24},{1,5},{5... | collective-permute-start | bytes 1179656 | tf_op jit(solution)/shard_map/ppermute | solution.py:239
  63.7 4.3 %collective-permute-start.13 = (bf16[512,384]{1,0:T(8,128)(2,1)S(1)}, bf16[512,384]{1,0:T(8,128)(2,1)S(1)}, u32[]{:S(2)}, u32[]{:S(2)}) collective-permute-start(bf16[512,384]{1,0:T(8,128)(2,1)S(1)} %get-tuple-element.55), channel_id=1, source_target_pairs={{0,28},{4,24},{24,4},{28,0},{1,29},{5,25},{25,5},{29,1},{2,30},{6,... | collective-permute-start | bytes 1179656 | tf_op jit(solution)/shard_map/ppermute | solution.py:239
  68.0 4.2 %collective-permute-done.8.refs_1_ = bf16[512,384]{1,0:T(8,128)(2,1)S(1)} collective-permute-done((bf16[512,384]{1,0:T(8,128)(2,1)S(1)}, bf16[512,384]{1,0:T(8,128)(2,1)S(1)}, u32[]{:S(2)}, u32[]{:S(2)}) %collective-permute-start.8) | collective-permute-done | bytes 393248 | tf_op jit(solution)/shard_map/ppermute | solution.py:239
  72.3 7.4 %collective-permute-done.9.refs_2_ = bf16[512,384]{1,0:T(8,128)(2,1)S(1)} collective-permute-done((bf16[512,384]{1,0:T(8,128)(2,1)S(1)}, bf16[512,384]{1,0:T(8,128)(2,1)S(1)}, u32[]{:S(2)}, u32[]{:S(2)}) %collective-permute-start.9) | collective-permute-done | bytes 393248 | tf_op jit(solution)/shard_map/ppermute | solution.py:239
  79.7 4.0 %couple.10.refs_3_ = f32[8,128,384]{2,1,0:T(8,128)S(1)} custom-call(bf16[7,8,256,512]{3,2,1,0:T(8,128)(2,1)S(1)} %spread.1.dense_ref, f32[1,128]{1,0:T(1,128)S(1)} %bitcast.7, bf16[512,384]{1,0:T(8,128)(2,1)S(1)} %get-tuple-element.47.refs_0_, bf16[512,384]{1,0:T(8,128)(2,1)S(1)} %collective-permute-done.8.refs_1_, ...), custom_call_target="tpu_custom_call" | custom-call | flops 2415919104 | bytes 4194304 | tf_op jit(solution)/shard_map/couple/pallas_call | solution.py:387
  83.7 0.0 collective-permute-done.7.refs_2_
  83.8 0.7 relay.3
  84.5 6.4 %collective-permute-start.11 = (bf16[512,384]{1,0:T(8,128)(2,1)S(1)}, bf16[512,384]{1,0:T(8,128)(2,1)S(1)}, u32[]{:S(2)}, u32[]{:S(2)}) collective-permute-start(bf16[512,384]{1,0:T(8,128)(2,1)S(1)} %get-tuple-element.52), channel_id=1, source_target_pairs={{0,20},{4,16},{8,4},{12,0},{16,28},{20,24},{24,12},{28,8},{1,21},{... | collective-permute-start | bytes 1179656 | tf_op jit(solution)/shard_map/ppermute | solution.py:251
  90.9 2.5 %collective-permute-start.10 = (bf16[512,384]{1,0:T(8,128)(2,1)S(1)}, bf16[512,384]{1,0:T(8,128)(2,1)S(1)}, u32[]{:S(2)}, u32[]{:S(2)}) collective-permute-start(bf16[512,384]{1,0:T(8,128)(2,1)S(1)} %get-tuple-element.51), channel_id=1, source_target_pairs={{0,24},{4,28},{8,12},{12,8},{16,20},{20,16},{24,0},{28,4},{1,25},{... | collective-permute-start | bytes 1179656 | tf_op jit(solution)/shard_map/ppermute | solution.py:250
  93.4 1.3 %prepare.1.refs_6_ = f32[8,384]{1,0:T(8,128)S(1)} custom-call(f32[3,1024,128]{2,1,0:T(8,128)S(1)} %copy-done, f32[8,128,384]{2,1,0:T(8,128)S(1)} %get-tuple-element.45.image_ref.refs_4_, bf16[512,384]{1,0:T(8,128)(2,1)S(1)} %get-tuple-element.54.refs_1_.refs_0_._), custom_call_target="tpu_custom_call" | custom-call | flops 8388608 | bytes 4194304 | tf_op jit(solution)/shard_map/prepare/pallas_call | solution.py:489
  94.7 3.0 %couple.13 = (f32[8,128,384]{2,1,0:T(8,128)}, f32[8,128,384]{2,1,0:T(8,128)S(1)}) custom-call(bf16[7,8,256,512]{3,2,1,0:T(8,128)(2,1)S(1)} %spread.1.dense_ref, f32[1,128]{1,0:T(1,128)S(1)} %bitcast.8, bf16[512,384]{1,0:T(8,128)(2,1)S(1)} %get-tuple-element.54.refs_1_.refs_0_._, bf16[528,384]{1,0:T(8,128)(2,1)S(1)} %collective-permute-done.3.refs_0_.refs_1_, ...), custom_call_target="tpu_custom_call" | custom-call | flops 805306368 | bytes 4194304 | tf_op jit(solution)/shard_map/couple/pallas_call | solution.py:387
  97.7 2.9 %couple.11.refs_1_ = f32[8,128,384]{2,1,0:T(8,128)S(1)} custom-call(bf16[7,8,256,512]{3,2,1,0:T(8,128)(2,1)S(1)} %spread.1.dense_ref, f32[1,128]{1,0:T(1,128)S(1)} %bitcast.9, bf16[512,384]{1,0:T(8,128)(2,1)S(1)} %collective-permute-done.12.refs_0_, bf16[512,384]{1,0:T(8,128)(2,1)S(1)} %get-tuple-element.54.refs_1_.refs_0_._, ...), custom_call_target="tpu_custom_call" | custom-call | flops 1610612736 | bytes 4194304 | tf_op jit(solution)/shard_map/couple/pallas_call | solution.py:387
  100.6 0.0 collective-permute-done.11.refs_0_
  100.6 1.8 %couple.12.refs_1_ = f32[8,128,384]{2,1,0:T(8,128)S(1)} custom-call(bf16[7,8,256,512]{3,2,1,0:T(8,128)(2,1)S(1)} %spread.1.dense_ref, f32[1,128]{1,0:T(1,128)S(1)} %bitcast.10, bf16[512,384]{1,0:T(8,128)(2,1)S(1)} %collective-permute-done.11.refs_0_, f32[8,128,384]{2,1,0:T(8,128)S(1)} %couple.11.refs_1_), custom_call_target="tpu_custom_call" | custom-call | flops 805306368 | bytes 4194304 | tf_op jit(solution)/shard_map/couple/pallas_call | solution.py:387
  102.4 1.8 %collective-permute-done.10.refs_0_ = bf16[512,384]{1,0:T(8,128)(2,1)S(1)} collective-permute-done((bf16[512,384]{1,0:T(8,128)(2,1)S(1)}, bf16[512,384]{1,0:T(8,128)(2,1)S(1)}, u32[]{:S(2)}, u32[]{:S(2)}) %collective-permute-start.10) | collective-permute-done | bytes 393248 | tf_op jit(solution)/shard_map/ppermute | solution.py:250
  104.2 2.4 %finish_second.1 = (f32[8,128,384]{2,1,0:T(8,128)S(1)}, f32[32,8,128]{2,1,0:T(8,128)S(1)}) custom-call(bf16[7,8,256,512]{3,2,1,0:T(8,128)(2,1)S(1)} %spread.1.dense_ref, f32[1,128]{1,0:T(1,128)S(1)} %bitcast.11, bf16[512,384]{1,0:T(8,128)(2,1)S(1)} %collective-permute-done.10.refs_0_, f32[8,128,384]{2,1,0:T(8,128)S(1)} %couple.12.refs_1_, ...), custom_call_target="tpu_custom_call" | custom-call | flops 805306368 | bytes 8388608 | tf_op jit(solution)/shard_map/finish_second/pallas_call | solution.py:546
  106.5 14.0 %all_to_all.5.gathered_ref = f32[32,8,128]{2,1,0:T(8,128)S(1)} all-to-all(f32[32,8,128]{2,1,0:T(8,128)S(1)} %get-tuple-element.59), channel_id=1, replica_groups=mesh['row'=8,'col'=4] {'row','col'}, dimensions={0} | all-to-all | bytes 262144 | tf_op jit(solution)/shard_map/all_to_all | solution.py:668
  120.5 2.6 %final.1 = (f32[3,1024,128]{2,1,0:T(8,128)}, f32[3,1024,128]{2,1,0:T(8,128)}) custom-call(f32[3,1024,128]{2,1,0:T(8,128)S(1)} %copy-done, f32[8,128,384]{2,1,0:T(8,128)S(1)} %get-tuple-element.45.image_ref.refs_4_, f32[8,128,384]{2,1,0:T(8,128)S(1)} %get-tuple-element.58.later_ref, f32[32,8,128]{2,1,0:T(8,128)S(1)} %all_to_all.5.gathered_ref), custom_call_target="tpu_custom_call" | custom-call | tf_op jit(solution)/shard_map/final/pallas_call | solution.py:622
  (11 shorter events, 0.0 us)
Async XLA Ops:
  0.6 0.7 copy-start.4
  1.3 0.7 copy-start.5
  2.0 14.3 %copy-start.6 = (s32[8,24]{1,0:T(8,128)S(1)}, s32[8,24]{1,0:T(8,128)}, u32[]{:S(2)}) copy-start(s32[8,24]{1,0:T(8,128)} %slot_ref.1) | copy-start | bytes 2308
  4.0 21.5 %collective-permute-start = (bf16[1040,384]{1,0:T(8,128)(2,1)S(1)}, bf16[1040,384]{1,0:T(8,128)(2,1)S(1)}, u32[]{:S(2)}, u32[]{:S(2)}) collective-permute-start(bf16[1040,384]{1,0:T(8,128)(2,1)S(1)} %get-tuple-element.31.refs_1_), channel_id=1, source_target_pairs={{8,16},{12,20},{16,8},{20,12},{9,17},{13,21},{17,9},{21,13},{10,18... | collective-permute-start | bytes 2396168 | tf_op jit(solution)/shard_map/ppermute | solution.py:244
  4.7 20.8 %collective-permute-start.1 = (bf16[528,384]{1,0:T(8,128)(2,1)S(1)}, bf16[528,384]{1,0:T(8,128)(2,1)S(1)}, u32[]{:S(2)}, u32[]{:S(2)}) collective-permute-start(bf16[528,384]{1,0:T(8,128)(2,1)S(1)} %get-tuple-element.33), channel_id=1, source_target_pairs={{0,4},{4,0},{8,12},{12,8},{16,20},{20,16},{24,28},{28,24},{1,5},{5... | collective-permute-start | bytes 1216520 | tf_op jit(solution)/shard_map/ppermute | solution.py:239
  7.8 17.8 %collective-permute-start.2 = (bf16[528,384]{1,0:T(8,128)(2,1)S(1)}, bf16[528,384]{1,0:T(8,128)(2,1)S(1)}, u32[]{:S(2)}, u32[]{:S(2)}) collective-permute-start(bf16[528,384]{1,0:T(8,128)(2,1)S(1)} %get-tuple-element.34), channel_id=1, source_target_pairs={{0,8},{4,12},{8,0},{12,4},{16,24},{20,28},{24,16},{28,20},{1,9},{5... | collective-permute-start | bytes 1216520 | tf_op jit(solution)/shard_map/ppermute | solution.py:239
  12.1 25.4 %collective-permute-start.5 = (bf16[528,384]{1,0:T(8,128)(2,1)S(1)}, bf16[528,384]{1,0:T(8,128)(2,1)S(1)}, u32[]{:S(2)}, u32[]{:S(2)}) collective-permute-start(bf16[528,384]{1,0:T(8,128)(2,1)S(1)} %get-tuple-element.38), channel_id=1, source_target_pairs={{0,12},{4,8},{8,4},{12,0},{16,28},{20,24},{24,20},{28,16},{1,13},{... | collective-permute-start | bytes 1216520 | tf_op jit(solution)/shard_map/ppermute | solution.py:239
  12.1 29.0 %collective-permute-start.6 = (bf16[528,384]{1,0:T(8,128)(2,1)S(1)}, bf16[528,384]{1,0:T(8,128)(2,1)S(1)}, u32[]{:S(2)}, u32[]{:S(2)}) collective-permute-start(bf16[528,384]{1,0:T(8,128)(2,1)S(1)} %get-tuple-element.40), channel_id=1, source_target_pairs={{0,28},{4,24},{24,4},{28,0},{1,29},{5,25},{25,5},{29,1},{2,30},{6,... | collective-permute-start | bytes 1216520 | tf_op jit(solution)/shard_map/ppermute | solution.py:239
  16.3 2.8 %copy-start.1 = (bf16[8,24,128,128]{3,2,1,0:T(8,128)(2,1)S(1)}, bf16[8,24,128,128]{3,2,1,0:T(8,128)(2,1)}, u32[]{:S(2)}) copy-start(bf16[8,24,128,128]{3,2,1,0:T(8,128)(2,1)} %ks_ref.1) | copy-start | bytes 18874372
  19.1 1.6 %copy-start.2 = (bf16[8,8,128,128]{3,2,1,0:T(8,128)(2,1)S(1)}, bf16[8,8,128,128]{3,2,1,0:T(8,128)(2,1)}, u32[]{:S(2)}) copy-start(bf16[8,8,128,128]{3,2,1,0:T(8,128)(2,1)} %correlation_ref.1) | copy-start | bytes 6291460
  20.7 4.9 %copy-start.3 = (f32[128]{0:T(128)S(1)}, f32[128]{0:T(128)}, u32[]{:S(2)}) copy-start(f32[128]{0:T(128)} %param.9) | copy-start | bytes 1540
  31.1 18.6 %collective-permute-start.4 = (bf16[528,384]{1,0:T(8,128)(2,1)S(1)}, bf16[528,384]{1,0:T(8,128)(2,1)S(1)}, u32[]{:S(2)}, u32[]{:S(2)}) collective-permute-start(bf16[528,384]{1,0:T(8,128)(2,1)S(1)} %get-tuple-element.37), channel_id=1, source_target_pairs={{0,20},{4,16},{8,4},{12,0},{16,28},{20,24},{24,12},{28,8},{1,21},{... | collective-permute-start | bytes 1216520 | tf_op jit(solution)/shard_map/ppermute | solution.py:251
  36.0 20.8 %collective-permute-start.3 = (bf16[528,384]{1,0:T(8,128)(2,1)S(1)}, bf16[528,384]{1,0:T(8,128)(2,1)S(1)}, u32[]{:S(2)}, u32[]{:S(2)}) collective-permute-start(bf16[528,384]{1,0:T(8,128)(2,1)S(1)} %get-tuple-element.36), channel_id=1, source_target_pairs={{0,24},{4,28},{8,12},{12,8},{16,20},{20,16},{24,0},{28,4},{1,25},{... | collective-permute-start | bytes 1216520 | tf_op jit(solution)/shard_map/ppermute | solution.py:250
  49.7 7.2 %copy-start = (f32[3,1024,128]{2,1,0:T(8,128)S(1)}, f32[3,1024,128]{2,1,0:T(8,128)}, u32[]{:S(2)}) copy-start(f32[3,1024,128]{2,1,0:T(8,128)} %right_ref.3) | copy-start | bytes 4718596
  59.5 24.3 %collective-permute-start.7 = (bf16[1024,384]{1,0:T(8,128)(2,1)S(1)}, bf16[1024,384]{1,0:T(8,128)(2,1)S(1)}, u32[]{:S(2)}, u32[]{:S(2)}) collective-permute-start(bf16[1024,384]{1,0:T(8,128)(2,1)S(1)} %get-tuple-element.46.refs_1_), channel_id=1, source_target_pairs={{8,16},{12,20},{16,8},{20,12},{9,17},{13,21},{17,9},{21,13},{10,18... | collective-permute-start | bytes 2359304 | tf_op jit(solution)/shard_map/ppermute | solution.py:244
  60.2 12.1 %collective-permute-start.8 = (bf16[512,384]{1,0:T(8,128)(2,1)S(1)}, bf16[512,384]{1,0:T(8,128)(2,1)S(1)}, u32[]{:S(2)}, u32[]{:S(2)}) collective-permute-start(bf16[512,384]{1,0:T(8,128)(2,1)S(1)} %get-tuple-element.48), channel_id=1, source_target_pairs={{0,8},{4,12},{8,0},{12,4},{16,24},{20,28},{24,16},{28,20},{1,9},{5... | collective-permute-start | bytes 1179656 | tf_op jit(solution)/shard_map/ppermute | solution.py:239
  60.3 19.5 %collective-permute-start.9 = (bf16[512,384]{1,0:T(8,128)(2,1)S(1)}, bf16[512,384]{1,0:T(8,128)(2,1)S(1)}, u32[]{:S(2)}, u32[]{:S(2)}) collective-permute-start(bf16[512,384]{1,0:T(8,128)(2,1)S(1)} %get-tuple-element.49), channel_id=1, source_target_pairs={{0,12},{4,8},{8,4},{12,0},{16,28},{20,24},{24,20},{28,16},{1,13},{... | collective-permute-start | bytes 1179656 | tf_op jit(solution)/shard_map/ppermute | solution.py:239
  62.2 35.5 %collective-permute-start.12 = (bf16[512,384]{1,0:T(8,128)(2,1)S(1)}, bf16[512,384]{1,0:T(8,128)(2,1)S(1)}, u32[]{:S(2)}, u32[]{:S(2)}) collective-permute-start(bf16[512,384]{1,0:T(8,128)(2,1)S(1)} %get-tuple-element.53), channel_id=1, source_target_pairs={{0,4},{4,0},{8,12},{12,8},{16,20},{20,16},{24,28},{28,24},{1,5},{5... | collective-permute-start | bytes 1179656 | tf_op jit(solution)/shard_map/ppermute | solution.py:239
  63.7 34.0 %collective-permute-start.13 = (bf16[512,384]{1,0:T(8,128)(2,1)S(1)}, bf16[512,384]{1,0:T(8,128)(2,1)S(1)}, u32[]{:S(2)}, u32[]{:S(2)}) collective-permute-start(bf16[512,384]{1,0:T(8,128)(2,1)S(1)} %get-tuple-element.55), channel_id=1, source_target_pairs={{0,28},{4,24},{24,4},{28,0},{1,29},{5,25},{25,5},{29,1},{2,30},{6,... | collective-permute-start | bytes 1179656 | tf_op jit(solution)/shard_map/ppermute | solution.py:239
  84.5 16.2 %collective-permute-start.11 = (bf16[512,384]{1,0:T(8,128)(2,1)S(1)}, bf16[512,384]{1,0:T(8,128)(2,1)S(1)}, u32[]{:S(2)}, u32[]{:S(2)}) collective-permute-start(bf16[512,384]{1,0:T(8,128)(2,1)S(1)} %get-tuple-element.52), channel_id=1, source_target_pairs={{0,20},{4,16},{8,4},{12,0},{16,28},{20,24},{24,12},{28,8},{1,21},{... | collective-permute-start | bytes 1179656 | tf_op jit(solution)/shard_map/ppermute | solution.py:251
  90.9 13.3 %collective-permute-start.10 = (bf16[512,384]{1,0:T(8,128)(2,1)S(1)}, bf16[512,384]{1,0:T(8,128)(2,1)S(1)}, u32[]{:S(2)}, u32[]{:S(2)}) collective-permute-start(bf16[512,384]{1,0:T(8,128)(2,1)S(1)} %get-tuple-element.51), channel_id=1, source_target_pairs={{0,24},{4,28},{8,12},{12,8},{16,20},{20,16},{24,0},{28,4},{1,25},{... | collective-permute-start | bytes 1179656 | tf_op jit(solution)/shard_map/ppermute | solution.py:250

commit v13 on v10

--- a/solution.py
+++ b/solution.py
@@ -10,6 +10,7 @@
 MIB = 2**20
 EXTRA = 16
 BATCH = 2
+EARLY = 1 << 34
 
 
 def shifted(array, axis, by):
@@ -73,11 +74,11 @@
         return jnp.minimum(value, self.span - 1) if self.relayed else value
 
     def early(self):
-        return [2, 3] if self.relayed else self.direct()
+        return [2] if self.relayed else self.direct()
 
     def direct(self):
         if self.relayed:
-            return [2, 3, 1, 7]
+            return [1, 2, 3, 7]
         far = range(self.middle, 0, -1)
         return [by for f in far for by in (f, -f)]
 
@@ -171,25 +172,33 @@
     return dict(zip(keys, messages)), full
 
 
+def hand_on(array, flops=0):
+    def kernel(array_ref, same_ref):
+        del array_ref, same_ref
+
+    return pl.pallas_call(
+        kernel,
+        out_shape=jax.ShapeDtypeStruct(array.shape, array.dtype),
+        in_specs=[vmem()],
+        out_specs=vmem(),
+        input_output_aliases={0: 0},
+        compiler_params=pltpu.CompilerParams(vmem_limit_bytes=12 * MIB),
+        cost_estimate=pl.CostEstimate(flops=flops, bytes_accessed=0, transcendentals=0),
+        name="hand_on",
+    )(array)
+
+
 def deal(plan, readers, full, served, width):
-    keys = [key for key in plan.direct() if key not in plan.early()]
-    lanes = full.shape[1]
-
-    def kernel(readers_ref, full_ref, same_ref, *messages):
+    keys = plan.direct()
+
+    def kernel(readers_ref, full_ref, *messages):
         fill(plan, keys, readers_ref, full_ref, messages, width)
 
-    message = jax.ShapeDtypeStruct((served * width + EXTRA, lanes), jnp.bfloat16)
-    full, *messages, own = pl.pallas_call(
-        kernel,
-        out_shape=[jax.ShapeDtypeStruct(full.shape, full.dtype)] + [message] * (len(keys) + 1),
-        in_specs=[smem(), vmem()],
-        out_specs=[vmem()] * (len(keys) + 2),
-        input_output_aliases={1: 0},
-        compiler_params=pltpu.CompilerParams(vmem_limit_bytes=12 * MIB),
-        cost_estimate=pl.CostEstimate(flops=0, bytes_accessed=MIB, transcendentals=0),
-        name="deal",
-    )(readers, full)
-    return dict(zip(keys, messages)), own, full
+    message = jax.ShapeDtypeStruct((served * width + EXTRA, full.shape[1]), jnp.bfloat16)
+    *messages, own = call(kernel, "deal", [message] * (len(keys) + 1), [smem(), vmem()])(
+        readers, full
+    )
+    return dict(zip(keys, messages)), own
 
 
 def fill(plan, keys, readers_ref, rounded, messages, width):
@@ -259,14 +268,21 @@
     return (messages, last) if chosen is None else (messages + [last], chosen)
 
 
-def exchange(plan, readers, direct, own, full, chosen, begin, served, width):
-    sent = {k: lax.ppermute(m, "row", plan.pairs(k)) for k, m in direct.items()}
+def exchange(plan, readers, early, direct, own, full, chosen, begin, near, served, width):
+    sent = {k: lax.ppermute(m, "row", plan.pairs(k)) for k, m in direct.items() if k not in early}
     if not plan.relayed:
+        sent |= {k: lax.ppermute(m, "row", plan.pairs(k)) for k, m in early.items()}
         items = [(own, 0)] + [(sent[k], k) for k in plan.direct()]
         sums = begin(items[:3])
         return items, sums, None, sums[0]
     theirs = lax.ppermute(full, "row", [(i, i ^ 6) for i in INNER])
-    items = [(own, 0), (sent[2], 2), (sent[3], 3), (sent[1], 1)]
+    for k, m in early.items():
+        inward = [(i, j) for i, j in plan.pairs(k) if j in INNER]
+        outward = [(i, j) for i, j in plan.pairs(k) if i in INNER]
+        first = hand_on(lax.ppermute(m, "row", inward), EARLY)
+        sent[k] = (first, lax.ppermute(direct[k], "row", outward))
+    items = [(own, 0)]
+    items += [(sent[k], (k, k) if k in early else k) for k in near]
     sums = begin(items[:3])
     (mine, near, far), chosen = relay(
         plan, readers, full, theirs, chosen, sums[0], served, width
@@ -674,17 +690,21 @@
         return sums, Vectors(plan, items[-1:])
 
     early, full = pack(plan, readers, right_side, onsite)
-    direct, own, full = deal(plan, readers, full, served, width)
-    direct = early | direct
+    full = hand_on(full)
+    direct, own = deal(plan, readers, full, served, width)
     dense = spread(tile_slot, ks_tiles, correlation_tiles, span, served)
-    items, sums, chosen, _ = exchange(plan, readers, direct, own, full, None, begin(8), served, width)
+    items, sums, chosen, _ = exchange(
+        plan, readers, early, direct, own, full, None, begin(1), (2, 1, 3), served, width
+    )
     level = levels(onsite)
     sums, last = partial(items, sums)
     image, full, direct, out = finish_first(
         plan, dense, last, energies, sums[0], right_side, level, own, readers
     )
 
-    items, begun, _, mark = exchange(plan, readers, direct, out, full, chosen, begin(1), served, width)
+    items, begun, _, mark = exchange(
+        plan, readers, {}, direct, out, full, chosen, begin(1), (2, 3, 1), served, width
+    )
     lines = prepare(right_side, image, mark)
     _, weighted = couple(dense, last, energies, sums, mark)
     (value,), last = partial(items, begun)

time: 126 us -> 124 us (0.984)
  starting transfers between devices: 40.1 us -> 38.4 us
    ppermute x2, starting transfers between devices: 14.3 us -> 9.99 us  [exchange(): lax.ppermute(far, 'row', [(i, i ^ (3 if i in INNER else 5)) for i in rang...]
    ppermute x8 -> x9, starting transfers between devices: 20.4 us -> 23.8 us  [the longest x7 17.4 us: exchange(): lax.ppermute(m, 'row', plan.pairs(k))]
    ppermute x2, waiting for transfers between devices: 7.01 us -> 9.81 us  [exchange(): lax.ppermute(far, 'row', [(i, i ^ (3 if i in INNER else 5)) for i in rang...]
    ppermute x2, waiting for transfers between devices: 8.63 us -> 5.99 us  [exchange(): lax.ppermute(near, 'row', [(i, i ^ (1 if i in INNER else 6)) for i in ran...]
    ppermute x8 -> x9, waiting for transfers between devices: 13.5 us -> 12.5 us  [the longest x7 12.5 us: exchange(): lax.ppermute(m, 'row', plan.pairs(k))]
    unnamed x14 -> x18, local copies, waits for them, and re-layouts: 4.3 us -> 4.18 us
  transfers between devices with their start and end apart: 14 -> 15, of which waited for: 7 -> 7; matrix products, arithmetic and copies ran while one was open for 0% -> 0% of each run, Pallas kernels for 24% -> 24%
where the time goes in v13:
time: 124 us
  Pallas kernels  39.2 us (32%)
  starting transfers between devices  38.4 us (31%)
  waiting for transfers between devices  28.3 us (23%)
  blocking collectives  12.8 us (10%)
  local copies, waits for them, and re-layouts  4.18 us (3%)
    pallas_call x7, Pallas kernels, couple(): call(kernel, 'couple', [shape] * outs, [vmem()] * 2 + [pl.BlockSpec(memor...  20.5 us
    ppermute x7, starting transfers between devices, exchange(): lax.ppermute(m, 'row', plan.pairs(k))  17.4 us
    all_to_all x1, blocking collectives, body(): gathered = lax.all_to_all(gathered, ('row', 'col'), 0, 0)  12.8 us
    ppermute x7, waiting for transfers between devices, exchange(): lax.ppermute(m, 'row', plan.pairs(k))  12.5 us
    ppermute x2, starting transfers between devices, exchange(): lax.ppermute(far, 'row', [(i, i ^ (3 if i in INNER else 5)) for i in rang...  9.99 us
    ppermute x2, waiting for transfers between devices, exchange(): lax.ppermute(far, 'row', [(i, i ^ (3 if i in INNER else 5)) for i in rang...  9.81 us
    ppermute x2, waiting for transfers between devices, exchange(): lax.ppermute(near, 'row', [(i, i ^ (1 if i in INNER else 6)) for i in ran...  5.99 us
    ppermute x1, starting transfers between devices, exchange(): first = hand_on(lax.ppermute(m, 'row', inward), EARLY)  5.08 us
  transfers between devices with their start and end apart: 15, of which 7 were waited for; matrix products, arithmetic and copies ran while one was open for 0% of the time, Pallas kernels for 24%

profile of v13, /device:TPU:0, one launch (start us, length us, event | category | flops | bytes accessed | tf_op | source)
XLA Modules:
  0.0 123.8 jit_solution(1694777926238149131)
XLA Ops:
  0.6 0.0 copy-start.3
  0.6 0.7 copy-done.3
  1.3 0.7 copy-done.6
  2.0 1.8 %pack.1 = (bf16[528,384]{1,0:T(8,128)(2,1)S(1)}, bf16[1040,384]{1,0:T(8,128)(2,1)S(1)}) custom-call(s32[1,4,7]{2,1,0:T(4,128)S(1)} %bitcast.3, f32[3,1024,128]{2,1,0:T(8,128)} %right_ref.3, f32[8,128]{1,0:T(8,128)S(1)} %bitcast.17), custom_call_target="tpu_custom_call" | custom-call | bytes 1048576 | tf_op jit(solution)/shard_map/pack/pallas_call | solution.py:158
  3.9 0.0 copy-start.2
  3.9 0.0 copy-start.8
  3.9 5.1 %collective-permute-start.1 = (bf16[528,384]{1,0:T(8,128)(2,1)S(1)}, bf16[528,384]{1,0:T(8,128)(2,1)S(1)}, u32[]{:S(2)}, u32[]{:S(2)}) collective-permute-start(bf16[528,384]{1,0:T(8,128)(2,1)S(1)} %get-tuple-element.34), channel_id=1, source_target_pairs={{0,8},{4,12},{24,16},{28,20},{1,9},{5,13},{25,17},{29,21},{2,10},{... | collective-permute-start | bytes 1216520 | tf_op jit(solution)/shard_map/ppermute | solution.py:282
  9.0 0.7 collective-permute-start
  9.7 0.8 deal.1
  10.5 1.3 %collective-permute-start.2 = (bf16[528,384]{1,0:T(8,128)(2,1)S(1)}, bf16[528,384]{1,0:T(8,128)(2,1)S(1)}, u32[]{:S(2)}, u32[]{:S(2)}) collective-permute-start(bf16[528,384]{1,0:T(8,128)(2,1)S(1)} %get-tuple-element.35), channel_id=1, source_target_pairs={{8,0},{12,4},{16,24},{20,28},{9,1},{13,5},{17,25},{21,29},{10,2},{... | collective-permute-start | bytes 1216520 | tf_op jit(solution)/shard_map/ppermute | solution.py:283
  11.8 1.6 %collective-permute-start.3 = (bf16[528,384]{1,0:T(8,128)(2,1)S(1)}, bf16[528,384]{1,0:T(8,128)(2,1)S(1)}, u32[]{:S(2)}, u32[]{:S(2)}) collective-permute-start(bf16[528,384]{1,0:T(8,128)(2,1)S(1)} %get-tuple-element.36), channel_id=1, source_target_pairs={{0,4},{4,0},{8,12},{12,8},{16,20},{20,16},{24,28},{28,24},{1,5},{5... | collective-permute-start | bytes 1216520 | tf_op jit(solution)/shard_map/ppermute | solution.py:272
  13.4 2.6 %collective-permute-start.6 = (bf16[528,384]{1,0:T(8,128)(2,1)S(1)}, bf16[528,384]{1,0:T(8,128)(2,1)S(1)}, u32[]{:S(2)}, u32[]{:S(2)}) collective-permute-start(bf16[528,384]{1,0:T(8,128)(2,1)S(1)} %get-tuple-element.40), channel_id=1, source_target_pairs={{0,12},{4,8},{8,4},{12,0},{16,28},{20,24},{24,20},{28,16},{1,13},{... | collective-permute-start | bytes 1216520 | tf_op jit(solution)/shard_map/ppermute | solution.py:272
  16.0 2.8 %copy-done.1 = bf16[8,24,128,128]{3,2,1,0:T(8,128)(2,1)S(1)} copy-done((bf16[8,24,128,128]{3,2,1,0:T(8,128)(2,1)S(1)}, bf16[8,24,128,128]{3,2,1,0:T(8,128)(2,1)}, u32[]{:S(2)}) %copy-start.1) | copy-done | bytes 6291480
  18.8 4.9 %spread.1.dense_ref = bf16[7,8,256,512]{3,2,1,0:T(8,128)(2,1)S(1)} custom-call(s32[8,24]{1,0:T(8,128)S(1)} %copy-done.8, bf16[8,24,128,128]{3,2,1,0:T(8,128)(2,1)S(1)} %copy-done.1, bf16[8,8,128,128]{3,2,1,0:T(8,128)(2,1)S(1)} %copy-done.2), custom_call_target="tpu_custom_call" | custom-call | bytes 16777216 | tf_op jit(solution)/shard_map/spread/pallas_call | solution.py:369
  23.6 0.0 copy-start.5
  23.7 5.3 %collective-permute-start.7 = (bf16[528,384]{1,0:T(8,128)(2,1)S(1)}, bf16[528,384]{1,0:T(8,128)(2,1)S(1)}, u32[]{:S(2)}, u32[]{:S(2)}) collective-permute-start(bf16[528,384]{1,0:T(8,128)(2,1)S(1)} %get-tuple-element.42), channel_id=1, source_target_pairs={{0,28},{4,24},{24,4},{28,0},{1,29},{5,25},{25,5},{29,1},{2,30},{6,... | collective-permute-start | bytes 1216520 | tf_op jit(solution)/shard_map/ppermute | solution.py:272
  29.1 4.1 %couple.7 = (f32[8,128,384]{2,1,0:T(8,128)S(1)}, f32[8,128,384]{2,1,0:T(8,128)S(1)}) custom-call(bf16[7,8,256,512]{3,2,1,0:T(8,128)(2,1)S(1)} %spread.1.dense_ref, f32[1,128]{1,0:T(1,128)S(1)} %bitcast.8, bf16[528,384]{1,0:T(8,128)(2,1)S(1)} %get-tuple-element.33.refs_0_.refs_4_, bf16[528,384]{1,0:T(8,128)(2,1)S(1)} %hand_on.3.refs_1_, ...), custom_call_target="tpu_custom_call" | custom-call | flops 2415919104 | bytes 4194304 | tf_op jit(solution)/shard_map/couple/pallas_call | solution.py:427
  33.2 0.0 copy-start.7
  33.2 1.4 %relay.2 = (bf16[528,384]{1,0:T(8,128)(2,1)S(1)}, bf16[528,384]{1,0:T(8,128)(2,1)S(1)}, bf16[528,384]{1,0:T(8,128)(2,1)S(1)}, s32[3,4]{1,0:T(4,128)S(1)}) custom-call(s32[1,4,7]{2,1,0:T(4,128)S(1)} %bitcast.5, bf16[1040,384]{1,0:T(8,128)(2,1)S(1)} %hand_on.2.full_ref.refs_1_, bf16[1040,384]{1,0:T(8,128)(2,1)S(1)} %collective-permute-done.refs_2_, ...), custom_call_target="tpu_custom_call" | custom-call | bytes 1048576 | tf_op jit(solution)/shard_map/relay/pallas_call | solution.py:259
  34.6 7.3 %collective-permute-start.5 = (bf16[528,384]{1,0:T(8,128)(2,1)S(1)}, bf16[528,384]{1,0:T(8,128)(2,1)S(1)}, u32[]{:S(2)}, u32[]{:S(2)}) collective-permute-start(bf16[528,384]{1,0:T(8,128)(2,1)S(1)} %get-tuple-element.39), channel_id=1, source_target_pairs={{0,20},{4,16},{8,4},{12,0},{16,28},{20,24},{24,12},{28,8},{1,21},{... | collective-permute-start | bytes 1216520 | tf_op jit(solution)/shard_map/ppermute | solution.py:291
  42.0 0.8 collective-permute-start.4
  42.7 0.2 levels.1.refs_3_
  42.9 0.1 collective-permute-done.6.refs_0_
  43.0 3.0 %couple.8 = (f32[8,128,384]{2,1,0:T(8,128)S(1)}, f32[8,128,384]{2,1,0:T(8,128)S(1)}) custom-call(bf16[7,8,256,512]{3,2,1,0:T(8,128)(2,1)S(1)} %spread.1.dense_ref, f32[1,128]{1,0:T(1,128)S(1)} %bitcast.9, bf16[528,384]{1,0:T(8,128)(2,1)S(1)} %collective-permute-done.6.refs_0_, bf16[528,384]{1,0:T(8,128)(2,1)S(1)} %get-tuple-element.41.refs_1_, ...), custom_call_target="tpu_custom_call" | custom-call | flops 1610612736 | bytes 4194304 | tf_op jit(solution)/shard_map/couple/pallas_call | solution.py:427
  46.0 6.8 %collective-permute-done.5.refs_0_ = bf16[528,384]{1,0:T(8,128)(2,1)S(1)} collective-permute-done((bf16[528,384]{1,0:T(8,128)(2,1)S(1)}, bf16[528,384]{1,0:T(8,128)(2,1)S(1)}, u32[]{:S(2)}, u32[]{:S(2)}) %collective-permute-start.5) | collective-permute-done | bytes 405536 | tf_op jit(solution)/shard_map/ppermute | solution.py:291
  52.8 1.8 %couple.9 = (f32[8,128,384]{2,1,0:T(8,128)S(1)}, f32[8,128,384]{2,1,0:T(8,128)S(1)}) custom-call(bf16[7,8,256,512]{3,2,1,0:T(8,128)(2,1)S(1)} %spread.1.dense_ref, f32[1,128]{1,0:T(1,128)S(1)} %bitcast.10, bf16[528,384]{1,0:T(8,128)(2,1)S(1)} %collective-permute-done.5.refs_0_, f32[8,128,384]{2,1,0:T(8,128)S(1)} %get-tuple-element.44.refs_1_, ...), custom_call_target="tpu_custom_call" | custom-call | flops 805306368 | bytes 4194304 | tf_op jit(solution)/shard_map/couple/pallas_call | solution.py:427
  54.6 4.4 %collective-permute-done.4.refs_0_.refs_1_ = bf16[528,384]{1,0:T(8,128)(2,1)S(1)} collective-permute-done((bf16[528,384]{1,0:T(8,128)(2,1)S(1)}, bf16[528,384]{1,0:T(8,128)(2,1)S(1)}, u32[]{:S(2)}, u32[]{:S(2)}) %collective-permute-start.4) | collective-permute-done | bytes 405536 | tf_op jit(solution)/shard_map/ppermute | solution.py:290
  59.1 2.6 %finish_first.1 = (f32[8,128,384]{2,1,0:T(8,128)S(1)}, bf16[1024,384]{1,0:T(8,128)(2,1)S(1)}, bf16[512,384]{1,0:T(8,128)(2,1)S(1)}, bf16[512,384]{1,0:T(8,128)(2...) custom-call(bf16[7,8,256,512]{3,2,1,0:T(8,128)(2,1)S(1)} %spread.1.dense_ref, ...), custom_call_target="tpu_custom_call" | custom-call | flops 805306368 | bytes 8388608 | tf_op jit(solution)/shard_map/finish_first/pallas_call | solution.py:473
  61.7 0.7 collective-permute-start.8
  62.4 1.6 %collective-permute-start.9 = (bf16[512,384]{1,0:T(8,128)(2,1)S(1)}, bf16[512,384]{1,0:T(8,128)(2,1)S(1)}, u32[]{:S(2)}, u32[]{:S(2)}) collective-permute-start(bf16[512,384]{1,0:T(8,128)(2,1)S(1)} %get-tuple-element.50), channel_id=1, source_target_pairs={{0,8},{4,12},{8,0},{12,4},{16,24},{20,28},{24,16},{28,20},{1,9},{5... | collective-permute-start | bytes 1179656 | tf_op jit(solution)/shard_map/ppermute | solution.py:272
  64.0 1.0 collective-permute-start.10
  65.0 0.9 collective-permute-start.13
  65.9 4.3 %collective-permute-start.14 = (bf16[512,384]{1,0:T(8,128)(2,1)S(1)}, bf16[512,384]{1,0:T(8,128)(2,1)S(1)}, u32[]{:S(2)}, u32[]{:S(2)}) collective-permute-start(bf16[512,384]{1,0:T(8,128)(2,1)S(1)} %get-tuple-element.57), channel_id=1, source_target_pairs={{0,28},{4,24},{24,4},{28,0},{1,29},{5,25},{25,5},{29,1},{2,30},{6,... | collective-permute-start | bytes 1179656 | tf_op jit(solution)/shard_map/ppermute | solution.py:272
  70.3 4.2 %collective-permute-done.9.refs_1_ = bf16[512,384]{1,0:T(8,128)(2,1)S(1)} collective-permute-done((bf16[512,384]{1,0:T(8,128)(2,1)S(1)}, bf16[512,384]{1,0:T(8,128)(2,1)S(1)}, u32[]{:S(2)}, u32[]{:S(2)}) %collective-permute-start.9) | collective-permute-done | bytes 393248 | tf_op jit(solution)/shard_map/ppermute | solution.py:272
  74.5 8.2 %collective-permute-done.10.refs_2_ = bf16[512,384]{1,0:T(8,128)(2,1)S(1)} collective-permute-done((bf16[512,384]{1,0:T(8,128)(2,1)S(1)}, bf16[512,384]{1,0:T(8,128)(2,1)S(1)}, u32[]{:S(2)}, u32[]{:S(2)}) %collective-permute-start.10) | collective-permute-done | bytes 393248 | tf_op jit(solution)/shard_map/ppermute | solution.py:272
  82.7 4.0 %couple.10.refs_3_ = f32[8,128,384]{2,1,0:T(8,128)S(1)} custom-call(bf16[7,8,256,512]{3,2,1,0:T(8,128)(2,1)S(1)} %spread.1.dense_ref, f32[1,128]{1,0:T(1,128)S(1)} %bitcast.12, bf16[512,384]{1,0:T(8,128)(2,1)S(1)} %get-tuple-element.49.refs_0_, bf16[512,384]{1,0:T(8,128)(2,1)S(1)} %collective-permute-done.9.refs_1_, ...), custom_call_target="tpu_custom_call" | custom-call | flops 2415919104 | bytes 4194304 | tf_op jit(solution)/shard_map/couple/pallas_call | solution.py:427
  86.7 0.7 relay.3
  87.4 2.7 %collective-permute-start.12 = (bf16[512,384]{1,0:T(8,128)(2,1)S(1)}, bf16[512,384]{1,0:T(8,128)(2,1)S(1)}, u32[]{:S(2)}, u32[]{:S(2)}) collective-permute-start(bf16[512,384]{1,0:T(8,128)(2,1)S(1)} %get-tuple-element.54), channel_id=1, source_target_pairs={{0,20},{4,16},{8,4},{12,0},{16,28},{20,24},{24,12},{28,8},{1,21},{... | collective-permute-start | bytes 1179656 | tf_op jit(solution)/shard_map/ppermute | solution.py:291
  90.1 2.5 %collective-permute-start.11 = (bf16[512,384]{1,0:T(8,128)(2,1)S(1)}, bf16[512,384]{1,0:T(8,128)(2,1)S(1)}, u32[]{:S(2)}, u32[]{:S(2)}) collective-permute-start(bf16[512,384]{1,0:T(8,128)(2,1)S(1)} %get-tuple-element.53), channel_id=1, source_target_pairs={{0,24},{4,28},{8,12},{12,8},{16,20},{20,16},{24,0},{28,4},{1,25},{... | collective-permute-start | bytes 1179656 | tf_op jit(solution)/shard_map/ppermute | solution.py:290
  92.5 1.3 %prepare.1.refs_6_ = f32[8,384]{1,0:T(8,128)S(1)} custom-call(f32[3,1024,128]{2,1,0:T(8,128)S(1)} %copy-done, f32[8,128,384]{2,1,0:T(8,128)S(1)} %get-tuple-element.47.image_ref.refs_4_, bf16[512,384]{1,0:T(8,128)(2,1)S(1)} %get-tuple-element.56.refs_1_.refs_0_._), custom_call_target="tpu_custom_call" | custom-call | flops 8388608 | bytes 4194304 | tf_op jit(solution)/shard_map/prepare/pallas_call | solution.py:529
  93.9 2.9 %couple.13 = (f32[8,128,384]{2,1,0:T(8,128)}, f32[8,128,384]{2,1,0:T(8,128)S(1)}) custom-call(bf16[7,8,256,512]{3,2,1,0:T(8,128)(2,1)S(1)} %spread.1.dense_ref, f32[1,128]{1,0:T(1,128)S(1)} %bitcast.13, bf16[512,384]{1,0:T(8,128)(2,1)S(1)} %get-tuple-element.56.refs_1_.refs_0_._, bf16[528,384]{1,0:T(8,128)(2,1)S(1)} %collective-permute-done.4.refs_0_.refs_1_, ...), custom_call_target="tpu_custom_call" | custom-call | flops 805306368 | bytes 4194304 | tf_op jit(solution)/shard_map/couple/pallas_call | solution.py:427
  96.8 2.9 %couple.11.refs_1_ = f32[8,128,384]{2,1,0:T(8,128)S(1)} custom-call(bf16[7,8,256,512]{3,2,1,0:T(8,128)(2,1)S(1)} %spread.1.dense_ref, f32[1,128]{1,0:T(1,128)S(1)} %bitcast.14, bf16[512,384]{1,0:T(8,128)(2,1)S(1)} %collective-permute-done.13.refs_0_, bf16[512,384]{1,0:T(8,128)(2,1)S(1)} %get-tuple-element.56.refs_1_.refs_0_._, ...), custom_call_target="tpu_custom_call" | custom-call | flops 1610612736 | bytes 4194304 | tf_op jit(solution)/shard_map/couple/pallas_call | solution.py:427
  99.8 3.0 %collective-permute-done.12.refs_0_ = bf16[512,384]{1,0:T(8,128)(2,1)S(1)} collective-permute-done((bf16[512,384]{1,0:T(8,128)(2,1)S(1)}, bf16[512,384]{1,0:T(8,128)(2,1)S(1)}, u32[]{:S(2)}, u32[]{:S(2)}) %collective-permute-start.12) | collective-permute-done | bytes 393248 | tf_op jit(solution)/shard_map/ppermute | solution.py:291
  102.7 1.8 %couple.12.refs_1_ = f32[8,128,384]{2,1,0:T(8,128)S(1)} custom-call(bf16[7,8,256,512]{3,2,1,0:T(8,128)(2,1)S(1)} %spread.1.dense_ref, f32[1,128]{1,0:T(1,128)S(1)} %bitcast.15, bf16[512,384]{1,0:T(8,128)(2,1)S(1)} %collective-permute-done.12.refs_0_, f32[8,128,384]{2,1,0:T(8,128)S(1)} %couple.11.refs_1_), custom_call_target="tpu_custom_call" | custom-call | flops 805306368 | bytes 4194304 | tf_op jit(solution)/shard_map/couple/pallas_call | solution.py:427
  104.5 1.6 %collective-permute-done.11.refs_0_ = bf16[512,384]{1,0:T(8,128)(2,1)S(1)} collective-permute-done((bf16[512,384]{1,0:T(8,128)(2,1)S(1)}, bf16[512,384]{1,0:T(8,128)(2,1)S(1)}, u32[]{:S(2)}, u32[]{:S(2)}) %collective-permute-start.11) | collective-permute-done | bytes 393248 | tf_op jit(solution)/shard_map/ppermute | solution.py:290
  106.1 2.4 %finish_second.1 = (f32[8,128,384]{2,1,0:T(8,128)S(1)}, f32[32,8,128]{2,1,0:T(8,128)S(1)}) custom-call(bf16[7,8,256,512]{3,2,1,0:T(8,128)(2,1)S(1)} %spread.1.dense_ref, f32[1,128]{1,0:T(1,128)S(1)} %bitcast.16, bf16[512,384]{1,0:T(8,128)(2,1)S(1)} %collective-permute-done.11.refs_0_, f32[8,128,384]{2,1,0:T(8,128)S(1)} %couple.12.refs_1_, ...), custom_call_target="tpu_custom_call" | custom-call | flops 805306368 | bytes 8388608 | tf_op jit(solution)/shard_map/finish_second/pallas_call | solution.py:586
  108.5 12.8 %all_to_all.5.gathered_ref = f32[32,8,128]{2,1,0:T(8,128)S(1)} all-to-all(f32[32,8,128]{2,1,0:T(8,128)S(1)} %get-tuple-element.61), channel_id=1, replica_groups=mesh['row'=8,'col'=4] {'row','col'}, dimensions={0} | all-to-all | bytes 262144 | tf_op jit(solution)/shard_map/all_to_all | solution.py:714
  121.2 2.6 %final.1 = (f32[3,1024,128]{2,1,0:T(8,128)}, f32[3,1024,128]{2,1,0:T(8,128)}) custom-call(f32[3,1024,128]{2,1,0:T(8,128)S(1)} %copy-done, f32[8,128,384]{2,1,0:T(8,128)S(1)} %get-tuple-element.47.image_ref.refs_4_, f32[8,128,384]{2,1,0:T(8,128)S(1)} %get-tuple-element.60.later_ref, f32[32,8,128]{2,1,0:T(8,128)S(1)} %all_to_all.5.gathered_ref), custom_call_target="tpu_custom_call" | custom-call | tf_op jit(solution)/shard_map/final/pallas_call | solution.py:662
  (20 shorter events, 0.0 us)
Async XLA Ops:
  0.6 0.7 copy-start.3
  1.3 0.7 copy-start.6
  3.9 12.1 %copy-start.2 = (bf16[8,8,128,128]{3,2,1,0:T(8,128)(2,1)S(1)}, bf16[8,8,128,128]{3,2,1,0:T(8,128)(2,1)}, u32[]{:S(2)}) copy-start(bf16[8,8,128,128]{3,2,1,0:T(8,128)(2,1)} %correlation_ref.1) | copy-start | bytes 6291460
  3.9 12.1 %copy-start.8 = (s32[8,24]{1,0:T(8,128)S(1)}, s32[8,24]{1,0:T(8,128)}, u32[]{:S(2)}) copy-start(s32[8,24]{1,0:T(8,128)} %slot_ref.1) | copy-start | bytes 2308
  3.9 19.8 %collective-permute-start.1 = (bf16[528,384]{1,0:T(8,128)(2,1)S(1)}, bf16[528,384]{1,0:T(8,128)(2,1)S(1)}, u32[]{:S(2)}, u32[]{:S(2)}) collective-permute-start(bf16[528,384]{1,0:T(8,128)(2,1)S(1)} %get-tuple-element.34), channel_id=1, source_target_pairs={{0,8},{4,12},{24,16},{28,20},{1,9},{5,13},{25,17},{29,21},{2,10},{... | collective-permute-start | bytes 1216520 | tf_op jit(solution)/shard_map/ppermute | solution.py:282
  9.0 24.2 %collective-permute-start = (bf16[1040,384]{1,0:T(8,128)(2,1)S(1)}, bf16[1040,384]{1,0:T(8,128)(2,1)S(1)}, u32[]{:S(2)}, u32[]{:S(2)}) collective-permute-start(bf16[1040,384]{1,0:T(8,128)(2,1)S(1)} %hand_on.2.full_ref.refs_1_), channel_id=1, source_target_pairs={{8,16},{12,20},{16,8},{20,12},{9,17},{13,21},{17,9},{21,13},{10,18... | collective-permute-start | bytes 2396168 | tf_op jit(solution)/shard_map/ppermute | solution.py:278
  10.5 18.5 %collective-permute-start.2 = (bf16[528,384]{1,0:T(8,128)(2,1)S(1)}, bf16[528,384]{1,0:T(8,128)(2,1)S(1)}, u32[]{:S(2)}, u32[]{:S(2)}) collective-permute-start(bf16[528,384]{1,0:T(8,128)(2,1)S(1)} %get-tuple-element.35), channel_id=1, source_target_pairs={{8,0},{12,4},{16,24},{20,28},{9,1},{13,5},{17,25},{21,29},{10,2},{... | collective-permute-start | bytes 1216520 | tf_op jit(solution)/shard_map/ppermute | solution.py:283
  11.8 17.2 %collective-permute-start.3 = (bf16[528,384]{1,0:T(8,128)(2,1)S(1)}, bf16[528,384]{1,0:T(8,128)(2,1)S(1)}, u32[]{:S(2)}, u32[]{:S(2)}) collective-permute-start(bf16[528,384]{1,0:T(8,128)(2,1)S(1)} %get-tuple-element.36), channel_id=1, source_target_pairs={{0,4},{4,0},{8,12},{12,8},{16,20},{20,16},{24,28},{28,24},{1,5},{5... | collective-permute-start | bytes 1216520 | tf_op jit(solution)/shard_map/ppermute | solution.py:272
  13.4 29.6 %collective-permute-start.6 = (bf16[528,384]{1,0:T(8,128)(2,1)S(1)}, bf16[528,384]{1,0:T(8,128)(2,1)S(1)}, u32[]{:S(2)}, u32[]{:S(2)}) collective-permute-start(bf16[528,384]{1,0:T(8,128)(2,1)S(1)} %get-tuple-element.40), channel_id=1, source_target_pairs={{0,12},{4,8},{8,4},{12,0},{16,28},{20,24},{24,20},{28,16},{1,13},{... | collective-permute-start | bytes 1216520 | tf_op jit(solution)/shard_map/ppermute | solution.py:272
  16.0 2.8 %copy-start.1 = (bf16[8,24,128,128]{3,2,1,0:T(8,128)(2,1)S(1)}, bf16[8,24,128,128]{3,2,1,0:T(8,128)(2,1)}, u32[]{:S(2)}) copy-start(bf16[8,24,128,128]{3,2,1,0:T(8,128)(2,1)} %ks_ref.1) | copy-start | bytes 18874372
  23.6 5.4 %copy-start.5 = (f32[128]{0:T(128)S(1)}, f32[128]{0:T(128)}, u32[]{:S(2)}) copy-start(f32[128]{0:T(128)} %param.9) | copy-start | bytes 1540
  23.7 19.4 %collective-permute-start.7 = (bf16[528,384]{1,0:T(8,128)(2,1)S(1)}, bf16[528,384]{1,0:T(8,128)(2,1)S(1)}, u32[]{:S(2)}, u32[]{:S(2)}) collective-permute-start(bf16[528,384]{1,0:T(8,128)(2,1)S(1)} %get-tuple-element.42), channel_id=1, source_target_pairs={{0,28},{4,24},{24,4},{28,0},{1,29},{5,25},{25,5},{29,1},{2,30},{6,... | collective-permute-start | bytes 1216520 | tf_op jit(solution)/shard_map/ppermute | solution.py:272
  29.0 4.1 %copy-start.4 = (s32[1,7,4]{1,2,0:T(4,128)S(1)}, s32[1,7,4]{1,2,0:T(4,128)}, u32[]{:S(2)}) copy-start(s32[1,7,4]{1,2,0:T(4,128)} %param.13) | copy-start | bytes 340
  33.2 9.5 %copy-start.7 = (f32[1024]{0:T(1024)S(1)}, f32[1024]{0:T(1024)}, u32[]{:S(2)}) copy-start(f32[1024]{0:T(1024)} %param.8) | copy-start | bytes 12292
  34.6 18.2 %collective-permute-start.5 = (bf16[528,384]{1,0:T(8,128)(2,1)S(1)}, bf16[528,384]{1,0:T(8,128)(2,1)S(1)}, u32[]{:S(2)}, u32[]{:S(2)}) collective-permute-start(bf16[528,384]{1,0:T(8,128)(2,1)S(1)} %get-tuple-element.39), channel_id=1, source_target_pairs={{0,20},{4,16},{8,4},{12,0},{16,28},{20,24},{24,12},{28,8},{1,21},{... | collective-permute-start | bytes 1216520 | tf_op jit(solution)/shard_map/ppermute | solution.py:291
  42.0 17.1 %collective-permute-start.4 = (bf16[528,384]{1,0:T(8,128)(2,1)S(1)}, bf16[528,384]{1,0:T(8,128)(2,1)S(1)}, u32[]{:S(2)}, u32[]{:S(2)}) collective-permute-start(bf16[528,384]{1,0:T(8,128)(2,1)S(1)} %get-tuple-element.38), channel_id=1, source_target_pairs={{0,24},{4,28},{8,12},{12,8},{16,20},{20,16},{24,0},{28,4},{1,25},{... | collective-permute-start | bytes 1216520 | tf_op jit(solution)/shard_map/ppermute | solution.py:290
  52.8 6.2 %copy-start = (f32[3,1024,128]{2,1,0:T(8,128)S(1)}, f32[3,1024,128]{2,1,0:T(8,128)}, u32[]{:S(2)}) copy-start(f32[3,1024,128]{2,1,0:T(8,128)} %right_ref.3) | copy-start | bytes 4718596
  61.7 25.0 %collective-permute-start.8 = (bf16[1024,384]{1,0:T(8,128)(2,1)S(1)}, bf16[1024,384]{1,0:T(8,128)(2,1)S(1)}, u32[]{:S(2)}, u32[]{:S(2)}) collective-permute-start(bf16[1024,384]{1,0:T(8,128)(2,1)S(1)} %get-tuple-element.48.refs_1_), channel_id=1, source_target_pairs={{8,16},{12,20},{16,8},{20,12},{9,17},{13,21},{17,9},{21,13},{10,18... | collective-permute-start | bytes 2359304 | tf_op jit(solution)/shard_map/ppermute | solution.py:278
  62.4 12.1 %collective-permute-start.9 = (bf16[512,384]{1,0:T(8,128)(2,1)S(1)}, bf16[512,384]{1,0:T(8,128)(2,1)S(1)}, u32[]{:S(2)}, u32[]{:S(2)}) collective-permute-start(bf16[512,384]{1,0:T(8,128)(2,1)S(1)} %get-tuple-element.50), channel_id=1, source_target_pairs={{0,8},{4,12},{8,0},{12,4},{16,24},{20,28},{24,16},{28,20},{1,9},{5... | collective-permute-start | bytes 1179656 | tf_op jit(solution)/shard_map/ppermute | solution.py:272
  64.0 18.7 %collective-permute-start.10 = (bf16[512,384]{1,0:T(8,128)(2,1)S(1)}, bf16[512,384]{1,0:T(8,128)(2,1)S(1)}, u32[]{:S(2)}, u32[]{:S(2)}) collective-permute-start(bf16[512,384]{1,0:T(8,128)(2,1)S(1)} %get-tuple-element.51), channel_id=1, source_target_pairs={{0,12},{4,8},{8,4},{12,0},{16,28},{20,24},{24,20},{28,16},{1,13},{... | collective-permute-start | bytes 1179656 | tf_op jit(solution)/shard_map/ppermute | solution.py:272
  65.0 31.8 %collective-permute-start.13 = (bf16[512,384]{1,0:T(8,128)(2,1)S(1)}, bf16[512,384]{1,0:T(8,128)(2,1)S(1)}, u32[]{:S(2)}, u32[]{:S(2)}) collective-permute-start(bf16[512,384]{1,0:T(8,128)(2,1)S(1)} %get-tuple-element.55), channel_id=1, source_target_pairs={{0,4},{4,0},{8,12},{12,8},{16,20},{20,16},{24,28},{28,24},{1,5},{5... | collective-permute-start | bytes 1179656 | tf_op jit(solution)/shard_map/ppermute | solution.py:272
  65.9 30.9 %collective-permute-start.14 = (bf16[512,384]{1,0:T(8,128)(2,1)S(1)}, bf16[512,384]{1,0:T(8,128)(2,1)S(1)}, u32[]{:S(2)}, u32[]{:S(2)}) collective-permute-start(bf16[512,384]{1,0:T(8,128)(2,1)S(1)} %get-tuple-element.57), channel_id=1, source_target_pairs={{0,28},{4,24},{24,4},{28,0},{1,29},{5,25},{25,5},{29,1},{2,30},{6,... | collective-permute-start | bytes 1179656 | tf_op jit(solution)/shard_map/ppermute | solution.py:272
  87.4 15.3 %collective-permute-start.12 = (bf16[512,384]{1,0:T(8,128)(2,1)S(1)}, bf16[512,384]{1,0:T(8,128)(2,1)S(1)}, u32[]{:S(2)}, u32[]{:S(2)}) collective-permute-start(bf16[512,384]{1,0:T(8,128)(2,1)S(1)} %get-tuple-element.54), channel_id=1, source_target_pairs={{0,20},{4,16},{8,4},{12,0},{16,28},{20,24},{24,12},{28,8},{1,21},{... | collective-permute-start | bytes 1179656 | tf_op jit(solution)/shard_map/ppermute | solution.py:291
  90.1 16.0 %collective-permute-start.11 = (bf16[512,384]{1,0:T(8,128)(2,1)S(1)}, bf16[512,384]{1,0:T(8,128)(2,1)S(1)}, u32[]{:S(2)}, u32[]{:S(2)}) collective-permute-start(bf16[512,384]{1,0:T(8,128)(2,1)S(1)} %get-tuple-element.53), channel_id=1, source_target_pairs={{0,24},{4,28},{8,12},{12,8},{16,20},{20,16},{24,0},{28,4},{1,25},{... | collective-permute-start | bytes 1179656 | tf_op jit(solution)/shard_map/ppermute | solution.py:290

commit v14 on v13

--- a/solution.py
+++ b/solution.py
@@ -78,7 +78,7 @@
 
     def direct(self):
         if self.relayed:
-            return [1, 2, 3, 7]
+            return [2, 3, 7]
         far = range(self.middle, 0, -1)
         return [by for f in far for by in (f, -f)]
 
@@ -226,7 +226,7 @@
     def kernel(*refs):
         readers_ref, mine_ref, full_ref, _, *refs = refs
         me = lax.axis_index("row")
-        *messages, chosen_ref = refs if chosen is None else [*refs[1:], refs[0]]
+        *messages, beside, chosen_ref = refs if chosen is None else [*refs[1:], refs[0]]
         if chosen is None:
             base = full_ref.shape[0] - EXTRA
             table = full_ref[base : base + EXTRA, 0:width].astype(jnp.float32)
@@ -249,10 +249,12 @@
                 clusters = [readers_ref[0, slot, offset] for slot in range(served)]
                 gather(clusters, mine_ref, out, width)
 
+        fill(plan, [1], readers_ref, mine_ref, [beside], width)
+
     inputs = [readers, mine, full, after] + ([] if chosen is None else [chosen])
     specs = [smem(), vmem(), vmem(), pl.BlockSpec(memory_space=pl.ANY)]
     specs += [] if chosen is None else [smem()]
-    shapes, outs = [message] * 3, [vmem()] * 3
+    shapes, outs = [message] * 4, [vmem()] * 4
     if chosen is None:
         shapes.append(jax.ShapeDtypeStruct((3, served), jnp.int32))
         outs.append(smem())
@@ -268,12 +270,12 @@
     return (messages, last) if chosen is None else (messages + [last], chosen)
 
 
-def exchange(plan, readers, early, direct, own, full, chosen, begin, near, served, width):
+def exchange(plan, readers, early, direct, own, full, chosen, begin, served, width):
     sent = {k: lax.ppermute(m, "row", plan.pairs(k)) for k, m in direct.items() if k not in early}
     if not plan.relayed:
         sent |= {k: lax.ppermute(m, "row", plan.pairs(k)) for k, m in early.items()}
         items = [(own, 0)] + [(sent[k], k) for k in plan.direct()]
-        sums = begin(items[:3])
+        sums = begin(items[:2])
         return items, sums, None, sums[0]
     theirs = lax.ppermute(full, "row", [(i, i ^ 6) for i in INNER])
     for k, m in early.items():
@@ -281,15 +283,15 @@
         outward = [(i, j) for i, j in plan.pairs(k) if i in INNER]
         first = hand_on(lax.ppermute(m, "row", inward), EARLY)
         sent[k] = (first, lax.ppermute(direct[k], "row", outward))
-    items = [(own, 0)]
-    items += [(sent[k], (k, k) if k in early else k) for k in near]
-    sums = begin(items[:3])
-    (mine, near, far), chosen = relay(
+    items = [(own, 0)] + [(sent[k], (k, k) if k in early else k) for k in (2, 3)]
+    sums = begin(items[:2])
+    (mine, near, far, beside), chosen = relay(
         plan, readers, full, theirs, chosen, sums[0], served, width
     )
+    beside = lax.ppermute(beside, "row", plan.pairs(1))
     near = lax.ppermute(near, "row", [(i, i ^ (1 if i in INNER else 6)) for i in range(plan.count)])
     far = lax.ppermute(far, "row", [(i, i ^ (3 if i in INNER else 5)) for i in range(plan.count)])
-    items += [((mine, sent[7]), (6, 7)), (far, 5), (near, (7, 6))]
+    items += [((mine, sent[7]), (6, 7)), (beside, 1), (far, 5), (near, (7, 6))]
     return items, sums, chosen, mine
 
 
@@ -396,7 +398,7 @@
     return 2 * len(items) * dense.shape[1] * dense.shape[2] * dense.shape[3] * lanes
 
 
-def couple(dense, vectors, energies, sums, after=None, weight=1):
+def couple(dense, vectors, energies, sums, after=None):
     _, clusters, height, depth = dense.shape
     lanes = vectors.lanes
     count = len(vectors.arrays)
@@ -432,7 +434,7 @@
         + [pl.BlockSpec(memory_space=pl.ANY)] * len(order)
         + [vmem()] * (len(vectors.arrays) + had),
         vectors.scratch,
-        flops=weight * work(dense, vectors.items, lanes),
+        flops=work(dense, vectors.items, lanes),
         moved=4 * MIB,
     )(*inputs)
 
@@ -681,11 +683,11 @@
     plan = Plan(rows, span, rows == 8 and span == 7)
     readers = jnp.swapaxes(readers, 1, 2)
 
-    def begin(weight):
-        return lambda items: couple(dense, Vectors(plan, items), energies, [], weight=weight)
+    def begin(items):
+        return couple(dense, Vectors(plan, items), energies, [])
 
     def partial(items, sums):
-        for group in (items[3:-2], items[-2:-1]):
+        for group in (items[2:4], items[4:6]):
             sums = couple(dense, Vectors(plan, group), energies, sums)
         return sums, Vectors(plan, items[-1:])
 
@@ -694,7 +696,7 @@
     direct, own = deal(plan, readers, full, served, width)
     dense = spread(tile_slot, ks_tiles, correlation_tiles, span, served)
     items, sums, chosen, _ = exchange(
-        plan, readers, early, direct, own, full, None, begin(1), (2, 1, 3), served, width
+        plan, readers, early, direct, own, full, None, begin, served, width
     )
     level = levels(onsite)
     sums, last = partial(items, sums)
@@ -703,7 +705,7 @@
     )
 
     items, begun, _, mark = exchange(
-        plan, readers, {}, direct, out, full, chosen, begin(1), (2, 3, 1), served, width
+        plan, readers, {}, direct, out, full, chosen, begin, served, width
     )
     lines = prepare(right_side, image, mark)
     _, weighted = couple(dense, last, energies, sums, mark)

time: 124 us -> 131 us (1.056)
  starting transfers between devices: 38.4 us -> 50.1 us
  waiting for transfers between devices: 28.3 us -> 20.7 us
  blocking collectives: 12.8 us -> 14.8 us
    ppermute x2, waiting for transfers between devices: 9.81 us -> 0.01 us  [exchange(): lax.ppermute(far, 'row', [(i, i ^ (3 if i in INNER else 5)) for i in rang...]
    ppermute x2, starting transfers between devices: 9.99 us -> 19.1 us  [exchange(): lax.ppermute(far, 'row', [(i, i ^ (3 if i in INNER else 5)) for i in rang...]
    ppermute x0 -> x2, waiting for transfers between devices: none -> 8.53 us  [exchange(): beside = lax.ppermute(beside, 'row', plan.pairs(1))]
    ppermute x2, waiting for transfers between devices: 5.99 us -> 0.29 us  [exchange(): lax.ppermute(near, 'row', [(i, i ^ (1 if i in INNER else 6)) for i in ran...]
    ppermute x0 -> x2, starting transfers between devices: none -> 3.61 us  [exchange(): beside = lax.ppermute(beside, 'row', plan.pairs(1))]
    all_to_all x1, blocking collectives: 12.8 us -> 14.8 us  [body(): gathered = lax.all_to_all(gathered, ('row', 'col'), 0, 0)]
    ppermute x2, starting transfers between devices: 3.23 us -> 1.74 us  [exchange(): lax.ppermute(near, 'row', [(i, i ^ (1 if i in INNER else 6)) for i in ran...]
    ppermute x7 -> x5, waiting for transfers between devices: 12.5 us -> 11.9 us  [exchange(): lax.ppermute(m, 'row', plan.pairs(k))]
  transfers between devices with their start and end apart: 15 -> 15, of which waited for: 7 -> 6; matrix products, arithmetic and copies ran while one was open for 0% -> 0% of each run, Pallas kernels for 24% -> 23%
where the time goes in v14:
time: 131 us
  starting transfers between devices  50.1 us (38%)
  Pallas kernels  39.2 us (30%)
  waiting for transfers between devices  20.7 us (16%)
  blocking collectives  14.8 us (11%)
  local copies, waits for them, and re-layouts  4.79 us (4%)
    pallas_call x7, Pallas kernels, couple(): call(kernel, 'couple', [shape] * outs, [vmem()] * 2 + [pl.BlockSpec(memor...  20.5 us
    ppermute x2, starting transfers between devices, exchange(): lax.ppermute(far, 'row', [(i, i ^ (3 if i in INNER else 5)) for i in rang...  19.1 us
    ppermute x5, starting transfers between devices, exchange(): lax.ppermute(m, 'row', plan.pairs(k))  17.9 us
    all_to_all x1, blocking collectives, body(): gathered = lax.all_to_all(gathered, ('row', 'col'), 0, 0)  14.8 us
    ppermute x5, waiting for transfers between devices, exchange(): lax.ppermute(m, 'row', plan.pairs(k))  11.9 us
    ppermute x2, waiting for transfers between devices, exchange(): beside = lax.ppermute(beside, 'row', plan.pairs(1))  8.53 us
    ppermute x1, starting transfers between devices, exchange(): first = hand_on(lax.ppermute(m, 'row', inward), EARLY)  5.08 us
    pallas_call x1, Pallas kernels, spread(): call(kernel, 'spread', jax.ShapeDtypeStruct((span, clusters, 2 * width, s...  4.86 us
  transfers between devices with their start and end apart: 15, of which 6 were waited for; matrix products, arithmetic and copies ran while one was open for 0% of the time, Pallas kernels for 23%

profile of v14, /device:TPU:0, one launch (start us, length us, event | category | flops | bytes accessed | tf_op | source)
XLA Modules:
  0.0 130.5 jit_solution(3053867971047002939)
XLA Ops:
  0.6 0.0 copy-start.3
  0.6 0.7 copy-done.3
  1.3 0.7 copy-done.6
  2.0 1.8 %pack.1 = (bf16[528,384]{1,0:T(8,128)(2,1)S(1)}, bf16[1040,384]{1,0:T(8,128)(2,1)S(1)}) custom-call(s32[1,4,7]{2,1,0:T(4,128)S(1)} %bitcast.3, f32[3,1024,128]{2,1,0:T(8,128)} %right_ref.3, f32[8,128]{1,0:T(8,128)S(1)} %bitcast.17), custom_call_target="tpu_custom_call" | custom-call | bytes 1048576 | tf_op jit(solution)/shard_map/pack/pallas_call | solution.py:158
  3.9 0.0 copy-start.2
  3.9 0.0 copy-start.8
  3.9 5.1 %collective-permute-start.1 = (bf16[528,384]{1,0:T(8,128)(2,1)S(1)}, bf16[528,384]{1,0:T(8,128)(2,1)S(1)}, u32[]{:S(2)}, u32[]{:S(2)}) collective-permute-start(bf16[528,384]{1,0:T(8,128)(2,1)S(1)} %get-tuple-element.34), channel_id=1, source_target_pairs={{0,8},{4,12},{24,16},{28,20},{1,9},{5,13},{25,17},{29,21},{2,10},{... | collective-permute-start | bytes 1216520 | tf_op jit(solution)/shard_map/ppermute | solution.py:284
  9.0 0.7 collective-permute-start
  9.7 0.7 deal.1
  10.4 1.3 collective-permute-start.2
  11.7 3.7 %collective-permute-start.6 = (bf16[528,384]{1,0:T(8,128)(2,1)S(1)}, bf16[528,384]{1,0:T(8,128)(2,1)S(1)}, u32[]{:S(2)}, u32[]{:S(2)}) collective-permute-start(bf16[528,384]{1,0:T(8,128)(2,1)S(1)} %get-tuple-element.40), channel_id=1, source_target_pairs={{0,12},{4,8},{8,4},{12,0},{16,28},{20,24},{24,20},{28,16},{1,13},{... | collective-permute-start | bytes 1216520 | tf_op jit(solution)/shard_map/ppermute | solution.py:274
  15.4 4.3 %collective-permute-start.7 = (bf16[528,384]{1,0:T(8,128)(2,1)S(1)}, bf16[528,384]{1,0:T(8,128)(2,1)S(1)}, u32[]{:S(2)}, u32[]{:S(2)}) collective-permute-start(bf16[528,384]{1,0:T(8,128)(2,1)S(1)} %get-tuple-element.42), channel_id=1, source_target_pairs={{0,28},{4,24},{24,4},{28,0},{1,29},{5,25},{25,5},{29,1},{2,30},{6,... | collective-permute-start | bytes 1216520 | tf_op jit(solution)/shard_map/ppermute | solution.py:274
  19.8 0.0 copy-start.1
  19.8 2.8 %copy-done.1 = bf16[8,24,128,128]{3,2,1,0:T(8,128)(2,1)S(1)} copy-done((bf16[8,24,128,128]{3,2,1,0:T(8,128)(2,1)S(1)}, bf16[8,24,128,128]{3,2,1,0:T(8,128)(2,1)}, u32[]{:S(2)}) %copy-start.1) | copy-done | bytes 6291480
  22.6 4.9 %spread.1.dense_ref = bf16[7,8,256,512]{3,2,1,0:T(8,128)(2,1)S(1)} custom-call(s32[8,24]{1,0:T(8,128)S(1)} %copy-done.8, bf16[8,24,128,128]{3,2,1,0:T(8,128)(2,1)S(1)} %copy-done.1, bf16[8,8,128,128]{3,2,1,0:T(8,128)(2,1)S(1)} %copy-done.2), custom_call_target="tpu_custom_call" | custom-call | bytes 16777216 | tf_op jit(solution)/shard_map/spread/pallas_call | solution.py:371
  27.5 0.6 copy-done.5
  28.1 2.9 %couple.7 = (f32[8,128,384]{2,1,0:T(8,128)S(1)}, f32[8,128,384]{2,1,0:T(8,128)S(1)}) custom-call(bf16[7,8,256,512]{3,2,1,0:T(8,128)(2,1)S(1)} %spread.1.dense_ref, f32[1,128]{1,0:T(1,128)S(1)} %bitcast.8, bf16[528,384]{1,0:T(8,128)(2,1)S(1)} %get-tuple-element.33.refs_0_.refs_4_, bf16[528,384]{1,0:T(8,128)(2,1)S(1)} %hand_on.3.refs_1_, ...), custom_call_target="tpu_custom_call" | custom-call | flops 1610612736 | bytes 4194304 | tf_op jit(solution)/shard_map/couple/pallas_call | solution.py:429
  31.0 0.0 copy-start.7
  31.0 1.4 %relay.2 = (bf16[528,384]{1,0:T(8,128)(2,1)S(1)}, bf16[528,384]{1,0:T(8,128)(2,1)S(1)}, bf16[528,384]{1,0:T(8,128)(2,1)S(1)}, bf16[528,384]{1,0:T(8,128)(2,1)S(1)}, s32[3,4]{1,0:T(4,128)S(1)}) custom-call(s32[1,4,7]{2,1,0:T(4,128)S(1)} %bitcast.5, bf16[1040,384]{1,0:T(8,128)(2,1)S(1)} %hand_on.2.full_ref.refs_1_, ...), custom_call_target="tpu_custom_call" | custom-call | bytes 1048576 | tf_op jit(solution)/shard_map/relay/pallas_call | solution.py:261
  32.5 1.6 %collective-permute-start.4 = (bf16[528,384]{1,0:T(8,128)(2,1)S(1)}, bf16[528,384]{1,0:T(8,128)(2,1)S(1)}, u32[]{:S(2)}, u32[]{:S(2)}) collective-permute-start(bf16[528,384]{1,0:T(8,128)(2,1)S(1)} %get-tuple-element.38), channel_id=1, source_target_pairs={{0,4},{4,0},{8,12},{12,8},{16,20},{20,16},{24,28},{28,24},{1,5},{5... | collective-permute-start | bytes 1216520 | tf_op jit(solution)/shard_map/ppermute | solution.py:291
  34.1 17.1 %collective-permute-start.5 = (bf16[528,384]{1,0:T(8,128)(2,1)S(1)}, bf16[528,384]{1,0:T(8,128)(2,1)S(1)}, u32[]{:S(2)}, u32[]{:S(2)}) collective-permute-start(bf16[528,384]{1,0:T(8,128)(2,1)S(1)} %get-tuple-element.39), channel_id=1, source_target_pairs={{0,20},{4,16},{8,4},{12,0},{16,28},{20,24},{24,12},{28,8},{1,21},{... | collective-permute-start | bytes 1216520 | tf_op jit(solution)/shard_map/ppermute | solution.py:293
  51.2 0.4 collective-permute-start.3
  51.6 0.2 levels.1.refs_3_
  51.8 3.1 %couple.8 = (f32[8,128,384]{2,1,0:T(8,128)S(1)}, f32[8,128,384]{2,1,0:T(8,128)S(1)}) custom-call(bf16[7,8,256,512]{3,2,1,0:T(8,128)(2,1)S(1)} %spread.1.dense_ref, f32[1,128]{1,0:T(1,128)S(1)} %bitcast.9, bf16[528,384]{1,0:T(8,128)(2,1)S(1)} %collective-permute-done.6.refs_0_, bf16[528,384]{1,0:T(8,128)(2,1)S(1)} %get-tuple-element.41.refs_1_, ...), custom_call_target="tpu_custom_call" | custom-call | flops 1610612736 | bytes 4194304 | tf_op jit(solution)/shard_map/couple/pallas_call | solution.py:429
  54.9 4.0 %collective-permute-done.4.refs_0_ = bf16[528,384]{1,0:T(8,128)(2,1)S(1)} collective-permute-done((bf16[528,384]{1,0:T(8,128)(2,1)S(1)}, bf16[528,384]{1,0:T(8,128)(2,1)S(1)}, u32[]{:S(2)}, u32[]{:S(2)}) %collective-permute-start.4) | collective-permute-done | bytes 405536 | tf_op jit(solution)/shard_map/ppermute | solution.py:291
  58.9 2.9 %couple.9 = (f32[8,128,384]{2,1,0:T(8,128)S(1)}, f32[8,128,384]{2,1,0:T(8,128)S(1)}) custom-call(bf16[7,8,256,512]{3,2,1,0:T(8,128)(2,1)S(1)} %spread.1.dense_ref, f32[1,128]{1,0:T(1,128)S(1)} %bitcast.10, bf16[528,384]{1,0:T(8,128)(2,1)S(1)} %collective-permute-done.4.refs_0_, bf16[528,384]{1,0:T(8,128)(2,1)S(1)} %collective-permute-done.5.refs_1_, ...), custom_call_target="tpu_custom_call" | custom-call | flops 1610612736 | bytes 4194304 | tf_op jit(solution)/shard_map/couple/pallas_call | solution.py:429
  61.8 0.2 collective-permute-done.3.refs_0_.refs_1_
  62.0 2.6 %finish_first.1 = (f32[8,128,384]{2,1,0:T(8,128)S(1)}, bf16[1024,384]{1,0:T(8,128)(2,1)S(1)}, bf16[512,384]{1,0:T(8,128)(2,1)S(1)}, bf16[512,384]{1,0:T(8,128)(2...) custom-call(bf16[7,8,256,512]{3,2,1,0:T(8,128)(2,1)S(1)} %spread.1.dense_ref, f32[1,128]{1,0:T(1,128)S(1)} %bitcast.11, ...), custom_call_target="tpu_custom_call" | custom-call | flops 805306368 | bytes 8388608 | tf_op jit(solution)/shard_map/finish_first/pallas_call | solution.py:475
  64.6 0.7 collective-permute-start.8
  65.3 6.1 %collective-permute-start.9 = (bf16[512,384]{1,0:T(8,128)(2,1)S(1)}, bf16[512,384]{1,0:T(8,128)(2,1)S(1)}, u32[]{:S(2)}, u32[]{:S(2)}) collective-permute-start(bf16[512,384]{1,0:T(8,128)(2,1)S(1)} %get-tuple-element.50), channel_id=1, source_target_pairs={{0,8},{4,12},{8,0},{12,4},{16,24},{20,28},{24,16},{28,20},{1,9},{5... | collective-permute-start | bytes 1179656 | tf_op jit(solution)/shard_map/ppermute | solution.py:274
  71.4 1.0 collective-permute-start.13
  72.5 2.8 %collective-permute-start.14 = (bf16[512,384]{1,0:T(8,128)(2,1)S(1)}, bf16[512,384]{1,0:T(8,128)(2,1)S(1)}, u32[]{:S(2)}, u32[]{:S(2)}) collective-permute-start(bf16[512,384]{1,0:T(8,128)(2,1)S(1)} %get-tuple-element.57), channel_id=1, source_target_pairs={{0,28},{4,24},{24,4},{28,0},{1,29},{5,25},{25,5},{29,1},{2,30},{6,... | collective-permute-start | bytes 1179656 | tf_op jit(solution)/shard_map/ppermute | solution.py:274
  75.2 7.7 %collective-permute-done.9.refs_1_ = bf16[512,384]{1,0:T(8,128)(2,1)S(1)} collective-permute-done((bf16[512,384]{1,0:T(8,128)(2,1)S(1)}, bf16[512,384]{1,0:T(8,128)(2,1)S(1)}, u32[]{:S(2)}, u32[]{:S(2)}) %collective-permute-start.9) | collective-permute-done | bytes 393248 | tf_op jit(solution)/shard_map/ppermute | solution.py:274
  82.9 2.9 %couple.10.refs_3_ = f32[8,128,384]{2,1,0:T(8,128)S(1)} custom-call(bf16[7,8,256,512]{3,2,1,0:T(8,128)(2,1)S(1)} %spread.1.dense_ref, f32[1,128]{1,0:T(1,128)S(1)} %bitcast.12, bf16[512,384]{1,0:T(8,128)(2,1)S(1)} %get-tuple-element.49.refs_0_, bf16[512,384]{1,0:T(8,128)(2,1)S(1)} %collective-permute-done.9.refs_1_), custom_call_target="tpu_custom_call" | custom-call | flops 1610612736 | bytes 4194304 | tf_op jit(solution)/shard_map/couple/pallas_call | solution.py:429
  85.8 0.7 relay.3
  86.5 2.0 %collective-permute-start.11 = (bf16[512,384]{1,0:T(8,128)(2,1)S(1)}, bf16[512,384]{1,0:T(8,128)(2,1)S(1)}, u32[]{:S(2)}, u32[]{:S(2)}) collective-permute-start(bf16[512,384]{1,0:T(8,128)(2,1)S(1)} %get-tuple-element.53), channel_id=1, source_target_pairs={{0,4},{4,0},{8,12},{12,8},{16,20},{20,16},{24,28},{28,24},{1,5},{5... | collective-permute-start | bytes 1179656 | tf_op jit(solution)/shard_map/ppermute | solution.py:291
  88.5 2.0 %collective-permute-start.12 = (bf16[512,384]{1,0:T(8,128)(2,1)S(1)}, bf16[512,384]{1,0:T(8,128)(2,1)S(1)}, u32[]{:S(2)}, u32[]{:S(2)}) collective-permute-start(bf16[512,384]{1,0:T(8,128)(2,1)S(1)} %get-tuple-element.54), channel_id=1, source_target_pairs={{0,20},{4,16},{8,4},{12,0},{16,28},{20,24},{24,12},{28,8},{1,21},{... | collective-permute-start | bytes 1179656 | tf_op jit(solution)/shard_map/ppermute | solution.py:293
  90.5 1.3 collective-permute-start.10
  91.8 1.3 %prepare.1.refs_6_ = f32[8,384]{1,0:T(8,128)S(1)} custom-call(f32[3,1024,128]{2,1,0:T(8,128)S(1)} %copy-done, f32[8,128,384]{2,1,0:T(8,128)S(1)} %get-tuple-element.47.image_ref.refs_4_, bf16[512,384]{1,0:T(8,128)(2,1)S(1)} %get-tuple-element.56.refs_1_.refs_0_._), custom_call_target="tpu_custom_call" | custom-call | flops 8388608 | bytes 4194304 | tf_op jit(solution)/shard_map/prepare/pallas_call | solution.py:531
  93.1 2.9 %couple.13 = (f32[8,128,384]{2,1,0:T(8,128)}, f32[8,128,384]{2,1,0:T(8,128)S(1)}) custom-call(bf16[7,8,256,512]{3,2,1,0:T(8,128)(2,1)S(1)} %spread.1.dense_ref, f32[1,128]{1,0:T(1,128)S(1)} %bitcast.13, bf16[512,384]{1,0:T(8,128)(2,1)S(1)} %get-tuple-element.56.refs_1_.refs_0_._, bf16[528,384]{1,0:T(8,128)(2,1)S(1)} %collective-permute-done.3.refs_0_.refs_1_, ...), custom_call_target="tpu_custom_call" | custom-call | flops 805306368 | bytes 4194304 | tf_op jit(solution)/shard_map/couple/pallas_call | solution.py:429
  96.1 4.2 %collective-permute-done.14.refs_2_ = bf16[512,384]{1,0:T(8,128)(2,1)S(1)} collective-permute-done((bf16[512,384]{1,0:T(8,128)(2,1)S(1)}, bf16[512,384]{1,0:T(8,128)(2,1)S(1)}, u32[]{:S(2)}, u32[]{:S(2)}) %collective-permute-start.14) | collective-permute-done | bytes 393248 | tf_op jit(solution)/shard_map/ppermute | solution.py:274
  100.3 2.9 %couple.11.refs_2_ = f32[8,128,384]{2,1,0:T(8,128)S(1)} custom-call(bf16[7,8,256,512]{3,2,1,0:T(8,128)(2,1)S(1)} %spread.1.dense_ref, f32[1,128]{1,0:T(1,128)S(1)} %bitcast.14, bf16[512,384]{1,0:T(8,128)(2,1)S(1)} %collective-permute-done.13.refs_0_, bf16[512,384]{1,0:T(8,128)(2,1)S(1)} %get-tuple-element.56.refs_1_.refs_0_._, ...), custom_call_target="tpu_custom_call" | custom-call | flops 1610612736 | bytes 4194304 | tf_op jit(solution)/shard_map/couple/pallas_call | solution.py:429
  103.2 4.5 %collective-permute-done.11.refs_0_ = bf16[512,384]{1,0:T(8,128)(2,1)S(1)} collective-permute-done((bf16[512,384]{1,0:T(8,128)(2,1)S(1)}, bf16[512,384]{1,0:T(8,128)(2,1)S(1)}, u32[]{:S(2)}, u32[]{:S(2)}) %collective-permute-start.11) | collective-permute-done | bytes 393248 | tf_op jit(solution)/shard_map/ppermute | solution.py:291
  107.8 2.9 %couple.12.refs_1_ = f32[8,128,384]{2,1,0:T(8,128)S(1)} custom-call(bf16[7,8,256,512]{3,2,1,0:T(8,128)(2,1)S(1)} %spread.1.dense_ref, f32[1,128]{1,0:T(1,128)S(1)} %bitcast.15, bf16[512,384]{1,0:T(8,128)(2,1)S(1)} %collective-permute-done.11.refs_0_, bf16[512,384]{1,0:T(8,128)(2,1)S(1)} %collective-permute-done.12.refs_1_, f32[8,128,384]{2,1,0:T(8,128)S(1)} %couple.11.refs_2_), custom_call_target="tpu_custom_call" | custom-call | flops 1610612736 | bytes 4194304 | tf_op jit(solution)/shard_map/couple/pallas_call | solution.py:429
  110.7 0.1 collective-permute-done.10.refs_0_
  110.8 2.4 %finish_second.1 = (f32[8,128,384]{2,1,0:T(8,128)S(1)}, f32[32,8,128]{2,1,0:T(8,128)S(1)}) custom-call(bf16[7,8,256,512]{3,2,1,0:T(8,128)(2,1)S(1)} %spread.1.dense_ref, f32[1,128]{1,0:T(1,128)S(1)} %bitcast.16, bf16[512,384]{1,0:T(8,128)(2,1)S(1)} %collective-permute-done.10.refs_0_, f32[8,128,384]{2,1,0:T(8,128)S(1)} %couple.12.refs_1_, ...), custom_call_target="tpu_custom_call" | custom-call | flops 805306368 | bytes 8388608 | tf_op jit(solution)/shard_map/finish_second/pallas_call | solution.py:588
  113.1 14.8 %all_to_all.5.gathered_ref = f32[32,8,128]{2,1,0:T(8,128)S(1)} all-to-all(f32[32,8,128]{2,1,0:T(8,128)S(1)} %get-tuple-element.61), channel_id=1, replica_groups=mesh['row'=8,'col'=4] {'row','col'}, dimensions={0} | all-to-all | bytes 262144 | tf_op jit(solution)/shard_map/all_to_all | solution.py:716
  127.9 2.6 %final.1 = (f32[3,1024,128]{2,1,0:T(8,128)}, f32[3,1024,128]{2,1,0:T(8,128)}) custom-call(f32[3,1024,128]{2,1,0:T(8,128)S(1)} %copy-done, f32[8,128,384]{2,1,0:T(8,128)S(1)} %get-tuple-element.47.image_ref.refs_4_, f32[8,128,384]{2,1,0:T(8,128)S(1)} %get-tuple-element.60.later_ref, f32[32,8,128]{2,1,0:T(8,128)S(1)} %all_to_all.5.gathered_ref), custom_call_target="tpu_custom_call" | custom-call | tf_op jit(solution)/shard_map/final/pallas_call | solution.py:664
  (20 shorter events, 0.0 us)
Async XLA Ops:
  0.6 0.7 copy-start.3
  1.3 0.7 copy-start.6
  3.9 15.9 %copy-start.2 = (bf16[8,8,128,128]{3,2,1,0:T(8,128)(2,1)S(1)}, bf16[8,8,128,128]{3,2,1,0:T(8,128)(2,1)}, u32[]{:S(2)}) copy-start(bf16[8,8,128,128]{3,2,1,0:T(8,128)(2,1)} %correlation_ref.1) | copy-start | bytes 6291460
  3.9 15.9 %copy-start.8 = (s32[8,24]{1,0:T(8,128)S(1)}, s32[8,24]{1,0:T(8,128)}, u32[]{:S(2)}) copy-start(s32[8,24]{1,0:T(8,128)} %slot_ref.1) | copy-start | bytes 2308
  3.9 23.6 %collective-permute-start.1 = (bf16[528,384]{1,0:T(8,128)(2,1)S(1)}, bf16[528,384]{1,0:T(8,128)(2,1)S(1)}, u32[]{:S(2)}, u32[]{:S(2)}) collective-permute-start(bf16[528,384]{1,0:T(8,128)(2,1)S(1)} %get-tuple-element.34), channel_id=1, source_target_pairs={{0,8},{4,12},{24,16},{28,20},{1,9},{5,13},{25,17},{29,21},{2,10},{... | collective-permute-start | bytes 1216520 | tf_op jit(solution)/shard_map/ppermute | solution.py:284
  9.0 22.0 %collective-permute-start = (bf16[1040,384]{1,0:T(8,128)(2,1)S(1)}, bf16[1040,384]{1,0:T(8,128)(2,1)S(1)}, u32[]{:S(2)}, u32[]{:S(2)}) collective-permute-start(bf16[1040,384]{1,0:T(8,128)(2,1)S(1)} %hand_on.2.full_ref.refs_1_), channel_id=1, source_target_pairs={{8,16},{12,20},{16,8},{20,12},{9,17},{13,21},{17,9},{21,13},{10,18... | collective-permute-start | bytes 2396168 | tf_op jit(solution)/shard_map/ppermute | solution.py:280
  10.4 17.0 %collective-permute-start.2 = (bf16[528,384]{1,0:T(8,128)(2,1)S(1)}, bf16[528,384]{1,0:T(8,128)(2,1)S(1)}, u32[]{:S(2)}, u32[]{:S(2)}) collective-permute-start(bf16[528,384]{1,0:T(8,128)(2,1)S(1)} %get-tuple-element.35), channel_id=1, source_target_pairs={{8,0},{12,4},{16,24},{20,28},{9,1},{13,5},{17,25},{21,29},{10,2},{... | collective-permute-start | bytes 1216520 | tf_op jit(solution)/shard_map/ppermute | solution.py:285
  11.7 40.1 %collective-permute-start.6 = (bf16[528,384]{1,0:T(8,128)(2,1)S(1)}, bf16[528,384]{1,0:T(8,128)(2,1)S(1)}, u32[]{:S(2)}, u32[]{:S(2)}) collective-permute-start(bf16[528,384]{1,0:T(8,128)(2,1)S(1)} %get-tuple-element.40), channel_id=1, source_target_pairs={{0,12},{4,8},{8,4},{12,0},{16,28},{20,24},{24,20},{28,16},{1,13},{... | collective-permute-start | bytes 1216520 | tf_op jit(solution)/shard_map/ppermute | solution.py:274
  15.4 36.4 %collective-permute-start.7 = (bf16[528,384]{1,0:T(8,128)(2,1)S(1)}, bf16[528,384]{1,0:T(8,128)(2,1)S(1)}, u32[]{:S(2)}, u32[]{:S(2)}) collective-permute-start(bf16[528,384]{1,0:T(8,128)(2,1)S(1)} %get-tuple-element.42), channel_id=1, source_target_pairs={{0,28},{4,24},{24,4},{28,0},{1,29},{5,25},{25,5},{29,1},{2,30},{6,... | collective-permute-start | bytes 1216520 | tf_op jit(solution)/shard_map/ppermute | solution.py:274
  19.8 2.8 %copy-start.1 = (bf16[8,24,128,128]{3,2,1,0:T(8,128)(2,1)S(1)}, bf16[8,24,128,128]{3,2,1,0:T(8,128)(2,1)}, u32[]{:S(2)}) copy-start(bf16[8,24,128,128]{3,2,1,0:T(8,128)(2,1)} %ks_ref.1) | copy-start | bytes 18874372
  27.4 0.7 copy-start.5
  28.1 2.9 %copy-start.4 = (s32[1,7,4]{1,2,0:T(4,128)S(1)}, s32[1,7,4]{1,2,0:T(4,128)}, u32[]{:S(2)}) copy-start(s32[1,7,4]{1,2,0:T(4,128)} %param.13) | copy-start | bytes 340
  31.0 20.6 %copy-start.7 = (f32[1024]{0:T(1024)S(1)}, f32[1024]{0:T(1024)}, u32[]{:S(2)}) copy-start(f32[1024]{0:T(1024)} %param.8) | copy-start | bytes 12292
  32.5 26.4 %collective-permute-start.4 = (bf16[528,384]{1,0:T(8,128)(2,1)S(1)}, bf16[528,384]{1,0:T(8,128)(2,1)S(1)}, u32[]{:S(2)}, u32[]{:S(2)}) collective-permute-start(bf16[528,384]{1,0:T(8,128)(2,1)S(1)} %get-tuple-element.38), channel_id=1, source_target_pairs={{0,4},{4,0},{8,12},{12,8},{16,20},{20,16},{24,28},{28,24},{1,5},{5... | collective-permute-start | bytes 1216520 | tf_op jit(solution)/shard_map/ppermute | solution.py:291
  34.1 24.8 %collective-permute-start.5 = (bf16[528,384]{1,0:T(8,128)(2,1)S(1)}, bf16[528,384]{1,0:T(8,128)(2,1)S(1)}, u32[]{:S(2)}, u32[]{:S(2)}) collective-permute-start(bf16[528,384]{1,0:T(8,128)(2,1)S(1)} %get-tuple-element.39), channel_id=1, source_target_pairs={{0,20},{4,16},{8,4},{12,0},{16,28},{20,24},{24,12},{28,8},{1,21},{... | collective-permute-start | bytes 1216520 | tf_op jit(solution)/shard_map/ppermute | solution.py:293
  51.2 10.8 %collective-permute-start.3 = (bf16[528,384]{1,0:T(8,128)(2,1)S(1)}, bf16[528,384]{1,0:T(8,128)(2,1)S(1)}, u32[]{:S(2)}, u32[]{:S(2)}) collective-permute-start(bf16[528,384]{1,0:T(8,128)(2,1)S(1)} %get-tuple-element.37), channel_id=1, source_target_pairs={{0,24},{4,28},{8,12},{12,8},{16,20},{20,16},{24,0},{28,4},{1,25},{... | collective-permute-start | bytes 1216520 | tf_op jit(solution)/shard_map/ppermute | solution.py:292
  58.9 3.1 %copy-start = (f32[3,1024,128]{2,1,0:T(8,128)S(1)}, f32[3,1024,128]{2,1,0:T(8,128)}, u32[]{:S(2)}) copy-start(f32[3,1024,128]{2,1,0:T(8,128)} %right_ref.3) | copy-start | bytes 4718596
  64.6 21.2 %collective-permute-start.8 = (bf16[1024,384]{1,0:T(8,128)(2,1)S(1)}, bf16[1024,384]{1,0:T(8,128)(2,1)S(1)}, u32[]{:S(2)}, u32[]{:S(2)}) collective-permute-start(bf16[1024,384]{1,0:T(8,128)(2,1)S(1)} %get-tuple-element.48.refs_1_), channel_id=1, source_target_pairs={{8,16},{12,20},{16,8},{20,12},{9,17},{13,21},{17,9},{21,13},{10,18... | collective-permute-start | bytes 2359304 | tf_op jit(solution)/shard_map/ppermute | solution.py:280
  65.3 17.6 %collective-permute-start.9 = (bf16[512,384]{1,0:T(8,128)(2,1)S(1)}, bf16[512,384]{1,0:T(8,128)(2,1)S(1)}, u32[]{:S(2)}, u32[]{:S(2)}) collective-permute-start(bf16[512,384]{1,0:T(8,128)(2,1)S(1)} %get-tuple-element.50), channel_id=1, source_target_pairs={{0,8},{4,12},{8,0},{12,4},{16,24},{20,28},{24,16},{28,20},{1,9},{5... | collective-permute-start | bytes 1179656 | tf_op jit(solution)/shard_map/ppermute | solution.py:274
  71.4 24.7 %collective-permute-start.13 = (bf16[512,384]{1,0:T(8,128)(2,1)S(1)}, bf16[512,384]{1,0:T(8,128)(2,1)S(1)}, u32[]{:S(2)}, u32[]{:S(2)}) collective-permute-start(bf16[512,384]{1,0:T(8,128)(2,1)S(1)} %get-tuple-element.55), channel_id=1, source_target_pairs={{0,12},{4,8},{8,4},{12,0},{16,28},{20,24},{24,20},{28,16},{1,13},{... | collective-permute-start | bytes 1179656 | tf_op jit(solution)/shard_map/ppermute | solution.py:274
  72.5 27.8 %collective-permute-start.14 = (bf16[512,384]{1,0:T(8,128)(2,1)S(1)}, bf16[512,384]{1,0:T(8,128)(2,1)S(1)}, u32[]{:S(2)}, u32[]{:S(2)}) collective-permute-start(bf16[512,384]{1,0:T(8,128)(2,1)S(1)} %get-tuple-element.57), channel_id=1, source_target_pairs={{0,28},{4,24},{24,4},{28,0},{1,29},{5,25},{25,5},{29,1},{2,30},{6,... | collective-permute-start | bytes 1179656 | tf_op jit(solution)/shard_map/ppermute | solution.py:274
  86.5 21.2 %collective-permute-start.11 = (bf16[512,384]{1,0:T(8,128)(2,1)S(1)}, bf16[512,384]{1,0:T(8,128)(2,1)S(1)}, u32[]{:S(2)}, u32[]{:S(2)}) collective-permute-start(bf16[512,384]{1,0:T(8,128)(2,1)S(1)} %get-tuple-element.53), channel_id=1, source_target_pairs={{0,4},{4,0},{8,12},{12,8},{16,20},{20,16},{24,28},{28,24},{1,5},{5... | collective-permute-start | bytes 1179656 | tf_op jit(solution)/shard_map/ppermute | solution.py:291
  88.5 19.2 %collective-permute-start.12 = (bf16[512,384]{1,0:T(8,128)(2,1)S(1)}, bf16[512,384]{1,0:T(8,128)(2,1)S(1)}, u32[]{:S(2)}, u32[]{:S(2)}) collective-permute-start(bf16[512,384]{1,0:T(8,128)(2,1)S(1)} %get-tuple-element.54), channel_id=1, source_target_pairs={{0,20},{4,16},{8,4},{12,0},{16,28},{20,24},{24,12},{28,8},{1,21},{... | collective-permute-start | bytes 1179656 | tf_op jit(solution)/shard_map/ppermute | solution.py:293
  90.5 20.3 %collective-permute-start.10 = (bf16[512,384]{1,0:T(8,128)(2,1)S(1)}, bf16[512,384]{1,0:T(8,128)(2,1)S(1)}, u32[]{:S(2)}, u32[]{:S(2)}) collective-permute-start(bf16[512,384]{1,0:T(8,128)(2,1)S(1)} %get-tuple-element.52), channel_id=1, source_target_pairs={{0,24},{4,28},{8,12},{12,8},{16,20},{20,16},{24,0},{28,4},{1,25},{... | collective-permute-start | bytes 1179656 | tf_op jit(solution)/shard_map/ppermute | solution.py:292

commit v15 on v12

--- a/solution.py
+++ b/solution.py
@@ -9,7 +9,7 @@
 
 MIB = 2**20
 EXTRA = 16
-BATCH = 2
+BATCH = 4
 
 
 def shifted(array, axis, by):
@@ -163,7 +163,7 @@
             pltpu.SemaphoreType.DMA((clusters,)),
             pltpu.SemaphoreType.DMA((2,)),
         ],
-        limit=51,
+        limit=54,
     )(readers, right_side, onsite)
     return dict(zip(keys, messages)), own, full
 

time: 123 us -> 123 us (level)
  waiting for transfers between devices: 27.9 us -> 30.9 us
  Pallas kernels: 38.6 us -> 36.9 us
  local copies, waits for them, and re-layouts: 5.74 us -> 4.4 us
    pallas_call x7, Pallas kernels: 20.5 us -> 18 us  [couple(): call(kernel, 'couple', [shape] * outs, [vmem()] * 2 + [pl.BlockSpec(memor...]
    ppermute x2, waiting for transfers between devices: 7.11 us -> 8.71 us  [exchange(): lax.ppermute(near, 'row', [(i, i ^ (1 if i in INNER else 6)) for i in ran...]
    pallas_call x1, Pallas kernels: 2.01 us -> 3.55 us  [pack(): call(kernel, 'pack', [message] * (len(keys) + 1) + [full], [pl.BlockSpec(...]
    unnamed x14 -> x18, local copies, waits for them, and re-layouts: 5.74 us -> 4.4 us
  transfers between devices with their start and end apart: 14 -> 14, of which waited for: 6 -> 7; matrix products, arithmetic and copies ran while one was open for 0% -> 0% of each run, Pallas kernels for 24% -> 22%
where the time goes in v15:
time: 123 us
  Pallas kernels  36.9 us (30%)
  starting transfers between devices  35.6 us (29%)
  waiting for transfers between devices  30.9 us (25%)
  blocking collectives  13.8 us (11%)
  local copies, waits for them, and re-layouts  4.4 us (4%)
    ppermute x8, starting transfers between devices, exchange(): sent = {k: lax.ppermute(m, 'row', plan.pairs(k)) for k, m in direct.items()}  19.4 us
    pallas_call x7, Pallas kernels, couple(): call(kernel, 'couple', [shape] * outs, [vmem()] * 2 + [pl.BlockSpec(memor...  18 us
    ppermute x8, waiting for transfers between devices, exchange(): sent = {k: lax.ppermute(m, 'row', plan.pairs(k)) for k, m in direct.items()}  15.6 us
    all_to_all x1, blocking collectives, body(): gathered = lax.all_to_all(gathered, ('row', 'col'), 0, 0)  13.8 us
    ppermute x2, starting transfers between devices, exchange(): lax.ppermute(far, 'row', [(i, i ^ (3 if i in INNER else 5)) for i in rang...  10.9 us
    ppermute x2, waiting for transfers between devices, exchange(): lax.ppermute(near, 'row', [(i, i ^ (1 if i in INNER else 6)) for i in ran...  8.71 us
    ppermute x2, waiting for transfers between devices, exchange(): lax.ppermute(far, 'row', [(i, i ^ (3 if i in INNER else 5)) for i in rang...  6.66 us
    pallas_call x1, Pallas kernels, spread(): call(kernel, 'spread', jax.ShapeDtypeStruct((span, clusters, 2 * width, s...  4.86 us
  transfers between devices with their start and end apart: 14, of which 7 were waited for; matrix products, arithmetic and copies ran while one was open for 0% of the time, Pallas kernels for 22%

profile of v15, /device:TPU:0, one launch (start us, length us, event | category | flops | bytes accessed | tf_op | source)
XLA Modules:
  0.0 122.6 jit_solution(14949347497686103523)
XLA Ops:
  0.6 3.5 %pack.1 = (bf16[528,384]{1,0:T(8,128)(2,1)}, bf16[528,384]{1,0:T(8,128)(2,1)}, bf16[528,384]{1,0:T(8,128)(2,1)}, bf16[528,384]{1,0:T(8,128)(2,1)}, bf16[528,384]{1,0:T(8,128)(2,1)}, /*index=5*/bf16[1040,384]{1,0:T(8,128)(2,1)}) custom-call(s32[1,4,7]{2,1,0:T(4,128)} %bitcast.12, f32[3,1024,128]{2,1,0:T(8,128)} %right_ref.3, f32[8,128]{1,0:T(8,128)} %bitcast.16), custom_call_target="tpu_custom_call" | custom-call | bytes 1048576 | tf_op jit(solution)/shard_map/pack/pallas_call | solution.py:154
  4.2 0.7 collective-permute-start
  4.9 3.0 %collective-permute-start.1 = (bf16[528,384]{1,0:T(8,128)(2,1)}, bf16[528,384]{1,0:T(8,128)(2,1)S(1)}, u32[]{:S(2)}, u32[]{:S(2)}) collective-permute-start(bf16[528,384]{1,0:T(8,128)(2,1)} %get-tuple-element.33), channel_id=1, source_target_pairs={{0,4},{4,0},{8,12},{12,8},{16,20},{20,16},{24,28},{28,24},{1,5},{5... | collective-permute-start | bytes 1216520 | tf_op jit(solution)/shard_map/ppermute | solution.py:239
  7.9 4.3 %collective-permute-start.2 = (bf16[528,384]{1,0:T(8,128)(2,1)}, bf16[528,384]{1,0:T(8,128)(2,1)S(1)}, u32[]{:S(2)}, u32[]{:S(2)}) collective-permute-start(bf16[528,384]{1,0:T(8,128)(2,1)} %get-tuple-element.34), channel_id=1, source_target_pairs={{0,8},{4,12},{8,0},{12,4},{16,24},{20,28},{24,16},{28,20},{1,9},{5... | collective-permute-start | bytes 1216520 | tf_op jit(solution)/shard_map/ppermute | solution.py:239
  12.3 0.0 collective-permute-start.5
  12.3 4.1 %collective-permute-start.6 = (bf16[528,384]{1,0:T(8,128)(2,1)}, bf16[528,384]{1,0:T(8,128)(2,1)S(1)}, u32[]{:S(2)}, u32[]{:S(2)}) collective-permute-start(bf16[528,384]{1,0:T(8,128)(2,1)} %get-tuple-element.40), channel_id=1, source_target_pairs={{0,28},{4,24},{24,4},{28,0},{1,29},{5,25},{25,5},{29,1},{2,30},{6,... | collective-permute-start | bytes 1216520 | tf_op jit(solution)/shard_map/ppermute | solution.py:239
  16.5 0.0 copy-start.1
  16.5 2.8 %copy-done.1 = bf16[8,24,128,128]{3,2,1,0:T(8,128)(2,1)S(1)} copy-done((bf16[8,24,128,128]{3,2,1,0:T(8,128)(2,1)S(1)}, bf16[8,24,128,128]{3,2,1,0:T(8,128)(2,1)}, u32[]{:S(2)}) %copy-start.1) | copy-done | bytes 6291480
  19.3 1.6 %copy-done.2 = bf16[8,8,128,128]{3,2,1,0:T(8,128)(2,1)S(1)} copy-done((bf16[8,8,128,128]{3,2,1,0:T(8,128)(2,1)S(1)}, bf16[8,8,128,128]{3,2,1,0:T(8,128)(2,1)}, u32[]{:S(2)}) %copy-start.2) | copy-done | bytes 2097176
  20.8 4.9 %spread.1.dense_ref = bf16[7,8,256,512]{3,2,1,0:T(8,128)(2,1)S(1)} custom-call(s32[8,24]{1,0:T(8,128)S(1)} %copy-done.8, bf16[8,24,128,128]{3,2,1,0:T(8,128)(2,1)S(1)} %copy-done.1, bf16[8,8,128,128]{3,2,1,0:T(8,128)(2,1)S(1)} %copy-done.2), custom_call_target="tpu_custom_call" | custom-call | bytes 16777216 | tf_op jit(solution)/shard_map/spread/pallas_call | solution.py:329
  25.7 0.0 collective-permute-done.1.refs_2_
  25.7 0.0 collective-permute-done.refs_0_.refs_2_
  25.8 0.0 copy-start.4
  25.8 0.0 copy-start.6
  25.8 3.7 %couple.7 = (f32[8,128,384]{2,1,0:T(8,128)S(1)}, f32[8,128,384]{2,1,0:T(8,128)S(1)}) custom-call(bf16[7,8,256,512]{3,2,1,0:T(8,128)(2,1)S(1)} %spread.1.dense_ref, f32[1,128]{1,0:T(1,128)S(1)} %bitcast.3, bf16[1040,384]{1,0:T(8,128)(2,1)S(1)} %collective-permute-done.refs_0_.refs_2_, bf16[528,384]{1,0:T(8,128)(2,1)S(1)} %copy-done.3, ...), custom_call_target="tpu_custom_call" | custom-call | flops 2415919104 | bytes 4194304 | tf_op jit(solution)/shard_map/couple/pallas_call | solution.py:387
  29.5 0.0 copy-start.7
  29.5 1.4 %relay.2 = (bf16[528,384]{1,0:T(8,128)(2,1)S(1)}, bf16[528,384]{1,0:T(8,128)(2,1)S(1)}, bf16[528,384]{1,0:T(8,128)(2,1)S(1)}, s32[3,4]{1,0:T(4,128)S(1)}) custom-call(s32[1,4,7]{2,1,0:T(4,128)S(1)} %bitcast.13, bf16[1040,384]{1,0:T(8,128)(2,1)S(1)} %copy-done.4, bf16[1040,384]{1,0:T(8,128)(2,1)S(1)} %collective-permute-done.refs_0_.refs_2_, ...), custom_call_target="tpu_custom_call" | custom-call | bytes 1048576 | tf_op jit(solution)/shard_map/relay/pallas_call | solution.py:226
  30.9 5.1 %collective-permute-start.4 = (bf16[528,384]{1,0:T(8,128)(2,1)S(1)}, bf16[528,384]{1,0:T(8,128)(2,1)S(1)}, u32[]{:S(2)}, u32[]{:S(2)}) collective-permute-start(bf16[528,384]{1,0:T(8,128)(2,1)S(1)} %get-tuple-element.37), channel_id=1, source_target_pairs={{0,20},{4,16},{8,4},{12,0},{16,28},{20,24},{24,12},{28,8},{1,21},{... | collective-permute-start | bytes 1216520 | tf_op jit(solution)/shard_map/ppermute | solution.py:251
  36.1 1.4 %collective-permute-start.3 = (bf16[528,384]{1,0:T(8,128)(2,1)S(1)}, bf16[528,384]{1,0:T(8,128)(2,1)S(1)}, u32[]{:S(2)}, u32[]{:S(2)}) collective-permute-start(bf16[528,384]{1,0:T(8,128)(2,1)S(1)} %get-tuple-element.36), channel_id=1, source_target_pairs={{0,24},{4,28},{8,12},{12,8},{16,20},{20,16},{24,0},{28,4},{1,25},{... | collective-permute-start | bytes 1216520 | tf_op jit(solution)/shard_map/ppermute | solution.py:250
  37.4 0.2 levels.1.refs_3_
  37.6 0.0 collective-permute-done.5.refs_0_
  37.6 3.9 %collective-permute-done.6.refs_2_ = bf16[528,384]{1,0:T(8,128)(2,1)S(1)} collective-permute-done((bf16[528,384]{1,0:T(8,128)(2,1)}, bf16[528,384]{1,0:T(8,128)(2,1)S(1)}, u32[]{:S(2)}, u32[]{:S(2)}) %collective-permute-start.6) | collective-permute-done | bytes 405536 | tf_op jit(solution)/shard_map/ppermute | solution.py:239
  41.5 2.7 %couple.8 = (f32[8,128,384]{2,1,0:T(8,128)S(1)}, f32[8,128,384]{2,1,0:T(8,128)S(1)}) custom-call(bf16[7,8,256,512]{3,2,1,0:T(8,128)(2,1)S(1)} %spread.1.dense_ref, f32[1,128]{1,0:T(1,128)S(1)} %bitcast.4, bf16[528,384]{1,0:T(8,128)(2,1)S(1)} %collective-permute-done.5.refs_0_, bf16[528,384]{1,0:T(8,128)(2,1)S(1)} %get-tuple-element.39.refs_1_, ...), custom_call_target="tpu_custom_call" | custom-call | flops 1610612736 | bytes 4194304 | tf_op jit(solution)/shard_map/couple/pallas_call | solution.py:387
  44.2 5.8 %collective-permute-done.4.refs_0_ = bf16[528,384]{1,0:T(8,128)(2,1)S(1)} collective-permute-done((bf16[528,384]{1,0:T(8,128)(2,1)S(1)}, bf16[528,384]{1,0:T(8,128)(2,1)S(1)}, u32[]{:S(2)}, u32[]{:S(2)}) %collective-permute-start.4) | collective-permute-done | bytes 405536 | tf_op jit(solution)/shard_map/ppermute | solution.py:251
  50.1 1.4 %couple.9 = (f32[8,128,384]{2,1,0:T(8,128)S(1)}, f32[8,128,384]{2,1,0:T(8,128)S(1)}) custom-call(bf16[7,8,256,512]{3,2,1,0:T(8,128)(2,1)S(1)} %spread.1.dense_ref, f32[1,128]{1,0:T(1,128)S(1)} %bitcast.5, bf16[528,384]{1,0:T(8,128)(2,1)S(1)} %collective-permute-done.4.refs_0_, f32[8,128,384]{2,1,0:T(8,128)S(1)} %get-tuple-element.42.refs_1_, ...), custom_call_target="tpu_custom_call" | custom-call | flops 805306368 | bytes 4194304 | tf_op jit(solution)/shard_map/couple/pallas_call | solution.py:387
  51.5 5.7 %collective-permute-done.3.refs_0_.refs_1_ = bf16[528,384]{1,0:T(8,128)(2,1)S(1)} collective-permute-done((bf16[528,384]{1,0:T(8,128)(2,1)S(1)}, bf16[528,384]{1,0:T(8,128)(2,1)S(1)}, u32[]{:S(2)}, u32[]{:S(2)}) %collective-permute-start.3) | collective-permute-done | bytes 405536 | tf_op jit(solution)/shard_map/ppermute | solution.py:250
  57.2 2.3 %finish_first.1 = (f32[8,128,384]{2,1,0:T(8,128)S(1)}, bf16[1024,384]{1,0:T(8,128)(2,1)S(1)}, bf16[512,384]{1,0:T(8,128)(2,1)S(1)}, bf16[512,384]{1,0:T(8,128)(2...) custom-call(bf16[7,8,256,512]{3,2,1,0:T(8,128)(2,1)S(1)} %spread.1.dense_ref, ...), custom_call_target="tpu_custom_call" | custom-call | flops 805306368 | bytes 8388608 | tf_op jit(solution)/shard_map/finish_first/pallas_call | solution.py:433
  59.5 0.7 collective-permute-start.7
  60.2 0.1 collective-permute-start.8
  60.3 2.0 %collective-permute-start.9 = (bf16[512,384]{1,0:T(8,128)(2,1)S(1)}, bf16[512,384]{1,0:T(8,128)(2,1)S(1)}, u32[]{:S(2)}, u32[]{:S(2)}) collective-permute-start(bf16[512,384]{1,0:T(8,128)(2,1)S(1)} %get-tuple-element.49), channel_id=1, source_target_pairs={{0,12},{4,8},{8,4},{12,0},{16,28},{20,24},{24,20},{28,16},{1,13},{... | collective-permute-start | bytes 1179656 | tf_op jit(solution)/shard_map/ppermute | solution.py:239
  62.3 1.5 %collective-permute-start.12 = (bf16[512,384]{1,0:T(8,128)(2,1)S(1)}, bf16[512,384]{1,0:T(8,128)(2,1)S(1)}, u32[]{:S(2)}, u32[]{:S(2)}) collective-permute-start(bf16[512,384]{1,0:T(8,128)(2,1)S(1)} %get-tuple-element.53), channel_id=1, source_target_pairs={{0,4},{4,0},{8,12},{12,8},{16,20},{20,16},{24,28},{28,24},{1,5},{5... | collective-permute-start | bytes 1179656 | tf_op jit(solution)/shard_map/ppermute | solution.py:239
  63.8 4.3 %collective-permute-start.13 = (bf16[512,384]{1,0:T(8,128)(2,1)S(1)}, bf16[512,384]{1,0:T(8,128)(2,1)S(1)}, u32[]{:S(2)}, u32[]{:S(2)}) collective-permute-start(bf16[512,384]{1,0:T(8,128)(2,1)S(1)} %get-tuple-element.55), channel_id=1, source_target_pairs={{0,28},{4,24},{24,4},{28,0},{1,29},{5,25},{25,5},{29,1},{2,30},{6,... | collective-permute-start | bytes 1179656 | tf_op jit(solution)/shard_map/ppermute | solution.py:239
  68.1 4.2 %collective-permute-done.8.refs_1_ = bf16[512,384]{1,0:T(8,128)(2,1)S(1)} collective-permute-done((bf16[512,384]{1,0:T(8,128)(2,1)S(1)}, bf16[512,384]{1,0:T(8,128)(2,1)S(1)}, u32[]{:S(2)}, u32[]{:S(2)}) %collective-permute-start.8) | collective-permute-done | bytes 393248 | tf_op jit(solution)/shard_map/ppermute | solution.py:239
  72.3 7.5 %collective-permute-done.9.refs_2_ = bf16[512,384]{1,0:T(8,128)(2,1)S(1)} collective-permute-done((bf16[512,384]{1,0:T(8,128)(2,1)S(1)}, bf16[512,384]{1,0:T(8,128)(2,1)S(1)}, u32[]{:S(2)}, u32[]{:S(2)}) %collective-permute-start.9) | collective-permute-done | bytes 393248 | tf_op jit(solution)/shard_map/ppermute | solution.py:239
  79.8 3.6 %couple.10.refs_3_ = f32[8,128,384]{2,1,0:T(8,128)S(1)} custom-call(bf16[7,8,256,512]{3,2,1,0:T(8,128)(2,1)S(1)} %spread.1.dense_ref, f32[1,128]{1,0:T(1,128)S(1)} %bitcast.7, bf16[512,384]{1,0:T(8,128)(2,1)S(1)} %get-tuple-element.47.refs_0_, bf16[512,384]{1,0:T(8,128)(2,1)S(1)} %collective-permute-done.8.refs_1_, ...), custom_call_target="tpu_custom_call" | custom-call | flops 2415919104 | bytes 4194304 | tf_op jit(solution)/shard_map/couple/pallas_call | solution.py:387
  83.4 0.0 collective-permute-done.7.refs_2_
  83.4 0.7 relay.3
  84.1 5.8 %collective-permute-start.11 = (bf16[512,384]{1,0:T(8,128)(2,1)S(1)}, bf16[512,384]{1,0:T(8,128)(2,1)S(1)}, u32[]{:S(2)}, u32[]{:S(2)}) collective-permute-start(bf16[512,384]{1,0:T(8,128)(2,1)S(1)} %get-tuple-element.52), channel_id=1, source_target_pairs={{0,20},{4,16},{8,4},{12,0},{16,28},{20,24},{24,12},{28,8},{1,21},{... | collective-permute-start | bytes 1179656 | tf_op jit(solution)/shard_map/ppermute | solution.py:251
  89.9 2.5 %collective-permute-start.10 = (bf16[512,384]{1,0:T(8,128)(2,1)S(1)}, bf16[512,384]{1,0:T(8,128)(2,1)S(1)}, u32[]{:S(2)}, u32[]{:S(2)}) collective-permute-start(bf16[512,384]{1,0:T(8,128)(2,1)S(1)} %get-tuple-element.51), channel_id=1, source_target_pairs={{0,24},{4,28},{8,12},{12,8},{16,20},{20,16},{24,0},{28,4},{1,25},{... | collective-permute-start | bytes 1179656 | tf_op jit(solution)/shard_map/ppermute | solution.py:250
  92.4 1.3 %prepare.1.refs_6_ = f32[8,384]{1,0:T(8,128)S(1)} custom-call(f32[3,1024,128]{2,1,0:T(8,128)S(1)} %copy-done, f32[8,128,384]{2,1,0:T(8,128)S(1)} %get-tuple-element.45.image_ref.refs_4_, bf16[512,384]{1,0:T(8,128)(2,1)S(1)} %get-tuple-element.54.refs_1_.refs_0_._), custom_call_target="tpu_custom_call" | custom-call | flops 8388608 | bytes 4194304 | tf_op jit(solution)/shard_map/prepare/pallas_call | solution.py:489
  93.8 2.6 %couple.13 = (f32[8,128,384]{2,1,0:T(8,128)}, f32[8,128,384]{2,1,0:T(8,128)S(1)}) custom-call(bf16[7,8,256,512]{3,2,1,0:T(8,128)(2,1)S(1)} %spread.1.dense_ref, f32[1,128]{1,0:T(1,128)S(1)} %bitcast.8, bf16[512,384]{1,0:T(8,128)(2,1)S(1)} %get-tuple-element.54.refs_1_.refs_0_._, bf16[528,384]{1,0:T(8,128)(2,1)S(1)} %collective-permute-done.3.refs_0_.refs_1_, ...), custom_call_target="tpu_custom_call" | custom-call | flops 805306368 | bytes 4194304 | tf_op jit(solution)/shard_map/couple/pallas_call | solution.py:387
  96.4 2.6 %couple.11.refs_1_ = f32[8,128,384]{2,1,0:T(8,128)S(1)} custom-call(bf16[7,8,256,512]{3,2,1,0:T(8,128)(2,1)S(1)} %spread.1.dense_ref, f32[1,128]{1,0:T(1,128)S(1)} %bitcast.9, bf16[512,384]{1,0:T(8,128)(2,1)S(1)} %collective-permute-done.12.refs_0_, bf16[512,384]{1,0:T(8,128)(2,1)S(1)} %get-tuple-element.54.refs_1_.refs_0_._, ...), custom_call_target="tpu_custom_call" | custom-call | flops 1610612736 | bytes 4194304 | tf_op jit(solution)/shard_map/couple/pallas_call | solution.py:387
  99.0 0.8 collective-permute-done.11.refs_0_
  99.8 1.4 %couple.12.refs_1_ = f32[8,128,384]{2,1,0:T(8,128)S(1)} custom-call(bf16[7,8,256,512]{3,2,1,0:T(8,128)(2,1)S(1)} %spread.1.dense_ref, f32[1,128]{1,0:T(1,128)S(1)} %bitcast.10, bf16[512,384]{1,0:T(8,128)(2,1)S(1)} %collective-permute-done.11.refs_0_, f32[8,128,384]{2,1,0:T(8,128)S(1)} %couple.11.refs_1_), custom_call_target="tpu_custom_call" | custom-call | flops 805306368 | bytes 4194304 | tf_op jit(solution)/shard_map/couple/pallas_call | solution.py:387
  101.3 3.0 %collective-permute-done.10.refs_0_ = bf16[512,384]{1,0:T(8,128)(2,1)S(1)} collective-permute-done((bf16[512,384]{1,0:T(8,128)(2,1)S(1)}, bf16[512,384]{1,0:T(8,128)(2,1)S(1)}, u32[]{:S(2)}, u32[]{:S(2)}) %collective-permute-start.10) | collective-permute-done | bytes 393248 | tf_op jit(solution)/shard_map/ppermute | solution.py:250
  104.2 2.0 %finish_second.1 = (f32[8,128,384]{2,1,0:T(8,128)S(1)}, f32[32,8,128]{2,1,0:T(8,128)S(1)}) custom-call(bf16[7,8,256,512]{3,2,1,0:T(8,128)(2,1)S(1)} %spread.1.dense_ref, f32[1,128]{1,0:T(1,128)S(1)} %bitcast.11, bf16[512,384]{1,0:T(8,128)(2,1)S(1)} %collective-permute-done.10.refs_0_, f32[8,128,384]{2,1,0:T(8,128)S(1)} %couple.12.refs_1_, ...), custom_call_target="tpu_custom_call" | custom-call | flops 805306368 | bytes 8388608 | tf_op jit(solution)/shard_map/finish_second/pallas_call | solution.py:546
  106.2 13.8 %all_to_all.5.gathered_ref = f32[32,8,128]{2,1,0:T(8,128)S(1)} all-to-all(f32[32,8,128]{2,1,0:T(8,128)S(1)} %get-tuple-element.59), channel_id=1, replica_groups=mesh['row'=8,'col'=4] {'row','col'}, dimensions={0} | all-to-all | bytes 262144 | tf_op jit(solution)/shard_map/all_to_all | solution.py:668
  120.0 2.6 %final.1 = (f32[3,1024,128]{2,1,0:T(8,128)}, f32[3,1024,128]{2,1,0:T(8,128)}) custom-call(f32[3,1024,128]{2,1,0:T(8,128)S(1)} %copy-done, f32[8,128,384]{2,1,0:T(8,128)S(1)} %get-tuple-element.45.image_ref.refs_4_, f32[8,128,384]{2,1,0:T(8,128)S(1)} %get-tuple-element.58.later_ref, f32[32,8,128]{2,1,0:T(8,128)S(1)} %all_to_all.5.gathered_ref), custom_call_target="tpu_custom_call" | custom-call | tf_op jit(solution)/shard_map/final/pallas_call | solution.py:622
  (15 shorter events, 0.0 us)
Async XLA Ops:
  0.6 15.8 %copy-start.8 = (s32[8,24]{1,0:T(8,128)S(1)}, s32[8,24]{1,0:T(8,128)}, u32[]{:S(2)}) copy-start(s32[8,24]{1,0:T(8,128)} %slot_ref.1) | copy-start | bytes 2308
  4.2 21.5 %collective-permute-start = (bf16[1040,384]{1,0:T(8,128)(2,1)}, bf16[1040,384]{1,0:T(8,128)(2,1)S(1)}, u32[]{:S(2)}, u32[]{:S(2)}) collective-permute-start(bf16[1040,384]{1,0:T(8,128)(2,1)} %get-tuple-element.31.refs_1_), channel_id=1, source_target_pairs={{8,16},{12,20},{16,8},{20,12},{9,17},{13,21},{17,9},{21,13},{10,18... | collective-permute-start | bytes 2396168 | tf_op jit(solution)/shard_map/ppermute | solution.py:244
  4.9 20.8 %collective-permute-start.1 = (bf16[528,384]{1,0:T(8,128)(2,1)}, bf16[528,384]{1,0:T(8,128)(2,1)S(1)}, u32[]{:S(2)}, u32[]{:S(2)}) collective-permute-start(bf16[528,384]{1,0:T(8,128)(2,1)} %get-tuple-element.33), channel_id=1, source_target_pairs={{0,4},{4,0},{8,12},{12,8},{16,20},{20,16},{24,28},{28,24},{1,5},{5... | collective-permute-start | bytes 1216520 | tf_op jit(solution)/shard_map/ppermute | solution.py:239
  7.9 17.8 %collective-permute-start.2 = (bf16[528,384]{1,0:T(8,128)(2,1)}, bf16[528,384]{1,0:T(8,128)(2,1)S(1)}, u32[]{:S(2)}, u32[]{:S(2)}) collective-permute-start(bf16[528,384]{1,0:T(8,128)(2,1)} %get-tuple-element.34), channel_id=1, source_target_pairs={{0,8},{4,12},{8,0},{12,4},{16,24},{20,28},{24,16},{28,20},{1,9},{5... | collective-permute-start | bytes 1216520 | tf_op jit(solution)/shard_map/ppermute | solution.py:239
  12.3 25.3 %collective-permute-start.5 = (bf16[528,384]{1,0:T(8,128)(2,1)}, bf16[528,384]{1,0:T(8,128)(2,1)S(1)}, u32[]{:S(2)}, u32[]{:S(2)}) collective-permute-start(bf16[528,384]{1,0:T(8,128)(2,1)} %get-tuple-element.38), channel_id=1, source_target_pairs={{0,12},{4,8},{8,4},{12,0},{16,28},{20,24},{24,20},{28,16},{1,13},{... | collective-permute-start | bytes 1216520 | tf_op jit(solution)/shard_map/ppermute | solution.py:239
  12.3 29.2 %collective-permute-start.6 = (bf16[528,384]{1,0:T(8,128)(2,1)}, bf16[528,384]{1,0:T(8,128)(2,1)S(1)}, u32[]{:S(2)}, u32[]{:S(2)}) collective-permute-start(bf16[528,384]{1,0:T(8,128)(2,1)} %get-tuple-element.40), channel_id=1, source_target_pairs={{0,28},{4,24},{24,4},{28,0},{1,29},{5,25},{25,5},{29,1},{2,30},{6,... | collective-permute-start | bytes 1216520 | tf_op jit(solution)/shard_map/ppermute | solution.py:239
  16.5 2.8 %copy-start.1 = (bf16[8,24,128,128]{3,2,1,0:T(8,128)(2,1)S(1)}, bf16[8,24,128,128]{3,2,1,0:T(8,128)(2,1)}, u32[]{:S(2)}) copy-start(bf16[8,24,128,128]{3,2,1,0:T(8,128)(2,1)} %ks_ref.1) | copy-start | bytes 18874372
  19.2 1.6 %copy-start.2 = (bf16[8,8,128,128]{3,2,1,0:T(8,128)(2,1)S(1)}, bf16[8,8,128,128]{3,2,1,0:T(8,128)(2,1)}, u32[]{:S(2)}) copy-start(bf16[8,8,128,128]{3,2,1,0:T(8,128)(2,1)} %correlation_ref.1) | copy-start | bytes 6291460
  20.8 4.9 %copy-start.3 = (bf16[528,384]{1,0:T(8,128)(2,1)S(1)}, bf16[528,384]{1,0:T(8,128)(2,1)}, u32[]{:S(2)}) copy-start(bf16[528,384]{1,0:T(8,128)(2,1)} %get-tuple-element.32.refs_1_.refs_4_) | copy-start | bytes 1216516
  20.8 4.9 %copy-start.5 = (f32[128]{0:T(128)S(1)}, f32[128]{0:T(128)}, u32[]{:S(2)}) copy-start(f32[128]{0:T(128)} %param.9) | copy-start | bytes 1540
  25.8 3.7 %copy-start.4 = (bf16[1040,384]{1,0:T(8,128)(2,1)S(1)}, bf16[1040,384]{1,0:T(8,128)(2,1)}, u32[]{:S(2)}) copy-start(bf16[1040,384]{1,0:T(8,128)(2,1)} %get-tuple-element.31.refs_1_) | copy-start | bytes 2396164
  25.8 3.7 %copy-start.6 = (s32[1,7,4]{1,2,0:T(4,128)S(1)}, s32[1,7,4]{1,2,0:T(4,128)}, u32[]{:S(2)}) copy-start(s32[1,7,4]{1,2,0:T(4,128)} %param.13) | copy-start | bytes 340
  29.5 7.9 %copy-start.7 = (f32[1024]{0:T(1024)S(1)}, f32[1024]{0:T(1024)}, u32[]{:S(2)}) copy-start(f32[1024]{0:T(1024)} %param.8) | copy-start | bytes 12292
  30.9 19.1 %collective-permute-start.4 = (bf16[528,384]{1,0:T(8,128)(2,1)S(1)}, bf16[528,384]{1,0:T(8,128)(2,1)S(1)}, u32[]{:S(2)}, u32[]{:S(2)}) collective-permute-start(bf16[528,384]{1,0:T(8,128)(2,1)S(1)} %get-tuple-element.37), channel_id=1, source_target_pairs={{0,20},{4,16},{8,4},{12,0},{16,28},{20,24},{24,12},{28,8},{1,21},{... | collective-permute-start | bytes 1216520 | tf_op jit(solution)/shard_map/ppermute | solution.py:251
  36.1 21.2 %collective-permute-start.3 = (bf16[528,384]{1,0:T(8,128)(2,1)S(1)}, bf16[528,384]{1,0:T(8,128)(2,1)S(1)}, u32[]{:S(2)}, u32[]{:S(2)}) collective-permute-start(bf16[528,384]{1,0:T(8,128)(2,1)S(1)} %get-tuple-element.36), channel_id=1, source_target_pairs={{0,24},{4,28},{8,12},{12,8},{16,20},{20,16},{24,0},{28,4},{1,25},{... | collective-permute-start | bytes 1216520 | tf_op jit(solution)/shard_map/ppermute | solution.py:250
  50.1 7.2 %copy-start = (f32[3,1024,128]{2,1,0:T(8,128)S(1)}, f32[3,1024,128]{2,1,0:T(8,128)}, u32[]{:S(2)}) copy-start(f32[3,1024,128]{2,1,0:T(8,128)} %right_ref.3) | copy-start | bytes 4718596
  59.5 23.9 %collective-permute-start.7 = (bf16[1024,384]{1,0:T(8,128)(2,1)S(1)}, bf16[1024,384]{1,0:T(8,128)(2,1)S(1)}, u32[]{:S(2)}, u32[]{:S(2)}) collective-permute-start(bf16[1024,384]{1,0:T(8,128)(2,1)S(1)} %get-tuple-element.46.refs_1_), channel_id=1, source_target_pairs={{8,16},{12,20},{16,8},{20,12},{9,17},{13,21},{17,9},{21,13},{10,18... | collective-permute-start | bytes 2359304 | tf_op jit(solution)/shard_map/ppermute | solution.py:244
  60.2 12.1 %collective-permute-start.8 = (bf16[512,384]{1,0:T(8,128)(2,1)S(1)}, bf16[512,384]{1,0:T(8,128)(2,1)S(1)}, u32[]{:S(2)}, u32[]{:S(2)}) collective-permute-start(bf16[512,384]{1,0:T(8,128)(2,1)S(1)} %get-tuple-element.48), channel_id=1, source_target_pairs={{0,8},{4,12},{8,0},{12,4},{16,24},{20,28},{24,16},{28,20},{1,9},{5... | collective-permute-start | bytes 1179656 | tf_op jit(solution)/shard_map/ppermute | solution.py:239
  60.3 19.5 %collective-permute-start.9 = (bf16[512,384]{1,0:T(8,128)(2,1)S(1)}, bf16[512,384]{1,0:T(8,128)(2,1)S(1)}, u32[]{:S(2)}, u32[]{:S(2)}) collective-permute-start(bf16[512,384]{1,0:T(8,128)(2,1)S(1)} %get-tuple-element.49), channel_id=1, source_target_pairs={{0,12},{4,8},{8,4},{12,0},{16,28},{20,24},{24,20},{28,16},{1,13},{... | collective-permute-start | bytes 1179656 | tf_op jit(solution)/shard_map/ppermute | solution.py:239
  62.3 34.1 %collective-permute-start.12 = (bf16[512,384]{1,0:T(8,128)(2,1)S(1)}, bf16[512,384]{1,0:T(8,128)(2,1)S(1)}, u32[]{:S(2)}, u32[]{:S(2)}) collective-permute-start(bf16[512,384]{1,0:T(8,128)(2,1)S(1)} %get-tuple-element.53), channel_id=1, source_target_pairs={{0,4},{4,0},{8,12},{12,8},{16,20},{20,16},{24,28},{28,24},{1,5},{5... | collective-permute-start | bytes 1179656 | tf_op jit(solution)/shard_map/ppermute | solution.py:239
  63.8 32.6 %collective-permute-start.13 = (bf16[512,384]{1,0:T(8,128)(2,1)S(1)}, bf16[512,384]{1,0:T(8,128)(2,1)S(1)}, u32[]{:S(2)}, u32[]{:S(2)}) collective-permute-start(bf16[512,384]{1,0:T(8,128)(2,1)S(1)} %get-tuple-element.55), channel_id=1, source_target_pairs={{0,28},{4,24},{24,4},{28,0},{1,29},{5,25},{25,5},{29,1},{2,30},{6,... | collective-permute-start | bytes 1179656 | tf_op jit(solution)/shard_map/ppermute | solution.py:239
  84.1 15.7 %collective-permute-start.11 = (bf16[512,384]{1,0:T(8,128)(2,1)S(1)}, bf16[512,384]{1,0:T(8,128)(2,1)S(1)}, u32[]{:S(2)}, u32[]{:S(2)}) collective-permute-start(bf16[512,384]{1,0:T(8,128)(2,1)S(1)} %get-tuple-element.52), channel_id=1, source_target_pairs={{0,20},{4,16},{8,4},{12,0},{16,28},{20,24},{24,12},{28,8},{1,21},{... | collective-permute-start | bytes 1179656 | tf_op jit(solution)/shard_map/ppermute | solution.py:251
  89.9 14.3 %collective-permute-start.10 = (bf16[512,384]{1,0:T(8,128)(2,1)S(1)}, bf16[512,384]{1,0:T(8,128)(2,1)S(1)}, u32[]{:S(2)}, u32[]{:S(2)}) collective-permute-start(bf16[512,384]{1,0:T(8,128)(2,1)S(1)} %get-tuple-element.51), channel_id=1, source_target_pairs={{0,24},{4,28},{8,12},{12,8},{16,20},{20,16},{24,0},{28,4},{1,25},{... | collective-permute-start | bytes 1179656 | tf_op jit(solution)/shard_map/ppermute | solution.py:250

commit v16 on v15

--- a/solution.py
+++ b/solution.py
@@ -77,6 +77,9 @@
             return [1, 2, 3, 7]
         far = range(self.middle, 0, -1)
         return [by for f in far for by in (f, -f)]
+
+    def again(self):
+        return [2, 3, 1] if self.relayed else self.direct()
 
     def reader(self, key, me):
         return me ^ key if self.relayed else lax.rem(me + key + self.count, self.count)
@@ -163,7 +166,7 @@
             pltpu.SemaphoreType.DMA((clusters,)),
             pltpu.SemaphoreType.DMA((2,)),
         ],
-        limit=54,
+        limit=51,
     )(readers, right_side, onsite)
     return dict(zip(keys, messages)), own, full
 
@@ -194,6 +197,8 @@
         readers_ref, mine_ref, full_ref, _, *refs = refs
         me = lax.axis_index("row")
         *messages, chosen_ref = refs if chosen is None else [*refs[1:], refs[0]]
+        beyond = messages[3:]
+        messages = messages[:3]
         if chosen is None:
             base = full_ref.shape[0] - EXTRA
             table = full_ref[base : base + EXTRA, 0:width].astype(jnp.float32)
@@ -211,7 +216,7 @@
 
         @pl.when(jnp.logical_not(is_inner(me)))
         def _():
-            for key, out in zip((6, 5), messages[1:]):
+            for key, out in zip((6, 5, 7), [*messages[1:], *beyond]):
                 offset = plan.offset(me, me ^ key)
                 clusters = [readers_ref[0, slot, offset] for slot in range(served)]
                 gather(clusters, mine_ref, out, width)
@@ -219,7 +224,8 @@
     inputs = [readers, mine, full, after] + ([] if chosen is None else [chosen])
     specs = [smem(), vmem(), vmem(), pl.BlockSpec(memory_space=pl.ANY)]
     specs += [] if chosen is None else [smem()]
-    shapes, outs = [message] * 3, [vmem()] * 3
+    count = 3 if chosen is None else 4
+    shapes, outs = [message] * count, [vmem()] * count
     if chosen is None:
         shapes.append(jax.ShapeDtypeStruct((3, served), jnp.int32))
         outs.append(smem())
@@ -239,17 +245,20 @@
     sent = {k: lax.ppermute(m, "row", plan.pairs(k)) for k, m in direct.items()}
     if not plan.relayed:
         items = [(own, 0)] + [(sent[k], k) for k in plan.direct()]
-        sums = begin(items[:3], None)
+        sums = begin(items[:2], None)
         return items, sums, None, sums[0]
     theirs = lax.ppermute(full, "row", [(i, i ^ 6) for i in INNER])
     items = [(own, 0)] + [(sent[k], k) for k in near]
-    sums = begin(items[:3], theirs if chosen is None else None)
-    (mine, near, far), chosen = relay(
+    first = chosen is None
+    sums = begin(items[:3], theirs) if first else begin(items[:2], None)
+    (mine, near, far, *beyond), chosen = relay(
         plan, readers, full, theirs, chosen, sums[0], served, width
     )
     near = lax.ppermute(near, "row", [(i, i ^ (1 if i in INNER else 6)) for i in range(plan.count)])
     far = lax.ppermute(far, "row", [(i, i ^ (3 if i in INNER else 5)) for i in range(plan.count)])
-    items += [((mine, sent[7]), (6, 7)), (far, 5), (near, (7, 6))]
+    over = sent[7] if first else lax.ppermute(beyond[0], "row", plan.pairs(7))
+    middle = [((mine, over), (6, 7)), (far, 5)]
+    items += (middle if first else middle[::-1]) + [(near, (7, 6))]
     return items, sums, chosen, mine
 
 
@@ -403,7 +412,7 @@
     fields = right_side.shape[0]
     width = height // 2
     count = len(vectors.arrays)
-    keys = plan.direct()
+    keys = plan.again()
     outs = len(keys) + 1
 
     def kernel(dense_ref, energies_ref, *refs):
@@ -644,8 +653,8 @@
     def begin(items, after):
         return couple(dense, Vectors(plan, items), energies, [], after)
 
-    def partial(items, sums):
-        for group in (items[3:-2], items[-2:-1]):
+    def partial(items, sums, begun):
+        for group in (items[begun:5], items[5:6]):
             sums = couple(dense, Vectors(plan, group), energies, sums)
         return sums, Vectors(plan, items[-1:])
 
@@ -653,7 +662,7 @@
     dense = spread(tile_slot, ks_tiles, correlation_tiles, span, served)
     items, sums, chosen, _ = exchange(plan, readers, direct, own, full, None, begin, (1, 2, 3), served, width)
     level = levels(onsite)
-    sums, last = partial(items, sums)
+    sums, last = partial(items, sums, 3 if plan.relayed else 2)
     image, full, direct, out = finish_first(
         plan, dense, last, energies, sums[0], right_side, level, own, readers
     )
@@ -661,7 +670,7 @@
     items, begun, _, mark = exchange(plan, readers, direct, out, full, chosen, begin, (2, 3, 1), served, width)
     lines = prepare(right_side, image, mark)
     _, weighted = couple(dense, last, energies, sums, mark)
-    (value,), last = partial(items, begun)
+    (value,), last = partial(items, begun, 2)
     later, gathered = finish_second(
         dense, last, energies, value, right_side, level, image, weighted, lines, devices
     )

time: 123 us -> 120 us (0.976)
  starting transfers between devices: 35.6 us -> 30.5 us
  waiting for transfers between devices: 30.9 us -> 35.7 us
  blocking collectives: 13.8 us -> 11.3 us
  Pallas kernels: 36.9 us -> 35.4 us
  local copies, waits for them, and re-layouts: 4.4 us -> 5.74 us
    ppermute x8 -> x7, waiting for transfers between devices: 15.6 us -> 20 us  [exchange(): sent = {k: lax.ppermute(m, 'row', plan.pairs(k)) for k, m in direct.items()}]
    ppermute x8 -> x7, starting transfers between devices: 19.4 us -> 15.1 us  [exchange(): sent = {k: lax.ppermute(m, 'row', plan.pairs(k)) for k, m in direct.items()}]
    ppermute x2, starting transfers between devices: 10.9 us -> 6.8 us  [exchange(): lax.ppermute(far, 'row', [(i, i ^ (3 if i in INNER else 5)) for i in rang...]
    ppermute x0 -> x1, starting transfers between devices: none -> 3.34 us  [exchange(): over = sent[7] if first else lax.ppermute(beyond[0], 'row', plan.pairs(7))]
    all_to_all x1, blocking collectives: 13.8 us -> 11.3 us  [body(): gathered = lax.all_to_all(gathered, ('row', 'col'), 0, 0)]
    pallas_call x1, Pallas kernels: 3.55 us -> 2.01 us  [pack(): call(kernel, 'pack', [message] * (len(keys) + 1) + [full], [pl.BlockSpec(...]
    unnamed x18 -> x14, local copies, waits for them, and re-layouts: 4.4 us -> 5.74 us
  transfers between devices with their start and end apart: 14 -> 14, of which waited for: 7 -> 6; matrix products, arithmetic and copies ran while one was open for 0% -> 0% of each run, Pallas kernels for 22% -> 22%
where the time goes in v16:
time: 120 us; the launch traced here: 119 us
  waiting for transfers between devices  35.7 us (30%)
  Pallas kernels  35.4 us (30%)
  starting transfers between devices  30.5 us (25%)
  blocking collectives  11.3 us (9%)
  local copies, waits for them, and re-layouts  5.74 us (5%)
    ppermute x7, waiting for transfers between devices, exchange(): sent = {k: lax.ppermute(m, 'row', plan.pairs(k)) for k, m in direct.items()}  20 us
    pallas_call x7, Pallas kernels, couple(): call(kernel, 'couple', [shape] * outs, [vmem()] * 2 + [pl.BlockSpec(memor...  18.1 us
    ppermute x7, starting transfers between devices, exchange(): sent = {k: lax.ppermute(m, 'row', plan.pairs(k)) for k, m in direct.items()}  15.1 us
    all_to_all x1, blocking collectives, body(): gathered = lax.all_to_all(gathered, ('row', 'col'), 0, 0)  11.3 us
    ppermute x2, waiting for transfers between devices, exchange(): lax.ppermute(near, 'row', [(i, i ^ (1 if i in INNER else 6)) for i in ran...  9.88 us
    ppermute x2, starting transfers between devices, exchange(): lax.ppermute(far, 'row', [(i, i ^ (3 if i in INNER else 5)) for i in rang...  6.8 us
    ppermute x2, waiting for transfers between devices, exchange(): lax.ppermute(far, 'row', [(i, i ^ (3 if i in INNER else 5)) for i in rang...  5.86 us
    unnamed x14, local copies, waits for them, and re-layouts  5.74 us
  transfers between devices with their start and end apart: 14, of which 6 were waited for; matrix products, arithmetic and copies ran while one was open for 0% of the time, Pallas kernels for 22%

profile of v16, /device:TPU:0, one launch (start us, length us, event | category | flops | bytes accessed | tf_op | source)
XLA Modules:
  0.0 119.5 jit_solution(13946894021945106145)
XLA Ops:
  0.6 0.7 copy-done.4
  1.3 0.7 copy-done.5
  2.0 2.0 %pack.1 = (bf16[528,384]{1,0:T(8,128)(2,1)S(1)}, bf16[528,384]{1,0:T(8,128)(2,1)S(1)}, bf16[528,384]{1,0:T(8,128)(2,1)S(1)}, bf16[528,384]{1,0:T(8,128)(2,1)S(1)...) custom-call(s32[1,4,7]{2,1,0:T(4,128)S(1)} %bitcast.12, f32[3,1024,128]{2,1,0:T(8,128)} %right_ref.3, ...), custom_call_target="tpu_custom_call" | custom-call | bytes 1048576 | tf_op jit(solution)/shard_map/pack/pallas_call | solution.py:157
  4.0 0.7 collective-permute-start
  4.7 3.0 %collective-permute-start.1 = (bf16[528,384]{1,0:T(8,128)(2,1)S(1)}, bf16[528,384]{1,0:T(8,128)(2,1)S(1)}, u32[]{:S(2)}, u32[]{:S(2)}) collective-permute-start(bf16[528,384]{1,0:T(8,128)(2,1)S(1)} %get-tuple-element.33), channel_id=1, source_target_pairs={{0,4},{4,0},{8,12},{12,8},{16,20},{20,16},{24,28},{28,24},{1,5},{5... | collective-permute-start | bytes 1216520 | tf_op jit(solution)/shard_map/ppermute | solution.py:245
  7.8 4.3 %collective-permute-start.2 = (bf16[528,384]{1,0:T(8,128)(2,1)S(1)}, bf16[528,384]{1,0:T(8,128)(2,1)S(1)}, u32[]{:S(2)}, u32[]{:S(2)}) collective-permute-start(bf16[528,384]{1,0:T(8,128)(2,1)S(1)} %get-tuple-element.34), channel_id=1, source_target_pairs={{0,8},{4,12},{8,0},{12,4},{16,24},{20,28},{24,16},{28,20},{1,9},{5... | collective-permute-start | bytes 1216520 | tf_op jit(solution)/shard_map/ppermute | solution.py:245
  12.1 0.0 collective-permute-start.5
  12.1 4.1 %collective-permute-start.6 = (bf16[528,384]{1,0:T(8,128)(2,1)S(1)}, bf16[528,384]{1,0:T(8,128)(2,1)S(1)}, u32[]{:S(2)}, u32[]{:S(2)}) collective-permute-start(bf16[528,384]{1,0:T(8,128)(2,1)S(1)} %get-tuple-element.40), channel_id=1, source_target_pairs={{0,28},{4,24},{24,4},{28,0},{1,29},{5,25},{25,5},{29,1},{2,30},{6,... | collective-permute-start | bytes 1216520 | tf_op jit(solution)/shard_map/ppermute | solution.py:245
  16.3 0.0 copy-start.1
  16.3 2.8 %copy-done.1 = bf16[8,24,128,128]{3,2,1,0:T(8,128)(2,1)S(1)} copy-done((bf16[8,24,128,128]{3,2,1,0:T(8,128)(2,1)S(1)}, bf16[8,24,128,128]{3,2,1,0:T(8,128)(2,1)}, u32[]{:S(2)}) %copy-start.1) | copy-done | bytes 6291480
  19.1 1.6 %copy-done.2 = bf16[8,8,128,128]{3,2,1,0:T(8,128)(2,1)S(1)} copy-done((bf16[8,8,128,128]{3,2,1,0:T(8,128)(2,1)S(1)}, bf16[8,8,128,128]{3,2,1,0:T(8,128)(2,1)}, u32[]{:S(2)}) %copy-start.2) | copy-done | bytes 2097176
  20.7 4.9 %spread.1.dense_ref = bf16[7,8,256,512]{3,2,1,0:T(8,128)(2,1)S(1)} custom-call(s32[8,24]{1,0:T(8,128)S(1)} %copy-done.6, bf16[8,24,128,128]{3,2,1,0:T(8,128)(2,1)S(1)} %copy-done.1, bf16[8,8,128,128]{3,2,1,0:T(8,128)(2,1)S(1)} %copy-done.2), custom_call_target="tpu_custom_call" | custom-call | bytes 16777216 | tf_op jit(solution)/shard_map/spread/pallas_call | solution.py:338
  25.5 0.0 collective-permute-done.1.refs_2_
  25.5 0.0 collective-permute-done.2.refs_3_
  25.6 0.0 collective-permute-done.refs_0_.refs_2_
  25.6 3.7 %couple.7 = (f32[8,128,384]{2,1,0:T(8,128)S(1)}, f32[8,128,384]{2,1,0:T(8,128)S(1)}) custom-call(bf16[7,8,256,512]{3,2,1,0:T(8,128)(2,1)S(1)} %spread.1.dense_ref, f32[1,128]{1,0:T(1,128)S(1)} %bitcast.3, bf16[1040,384]{1,0:T(8,128)(2,1)S(1)} %collective-permute-done.refs_0_.refs_2_, bf16[528,384]{1,0:T(8,128)(2,1)S(1)} %get-tuple-element.32.refs_1_.refs_4_, ...), custom_call_target="tpu_custom_call" | custom-call | flops 2415919104 | bytes 4194304 | tf_op jit(solution)/shard_map/couple/pallas_call | solution.py:396
  29.3 1.4 %relay.2 = (bf16[528,384]{1,0:T(8,128)(2,1)S(1)}, bf16[528,384]{1,0:T(8,128)(2,1)S(1)}, bf16[528,384]{1,0:T(8,128)(2,1)S(1)}, s32[3,4]{1,0:T(4,128)S(1)}) custom-call(s32[1,4,7]{2,1,0:T(4,128)S(1)} %bitcast.13, bf16[1040,384]{1,0:T(8,128)(2,1)S(1)} %get-tuple-element.31.refs_1_, bf16[1040,384]{1,0:T(8,128)(2,1)S(1)} %collective-permute-done.refs_0_.refs_2_, ...), custom_call_target="tpu_custom_call" | custom-call | bytes 1048576 | tf_op jit(solution)/shard_map/relay/pallas_call | solution.py:232
  30.7 4.9 %collective-permute-start.4 = (bf16[528,384]{1,0:T(8,128)(2,1)S(1)}, bf16[528,384]{1,0:T(8,128)(2,1)S(1)}, u32[]{:S(2)}, u32[]{:S(2)}) collective-permute-start(bf16[528,384]{1,0:T(8,128)(2,1)S(1)} %get-tuple-element.37), channel_id=1, source_target_pairs={{0,20},{4,16},{8,4},{12,0},{16,28},{20,24},{24,12},{28,8},{1,21},{... | collective-permute-start | bytes 1216520 | tf_op jit(solution)/shard_map/ppermute | solution.py:258
  35.6 1.3 %collective-permute-start.3 = (bf16[528,384]{1,0:T(8,128)(2,1)S(1)}, bf16[528,384]{1,0:T(8,128)(2,1)S(1)}, u32[]{:S(2)}, u32[]{:S(2)}) collective-permute-start(bf16[528,384]{1,0:T(8,128)(2,1)S(1)} %get-tuple-element.36), channel_id=1, source_target_pairs={{0,24},{4,28},{8,12},{12,8},{16,20},{20,16},{24,0},{28,4},{1,25},{... | collective-permute-start | bytes 1216520 | tf_op jit(solution)/shard_map/ppermute | solution.py:257
  37.0 0.2 levels.1.refs_3_
  37.2 0.0 collective-permute-done.5.refs_0_
  37.2 3.9 %collective-permute-done.6.refs_2_ = bf16[528,384]{1,0:T(8,128)(2,1)S(1)} collective-permute-done((bf16[528,384]{1,0:T(8,128)(2,1)S(1)}, bf16[528,384]{1,0:T(8,128)(2,1)S(1)}, u32[]{:S(2)}, u32[]{:S(2)}) %collective-permute-start.6) | collective-permute-done | bytes 405536 | tf_op jit(solution)/shard_map/ppermute | solution.py:245
  41.1 2.7 %couple.8 = (f32[8,128,384]{2,1,0:T(8,128)S(1)}, f32[8,128,384]{2,1,0:T(8,128)S(1)}) custom-call(bf16[7,8,256,512]{3,2,1,0:T(8,128)(2,1)S(1)} %spread.1.dense_ref, f32[1,128]{1,0:T(1,128)S(1)} %bitcast.4, bf16[528,384]{1,0:T(8,128)(2,1)S(1)} %collective-permute-done.5.refs_0_, bf16[528,384]{1,0:T(8,128)(2,1)S(1)} %get-tuple-element.39.refs_1_, ...), custom_call_target="tpu_custom_call" | custom-call | flops 1610612736 | bytes 4194304 | tf_op jit(solution)/shard_map/couple/pallas_call | solution.py:396
  43.8 5.9 %collective-permute-done.4.refs_0_ = bf16[528,384]{1,0:T(8,128)(2,1)S(1)} collective-permute-done((bf16[528,384]{1,0:T(8,128)(2,1)S(1)}, bf16[528,384]{1,0:T(8,128)(2,1)S(1)}, u32[]{:S(2)}, u32[]{:S(2)}) %collective-permute-start.4) | collective-permute-done | bytes 405536 | tf_op jit(solution)/shard_map/ppermute | solution.py:258
  49.7 1.4 %couple.9 = (f32[8,128,384]{2,1,0:T(8,128)S(1)}, f32[8,128,384]{2,1,0:T(8,128)S(1)}) custom-call(bf16[7,8,256,512]{3,2,1,0:T(8,128)(2,1)S(1)} %spread.1.dense_ref, f32[1,128]{1,0:T(1,128)S(1)} %bitcast.5, bf16[528,384]{1,0:T(8,128)(2,1)S(1)} %collective-permute-done.4.refs_0_, f32[8,128,384]{2,1,0:T(8,128)S(1)} %get-tuple-element.42.refs_1_, ...), custom_call_target="tpu_custom_call" | custom-call | flops 805306368 | bytes 4194304 | tf_op jit(solution)/shard_map/couple/pallas_call | solution.py:396
  51.1 5.7 %collective-permute-done.3.refs_0_.refs_1_ = bf16[528,384]{1,0:T(8,128)(2,1)S(1)} collective-permute-done((bf16[528,384]{1,0:T(8,128)(2,1)S(1)}, bf16[528,384]{1,0:T(8,128)(2,1)S(1)}, u32[]{:S(2)}, u32[]{:S(2)}) %collective-permute-start.3) | collective-permute-done | bytes 405536 | tf_op jit(solution)/shard_map/ppermute | solution.py:257
  56.8 2.2 %finish_first.1 = (f32[8,128,384]{2,1,0:T(8,128)S(1)}, bf16[1024,384]{1,0:T(8,128)(2,1)S(1)}, bf16[512,384]{1,0:T(8,128)(2,1)S(1)}, bf16[512,384]{1,0:T(8,128)(2...) custom-call(bf16[7,8,256,512]{3,2,1,0:T(8,128)(2,1)S(1)} %spread.1.dense_ref, f32[1,128]{1,0:T(1,128)S(1)} %bitcast.6, ...), custom_call_target="tpu_custom_call" | custom-call | flops 805306368 | bytes 8388608 | tf_op jit(solution)/shard_map/finish_first/pallas_call | solution.py:442
  59.1 0.7 collective-permute-start.7
  59.8 0.1 collective-permute-start.8
  59.9 2.0 %collective-permute-start.11 = (bf16[512,384]{1,0:T(8,128)(2,1)S(1)}, bf16[512,384]{1,0:T(8,128)(2,1)S(1)}, u32[]{:S(2)}, u32[]{:S(2)}) collective-permute-start(bf16[512,384]{1,0:T(8,128)(2,1)S(1)} %get-tuple-element.53), channel_id=1, source_target_pairs={{0,12},{4,8},{8,4},{12,0},{16,28},{20,24},{24,20},{28,16},{1,13},{... | collective-permute-start | bytes 1179656 | tf_op jit(solution)/shard_map/ppermute | solution.py:245
  61.8 1.5 %collective-permute-start.12 = (bf16[512,384]{1,0:T(8,128)(2,1)S(1)}, bf16[512,384]{1,0:T(8,128)(2,1)S(1)}, u32[]{:S(2)}, u32[]{:S(2)}) collective-permute-start(bf16[512,384]{1,0:T(8,128)(2,1)S(1)} %get-tuple-element.54), channel_id=1, source_target_pairs={{0,4},{4,0},{8,12},{12,8},{16,20},{20,16},{24,28},{28,24},{1,5},{5... | collective-permute-start | bytes 1179656 | tf_op jit(solution)/shard_map/ppermute | solution.py:245
  63.4 8.6 %collective-permute-done.8.refs_1_ = bf16[512,384]{1,0:T(8,128)(2,1)S(1)} collective-permute-done((bf16[512,384]{1,0:T(8,128)(2,1)S(1)}, bf16[512,384]{1,0:T(8,128)(2,1)S(1)}, u32[]{:S(2)}, u32[]{:S(2)}) %collective-permute-start.8) | collective-permute-done | bytes 393248 | tf_op jit(solution)/shard_map/ppermute | solution.py:245
  71.9 2.5 %couple.10.refs_3_ = f32[8,128,384]{2,1,0:T(8,128)S(1)} custom-call(bf16[7,8,256,512]{3,2,1,0:T(8,128)(2,1)S(1)} %spread.1.dense_ref, f32[1,128]{1,0:T(1,128)S(1)} %bitcast.7, bf16[512,384]{1,0:T(8,128)(2,1)S(1)} %get-tuple-element.47.refs_0_, bf16[512,384]{1,0:T(8,128)(2,1)S(1)} %collective-permute-done.8.refs_1_), custom_call_target="tpu_custom_call" | custom-call | flops 1610612736 | bytes 4194304 | tf_op jit(solution)/shard_map/couple/pallas_call | solution.py:396
  74.4 0.0 collective-permute-done.7.refs_2_
  74.4 0.7 relay.3
  75.2 1.9 %collective-permute-start.13 = (bf16[512,384]{1,0:T(8,128)(2,1)S(1)}, bf16[512,384]{1,0:T(8,128)(2,1)S(1)}, u32[]{:S(2)}, u32[]{:S(2)}) collective-permute-start(bf16[512,384]{1,0:T(8,128)(2,1)S(1)} %get-tuple-element.55), channel_id=1, source_target_pairs={{0,20},{4,16},{8,4},{12,0},{16,28},{20,24},{24,12},{28,8},{1,21},{... | collective-permute-start | bytes 1179656 | tf_op jit(solution)/shard_map/ppermute | solution.py:258
  77.0 3.3 %collective-permute-start.10 = (bf16[512,384]{1,0:T(8,128)(2,1)S(1)}, bf16[512,384]{1,0:T(8,128)(2,1)S(1)}, u32[]{:S(2)}, u32[]{:S(2)}) collective-permute-start(bf16[512,384]{1,0:T(8,128)(2,1)S(1)} %get-tuple-element.52), channel_id=1, source_target_pairs={{0,28},{4,24},{24,4},{28,0},{1,29},{5,25},{25,5},{29,1},{2,30},{6,... | collective-permute-start | bytes 1179656 | tf_op jit(solution)/shard_map/ppermute | solution.py:259
  80.4 2.5 %collective-permute-start.9 = (bf16[512,384]{1,0:T(8,128)(2,1)S(1)}, bf16[512,384]{1,0:T(8,128)(2,1)S(1)}, u32[]{:S(2)}, u32[]{:S(2)}) collective-permute-start(bf16[512,384]{1,0:T(8,128)(2,1)S(1)} %get-tuple-element.50), channel_id=1, source_target_pairs={{0,24},{4,28},{8,12},{12,8},{16,20},{20,16},{24,0},{28,4},{1,25},{... | collective-permute-start | bytes 1179656 | tf_op jit(solution)/shard_map/ppermute | solution.py:257
  82.9 1.3 %prepare.1.refs_6_ = f32[8,384]{1,0:T(8,128)S(1)} custom-call(f32[3,1024,128]{2,1,0:T(8,128)S(1)} %copy-done, f32[8,128,384]{2,1,0:T(8,128)S(1)} %get-tuple-element.45.image_ref.refs_4_, bf16[512,384]{1,0:T(8,128)(2,1)S(1)} %get-tuple-element.51.refs_0_._), custom_call_target="tpu_custom_call" | custom-call | flops 8388608 | bytes 4194304 | tf_op jit(solution)/shard_map/prepare/pallas_call | solution.py:498
  84.3 2.6 %couple.13 = (f32[8,128,384]{2,1,0:T(8,128)}, f32[8,128,384]{2,1,0:T(8,128)S(1)}) custom-call(bf16[7,8,256,512]{3,2,1,0:T(8,128)(2,1)S(1)} %spread.1.dense_ref, f32[1,128]{1,0:T(1,128)S(1)} %bitcast.8, bf16[512,384]{1,0:T(8,128)(2,1)S(1)} %get-tuple-element.51.refs_0_._, bf16[528,384]{1,0:T(8,128)(2,1)S(1)} %collective-permute-done.3.refs_0_.refs_1_, ...), custom_call_target="tpu_custom_call" | custom-call | flops 805306368 | bytes 4194304 | tf_op jit(solution)/shard_map/couple/pallas_call | solution.py:396
  86.9 7.4 %collective-permute-done.12.refs_1_ = bf16[512,384]{1,0:T(8,128)(2,1)S(1)} collective-permute-done((bf16[512,384]{1,0:T(8,128)(2,1)S(1)}, bf16[512,384]{1,0:T(8,128)(2,1)S(1)}, u32[]{:S(2)}, u32[]{:S(2)}) %collective-permute-start.12) | collective-permute-done | bytes 393248 | tf_op jit(solution)/shard_map/ppermute | solution.py:245
  94.3 0.0 collective-permute-done.13.refs_2_
  94.3 3.7 %couple.11.refs_2_ = f32[8,128,384]{2,1,0:T(8,128)S(1)} custom-call(bf16[7,8,256,512]{3,2,1,0:T(8,128)(2,1)S(1)} %spread.1.dense_ref, f32[1,128]{1,0:T(1,128)S(1)} %bitcast.9, bf16[512,384]{1,0:T(8,128)(2,1)S(1)} %collective-permute-done.11.refs_0_, bf16[512,384]{1,0:T(8,128)(2,1)S(1)} %collective-permute-done.12.refs_1_, ...), custom_call_target="tpu_custom_call" | custom-call | flops 2415919104 | bytes 4194304 | tf_op jit(solution)/shard_map/couple/pallas_call | solution.py:396
  98.0 1.5 %couple.12.refs_1_ = f32[8,128,384]{2,1,0:T(8,128)S(1)} custom-call(bf16[7,8,256,512]{3,2,1,0:T(8,128)(2,1)S(1)} %spread.1.dense_ref, f32[1,128]{1,0:T(1,128)S(1)} %bitcast.10, bf16[512,384]{1,0:T(8,128)(2,1)S(1)} %get-tuple-element.51.refs_0_._, bf16[512,384]{1,0:T(8,128)(2,1)S(1)} %collective-permute-done.10.refs_1_, f32[8,128,384]{2,1,0:T(8,128)S(1)} %couple.11.refs_2_), custom_call_target="tpu_custom_call" | custom-call | flops 805306368 | bytes 4194304 | tf_op jit(solution)/shard_map/couple/pallas_call | solution.py:396
  99.5 4.2 %collective-permute-done.9.refs_0_ = bf16[512,384]{1,0:T(8,128)(2,1)S(1)} collective-permute-done((bf16[512,384]{1,0:T(8,128)(2,1)S(1)}, bf16[512,384]{1,0:T(8,128)(2,1)S(1)}, u32[]{:S(2)}, u32[]{:S(2)}) %collective-permute-start.9) | collective-permute-done | bytes 393248 | tf_op jit(solution)/shard_map/ppermute | solution.py:257
  103.7 1.9 %finish_second.1 = (f32[8,128,384]{2,1,0:T(8,128)S(1)}, f32[32,8,128]{2,1,0:T(8,128)S(1)}) custom-call(bf16[7,8,256,512]{3,2,1,0:T(8,128)(2,1)S(1)} %spread.1.dense_ref, f32[1,128]{1,0:T(1,128)S(1)} %bitcast.11, bf16[512,384]{1,0:T(8,128)(2,1)S(1)} %collective-permute-done.9.refs_0_, f32[8,128,384]{2,1,0:T(8,128)S(1)} %couple.12.refs_1_, ...), custom_call_target="tpu_custom_call" | custom-call | flops 805306368 | bytes 8388608 | tf_op jit(solution)/shard_map/finish_second/pallas_call | solution.py:555
  105.6 11.3 %all_to_all.5.gathered_ref = f32[32,8,128]{2,1,0:T(8,128)S(1)} all-to-all(f32[32,8,128]{2,1,0:T(8,128)S(1)} %get-tuple-element.59), channel_id=1, replica_groups=mesh['row'=8,'col'=4] {'row','col'}, dimensions={0} | all-to-all | bytes 262144 | tf_op jit(solution)/shard_map/all_to_all | solution.py:677
  116.9 2.6 %final.1 = (f32[3,1024,128]{2,1,0:T(8,128)}, f32[3,1024,128]{2,1,0:T(8,128)}) custom-call(f32[3,1024,128]{2,1,0:T(8,128)S(1)} %copy-done, f32[8,128,384]{2,1,0:T(8,128)S(1)} %get-tuple-element.45.image_ref.refs_4_, f32[8,128,384]{2,1,0:T(8,128)S(1)} %get-tuple-element.58.later_ref, f32[32,8,128]{2,1,0:T(8,128)S(1)} %all_to_all.5.gathered_ref), custom_call_target="tpu_custom_call" | custom-call | tf_op jit(solution)/shard_map/final/pallas_call | solution.py:631
  (11 shorter events, 0.0 us)
Async XLA Ops:
  0.6 0.7 copy-start.4
  1.3 0.7 copy-start.5
  2.0 14.3 %copy-start.6 = (s32[8,24]{1,0:T(8,128)S(1)}, s32[8,24]{1,0:T(8,128)}, u32[]{:S(2)}) copy-start(s32[8,24]{1,0:T(8,128)} %slot_ref.1) | copy-start | bytes 2308
  4.0 21.5 %collective-permute-start = (bf16[1040,384]{1,0:T(8,128)(2,1)S(1)}, bf16[1040,384]{1,0:T(8,128)(2,1)S(1)}, u32[]{:S(2)}, u32[]{:S(2)}) collective-permute-start(bf16[1040,384]{1,0:T(8,128)(2,1)S(1)} %get-tuple-element.31.refs_1_), channel_id=1, source_target_pairs={{8,16},{12,20},{16,8},{20,12},{9,17},{13,21},{17,9},{21,13},{10,18... | collective-permute-start | bytes 2396168 | tf_op jit(solution)/shard_map/ppermute | solution.py:250
  4.7 20.8 %collective-permute-start.1 = (bf16[528,384]{1,0:T(8,128)(2,1)S(1)}, bf16[528,384]{1,0:T(8,128)(2,1)S(1)}, u32[]{:S(2)}, u32[]{:S(2)}) collective-permute-start(bf16[528,384]{1,0:T(8,128)(2,1)S(1)} %get-tuple-element.33), channel_id=1, source_target_pairs={{0,4},{4,0},{8,12},{12,8},{16,20},{20,16},{24,28},{28,24},{1,5},{5... | collective-permute-start | bytes 1216520 | tf_op jit(solution)/shard_map/ppermute | solution.py:245
  7.8 17.8 %collective-permute-start.2 = (bf16[528,384]{1,0:T(8,128)(2,1)S(1)}, bf16[528,384]{1,0:T(8,128)(2,1)S(1)}, u32[]{:S(2)}, u32[]{:S(2)}) collective-permute-start(bf16[528,384]{1,0:T(8,128)(2,1)S(1)} %get-tuple-element.34), channel_id=1, source_target_pairs={{0,8},{4,12},{8,0},{12,4},{16,24},{20,28},{24,16},{28,20},{1,9},{5... | collective-permute-start | bytes 1216520 | tf_op jit(solution)/shard_map/ppermute | solution.py:245
  12.1 25.1 %collective-permute-start.5 = (bf16[528,384]{1,0:T(8,128)(2,1)S(1)}, bf16[528,384]{1,0:T(8,128)(2,1)S(1)}, u32[]{:S(2)}, u32[]{:S(2)}) collective-permute-start(bf16[528,384]{1,0:T(8,128)(2,1)S(1)} %get-tuple-element.38), channel_id=1, source_target_pairs={{0,12},{4,8},{8,4},{12,0},{16,28},{20,24},{24,20},{28,16},{1,13},{... | collective-permute-start | bytes 1216520 | tf_op jit(solution)/shard_map/ppermute | solution.py:245
  12.1 29.0 %collective-permute-start.6 = (bf16[528,384]{1,0:T(8,128)(2,1)S(1)}, bf16[528,384]{1,0:T(8,128)(2,1)S(1)}, u32[]{:S(2)}, u32[]{:S(2)}) collective-permute-start(bf16[528,384]{1,0:T(8,128)(2,1)S(1)} %get-tuple-element.40), channel_id=1, source_target_pairs={{0,28},{4,24},{24,4},{28,0},{1,29},{5,25},{25,5},{29,1},{2,30},{6,... | collective-permute-start | bytes 1216520 | tf_op jit(solution)/shard_map/ppermute | solution.py:245
  16.3 2.8 %copy-start.1 = (bf16[8,24,128,128]{3,2,1,0:T(8,128)(2,1)S(1)}, bf16[8,24,128,128]{3,2,1,0:T(8,128)(2,1)}, u32[]{:S(2)}) copy-start(bf16[8,24,128,128]{3,2,1,0:T(8,128)(2,1)} %ks_ref.1) | copy-start | bytes 18874372
  19.1 1.6 %copy-start.2 = (bf16[8,8,128,128]{3,2,1,0:T(8,128)(2,1)S(1)}, bf16[8,8,128,128]{3,2,1,0:T(8,128)(2,1)}, u32[]{:S(2)}) copy-start(bf16[8,8,128,128]{3,2,1,0:T(8,128)(2,1)} %correlation_ref.1) | copy-start | bytes 6291460
  20.7 4.9 %copy-start.3 = (f32[128]{0:T(128)S(1)}, f32[128]{0:T(128)}, u32[]{:S(2)}) copy-start(f32[128]{0:T(128)} %param.9) | copy-start | bytes 1540
  30.7 19.0 %collective-permute-start.4 = (bf16[528,384]{1,0:T(8,128)(2,1)S(1)}, bf16[528,384]{1,0:T(8,128)(2,1)S(1)}, u32[]{:S(2)}, u32[]{:S(2)}) collective-permute-start(bf16[528,384]{1,0:T(8,128)(2,1)S(1)} %get-tuple-element.37), channel_id=1, source_target_pairs={{0,20},{4,16},{8,4},{12,0},{16,28},{20,24},{24,12},{28,8},{1,21},{... | collective-permute-start | bytes 1216520 | tf_op jit(solution)/shard_map/ppermute | solution.py:258
  35.6 21.2 %collective-permute-start.3 = (bf16[528,384]{1,0:T(8,128)(2,1)S(1)}, bf16[528,384]{1,0:T(8,128)(2,1)S(1)}, u32[]{:S(2)}, u32[]{:S(2)}) collective-permute-start(bf16[528,384]{1,0:T(8,128)(2,1)S(1)} %get-tuple-element.36), channel_id=1, source_target_pairs={{0,24},{4,28},{8,12},{12,8},{16,20},{20,16},{24,0},{28,4},{1,25},{... | collective-permute-start | bytes 1216520 | tf_op jit(solution)/shard_map/ppermute | solution.py:257
  49.7 7.2 %copy-start = (f32[3,1024,128]{2,1,0:T(8,128)S(1)}, f32[3,1024,128]{2,1,0:T(8,128)}, u32[]{:S(2)}) copy-start(f32[3,1024,128]{2,1,0:T(8,128)} %right_ref.3) | copy-start | bytes 4718596
  59.1 15.4 %collective-permute-start.7 = (bf16[1024,384]{1,0:T(8,128)(2,1)S(1)}, bf16[1024,384]{1,0:T(8,128)(2,1)S(1)}, u32[]{:S(2)}, u32[]{:S(2)}) collective-permute-start(bf16[1024,384]{1,0:T(8,128)(2,1)S(1)} %get-tuple-element.46.refs_1_), channel_id=1, source_target_pairs={{8,16},{12,20},{16,8},{20,12},{9,17},{13,21},{17,9},{21,13},{10,18... | collective-permute-start | bytes 2359304 | tf_op jit(solution)/shard_map/ppermute | solution.py:250
  59.8 12.1 %collective-permute-start.8 = (bf16[512,384]{1,0:T(8,128)(2,1)S(1)}, bf16[512,384]{1,0:T(8,128)(2,1)S(1)}, u32[]{:S(2)}, u32[]{:S(2)}) collective-permute-start(bf16[512,384]{1,0:T(8,128)(2,1)S(1)} %get-tuple-element.48), channel_id=1, source_target_pairs={{0,8},{4,12},{8,0},{12,4},{16,24},{20,28},{24,16},{28,20},{1,9},{5... | collective-permute-start | bytes 1179656 | tf_op jit(solution)/shard_map/ppermute | solution.py:245
  59.9 27.0 %collective-permute-start.11 = (bf16[512,384]{1,0:T(8,128)(2,1)S(1)}, bf16[512,384]{1,0:T(8,128)(2,1)S(1)}, u32[]{:S(2)}, u32[]{:S(2)}) collective-permute-start(bf16[512,384]{1,0:T(8,128)(2,1)S(1)} %get-tuple-element.53), channel_id=1, source_target_pairs={{0,12},{4,8},{8,4},{12,0},{16,28},{20,24},{24,20},{28,16},{1,13},{... | collective-permute-start | bytes 1179656 | tf_op jit(solution)/shard_map/ppermute | solution.py:245
  61.8 32.5 %collective-permute-start.12 = (bf16[512,384]{1,0:T(8,128)(2,1)S(1)}, bf16[512,384]{1,0:T(8,128)(2,1)S(1)}, u32[]{:S(2)}, u32[]{:S(2)}) collective-permute-start(bf16[512,384]{1,0:T(8,128)(2,1)S(1)} %get-tuple-element.54), channel_id=1, source_target_pairs={{0,4},{4,0},{8,12},{12,8},{16,20},{20,16},{24,28},{28,24},{1,5},{5... | collective-permute-start | bytes 1179656 | tf_op jit(solution)/shard_map/ppermute | solution.py:245
  75.2 19.1 %collective-permute-start.13 = (bf16[512,384]{1,0:T(8,128)(2,1)S(1)}, bf16[512,384]{1,0:T(8,128)(2,1)S(1)}, u32[]{:S(2)}, u32[]{:S(2)}) collective-permute-start(bf16[512,384]{1,0:T(8,128)(2,1)S(1)} %get-tuple-element.55), channel_id=1, source_target_pairs={{0,20},{4,16},{8,4},{12,0},{16,28},{20,24},{24,12},{28,8},{1,21},{... | collective-permute-start | bytes 1179656 | tf_op jit(solution)/shard_map/ppermute | solution.py:258
  77.0 21.0 %collective-permute-start.10 = (bf16[512,384]{1,0:T(8,128)(2,1)S(1)}, bf16[512,384]{1,0:T(8,128)(2,1)S(1)}, u32[]{:S(2)}, u32[]{:S(2)}) collective-permute-start(bf16[512,384]{1,0:T(8,128)(2,1)S(1)} %get-tuple-element.52), channel_id=1, source_target_pairs={{0,28},{4,24},{24,4},{28,0},{1,29},{5,25},{25,5},{29,1},{2,30},{6,... | collective-permute-start | bytes 1179656 | tf_op jit(solution)/shard_map/ppermute | solution.py:259
  80.4 23.3 %collective-permute-start.9 = (bf16[512,384]{1,0:T(8,128)(2,1)S(1)}, bf16[512,384]{1,0:T(8,128)(2,1)S(1)}, u32[]{:S(2)}, u32[]{:S(2)}) collective-permute-start(bf16[512,384]{1,0:T(8,128)(2,1)S(1)} %get-tuple-element.50), channel_id=1, source_target_pairs={{0,24},{4,28},{8,12},{12,8},{16,20},{20,16},{24,0},{28,4},{1,25},{... | collective-permute-start | bytes 1179656 | tf_op jit(solution)/shard_map/ppermute | solution.py:257

commit v17 on v16

--- a/solution.py
+++ b/solution.py
@@ -660,7 +660,7 @@
 
     direct, own, full = pack(plan, readers, right_side, onsite)
     dense = spread(tile_slot, ks_tiles, correlation_tiles, span, served)
-    items, sums, chosen, _ = exchange(plan, readers, direct, own, full, None, begin, (1, 2, 3), served, width)
+    items, sums, chosen, _ = exchange(plan, readers, direct, own, full, None, begin, (2, 1, 3), served, width)
     level = levels(onsite)
     sums, last = partial(items, sums, 3 if plan.relayed else 2)
     image, full, direct, out = finish_first(

time: 120 us -> 126 us (1.050)
  starting transfers between devices: 30.5 us -> 33.5 us
  waiting for transfers between devices: 35.7 us -> 37.4 us
  blocking collectives: 11.3 us -> 12.8 us
    ppermute x2, waiting for transfers between devices: 9.88 us -> 0.69 us  [exchange(): lax.ppermute(near, 'row', [(i, i ^ (1 if i in INNER else 6)) for i in ran...]
    ppermute x1, starting transfers between devices: 3.34 us -> 11.8 us  [exchange(): over = sent[7] if first else lax.ppermute(beyond[0], 'row', plan.pairs(7))]
    ppermute x2, waiting for transfers between devices: 5.86 us -> 12.3 us  [exchange(): lax.ppermute(far, 'row', [(i, i ^ (3 if i in INNER else 5)) for i in rang...]
    ppermute x7, waiting for transfers between devices: 20 us -> 24.3 us  [exchange(): sent = {k: lax.ppermute(m, 'row', plan.pairs(k)) for k, m in direct.items()}]
    ppermute x2, starting transfers between devices: 6.8 us -> 2.71 us  [exchange(): lax.ppermute(far, 'row', [(i, i ^ (3 if i in INNER else 5)) for i in rang...]
    ppermute x2, starting transfers between devices: 3.89 us -> 0.44 us  [exchange(): lax.ppermute(near, 'row', [(i, i ^ (1 if i in INNER else 6)) for i in ran...]
    ppermute x7, starting transfers between devices: 15.1 us -> 17.1 us  [exchange(): sent = {k: lax.ppermute(m, 'row', plan.pairs(k)) for k, m in direct.items()}]
    all_to_all x1, blocking collectives: 11.3 us -> 12.8 us  [body(): gathered = lax.all_to_all(gathered, ('row', 'col'), 0, 0)]
  transfers between devices with their start and end apart: 14 -> 14, of which waited for: 6 -> 5; matrix products, arithmetic and copies ran while one was open for 0% -> 0% of each run, Pallas kernels for 22% -> 21%
where the time goes in v17:
time: 126 us
  waiting for transfers between devices  37.4 us (30%)
  Pallas kernels  35.4 us (28%)
  starting transfers between devices  33.5 us (27%)
  blocking collectives  12.8 us (10%)
  local copies, waits for them, and re-layouts  5.74 us (5%)
    ppermute x7, waiting for transfers between devices, exchange(): sent = {k: lax.ppermute(m, 'row', plan.pairs(k)) for k, m in direct.items()}  24.3 us
    pallas_call x7, Pallas kernels, couple(): call(kernel, 'couple', [shape] * outs, [vmem()] * 2 + [pl.BlockSpec(memor...  18.1 us
    ppermute x7, starting transfers between devices, exchange(): sent = {k: lax.ppermute(m, 'row', plan.pairs(k)) for k, m in direct.items()}  17.1 us
    all_to_all x1, blocking collectives, body(): gathered = lax.all_to_all(gathered, ('row', 'col'), 0, 0)  12.8 us
    ppermute x2, waiting for transfers between devices, exchange(): lax.ppermute(far, 'row', [(i, i ^ (3 if i in INNER else 5)) for i in rang...  12.3 us
    ppermute x1, starting transfers between devices, exchange(): over = sent[7] if first else lax.ppermute(beyond[0], 'row', plan.pairs(7))  11.8 us
    unnamed x14, local copies, waits for them, and re-layouts  5.74 us
    pallas_call x1, Pallas kernels, spread(): call(kernel, 'spread', jax.ShapeDtypeStruct((span, clusters, 2 * width, s...  4.86 us
  transfers between devices with their start and end apart: 14, of which 5 were waited for; matrix products, arithmetic and copies ran while one was open for 0% of the time, Pallas kernels for 21%

profile of v17, /device:TPU:0, one launch (start us, length us, event | category | flops | bytes accessed | tf_op | source)
XLA Modules:
  0.0 125.7 jit_solution(9086552124209456041)
XLA Ops:
  0.6 0.7 copy-done.4
  1.3 0.7 copy-done.5
  2.0 2.0 %pack.1 = (bf16[528,384]{1,0:T(8,128)(2,1)S(1)}, bf16[528,384]{1,0:T(8,128)(2,1)S(1)}, bf16[528,384]{1,0:T(8,128)(2,1)S(1)}, bf16[528,384]{1,0:T(8,128)(2,1)S(1)...) custom-call(s32[1,4,7]{2,1,0:T(4,128)S(1)} %bitcast.12, f32[3,1024,128]{2,1,0:T(8,128)} %right_ref.3, ...), custom_call_target="tpu_custom_call" | custom-call | bytes 1048576 | tf_op jit(solution)/shard_map/pack/pallas_call | solution.py:157
  4.0 0.7 collective-permute-start
  4.7 5.9 %collective-permute-start.1 = (bf16[528,384]{1,0:T(8,128)(2,1)S(1)}, bf16[528,384]{1,0:T(8,128)(2,1)S(1)}, u32[]{:S(2)}, u32[]{:S(2)}) collective-permute-start(bf16[528,384]{1,0:T(8,128)(2,1)S(1)} %get-tuple-element.33), channel_id=1, source_target_pairs={{0,8},{4,12},{8,0},{12,4},{16,24},{20,28},{24,16},{28,20},{1,9},{5... | collective-permute-start | bytes 1216520 | tf_op jit(solution)/shard_map/ppermute | solution.py:245
  10.6 1.5 %collective-permute-start.2 = (bf16[528,384]{1,0:T(8,128)(2,1)S(1)}, bf16[528,384]{1,0:T(8,128)(2,1)S(1)}, u32[]{:S(2)}, u32[]{:S(2)}) collective-permute-start(bf16[528,384]{1,0:T(8,128)(2,1)S(1)} %get-tuple-element.34), channel_id=1, source_target_pairs={{0,4},{4,0},{8,12},{12,8},{16,20},{20,16},{24,28},{28,24},{1,5},{5... | collective-permute-start | bytes 1216520 | tf_op jit(solution)/shard_map/ppermute | solution.py:245
  12.1 0.0 collective-permute-start.5
  12.1 4.2 %collective-permute-start.6 = (bf16[528,384]{1,0:T(8,128)(2,1)S(1)}, bf16[528,384]{1,0:T(8,128)(2,1)S(1)}, u32[]{:S(2)}, u32[]{:S(2)}) collective-permute-start(bf16[528,384]{1,0:T(8,128)(2,1)S(1)} %get-tuple-element.40), channel_id=1, source_target_pairs={{0,28},{4,24},{24,4},{28,0},{1,29},{5,25},{25,5},{29,1},{2,30},{6,... | collective-permute-start | bytes 1216520 | tf_op jit(solution)/shard_map/ppermute | solution.py:245
  16.4 0.0 copy-start.1
  16.4 2.8 %copy-done.1 = bf16[8,24,128,128]{3,2,1,0:T(8,128)(2,1)S(1)} copy-done((bf16[8,24,128,128]{3,2,1,0:T(8,128)(2,1)S(1)}, bf16[8,24,128,128]{3,2,1,0:T(8,128)(2,1)}, u32[]{:S(2)}) %copy-start.1) | copy-done | bytes 6291480
  19.1 1.6 %copy-done.2 = bf16[8,8,128,128]{3,2,1,0:T(8,128)(2,1)S(1)} copy-done((bf16[8,8,128,128]{3,2,1,0:T(8,128)(2,1)S(1)}, bf16[8,8,128,128]{3,2,1,0:T(8,128)(2,1)}, u32[]{:S(2)}) %copy-start.2) | copy-done | bytes 2097176
  20.7 4.9 %spread.1.dense_ref = bf16[7,8,256,512]{3,2,1,0:T(8,128)(2,1)S(1)} custom-call(s32[8,24]{1,0:T(8,128)S(1)} %copy-done.6, bf16[8,24,128,128]{3,2,1,0:T(8,128)(2,1)S(1)} %copy-done.1, bf16[8,8,128,128]{3,2,1,0:T(8,128)(2,1)S(1)} %copy-done.2), custom_call_target="tpu_custom_call" | custom-call | bytes 16777216 | tf_op jit(solution)/shard_map/spread/pallas_call | solution.py:338
  25.6 0.0 collective-permute-done.1.refs_2_
  25.6 16.3 %collective-permute-done.2.refs_3_ = bf16[528,384]{1,0:T(8,128)(2,1)S(1)} collective-permute-done((bf16[528,384]{1,0:T(8,128)(2,1)S(1)}, bf16[528,384]{1,0:T(8,128)(2,1)S(1)}, u32[]{:S(2)}, u32[]{:S(2)}) %collective-permute-start.2) | collective-permute-done | bytes 405536 | tf_op jit(solution)/shard_map/ppermute | solution.py:245
  42.0 0.0 collective-permute-done.refs_0_.refs_2_
  42.0 3.7 %couple.7 = (f32[8,128,384]{2,1,0:T(8,128)S(1)}, f32[8,128,384]{2,1,0:T(8,128)S(1)}) custom-call(bf16[7,8,256,512]{3,2,1,0:T(8,128)(2,1)S(1)} %spread.1.dense_ref, f32[1,128]{1,0:T(1,128)S(1)} %bitcast.3, bf16[1040,384]{1,0:T(8,128)(2,1)S(1)} %collective-permute-done.refs_0_.refs_2_, bf16[528,384]{1,0:T(8,128)(2,1)S(1)} %get-tuple-element.32.refs_1_.refs_4_, ...), custom_call_target="tpu_custom_call" | custom-call | flops 2415919104 | bytes 4194304 | tf_op jit(solution)/shard_map/couple/pallas_call | solution.py:396
  45.6 1.4 %relay.2 = (bf16[528,384]{1,0:T(8,128)(2,1)S(1)}, bf16[528,384]{1,0:T(8,128)(2,1)S(1)}, bf16[528,384]{1,0:T(8,128)(2,1)S(1)}, s32[3,4]{1,0:T(4,128)S(1)}) custom-call(s32[1,4,7]{2,1,0:T(4,128)S(1)} %bitcast.13, bf16[1040,384]{1,0:T(8,128)(2,1)S(1)} %get-tuple-element.31.refs_1_, bf16[1040,384]{1,0:T(8,128)(2,1)S(1)} %collective-permute-done.refs_0_.refs_2_, ...), custom_call_target="tpu_custom_call" | custom-call | bytes 1048576 | tf_op jit(solution)/shard_map/relay/pallas_call | solution.py:232
  47.1 0.1 collective-permute-start.4
  47.1 0.1 collective-permute-start.3
  47.2 0.2 levels.1.refs_3_
  47.4 0.0 collective-permute-done.6.refs_2_
  47.4 2.7 %couple.8 = (f32[8,128,384]{2,1,0:T(8,128)S(1)}, f32[8,128,384]{2,1,0:T(8,128)S(1)}) custom-call(bf16[7,8,256,512]{3,2,1,0:T(8,128)(2,1)S(1)} %spread.1.dense_ref, f32[1,128]{1,0:T(1,128)S(1)} %bitcast.4, bf16[528,384]{1,0:T(8,128)(2,1)S(1)} %collective-permute-done.5.refs_0_, bf16[528,384]{1,0:T(8,128)(2,1)S(1)} %get-tuple-element.39.refs_1_, ...), custom_call_target="tpu_custom_call" | custom-call | flops 1610612736 | bytes 4194304 | tf_op jit(solution)/shard_map/couple/pallas_call | solution.py:396
  50.1 12.3 %collective-permute-done.4.refs_0_ = bf16[528,384]{1,0:T(8,128)(2,1)S(1)} collective-permute-done((bf16[528,384]{1,0:T(8,128)(2,1)S(1)}, bf16[528,384]{1,0:T(8,128)(2,1)S(1)}, u32[]{:S(2)}, u32[]{:S(2)}) %collective-permute-start.4) | collective-permute-done | bytes 405536 | tf_op jit(solution)/shard_map/ppermute | solution.py:258
  62.5 1.4 %couple.9 = (f32[8,128,384]{2,1,0:T(8,128)S(1)}, f32[8,128,384]{2,1,0:T(8,128)S(1)}) custom-call(bf16[7,8,256,512]{3,2,1,0:T(8,128)(2,1)S(1)} %spread.1.dense_ref, f32[1,128]{1,0:T(1,128)S(1)} %bitcast.5, bf16[528,384]{1,0:T(8,128)(2,1)S(1)} %collective-permute-done.4.refs_0_, f32[8,128,384]{2,1,0:T(8,128)S(1)} %get-tuple-element.42.refs_1_, ...), custom_call_target="tpu_custom_call" | custom-call | flops 805306368 | bytes 4194304 | tf_op jit(solution)/shard_map/couple/pallas_call | solution.py:396
  63.9 2.2 %finish_first.1 = (f32[8,128,384]{2,1,0:T(8,128)S(1)}, bf16[1024,384]{1,0:T(8,128)(2,1)S(1)}, bf16[512,384]{1,0:T(8,128)(2,1)S(1)}, bf16[512,384]{1,0:T(8,128)(2...) custom-call(bf16[7,8,256,512]{3,2,1,0:T(8,128)(2,1)S(1)} %spread.1.dense_ref, f32[1,128]{1,0:T(1,128)S(1)} %bitcast.6, ...), custom_call_target="tpu_custom_call" | custom-call | flops 805306368 | bytes 8388608 | tf_op jit(solution)/shard_map/finish_first/pallas_call | solution.py:442
  66.2 0.7 collective-permute-start.7
  66.9 3.3 %collective-permute-start.8 = (bf16[512,384]{1,0:T(8,128)(2,1)S(1)}, bf16[512,384]{1,0:T(8,128)(2,1)S(1)}, u32[]{:S(2)}, u32[]{:S(2)}) collective-permute-start(bf16[512,384]{1,0:T(8,128)(2,1)S(1)} %get-tuple-element.48), channel_id=1, source_target_pairs={{0,8},{4,12},{8,0},{12,4},{16,24},{20,28},{24,16},{28,20},{1,9},{5... | collective-permute-start | bytes 1179656 | tf_op jit(solution)/shard_map/ppermute | solution.py:245
  70.3 2.2 %collective-permute-start.11 = (bf16[512,384]{1,0:T(8,128)(2,1)S(1)}, bf16[512,384]{1,0:T(8,128)(2,1)S(1)}, u32[]{:S(2)}, u32[]{:S(2)}) collective-permute-start(bf16[512,384]{1,0:T(8,128)(2,1)S(1)} %get-tuple-element.53), channel_id=1, source_target_pairs={{0,12},{4,8},{8,4},{12,0},{16,28},{20,24},{24,20},{28,16},{1,13},{... | collective-permute-start | bytes 1179656 | tf_op jit(solution)/shard_map/ppermute | solution.py:245
  72.4 0.0 collective-permute-start.12
  72.4 8.0 %collective-permute-done.8.refs_1_ = bf16[512,384]{1,0:T(8,128)(2,1)S(1)} collective-permute-done((bf16[512,384]{1,0:T(8,128)(2,1)S(1)}, bf16[512,384]{1,0:T(8,128)(2,1)S(1)}, u32[]{:S(2)}, u32[]{:S(2)}) %collective-permute-start.8) | collective-permute-done | bytes 393248 | tf_op jit(solution)/shard_map/ppermute | solution.py:245
  80.4 2.5 %couple.10.refs_3_ = f32[8,128,384]{2,1,0:T(8,128)S(1)} custom-call(bf16[7,8,256,512]{3,2,1,0:T(8,128)(2,1)S(1)} %spread.1.dense_ref, f32[1,128]{1,0:T(1,128)S(1)} %bitcast.7, bf16[512,384]{1,0:T(8,128)(2,1)S(1)} %get-tuple-element.47.refs_0_, bf16[512,384]{1,0:T(8,128)(2,1)S(1)} %collective-permute-done.8.refs_1_), custom_call_target="tpu_custom_call" | custom-call | flops 1610612736 | bytes 4194304 | tf_op jit(solution)/shard_map/couple/pallas_call | solution.py:396
  82.9 0.0 collective-permute-done.7.refs_2_
  82.9 0.7 relay.3
  83.7 2.7 %collective-permute-start.13 = (bf16[512,384]{1,0:T(8,128)(2,1)S(1)}, bf16[512,384]{1,0:T(8,128)(2,1)S(1)}, u32[]{:S(2)}, u32[]{:S(2)}) collective-permute-start(bf16[512,384]{1,0:T(8,128)(2,1)S(1)} %get-tuple-element.55), channel_id=1, source_target_pairs={{0,20},{4,16},{8,4},{12,0},{16,28},{20,24},{24,12},{28,8},{1,21},{... | collective-permute-start | bytes 1179656 | tf_op jit(solution)/shard_map/ppermute | solution.py:258
  86.3 11.8 %collective-permute-start.10 = (bf16[512,384]{1,0:T(8,128)(2,1)S(1)}, bf16[512,384]{1,0:T(8,128)(2,1)S(1)}, u32[]{:S(2)}, u32[]{:S(2)}) collective-permute-start(bf16[512,384]{1,0:T(8,128)(2,1)S(1)} %get-tuple-element.52), channel_id=1, source_target_pairs={{0,28},{4,24},{24,4},{28,0},{1,29},{5,25},{25,5},{29,1},{2,30},{6,... | collective-permute-start | bytes 1179656 | tf_op jit(solution)/shard_map/ppermute | solution.py:259
  98.1 0.4 collective-permute-start.9
  98.5 1.3 %prepare.1.refs_6_ = f32[8,384]{1,0:T(8,128)S(1)} custom-call(f32[3,1024,128]{2,1,0:T(8,128)S(1)} %copy-done, f32[8,128,384]{2,1,0:T(8,128)S(1)} %get-tuple-element.45.image_ref.refs_4_, bf16[512,384]{1,0:T(8,128)(2,1)S(1)} %get-tuple-element.51.refs_0_._), custom_call_target="tpu_custom_call" | custom-call | flops 8388608 | bytes 4194304 | tf_op jit(solution)/shard_map/prepare/pallas_call | solution.py:498
  99.8 2.6 %couple.13 = (f32[8,128,384]{2,1,0:T(8,128)}, f32[8,128,384]{2,1,0:T(8,128)S(1)}) custom-call(bf16[7,8,256,512]{3,2,1,0:T(8,128)(2,1)S(1)} %spread.1.dense_ref, f32[1,128]{1,0:T(1,128)S(1)} %bitcast.8, bf16[512,384]{1,0:T(8,128)(2,1)S(1)} %get-tuple-element.51.refs_0_._, bf16[528,384]{1,0:T(8,128)(2,1)S(1)} %collective-permute-done.3.refs_0_.refs_1_, ...), custom_call_target="tpu_custom_call" | custom-call | flops 805306368 | bytes 4194304 | tf_op jit(solution)/shard_map/couple/pallas_call | solution.py:396
  102.4 0.0 collective-permute-done.11.refs_0_
  102.4 0.0 collective-permute-done.12.refs_1_
  102.4 0.0 collective-permute-done.13.refs_2_
  102.4 3.7 %couple.11.refs_2_ = f32[8,128,384]{2,1,0:T(8,128)S(1)} custom-call(bf16[7,8,256,512]{3,2,1,0:T(8,128)(2,1)S(1)} %spread.1.dense_ref, f32[1,128]{1,0:T(1,128)S(1)} %bitcast.9, bf16[512,384]{1,0:T(8,128)(2,1)S(1)} %collective-permute-done.11.refs_0_, bf16[512,384]{1,0:T(8,128)(2,1)S(1)} %collective-permute-done.12.refs_1_, ...), custom_call_target="tpu_custom_call" | custom-call | flops 2415919104 | bytes 4194304 | tf_op jit(solution)/shard_map/couple/pallas_call | solution.py:396
  106.1 0.1 collective-permute-done.10.refs_1_
  106.2 1.4 %couple.12.refs_1_ = f32[8,128,384]{2,1,0:T(8,128)S(1)} custom-call(bf16[7,8,256,512]{3,2,1,0:T(8,128)(2,1)S(1)} %spread.1.dense_ref, f32[1,128]{1,0:T(1,128)S(1)} %bitcast.10, bf16[512,384]{1,0:T(8,128)(2,1)S(1)} %get-tuple-element.51.refs_0_._, bf16[512,384]{1,0:T(8,128)(2,1)S(1)} %collective-permute-done.10.refs_1_, f32[8,128,384]{2,1,0:T(8,128)S(1)} %couple.11.refs_2_), custom_call_target="tpu_custom_call" | custom-call | flops 805306368 | bytes 4194304 | tf_op jit(solution)/shard_map/couple/pallas_call | solution.py:396
  107.7 0.7 collective-permute-done.9.refs_0_
  108.3 1.9 %finish_second.1 = (f32[8,128,384]{2,1,0:T(8,128)S(1)}, f32[32,8,128]{2,1,0:T(8,128)S(1)}) custom-call(bf16[7,8,256,512]{3,2,1,0:T(8,128)(2,1)S(1)} %spread.1.dense_ref, f32[1,128]{1,0:T(1,128)S(1)} %bitcast.11, bf16[512,384]{1,0:T(8,128)(2,1)S(1)} %collective-permute-done.9.refs_0_, f32[8,128,384]{2,1,0:T(8,128)S(1)} %couple.12.refs_1_, ...), custom_call_target="tpu_custom_call" | custom-call | flops 805306368 | bytes 8388608 | tf_op jit(solution)/shard_map/finish_second/pallas_call | solution.py:555
  110.3 12.8 %all_to_all.5.gathered_ref = f32[32,8,128]{2,1,0:T(8,128)S(1)} all-to-all(f32[32,8,128]{2,1,0:T(8,128)S(1)} %get-tuple-element.59), channel_id=1, replica_groups=mesh['row'=8,'col'=4] {'row','col'}, dimensions={0} | all-to-all | bytes 262144 | tf_op jit(solution)/shard_map/all_to_all | solution.py:677
  123.1 2.6 %final.1 = (f32[3,1024,128]{2,1,0:T(8,128)}, f32[3,1024,128]{2,1,0:T(8,128)}) custom-call(f32[3,1024,128]{2,1,0:T(8,128)S(1)} %copy-done, f32[8,128,384]{2,1,0:T(8,128)S(1)} %get-tuple-element.45.image_ref.refs_4_, f32[8,128,384]{2,1,0:T(8,128)S(1)} %get-tuple-element.58.later_ref, f32[32,8,128]{2,1,0:T(8,128)S(1)} %all_to_all.5.gathered_ref), custom_call_target="tpu_custom_call" | custom-call | tf_op jit(solution)/shard_map/final/pallas_call | solution.py:631
  (11 shorter events, 0.0 us)
Async XLA Ops:
  0.6 0.7 copy-start.4
  1.3 0.7 copy-start.5
  2.0 14.4 %copy-start.6 = (s32[8,24]{1,0:T(8,128)S(1)}, s32[8,24]{1,0:T(8,128)}, u32[]{:S(2)}) copy-start(s32[8,24]{1,0:T(8,128)} %slot_ref.1) | copy-start | bytes 2308
  4.0 37.9 %collective-permute-start = (bf16[1040,384]{1,0:T(8,128)(2,1)S(1)}, bf16[1040,384]{1,0:T(8,128)(2,1)S(1)}, u32[]{:S(2)}, u32[]{:S(2)}) collective-permute-start(bf16[1040,384]{1,0:T(8,128)(2,1)S(1)} %get-tuple-element.31.refs_1_), channel_id=1, source_target_pairs={{8,16},{12,20},{16,8},{20,12},{9,17},{13,21},{17,9},{21,13},{10,18... | collective-permute-start | bytes 2396168 | tf_op jit(solution)/shard_map/ppermute | solution.py:250
  4.7 20.9 %collective-permute-start.1 = (bf16[528,384]{1,0:T(8,128)(2,1)S(1)}, bf16[528,384]{1,0:T(8,128)(2,1)S(1)}, u32[]{:S(2)}, u32[]{:S(2)}) collective-permute-start(bf16[528,384]{1,0:T(8,128)(2,1)S(1)} %get-tuple-element.33), channel_id=1, source_target_pairs={{0,8},{4,12},{8,0},{12,4},{16,24},{20,28},{24,16},{28,20},{1,9},{5... | collective-permute-start | bytes 1216520 | tf_op jit(solution)/shard_map/ppermute | solution.py:245
  10.6 31.4 %collective-permute-start.2 = (bf16[528,384]{1,0:T(8,128)(2,1)S(1)}, bf16[528,384]{1,0:T(8,128)(2,1)S(1)}, u32[]{:S(2)}, u32[]{:S(2)}) collective-permute-start(bf16[528,384]{1,0:T(8,128)(2,1)S(1)} %get-tuple-element.34), channel_id=1, source_target_pairs={{0,4},{4,0},{8,12},{12,8},{16,20},{20,16},{24,28},{28,24},{1,5},{5... | collective-permute-start | bytes 1216520 | tf_op jit(solution)/shard_map/ppermute | solution.py:245
  12.1 35.3 %collective-permute-start.5 = (bf16[528,384]{1,0:T(8,128)(2,1)S(1)}, bf16[528,384]{1,0:T(8,128)(2,1)S(1)}, u32[]{:S(2)}, u32[]{:S(2)}) collective-permute-start(bf16[528,384]{1,0:T(8,128)(2,1)S(1)} %get-tuple-element.38), channel_id=1, source_target_pairs={{0,12},{4,8},{8,4},{12,0},{16,28},{20,24},{24,20},{28,16},{1,13},{... | collective-permute-start | bytes 1216520 | tf_op jit(solution)/shard_map/ppermute | solution.py:245
  12.1 35.3 %collective-permute-start.6 = (bf16[528,384]{1,0:T(8,128)(2,1)S(1)}, bf16[528,384]{1,0:T(8,128)(2,1)S(1)}, u32[]{:S(2)}, u32[]{:S(2)}) collective-permute-start(bf16[528,384]{1,0:T(8,128)(2,1)S(1)} %get-tuple-element.40), channel_id=1, source_target_pairs={{0,28},{4,24},{24,4},{28,0},{1,29},{5,25},{25,5},{29,1},{2,30},{6,... | collective-permute-start | bytes 1216520 | tf_op jit(solution)/shard_map/ppermute | solution.py:245
  16.4 2.8 %copy-start.1 = (bf16[8,24,128,128]{3,2,1,0:T(8,128)(2,1)S(1)}, bf16[8,24,128,128]{3,2,1,0:T(8,128)(2,1)}, u32[]{:S(2)}) copy-start(bf16[8,24,128,128]{3,2,1,0:T(8,128)(2,1)} %ks_ref.1) | copy-start | bytes 18874372
  19.1 1.6 %copy-start.2 = (bf16[8,8,128,128]{3,2,1,0:T(8,128)(2,1)S(1)}, bf16[8,8,128,128]{3,2,1,0:T(8,128)(2,1)}, u32[]{:S(2)}) copy-start(bf16[8,8,128,128]{3,2,1,0:T(8,128)(2,1)} %correlation_ref.1) | copy-start | bytes 6291460
  20.7 21.2 %copy-start.3 = (f32[128]{0:T(128)S(1)}, f32[128]{0:T(128)}, u32[]{:S(2)}) copy-start(f32[128]{0:T(128)} %param.9) | copy-start | bytes 1540
  47.1 15.4 %collective-permute-start.4 = (bf16[528,384]{1,0:T(8,128)(2,1)S(1)}, bf16[528,384]{1,0:T(8,128)(2,1)S(1)}, u32[]{:S(2)}, u32[]{:S(2)}) collective-permute-start(bf16[528,384]{1,0:T(8,128)(2,1)S(1)} %get-tuple-element.37), channel_id=1, source_target_pairs={{0,20},{4,16},{8,4},{12,0},{16,28},{20,24},{24,12},{28,8},{1,21},{... | collective-permute-start | bytes 1216520 | tf_op jit(solution)/shard_map/ppermute | solution.py:258
  47.1 16.8 %collective-permute-start.3 = (bf16[528,384]{1,0:T(8,128)(2,1)S(1)}, bf16[528,384]{1,0:T(8,128)(2,1)S(1)}, u32[]{:S(2)}, u32[]{:S(2)}) collective-permute-start(bf16[528,384]{1,0:T(8,128)(2,1)S(1)} %get-tuple-element.36), channel_id=1, source_target_pairs={{0,24},{4,28},{8,12},{12,8},{16,20},{20,16},{24,0},{28,4},{1,25},{... | collective-permute-start | bytes 1216520 | tf_op jit(solution)/shard_map/ppermute | solution.py:257
  62.5 1.5 %copy-start = (f32[3,1024,128]{2,1,0:T(8,128)S(1)}, f32[3,1024,128]{2,1,0:T(8,128)}, u32[]{:S(2)}) copy-start(f32[3,1024,128]{2,1,0:T(8,128)} %right_ref.3) | copy-start | bytes 4718596
  66.2 16.7 %collective-permute-start.7 = (bf16[1024,384]{1,0:T(8,128)(2,1)S(1)}, bf16[1024,384]{1,0:T(8,128)(2,1)S(1)}, u32[]{:S(2)}, u32[]{:S(2)}) collective-permute-start(bf16[1024,384]{1,0:T(8,128)(2,1)S(1)} %get-tuple-element.46.refs_1_), channel_id=1, source_target_pairs={{8,16},{12,20},{16,8},{20,12},{9,17},{13,21},{17,9},{21,13},{10,18... | collective-permute-start | bytes 2359304 | tf_op jit(solution)/shard_map/ppermute | solution.py:250
  66.9 13.5 %collective-permute-start.8 = (bf16[512,384]{1,0:T(8,128)(2,1)S(1)}, bf16[512,384]{1,0:T(8,128)(2,1)S(1)}, u32[]{:S(2)}, u32[]{:S(2)}) collective-permute-start(bf16[512,384]{1,0:T(8,128)(2,1)S(1)} %get-tuple-element.48), channel_id=1, source_target_pairs={{0,8},{4,12},{8,0},{12,4},{16,24},{20,28},{24,16},{28,20},{1,9},{5... | collective-permute-start | bytes 1179656 | tf_op jit(solution)/shard_map/ppermute | solution.py:245
  70.3 32.1 %collective-permute-start.11 = (bf16[512,384]{1,0:T(8,128)(2,1)S(1)}, bf16[512,384]{1,0:T(8,128)(2,1)S(1)}, u32[]{:S(2)}, u32[]{:S(2)}) collective-permute-start(bf16[512,384]{1,0:T(8,128)(2,1)S(1)} %get-tuple-element.53), channel_id=1, source_target_pairs={{0,12},{4,8},{8,4},{12,0},{16,28},{20,24},{24,20},{28,16},{1,13},{... | collective-permute-start | bytes 1179656 | tf_op jit(solution)/shard_map/ppermute | solution.py:245
  72.4 30.0 %collective-permute-start.12 = (bf16[512,384]{1,0:T(8,128)(2,1)S(1)}, bf16[512,384]{1,0:T(8,128)(2,1)S(1)}, u32[]{:S(2)}, u32[]{:S(2)}) collective-permute-start(bf16[512,384]{1,0:T(8,128)(2,1)S(1)} %get-tuple-element.54), channel_id=1, source_target_pairs={{0,4},{4,0},{8,12},{12,8},{16,20},{20,16},{24,28},{28,24},{1,5},{5... | collective-permute-start | bytes 1179656 | tf_op jit(solution)/shard_map/ppermute | solution.py:245
  83.7 18.7 %collective-permute-start.13 = (bf16[512,384]{1,0:T(8,128)(2,1)S(1)}, bf16[512,384]{1,0:T(8,128)(2,1)S(1)}, u32[]{:S(2)}, u32[]{:S(2)}) collective-permute-start(bf16[512,384]{1,0:T(8,128)(2,1)S(1)} %get-tuple-element.55), channel_id=1, source_target_pairs={{0,20},{4,16},{8,4},{12,0},{16,28},{20,24},{24,12},{28,8},{1,21},{... | collective-permute-start | bytes 1179656 | tf_op jit(solution)/shard_map/ppermute | solution.py:258
  86.3 19.9 %collective-permute-start.10 = (bf16[512,384]{1,0:T(8,128)(2,1)S(1)}, bf16[512,384]{1,0:T(8,128)(2,1)S(1)}, u32[]{:S(2)}, u32[]{:S(2)}) collective-permute-start(bf16[512,384]{1,0:T(8,128)(2,1)S(1)} %get-tuple-element.52), channel_id=1, source_target_pairs={{0,28},{4,24},{24,4},{28,0},{1,29},{5,25},{25,5},{29,1},{2,30},{6,... | collective-permute-start | bytes 1179656 | tf_op jit(solution)/shard_map/ppermute | solution.py:259
  98.1 10.2 %collective-permute-start.9 = (bf16[512,384]{1,0:T(8,128)(2,1)S(1)}, bf16[512,384]{1,0:T(8,128)(2,1)S(1)}, u32[]{:S(2)}, u32[]{:S(2)}) collective-permute-start(bf16[512,384]{1,0:T(8,128)(2,1)S(1)} %get-tuple-element.50), channel_id=1, source_target_pairs={{0,24},{4,28},{8,12},{12,8},{16,20},{20,16},{24,0},{28,4},{1,25},{... | collective-permute-start | bytes 1179656 | tf_op jit(solution)/shard_map/ppermute | solution.py:257
